TPU v7x, 256 devices: a whole 4x4x8 slice. The times are simulated.
256 devices in a mesh: day: 8 (over x, core), tile: 32 (over z, y).
Axes of the slice: x: 4, y: 4, z: 8, core: 2. Of those that a mesh axis runs over, the one named last changes fastest.
Arguments:
- seeds: bfloat16 [8, 65536, 128], P('day', 'tile'), may hold values from -6 to 6
- blocks: bfloat16 [8, 512, 3, 128, 128], P('day', 'tile'), may hold values from -0.3125 to 0.3125
- dest_tiles: int32 [8, 512, 3], P('day', 'tile'), may hold values from 0 to 511, as said below
Outputs:
- ftle: float32 [8, 64, 65536], P('day', None, 'tile')
- minor: float32 [8, 64, 65536], P('day', None, 'tile')
Inputs may be any that keep to these rules, and one draw needn't show every extreme that they name: dest_tiles[d, t, 0] = t. For each section and each aligned block of 16 tiles, at most one of its blocks names a tile of any one other aligned block; in each section some aligned block names a tile in every other aligned block. The other destinations lie in the source tile's own aligned block.
All inputs are finite; a program needn't handle non-finite values.
Results may differ from a plain program's by a relative error of at most 0.035.
Values may be sent and summed in bfloat16 or wider, within the bound.
No kernel may reach another device: no remote copies, remote signals or barrier semaphores. Data moves between devices by JAX's collectives and lax.ppermute only.
A program may use at most 64 MiB of HBM per device.

v0:
```python
import functools

import jax
import jax.numpy as jnp
from jax import lax
from jax.experimental import pallas as pl
from jax.experimental.pallas import tpu as pltpu
from jax.sharding import PartitionSpec as P

VMEM = pl.BlockSpec(memory_space=pltpu.VMEM)
SMEM = pl.BlockSpec(memory_space=pltpu.SMEM)
HBM = pl.BlockSpec(memory_space=pltpu.HBM)
PARAMS = pltpu.CompilerParams(vmem_limit_bytes=56 * 1024 * 1024)
SMALL = pltpu.CompilerParams(vmem_limit_bytes=16 * 1024 * 1024)
PART = 8
BLOCK, SOURCE, HOME, LANDING = range(4)


def shifted(n, by):
    return [(i, (i + by) % n) for i in range(n)]


def product(v, block):
    return lax.dot_general(v, block, (((1,), (1,)), ((), ())), preferred_element_type=jnp.float32)


def send_products(table, state_ref, blocks_scr, out_ref, stage, out_sems):
    peers = stage.shape[0]
    copies = []
    for p in range(peers):
        v = state_ref[table[SOURCE, p]]
        stage[p] = product(v, blocks_scr[table[BLOCK, p]]).astype(jnp.bfloat16)
        if p % PART == PART - 1:
            part = pl.ds(p + 1 - PART, PART)
            copy = pltpu.make_async_copy(stage.at[part], out_ref.at[part], out_sems.at[p // PART])
            copy.start()
            copies.append(copy)
    for copy in copies:
        copy.wait()


def arrival_copies(arrived_ref, arrived_scr, sems):
    parts = [pl.ds(p, PART) for p in range(0, arrived_scr.shape[0], PART)]
    return [
        pltpu.make_async_copy(arrived_ref.at[part], arrived_scr.at[part], sems.at[n]) for n, part in enumerate(parts)
    ]


def add_arrived(table, copies, arrived_scr, gathered):
    gathered[...] = jnp.zeros_like(gathered)
    for n, copy in enumerate(copies):
        copy.wait()
        for p in range(n * PART, (n + 1) * PART):
            home = table[LANDING, p]
            gathered[home] = gathered[home] + arrived_scr[p].astype(jnp.float32)


def first_body(table, seeds_ref, blocks_ref, out_ref, state_ref, blocks_scr, stage, state_scr, sems, out_sems):
    load = pltpu.make_async_copy(blocks_ref, blocks_scr, sems.at[0])
    load.start()
    for t in range(state_scr.shape[0]):
        state_scr[t] = jnp.transpose(seeds_ref[t].astype(jnp.float32)).astype(jnp.bfloat16)
    store = pltpu.make_async_copy(state_scr, state_ref, sems.at[2])
    store.start()
    load.wait()
    send_products(table, state_scr, blocks_scr, out_ref, stage, out_sems)
    store.wait()


def send_body(
    before, table, arrived_ref, local_ref, blocks_ref, out_ref, state_ref,
    blocks_scr, stage, state_scr, arrived_scr, gathered, local_scr, sems, out_sems, in_sems,
):
    arrivals = arrival_copies(arrived_ref, arrived_scr, in_sems)
    load_local = pltpu.make_async_copy(local_ref, local_scr, sems.at[1])
    load = pltpu.make_async_copy(blocks_ref, blocks_scr, sems.at[0])
    for copy in [*arrivals, load_local, load]:
        copy.start()
    add_arrived(before, arrivals, arrived_scr, gathered)
    load_local.wait()
    for t in range(state_scr.shape[0]):
        state_scr[t] = (gathered[t] + local_scr[t]).astype(jnp.bfloat16)
    store = pltpu.make_async_copy(state_scr, state_ref, sems.at[2])
    store.start()
    load.wait()
    send_products(table, state_scr, blocks_scr, out_ref, stage, out_sems)
    store.wait()


def send(tables, carried, blocks, peers):
    points = blocks.shape[1]
    first = len(carried) == 1
    rows = points
    tiles = carried[-1].shape[0]
    scratch = [
        pltpu.VMEM(blocks.shape, jnp.bfloat16),
        pltpu.VMEM((peers, rows, points), jnp.bfloat16),
        pltpu.VMEM((tiles, rows, points), jnp.bfloat16),
    ]
    if not first:
        scratch += [
            pltpu.VMEM((peers, rows, points), jnp.bfloat16),
            pltpu.VMEM((tiles + 1, rows, points), jnp.float32),
            pltpu.VMEM((tiles, rows, points), jnp.float32),
        ]
    scratch += [pltpu.SemaphoreType.DMA((3,)), pltpu.SemaphoreType.DMA((peers // PART,))]
    if not first:
        scratch.append(pltpu.SemaphoreType.DMA((peers // PART,)))
    return pl.pallas_call(
        first_body if first else send_body,
        out_shape=(
            jax.ShapeDtypeStruct((peers, rows, points), jnp.bfloat16),
            jax.ShapeDtypeStruct((tiles, rows, points), jnp.bfloat16),
        ),
        in_specs=[SMEM] * len(tables) + ([VMEM] if first else [HBM, HBM]) + [HBM],
        out_specs=(HBM, HBM),
        scratch_shapes=scratch,
        compiler_params=PARAMS,
        cost_estimate=pl.CostEstimate(
            flops=2 * peers * points * points * rows, bytes_accessed=4 << 20, transcendentals=0
        ),
    )(*tables, *carried, blocks)


def keep_body(table, state_ref, blocks_ref, local_ref, total, sem):
    tiles = state_ref.shape[0]
    nnz = blocks_ref.shape[0] // tiles
    for t in range(tiles):
        total[t] = product(state_ref[t], blocks_ref[t * nnz])
    for t in range(tiles):
        for k in range(nnz - 1):
            home = table[HOME, t * (nnz - 1) + k]
            total[home] = total[home] + product(state_ref[t], blocks_ref[t * nnz + 1 + k])
    store = pltpu.make_async_copy(total.at[pl.ds(0, tiles)], local_ref, sem)
    store.start()
    store.wait()


def keep(table, state, blocks):
    tiles, rows, points = state.shape
    return pl.pallas_call(
        keep_body,
        out_shape=jax.ShapeDtypeStruct((tiles, rows, points), jnp.float32),
        in_specs=[SMEM, VMEM, VMEM],
        out_specs=HBM,
        scratch_shapes=[pltpu.VMEM((tiles + 1, rows, points), jnp.float32), pltpu.SemaphoreType.DMA],
        compiler_params=PARAMS,
        cost_estimate=pl.CostEstimate(
            flops=2 * blocks.shape[0] * points * points * rows, bytes_accessed=4 << 20, transcendentals=0
        ),
    )(table, state, blocks)


def last_body(before, arrived_ref, local_ref, final_ref, edges_ref, arrived_scr, gathered, local_scr, sem, in_sems):
    arrivals = arrival_copies(arrived_ref, arrived_scr, in_sems)
    load_local = pltpu.make_async_copy(local_ref, local_scr, sem)
    for copy in [*arrivals, load_local]:
        copy.start()
    add_arrived(before, arrivals, arrived_scr, gathered)
    load_local.wait()
    tiles = final_ref.shape[0]
    for t in range(tiles):
        final_ref[t] = (gathered[t] + local_scr[t]).astype(jnp.bfloat16)
    edges_ref[0] = final_ref[0]
    edges_ref[1] = final_ref[tiles - 1]


def last_sum(before, arrived, local):
    tiles, rows, points = local.shape
    return pl.pallas_call(
        last_body,
        out_shape=(
            jax.ShapeDtypeStruct((tiles, rows, points), jnp.bfloat16),
            jax.ShapeDtypeStruct((2, rows, points), jnp.bfloat16),
        ),
        in_specs=[SMEM, HBM, HBM],
        out_specs=(VMEM, VMEM),
        scratch_shapes=[
            pltpu.VMEM(arrived.shape, jnp.bfloat16),
            pltpu.VMEM((tiles + 1, rows, points), jnp.float32),
            pltpu.VMEM((tiles, rows, points), jnp.float32),
            pltpu.SemaphoreType.DMA,
            pltpu.SemaphoreType.DMA((arrived.shape[0] // PART,)),
        ],
        compiler_params=SMALL,
    )(before, arrived, local)


def stretch_tile(ndays, here, dy):
    rows, points = here.shape
    half = rows // 2
    lane = lax.broadcasted_iota(jnp.int32, (rows, points), 1)
    right = pltpu.roll(here, points - 1, 1)
    left = pltpu.roll(here, 1, 1)
    dx = jnp.where(lane == 0, right - here, jnp.where(lane == points - 1, here - left, (right - left) * 0.5))
    a, c = dx[:half], dx[half:]
    b, e = dy[:half], dy[half:]
    c11 = a * a + c * c
    c12 = a * b + c * e
    c22 = b * b + e * e
    gap = c11 - c22
    major = 0.5 * (c11 + c22 + jnp.sqrt(gap * gap + 4.0 * c12 * c12))
    lead = jnp.maximum(major, 1.0)
    det = a * e - b * c
    return jnp.log(lead) / (2.0 * ndays), det * det / lead


def inner_body(ndays, final_ref, ftle_ref, minor_ref):
    tiles, rows, points = final_ref.shape
    for t in range(1, tiles - 1):
        here = final_ref[t].astype(jnp.float32)
        dy = (final_ref[t + 1].astype(jnp.float32) - final_ref[t - 1].astype(jnp.float32)) * 0.5
        at = slice(t * points, (t + 1) * points)
        ftle_ref[:, at], minor_ref[:, at] = stretch_tile(ndays, here, dy)


def edge_body(ndays, place, final_ref, low_ref, high_ref, ftle_in, minor_in, ftle_ref, minor_ref, ftle_scr, minor_scr, sems):
    tiles, rows, points = final_ref.shape
    copies = []
    for i, t in enumerate((0, tiles - 1)):
        here = final_ref[t].astype(jnp.float32)
        below = (final_ref[t - 1] if t > 0 else low_ref[0]).astype(jnp.float32)
        above = (final_ref[t + 1] if t < tiles - 1 else high_ref[0]).astype(jnp.float32)
        one_sided = above - here if t == 0 else here - below
        dy = jnp.where(place[i] == 1, one_sided, (above - below) * 0.5)
        ftle_scr[i], minor_scr[i] = stretch_tile(ndays, here, dy)
        at = pl.ds(t * points, points)
        for n, (scr, ref) in enumerate(((ftle_scr, ftle_ref), (minor_scr, minor_ref))):
            copy = pltpu.make_async_copy(scr.at[i], ref.at[:, at], sems.at[2 * i + n])
            copy.start()
            copies.append(copy)
    for copy in copies:
        copy.wait()


def stretch_inner(final, ndays):
    tiles, rows, points = final.shape
    shape = jax.ShapeDtypeStruct((rows // 2, tiles * points), jnp.float32)
    return pl.pallas_call(
        functools.partial(inner_body, float(ndays)),
        out_shape=(shape, shape),
        in_specs=[VMEM],
        out_specs=(VMEM, VMEM),
        compiler_params=SMALL,
        cost_estimate=pl.CostEstimate(flops=40 * rows * tiles * points, bytes_accessed=2 << 20, transcendentals=0),
    )(final)


def stretch_edges(place, final, low, high, inner, ndays):
    tiles, rows, points = final.shape
    shape = jax.ShapeDtypeStruct((rows // 2, tiles * points), jnp.float32)
    scr = pltpu.VMEM((2, rows // 2, points), jnp.float32)
    return pl.pallas_call(
        functools.partial(edge_body, float(ndays)),
        out_shape=(shape, shape),
        in_specs=[SMEM, VMEM, VMEM, VMEM, HBM, HBM],
        out_specs=(HBM, HBM),
        scratch_shapes=[scr, scr, pltpu.SemaphoreType.DMA((4,))],
        input_output_aliases={4: 0, 5: 1},
        compiler_params=SMALL,
    )(place, final, low, high, *inner)


def own_rows(dest, me, tiles, peers, nnz):
    flat = dest.reshape(tiles * nnz)
    off = dest[:, 1:].reshape(tiles * (nnz - 1))
    peer = jnp.arange(peers, dtype=jnp.int32)
    order = jnp.arange(tiles * nnz, dtype=jnp.int32)
    block = jnp.max(jnp.where(flat[None, :] // tiles == peer[:, None], order, 0), axis=1)
    home = jnp.where(off // tiles == me, off % tiles, tiles)
    return block, block // nnz, home


def landing_row(dest, me, tiles, peers):
    known = dest.reshape(1, -1)
    step = 1
    while step < peers:
        known = jnp.concatenate([known, lax.ppermute(known, "tile", [(i, i ^ step) for i in range(peers)])], axis=0)
        step *= 2
    row_of = jnp.arange(peers, dtype=jnp.int32)
    lands = jnp.max(jnp.where(known // tiles == me, known % tiles, -1), axis=1)
    lands = jnp.where((lands < 0) | (row_of == 0), tiles, lands)
    match = (row_of[:, None] ^ row_of[None, :]) == me
    return jnp.sum(jnp.where(match, lands[None, :], 0), axis=1)


def body(seeds, blocks, dest_tiles):
    tiles, nnz, points = blocks.shape[1:4]
    width = seeds.shape[2]
    ndays, peers = lax.axis_size("day"), lax.axis_size("tile")
    me = lax.axis_index("tile")

    block, source, home = own_rows(dest_tiles[0], me, tiles, peers, nnz)
    first_table = jnp.stack([block, source, home, jnp.zeros_like(home)])
    table = first_table
    seeds = seeds.reshape(tiles, points, width)
    wblk = blocks.reshape(tiles * nnz, points, points)

    for step in range(ndays):
        if step == 0:
            out, state = send((first_table,), (seeds,), wblk, peers)
        else:
            out, state = send((before, table), (arrived, local), wblk, peers)
        arrived = lax.all_to_all(out, "tile", split_axis=0, concat_axis=0, tiled=True)
        local = keep(table, state, wblk)
        if step == 0:
            dest, local = lax.optimization_barrier((dest_tiles[0], local))
            landing = landing_row(dest, me, tiles, peers)
            table = jnp.stack([block, source, home, landing])
        before = table
        if step < ndays - 1:
            table = lax.ppermute(table, "day", shifted(ndays, -1))
            wblk = lax.ppermute(wblk, "day", shifted(ndays, -1))
    final, edges = last_sum(before, arrived, local)
    low = lax.ppermute(edges[1:], "tile", [(i, i + 1) for i in range(peers - 1)])
    high = lax.ppermute(edges[:1], "tile", [(i + 1, i) for i in range(peers - 1)])
    place = jnp.stack([me == 0, me == peers - 1]).astype(jnp.int32)
    inner = stretch_inner(final, ndays)
    ftle, minor = stretch_edges(place, final, low, high, inner, ndays)
    return ftle[None], minor[None]


def solution(mesh):
    in_specs = (P("day", "tile", None), P("day", "tile", None, None, None), P("day", "tile", None))
    out_specs = (P("day", None, "tile"), P("day", None, "tile"))
    return jax.shard_map(body, mesh=mesh, in_specs=in_specs, out_specs=out_specs, check_vma=False)
```

profile of v0, /device:TPU:56, one launch (start us, length us, event | category | flops | bytes accessed | tf_op | source)
XLA Modules:
  0.0 341.0 jit_solution(13260100892791364127)
XLA Ops:
  1.3 0.8 copy.13
  3.1 4.3 %shard_map.50 = (bf16[32,128,128]{2,1,0:T(8,128)(2,1)}, bf16[16,128,128]{2,1,0:T(8,128)(2,1)}) custom-call(s32[4,32]{1,0:T(4,128)} %pad_add_fusion.1.table, bf16[16,128,128]{2,1,0:T(8,128)(2,1)} %bitcast.15, bf16[48,128,128]{2,1,0:T(8,128)(2,1)} %bitcast.12), custom_call_target="tpu_custom_call" | custom-call | flops 134217728 | bytes 4194304 | tf_op jit(solution)/shard_map/pallas_call | solution.py:109
  7.4 11.2 %all-to-all-start = ((bf16[32,128,128]{2,1,0:T(8,128)(2,1)}), bf16[32,128,128]{2,1,0:T(8,128)(2,1)}, u32[]{:S(2)}, u32[]{:S(2)}) async-start(bf16[32,128,128]{2,1,0:T(8,128)(2,1)} %get-tuple-element.28), calls=%async_computation | async-start | bytes 2097152 | tf_op jit(solution)/shard_map/all_to_all | solution.py:304
  18.6 1.6 collective-permute-start.12
  20.3 3.8 %shard_map.51.local_ref = f32[16,128,128]{2,1,0:T(8,128)} custom-call(s32[4,32]{1,0:T(4,128)} %pad_add_fusion.1.table, bf16[16,128,128]{2,1,0:T(8,128)(2,1)} %get-tuple-element.26.state_ref, bf16[48,128,128]{2,1,0:T(8,128)(2,1)} %bitcast.13), custom_call_target="tpu_custom_call" | custom-call | flops 201326592 | bytes 4194304 | tf_op jit(solution)/shard_map/pallas_call | solution.py:141
  24.3 1.0 collective-permute-start
  25.2 2.7 collective-permute-done
  27.9 1.5 collective-permute-start.1
  29.4 3.6 %collective-permute-done.1 = s32[2,48]{1,0:T(2,128)S(1)} collective-permute-done((s32[2,48]{1,0:T(2,128)S(1)}, s32[2,48]{1,0:T(2,128)S(1)}, u32[]{:S(2)}, u32[]{:S(2)}) %collective-permute-start.1) | collective-permute-done | bytes 416 | tf_op jit(solution)/shard_map/ppermute | solution.py:278
  33.7 7.1 %collective-permute-done.2 = s32[4,48]{1,0:T(4,128)S(1)} collective-permute-done((s32[4,48]{1,0:T(4,128)S(1)}, s32[4,48]{1,0:T(4,128)S(1)}, u32[]{:S(2)}, u32[]{:S(2)}) %collective-permute-start.2) | collective-permute-done | bytes 800 | tf_op jit(solution)/shard_map/ppermute | solution.py:278
  40.9 3.5 %collective-permute-start.3 = (s32[8,48]{1,0:T(8,128)S(1)}, s32[8,48]{1,0:T(8,128)S(1)}, u32[]{:S(2)}, u32[]{:S(2)}) collective-permute-start(s32[8,48]{1,0:T(8,128)S(1)} %pad_add_fusion), channel_id=1, source_target_pairs={{0,8},{1,9},{2,10},{3,11},{4,12},{5,13},{6,14},{7,15},{8,0},{9,1},... | collective-permute-start | bytes 4616 | tf_op jit(solution)/shard_map/ppermute | solution.py:278
  44.3 1.6 collective-permute-done.3
  45.9 6.0 %collective-permute-start.4 = (s32[16,48]{1,0:T(8,128)S(1)}, s32[16,48]{1,0:T(8,128)S(1)}, u32[]{:S(2)}, u32[]{:S(2)}) collective-permute-start(s32[16,48]{1,0:T(8,128)S(1)} %concatenate.22), channel_id=1, source_target_pairs={{0,16},{1,17},{2,18},{3,19},{4,20},{5,21},{6,22},{7,23},{8,24},{9,... | collective-permute-start | bytes 9224 | tf_op jit(solution)/shard_map/ppermute | solution.py:278
  51.9 1.6 collective-permute-done.4
  54.4 1.3 collective-permute-done.5.table.before
  56.9 4.4 %shard_map.52 = (bf16[32,128,128]{2,1,0:T(8,128)(2,1)}, bf16[16,128,128]{2,1,0:T(8,128)(2,1)}) custom-call(s32[4,32]{1,0:T(4,128)} %copy-done.29, s32[4,32]{1,0:T(4,128)} %copy-done.27, bf16[32,128,128]{2,1,0:T(8,128)(2,1)} %all-to-all-done.arrived_ref, f32[16,128,128]{2,1,0:T(8,128)} %shard_map.51.local_ref, bf16[48,128,128]{2,1,0:T(8,128)(2,1)} %copy-done.4), custom_call_target="tpu_custom_call" | custom-call | flops 134217728 | bytes 4194304 | tf_op jit(solution)/shard_map/pallas_call | solution.py:109
  61.4 10.0 %all-to-all-start.1 = ((bf16[32,128,128]{2,1,0:T(8,128)(2,1)}), bf16[32,128,128]{2,1,0:T(8,128)(2,1)}, u32[]{:S(2)}, u32[]{:S(2)}) async-start(bf16[32,128,128]{2,1,0:T(8,128)(2,1)} %get-tuple-element.30), calls=%async_computation.1 | async-start | bytes 2097152 | tf_op jit(solution)/shard_map/all_to_all | solution.py:304
  71.4 2.4 collective-permute-start.13
  74.3 3.8 %shard_map.53.local_ref = f32[16,128,128]{2,1,0:T(8,128)} custom-call(s32[4,32]{1,0:T(4,128)} %copy-done.27, bf16[16,128,128]{2,1,0:T(8,128)(2,1)} %get-tuple-element.31.state_ref, bf16[48,128,128]{2,1,0:T(8,128)(2,1)} %copy-done.4), custom_call_target="tpu_custom_call" | custom-call | flops 201326592 | bytes 4194304 | tf_op jit(solution)/shard_map/pallas_call | solution.py:141
  78.1 13.6 %collective-permute-done.6.table.before = s32[4,32]{1,0:T(4,128)S(1)} collective-permute-done((s32[4,32]{1,0:T(4,128)S(1)}, s32[4,32]{1,0:T(4,128)S(1)}, u32[]{:S(2)}, u32[]{:S(2)}) %collective-permute-start.6) | collective-permute-done | bytes 544 | tf_op jit(solution)/shard_map/ppermute | solution.py:312
  91.7 8.2 %all-to-all-done.1.arrived_ref = bf16[32,128,128]{2,1,0:T(8,128)(2,1)} async-done(((bf16[32,128,128]{2,1,0:T(8,128)(2,1)}), bf16[32,128,128]{2,1,0:T(8,128)(2,1)}, u32[]{:S(2)}, u32[]{:S(2)}) %all-to-all-start.1) | async-done | bytes 1048608 | tf_op jit(solution)/shard_map/all_to_all | solution.py:304
  99.9 4.4 %shard_map.54 = (bf16[32,128,128]{2,1,0:T(8,128)(2,1)}, bf16[16,128,128]{2,1,0:T(8,128)(2,1)}) custom-call(s32[4,32]{1,0:T(4,128)} %copy-done.27, s32[4,32]{1,0:T(4,128)} %copy-done.17, bf16[32,128,128]{2,1,0:T(8,128)(2,1)} %all-to-all-done.1.arrived_ref, f32[16,128,128]{2,1,0:T(8,128)} %shard_map.53.local_ref, bf16[48,128,128]{2,1,0:T(8,128)(2,1)} %copy-done.6), custom_call_target="tpu_custom_call" | custom-call | flops 134217728 | bytes 4194304 | tf_op jit(solution)/shard_map/pallas_call | solution.py:109
  104.4 6.1 %all-to-all-start.2 = ((bf16[32,128,128]{2,1,0:T(8,128)(2,1)}), bf16[32,128,128]{2,1,0:T(8,128)(2,1)}, u32[]{:S(2)}, u32[]{:S(2)}) async-start(bf16[32,128,128]{2,1,0:T(8,128)(2,1)} %get-tuple-element.32), calls=%async_computation.2 | async-start | bytes 2097152 | tf_op jit(solution)/shard_map/all_to_all | solution.py:304
  110.5 1.0 collective-permute-start.14
  111.5 1.9 collective-permute-start.7
  113.3 3.8 %shard_map.55.local_ref = f32[16,128,128]{2,1,0:T(8,128)} custom-call(s32[4,32]{1,0:T(4,128)} %copy-done.17, bf16[16,128,128]{2,1,0:T(8,128)(2,1)} %get-tuple-element.33.state_ref, bf16[48,128,128]{2,1,0:T(8,128)(2,1)} %copy-done.6), custom_call_target="tpu_custom_call" | custom-call | flops 201326592 | bytes 4194304 | tf_op jit(solution)/shard_map/pallas_call | solution.py:141
  117.2 12.3 %collective-permute-done.7.table.before = s32[4,32]{1,0:T(4,128)S(1)} collective-permute-done((s32[4,32]{1,0:T(4,128)S(1)}, s32[4,32]{1,0:T(4,128)S(1)}, u32[]{:S(2)}, u32[]{:S(2)}) %collective-permute-start.7) | collective-permute-done | bytes 544 | tf_op jit(solution)/shard_map/ppermute | solution.py:312
  129.4 8.9 %all-to-all-done.2.arrived_ref = bf16[32,128,128]{2,1,0:T(8,128)(2,1)} async-done(((bf16[32,128,128]{2,1,0:T(8,128)(2,1)}), bf16[32,128,128]{2,1,0:T(8,128)(2,1)}, u32[]{:S(2)}, u32[]{:S(2)}) %all-to-all-start.2) | async-done | bytes 1048608 | tf_op jit(solution)/shard_map/all_to_all | solution.py:304
  138.4 4.4 %shard_map.56 = (bf16[32,128,128]{2,1,0:T(8,128)(2,1)}, bf16[16,128,128]{2,1,0:T(8,128)(2,1)}) custom-call(s32[4,32]{1,0:T(4,128)} %copy-done.17, s32[4,32]{1,0:T(4,128)} %copy-done.19, bf16[32,128,128]{2,1,0:T(8,128)(2,1)} %all-to-all-done.2.arrived_ref, f32[16,128,128]{2,1,0:T(8,128)} %shard_map.55.local_ref, bf16[48,128,128]{2,1,0:T(8,128)(2,1)} %copy-done.8), custom_call_target="tpu_custom_call" | custom-call | flops 134217728 | bytes 4194304 | tf_op jit(solution)/shard_map/pallas_call | solution.py:109
  142.9 6.6 %all-to-all-start.3 = ((bf16[32,128,128]{2,1,0:T(8,128)(2,1)}), bf16[32,128,128]{2,1,0:T(8,128)(2,1)}, u32[]{:S(2)}, u32[]{:S(2)}) async-start(bf16[32,128,128]{2,1,0:T(8,128)(2,1)} %get-tuple-element.34), calls=%async_computation.3 | async-start | bytes 2097152 | tf_op jit(solution)/shard_map/all_to_all | solution.py:304
  149.5 1.5 collective-permute-start.8
  151.1 3.8 %shard_map.57.local_ref = f32[16,128,128]{2,1,0:T(8,128)} custom-call(s32[4,32]{1,0:T(4,128)} %copy-done.19, bf16[16,128,128]{2,1,0:T(8,128)(2,1)} %get-tuple-element.35.state_ref, bf16[48,128,128]{2,1,0:T(8,128)(2,1)} %copy-done.8), custom_call_target="tpu_custom_call" | custom-call | flops 201326592 | bytes 4194304 | tf_op jit(solution)/shard_map/pallas_call | solution.py:141
  154.9 12.6 %collective-permute-done.8.table.before = s32[4,32]{1,0:T(4,128)S(1)} collective-permute-done((s32[4,32]{1,0:T(4,128)S(1)}, s32[4,32]{1,0:T(4,128)S(1)}, u32[]{:S(2)}, u32[]{:S(2)}) %collective-permute-start.8) | collective-permute-done | bytes 544 | tf_op jit(solution)/shard_map/ppermute | solution.py:312
  167.5 8.6 %all-to-all-done.3.arrived_ref = bf16[32,128,128]{2,1,0:T(8,128)(2,1)} async-done(((bf16[32,128,128]{2,1,0:T(8,128)(2,1)}), bf16[32,128,128]{2,1,0:T(8,128)(2,1)}, u32[]{:S(2)}, u32[]{:S(2)}) %all-to-all-start.3) | async-done | bytes 1048608 | tf_op jit(solution)/shard_map/all_to_all | solution.py:304
  176.1 4.4 %shard_map.58 = (bf16[32,128,128]{2,1,0:T(8,128)(2,1)}, bf16[16,128,128]{2,1,0:T(8,128)(2,1)}) custom-call(s32[4,32]{1,0:T(4,128)} %copy-done.19, s32[4,32]{1,0:T(4,128)} %copy-done.21, bf16[32,128,128]{2,1,0:T(8,128)(2,1)} %all-to-all-done.3.arrived_ref, f32[16,128,128]{2,1,0:T(8,128)} %shard_map.57.local_ref, bf16[48,128,128]{2,1,0:T(8,128)(2,1)} %copy-done.10), custom_call_target="tpu_custom_call" | custom-call | flops 134217728 | bytes 4194304 | tf_op jit(solution)/shard_map/pallas_call | solution.py:109
  180.6 6.6 %all-to-all-start.4 = ((bf16[32,128,128]{2,1,0:T(8,128)(2,1)}), bf16[32,128,128]{2,1,0:T(8,128)(2,1)}, u32[]{:S(2)}, u32[]{:S(2)}) async-start(bf16[32,128,128]{2,1,0:T(8,128)(2,1)} %get-tuple-element.36), calls=%async_computation.4 | async-start | bytes 2097152 | tf_op jit(solution)/shard_map/all_to_all | solution.py:304
  187.3 0.8 collective-permute-start.9
  188.1 3.8 %shard_map.59.local_ref = f32[16,128,128]{2,1,0:T(8,128)} custom-call(s32[4,32]{1,0:T(4,128)} %copy-done.21, bf16[16,128,128]{2,1,0:T(8,128)(2,1)} %get-tuple-element.37.state_ref, bf16[48,128,128]{2,1,0:T(8,128)(2,1)} %copy-done.10), custom_call_target="tpu_custom_call" | custom-call | flops 201326592 | bytes 4194304 | tf_op jit(solution)/shard_map/pallas_call | solution.py:141
  191.9 13.3 %collective-permute-done.9.table.before = s32[4,32]{1,0:T(4,128)S(1)} collective-permute-done((s32[4,32]{1,0:T(4,128)S(1)}, s32[4,32]{1,0:T(4,128)S(1)}, u32[]{:S(2)}, u32[]{:S(2)}) %collective-permute-start.9) | collective-permute-done | bytes 544 | tf_op jit(solution)/shard_map/ppermute | solution.py:312
  205.2 7.9 %all-to-all-done.4.arrived_ref = bf16[32,128,128]{2,1,0:T(8,128)(2,1)} async-done(((bf16[32,128,128]{2,1,0:T(8,128)(2,1)}), bf16[32,128,128]{2,1,0:T(8,128)(2,1)}, u32[]{:S(2)}, u32[]{:S(2)}) %all-to-all-start.4) | async-done | bytes 1048608 | tf_op jit(solution)/shard_map/all_to_all | solution.py:304
  213.1 4.4 %shard_map.60 = (bf16[32,128,128]{2,1,0:T(8,128)(2,1)}, bf16[16,128,128]{2,1,0:T(8,128)(2,1)}) custom-call(s32[4,32]{1,0:T(4,128)} %copy-done.21, s32[4,32]{1,0:T(4,128)} %copy-done.23, bf16[32,128,128]{2,1,0:T(8,128)(2,1)} %all-to-all-done.4.arrived_ref, f32[16,128,128]{2,1,0:T(8,128)} %shard_map.59.local_ref, bf16[48,128,128]{2,1,0:T(8,128)(2,1)} %copy-done.12), custom_call_target="tpu_custom_call" | custom-call | flops 134217728 | bytes 4194304 | tf_op jit(solution)/shard_map/pallas_call | solution.py:109
  217.6 6.6 %all-to-all-start.5 = ((bf16[32,128,128]{2,1,0:T(8,128)(2,1)}), bf16[32,128,128]{2,1,0:T(8,128)(2,1)}, u32[]{:S(2)}, u32[]{:S(2)}) async-start(bf16[32,128,128]{2,1,0:T(8,128)(2,1)} %get-tuple-element.38), calls=%async_computation.5 | async-start | bytes 2097152 | tf_op jit(solution)/shard_map/all_to_all | solution.py:304
  224.3 1.4 collective-permute-start.10
  225.6 3.8 %shard_map.61.local_ref = f32[16,128,128]{2,1,0:T(8,128)} custom-call(s32[4,32]{1,0:T(4,128)} %copy-done.23, bf16[16,128,128]{2,1,0:T(8,128)(2,1)} %get-tuple-element.39.state_ref, bf16[48,128,128]{2,1,0:T(8,128)(2,1)} %copy-done.12), custom_call_target="tpu_custom_call" | custom-call | flops 201326592 | bytes 4194304 | tf_op jit(solution)/shard_map/pallas_call | solution.py:141
  229.5 12.7 %collective-permute-done.10.table.before = s32[4,32]{1,0:T(4,128)S(1)} collective-permute-done((s32[4,32]{1,0:T(4,128)S(1)}, s32[4,32]{1,0:T(4,128)S(1)}, u32[]{:S(2)}, u32[]{:S(2)}) %collective-permute-start.10) | collective-permute-done | bytes 544 | tf_op jit(solution)/shard_map/ppermute | solution.py:312
  242.2 8.2 %all-to-all-done.5.arrived_ref = bf16[32,128,128]{2,1,0:T(8,128)(2,1)} async-done(((bf16[32,128,128]{2,1,0:T(8,128)(2,1)}), bf16[32,128,128]{2,1,0:T(8,128)(2,1)}, u32[]{:S(2)}, u32[]{:S(2)}) %all-to-all-start.5) | async-done | bytes 1048608 | tf_op jit(solution)/shard_map/all_to_all | solution.py:304
  250.4 4.4 %shard_map.62 = (bf16[32,128,128]{2,1,0:T(8,128)(2,1)}, bf16[16,128,128]{2,1,0:T(8,128)(2,1)}) custom-call(s32[4,32]{1,0:T(4,128)} %copy-done.23, s32[4,32]{1,0:T(4,128)} %copy-done.25, bf16[32,128,128]{2,1,0:T(8,128)(2,1)} %all-to-all-done.5.arrived_ref, f32[16,128,128]{2,1,0:T(8,128)} %shard_map.61.local_ref, bf16[48,128,128]{2,1,0:T(8,128)(2,1)} %copy-done.14), custom_call_target="tpu_custom_call" | custom-call | flops 134217728 | bytes 4194304 | tf_op jit(solution)/shard_map/pallas_call | solution.py:109
  254.8 6.6 %all-to-all-start.6 = ((bf16[32,128,128]{2,1,0:T(8,128)(2,1)}), bf16[32,128,128]{2,1,0:T(8,128)(2,1)S(1)}, u32[]{:S(2)}, u32[]{:S(2)}) async-start(bf16[32,128,128]{2,1,0:T(8,128)(2,1)} %get-tuple-element.40), calls=%async_computation.6 | async-start | bytes 2097152 | tf_op jit(solution)/shard_map/all_to_all | solution.py:304
  261.5 1.9 collective-permute-start.11
  263.3 3.8 %shard_map.63.local_ref = f32[16,128,128]{2,1,0:T(8,128)} custom-call(s32[4,32]{1,0:T(4,128)} %copy-done.25, bf16[16,128,128]{2,1,0:T(8,128)(2,1)} %get-tuple-element.41.state_ref, bf16[48,128,128]{2,1,0:T(8,128)(2,1)} %copy-done.14), custom_call_target="tpu_custom_call" | custom-call | flops 201326592 | bytes 4194304 | tf_op jit(solution)/shard_map/pallas_call | solution.py:141
  267.1 12.3 %collective-permute-done.11.table.before = s32[4,32]{1,0:T(4,128)S(1)} collective-permute-done((s32[4,32]{1,0:T(4,128)S(1)}, s32[4,32]{1,0:T(4,128)S(1)}, u32[]{:S(2)}, u32[]{:S(2)}) %collective-permute-start.11) | collective-permute-done | bytes 544 | tf_op jit(solution)/shard_map/ppermute | solution.py:312
  279.4 7.9 %all-to-all-done.6.arrived_ref = bf16[32,128,128]{2,1,0:T(8,128)(2,1)S(1)} async-done(((bf16[32,128,128]{2,1,0:T(8,128)(2,1)}), bf16[32,128,128]{2,1,0:T(8,128)(2,1)S(1)}, u32[]{:S(2)}, u32[]{:S(2)}) %all-to-all-start.6) | async-done | bytes 1048608 | tf_op jit(solution)/shard_map/all_to_all | solution.py:304
  287.3 1.0 copy-done.16
  288.3 4.4 %shard_map.64 = (bf16[32,128,128]{2,1,0:T(8,128)(2,1)}, bf16[16,128,128]{2,1,0:T(8,128)(2,1)}) custom-call(s32[4,32]{1,0:T(4,128)} %copy-done.25, s32[4,32]{1,0:T(4,128)} %copy-done.1, bf16[32,128,128]{2,1,0:T(8,128)(2,1)} %copy-done.16, f32[16,128,128]{2,1,0:T(8,128)} %shard_map.63.local_ref, bf16[48,128,128]{2,1,0:T(8,128)(2,1)} %collective-permute-done.18.blocks_ref), custom_call_target="tpu_custom_call" | custom-call | flops 134217728 | bytes 4194304 | tf_op jit(solution)/shard_map/pallas_call | solution.py:109
  292.7 6.4 %all-to-all-start.7 = ((bf16[32,128,128]{2,1,0:T(8,128)(2,1)}), bf16[32,128,128]{2,1,0:T(8,128)(2,1)S(1)}, u32[]{:S(2)}, u32[]{:S(2)}) async-start(bf16[32,128,128]{2,1,0:T(8,128)(2,1)} %get-tuple-element.42), calls=%async_computation.7 | async-start | bytes 2097152 | tf_op jit(solution)/shard_map/all_to_all | solution.py:304
  299.2 3.8 %shard_map.65.local_ref = f32[16,128,128]{2,1,0:T(8,128)} custom-call(s32[4,32]{1,0:T(4,128)} %copy-done.1, bf16[16,128,128]{2,1,0:T(8,128)(2,1)} %get-tuple-element.43.state_ref, bf16[48,128,128]{2,1,0:T(8,128)(2,1)} %collective-permute-done.18.blocks_ref), custom_call_target="tpu_custom_call" | custom-call | flops 201326592 | bytes 4194304 | tf_op jit(solution)/shard_map/pallas_call | solution.py:141
  303.0 21.7 %all-to-all-done.7.arrived_ref = bf16[32,128,128]{2,1,0:T(8,128)(2,1)S(1)} async-done(((bf16[32,128,128]{2,1,0:T(8,128)(2,1)}), bf16[32,128,128]{2,1,0:T(8,128)(2,1)S(1)}, u32[]{:S(2)}, u32[]{:S(2)}) %all-to-all-start.7) | async-done | bytes 1048608 | tf_op jit(solution)/shard_map/all_to_all | solution.py:304
  324.8 1.2 copy-done
  326.0 1.2 shard_map.66
  327.2 4.3 %collective-permute-start.19 = (bf16[1,128,128]{2,1,0:T(8,128)(2,1)S(1)}, bf16[1,128,128]{2,1,0:T(8,128)(2,1)S(1)}, u32[]{:S(2)}, u32[]{:S(2)}) collective-permute-start(bf16[1,128,128]{2,1,0:T(8,128)(2,1)S(1)} %get-tuple-element.51), channel_id=1, source_target_pairs={{0,1},{1,2},{2,3},{3,4},{4,5},{5,6},{6,7},{7,8},{8,9},{9,10},{10,1... | collective-permute-start | bytes 98312 | tf_op jit(solution)/shard_map/ppermute | solution.py:315
  331.5 1.9 collective-permute-start.20
  333.5 2.0 shard_map.67
  335.5 3.9 %collective-permute-done.20.high_ref = bf16[1,128,128]{2,1,0:T(8,128)(2,1)S(1)} collective-permute-done((bf16[1,128,128]{2,1,0:T(8,128)(2,1)S(1)}, bf16[1,128,128]{2,1,0:T(8,128)(2,1)S(1)}, u32[]{:S(2)}, u32[]{:S(2)}) %collective-permute-start.20) | collective-permute-done | bytes 32800 | tf_op jit(solution)/shard_map/ppermute | solution.py:316
  339.4 1.4 shard_map.68
  (97 shorter events, 5.3 us)
Async XLA Ops:
  7.4 11.2 %copy-start.3 = (bf16[1,16,3,128,128]{4,3,2,1,0:T(8,128)(2,1)S(1)}, bf16[1,16,3,128,128]{4,3,2,1,0:T(8,128)(2,1)}, u32[]{:S(2)}) copy-start(bf16[1,16,3,128,128]{4,3,2,1,0:T(8,128)(2,1)} %param.4) | copy-start | bytes 4718596
  7.4 48.4 %all-to-all-start = ((bf16[32,128,128]{2,1,0:T(8,128)(2,1)}), bf16[32,128,128]{2,1,0:T(8,128)(2,1)}, u32[]{:S(2)}, u32[]{:S(2)}) async-start(bf16[32,128,128]{2,1,0:T(8,128)(2,1)} %get-tuple-element.28), calls=%async_computation | async-start | bytes 2097152 | tf_op jit(solution)/shard_map/all_to_all | solution.py:304
  18.6 37.1 %collective-permute-start.12 = (bf16[48,128,128]{2,1,0:T(8,128)(2,1)S(1)}, bf16[48,128,128]{2,1,0:T(8,128)(2,1)S(1)}, u32[]{:S(2)}, u32[]{:S(2)}) collective-permute-start(bf16[48,128,128]{2,1,0:T(8,128)(2,1)S(1)} %bitcast.14), channel_id=1, source_target_pairs={{0,224},{32,0},{64,32},{96,64},{128,96},{160,128},{192,160},{224,1... | collective-permute-start | bytes 4718600 | tf_op jit(solution)/shard_map/ppermute | solution.py:313
  24.3 3.6 %collective-permute-start = (s32[1,48]{1,0:T(1,128)S(1)}, s32[1,48]{1,0:T(1,128)S(1)}, u32[]{:S(2)}, u32[]{:S(2)}) collective-permute-start(s32[1,48]{1,0:T(1,128)S(1)} %reshape.216), channel_id=1, source_target_pairs={{0,1},{1,0},{2,3},{3,2},{4,5},{5,4},{6,7},{7,6},{8,9},{9,8},{10,11... | collective-permute-start | bytes 584 | tf_op jit(solution)/shard_map/ppermute | solution.py:278
  27.9 5.2 %collective-permute-start.1 = (s32[2,48]{1,0:T(2,128)S(1)}, s32[2,48]{1,0:T(2,128)S(1)}, u32[]{:S(2)}, u32[]{:S(2)}) collective-permute-start(s32[2,48]{1,0:T(2,128)S(1)} %pad_add_fusion.5), channel_id=1, source_target_pairs={{0,2},{1,3},{2,0},{3,1},{4,6},{5,7},{6,4},{7,5},{8,10},{9,11},{10,... | collective-permute-start | bytes 1160 | tf_op jit(solution)/shard_map/ppermute | solution.py:278
  33.1 7.8 %collective-permute-start.2 = (s32[4,48]{1,0:T(4,128)S(1)}, s32[4,48]{1,0:T(4,128)S(1)}, u32[]{:S(2)}, u32[]{:S(2)}) collective-permute-start(s32[4,48]{1,0:T(4,128)S(1)} %pad_add_fusion.2), channel_id=1, source_target_pairs={{0,4},{1,5},{2,6},{3,7},{4,0},{5,1},{6,2},{7,3},{8,12},{9,13},{10,... | collective-permute-start | bytes 2312 | tf_op jit(solution)/shard_map/ppermute | solution.py:278
  40.9 5.0 %collective-permute-start.3 = (s32[8,48]{1,0:T(8,128)S(1)}, s32[8,48]{1,0:T(8,128)S(1)}, u32[]{:S(2)}, u32[]{:S(2)}) collective-permute-start(s32[8,48]{1,0:T(8,128)S(1)} %pad_add_fusion), channel_id=1, source_target_pairs={{0,8},{1,9},{2,10},{3,11},{4,12},{5,13},{6,14},{7,15},{8,0},{9,1},... | collective-permute-start | bytes 4616 | tf_op jit(solution)/shard_map/ppermute | solution.py:278
  45.9 7.7 %collective-permute-start.4 = (s32[16,48]{1,0:T(8,128)S(1)}, s32[16,48]{1,0:T(8,128)S(1)}, u32[]{:S(2)}, u32[]{:S(2)}) collective-permute-start(s32[16,48]{1,0:T(8,128)S(1)} %concatenate.22), channel_id=1, source_target_pairs={{0,16},{1,17},{2,18},{3,19},{4,20},{5,21},{6,22},{7,23},{8,24},{9,... | collective-permute-start | bytes 9224 | tf_op jit(solution)/shard_map/ppermute | solution.py:278
  53.9 1.9 copy-start.29
  53.9 1.9 collective-permute-start.5
  55.7 0.6 copy-start.27
  55.7 1.1 copy-start.4
  61.3 10.0 %copy-start.5 = (bf16[48,128,128]{2,1,0:T(8,128)(2,1)S(1)}, bf16[48,128,128]{2,1,0:T(8,128)(2,1)}, u32[]{:S(2)}) copy-start(bf16[48,128,128]{2,1,0:T(8,128)(2,1)} %copy-done.4) | copy-start | bytes 4718596
  61.3 12.4 %copy-start.28 = (s32[4,32]{1,0:T(4,128)S(1)}, s32[4,32]{1,0:T(4,128)}, u32[]{:S(2)}) copy-start(s32[4,32]{1,0:T(4,128)} %copy-done.27) | copy-start | bytes 1540
  61.4 38.6 %all-to-all-start.1 = ((bf16[32,128,128]{2,1,0:T(8,128)(2,1)}), bf16[32,128,128]{2,1,0:T(8,128)(2,1)}, u32[]{:S(2)}, u32[]{:S(2)}) async-start(bf16[32,128,128]{2,1,0:T(8,128)(2,1)} %get-tuple-element.30), calls=%async_computation.1 | async-start | bytes 2097152 | tf_op jit(solution)/shard_map/all_to_all | solution.py:304
  71.4 20.3 %collective-permute-start.13 = (bf16[48,128,128]{2,1,0:T(8,128)(2,1)S(1)}, bf16[48,128,128]{2,1,0:T(8,128)(2,1)S(1)}, u32[]{:S(2)}, u32[]{:S(2)}) collective-permute-start(bf16[48,128,128]{2,1,0:T(8,128)(2,1)S(1)} %copy-done.5), channel_id=1, source_target_pairs={{0,224},{32,0},{64,32},{96,64},{128,96},{160,128},{192,160},{224,1... | collective-permute-start | bytes 4718600 | tf_op jit(solution)/shard_map/ppermute | solution.py:313
  73.7 18.0 %collective-permute-start.6 = (s32[4,32]{1,0:T(4,128)S(1)}, s32[4,32]{1,0:T(4,128)S(1)}, u32[]{:S(2)}, u32[]{:S(2)}) collective-permute-start(s32[4,32]{1,0:T(4,128)S(1)} %copy-done.28), channel_id=1, source_target_pairs={{0,224},{32,0},{64,32},{96,64},{128,96},{160,128},{192,160},{224,1... | collective-permute-start | bytes 1544 | tf_op jit(solution)/shard_map/ppermute | solution.py:312
  91.7 8.2 %copy-start.17 = (s32[4,32]{1,0:T(4,128)}, s32[4,32]{1,0:T(4,128)S(1)}, u32[]{:S(2)}) copy-start(s32[4,32]{1,0:T(4,128)S(1)} %collective-permute-done.6.table.before) | copy-start | bytes 1540
  91.7 8.2 %copy-start.6 = (bf16[48,128,128]{2,1,0:T(8,128)(2,1)}, bf16[48,128,128]{2,1,0:T(8,128)(2,1)S(1)}, u32[]{:S(2)}) copy-start(bf16[48,128,128]{2,1,0:T(8,128)(2,1)S(1)} %collective-permute-done.13.blocks_ref) | copy-start | bytes 4718596
  104.4 6.1 %copy-start.7 = (bf16[48,128,128]{2,1,0:T(8,128)(2,1)S(1)}, bf16[48,128,128]{2,1,0:T(8,128)(2,1)}, u32[]{:S(2)}) copy-start(bf16[48,128,128]{2,1,0:T(8,128)(2,1)} %copy-done.6) | copy-start | bytes 4718596
  104.4 7.1 %copy-start.18 = (s32[4,32]{1,0:T(4,128)S(1)}, s32[4,32]{1,0:T(4,128)}, u32[]{:S(2)}) copy-start(s32[4,32]{1,0:T(4,128)} %copy-done.17) | copy-start | bytes 1540
  104.4 34.0 %all-to-all-start.2 = ((bf16[32,128,128]{2,1,0:T(8,128)(2,1)}), bf16[32,128,128]{2,1,0:T(8,128)(2,1)}, u32[]{:S(2)}, u32[]{:S(2)}) async-start(bf16[32,128,128]{2,1,0:T(8,128)(2,1)} %get-tuple-element.32), calls=%async_computation.2 | async-start | bytes 2097152 | tf_op jit(solution)/shard_map/all_to_all | solution.py:304
  110.5 18.9 %collective-permute-start.14 = (bf16[48,128,128]{2,1,0:T(8,128)(2,1)S(1)}, bf16[48,128,128]{2,1,0:T(8,128)(2,1)S(1)}, u32[]{:S(2)}, u32[]{:S(2)}) collective-permute-start(bf16[48,128,128]{2,1,0:T(8,128)(2,1)S(1)} %copy-done.7), channel_id=1, source_target_pairs={{0,224},{32,0},{64,32},{96,64},{128,96},{160,128},{192,160},{224,1... | collective-permute-start | bytes 4718600 | tf_op jit(solution)/shard_map/ppermute | solution.py:313
  111.5 18.0 %collective-permute-start.7 = (s32[4,32]{1,0:T(4,128)S(1)}, s32[4,32]{1,0:T(4,128)S(1)}, u32[]{:S(2)}, u32[]{:S(2)}) collective-permute-start(s32[4,32]{1,0:T(4,128)S(1)} %copy-done.18), channel_id=1, source_target_pairs={{0,224},{32,0},{64,32},{96,64},{128,96},{160,128},{192,160},{224,1... | collective-permute-start | bytes 1544 | tf_op jit(solution)/shard_map/ppermute | solution.py:312
  129.4 9.0 %copy-start.19 = (s32[4,32]{1,0:T(4,128)}, s32[4,32]{1,0:T(4,128)S(1)}, u32[]{:S(2)}) copy-start(s32[4,32]{1,0:T(4,128)S(1)} %collective-permute-done.7.table.before) | copy-start | bytes 1540
  129.4 9.0 %copy-start.8 = (bf16[48,128,128]{2,1,0:T(8,128)(2,1)}, bf16[48,128,128]{2,1,0:T(8,128)(2,1)S(1)}, u32[]{:S(2)}) copy-start(bf16[48,128,128]{2,1,0:T(8,128)(2,1)S(1)} %collective-permute-done.14.blocks_ref) | copy-start | bytes 4718596
  142.8 6.7 %copy-start.9 = (bf16[48,128,128]{2,1,0:T(8,128)(2,1)S(1)}, bf16[48,128,128]{2,1,0:T(8,128)(2,1)}, u32[]{:S(2)}) copy-start(bf16[48,128,128]{2,1,0:T(8,128)(2,1)} %copy-done.8) | copy-start | bytes 4718596
  142.8 6.7 %copy-start.20 = (s32[4,32]{1,0:T(4,128)S(1)}, s32[4,32]{1,0:T(4,128)}, u32[]{:S(2)}) copy-start(s32[4,32]{1,0:T(4,128)} %copy-done.19) | copy-start | bytes 1540
  142.9 33.2 %all-to-all-start.3 = ((bf16[32,128,128]{2,1,0:T(8,128)(2,1)}), bf16[32,128,128]{2,1,0:T(8,128)(2,1)}, u32[]{:S(2)}, u32[]{:S(2)}) async-start(bf16[32,128,128]{2,1,0:T(8,128)(2,1)} %get-tuple-element.34), calls=%async_computation.3 | async-start | bytes 2097152 | tf_op jit(solution)/shard_map/all_to_all | solution.py:304
  149.5 18.0 %collective-permute-start.15 = (bf16[48,128,128]{2,1,0:T(8,128)(2,1)S(1)}, bf16[48,128,128]{2,1,0:T(8,128)(2,1)S(1)}, u32[]{:S(2)}, u32[]{:S(2)}) collective-permute-start(bf16[48,128,128]{2,1,0:T(8,128)(2,1)S(1)} %copy-done.9), channel_id=1, source_target_pairs={{0,224},{32,0},{64,32},{96,64},{128,96},{160,128},{192,160},{224,1... | collective-permute-start | bytes 4718600 | tf_op jit(solution)/shard_map/ppermute | solution.py:313
  149.5 17.9 %collective-permute-start.8 = (s32[4,32]{1,0:T(4,128)S(1)}, s32[4,32]{1,0:T(4,128)S(1)}, u32[]{:S(2)}, u32[]{:S(2)}) collective-permute-start(s32[4,32]{1,0:T(4,128)S(1)} %copy-done.20), channel_id=1, source_target_pairs={{0,224},{32,0},{64,32},{96,64},{128,96},{160,128},{192,160},{224,1... | collective-permute-start | bytes 1544 | tf_op jit(solution)/shard_map/ppermute | solution.py:312
  167.5 8.6 %copy-start.21 = (s32[4,32]{1,0:T(4,128)}, s32[4,32]{1,0:T(4,128)S(1)}, u32[]{:S(2)}) copy-start(s32[4,32]{1,0:T(4,128)S(1)} %collective-permute-done.8.table.before) | copy-start | bytes 1540
  167.5 8.6 %copy-start.10 = (bf16[48,128,128]{2,1,0:T(8,128)(2,1)}, bf16[48,128,128]{2,1,0:T(8,128)(2,1)S(1)}, u32[]{:S(2)}) copy-start(bf16[48,128,128]{2,1,0:T(8,128)(2,1)S(1)} %collective-permute-done.15.blocks_ref) | copy-start | bytes 4718596
  180.5 6.7 %copy-start.11 = (bf16[48,128,128]{2,1,0:T(8,128)(2,1)S(1)}, bf16[48,128,128]{2,1,0:T(8,128)(2,1)}, u32[]{:S(2)}) copy-start(bf16[48,128,128]{2,1,0:T(8,128)(2,1)} %copy-done.10) | copy-start | bytes 4718596
  180.5 6.7 %copy-start.22 = (s32[4,32]{1,0:T(4,128)S(1)}, s32[4,32]{1,0:T(4,128)}, u32[]{:S(2)}) copy-start(s32[4,32]{1,0:T(4,128)} %copy-done.21) | copy-start | bytes 1540
  180.6 32.6 %all-to-all-start.4 = ((bf16[32,128,128]{2,1,0:T(8,128)(2,1)}), bf16[32,128,128]{2,1,0:T(8,128)(2,1)}, u32[]{:S(2)}, u32[]{:S(2)}) async-start(bf16[32,128,128]{2,1,0:T(8,128)(2,1)} %get-tuple-element.36), calls=%async_computation.4 | async-start | bytes 2097152 | tf_op jit(solution)/shard_map/all_to_all | solution.py:304
  187.2 18.0 %collective-permute-start.16 = (bf16[48,128,128]{2,1,0:T(8,128)(2,1)S(1)}, bf16[48,128,128]{2,1,0:T(8,128)(2,1)S(1)}, u32[]{:S(2)}, u32[]{:S(2)}) collective-permute-start(bf16[48,128,128]{2,1,0:T(8,128)(2,1)S(1)} %copy-done.11), channel_id=1, source_target_pairs={{0,224},{32,0},{64,32},{96,64},{128,96},{160,128},{192,160},{224,1... | collective-permute-start | bytes 4718600 | tf_op jit(solution)/shard_map/ppermute | solution.py:313
  187.3 17.9 %collective-permute-start.9 = (s32[4,32]{1,0:T(4,128)S(1)}, s32[4,32]{1,0:T(4,128)S(1)}, u32[]{:S(2)}, u32[]{:S(2)}) collective-permute-start(s32[4,32]{1,0:T(4,128)S(1)} %copy-done.22), channel_id=1, source_target_pairs={{0,224},{32,0},{64,32},{96,64},{128,96},{160,128},{192,160},{224,1... | collective-permute-start | bytes 1544 | tf_op jit(solution)/shard_map/ppermute | solution.py:312
  205.2 7.9 %copy-start.23 = (s32[4,32]{1,0:T(4,128)}, s32[4,32]{1,0:T(4,128)S(1)}, u32[]{:S(2)}) copy-start(s32[4,32]{1,0:T(4,128)S(1)} %collective-permute-done.9.table.before) | copy-start | bytes 1540
  205.2 7.9 %copy-start.12 = (bf16[48,128,128]{2,1,0:T(8,128)(2,1)}, bf16[48,128,128]{2,1,0:T(8,128)(2,1)S(1)}, u32[]{:S(2)}) copy-start(bf16[48,128,128]{2,1,0:T(8,128)(2,1)S(1)} %collective-permute-done.16.blocks_ref) | copy-start | bytes 4718596
  217.6 6.7 %copy-start.13 = (bf16[48,128,128]{2,1,0:T(8,128)(2,1)S(1)}, bf16[48,128,128]{2,1,0:T(8,128)(2,1)}, u32[]{:S(2)}) copy-start(bf16[48,128,128]{2,1,0:T(8,128)(2,1)} %copy-done.12) | copy-start | bytes 4718596
  217.6 6.7 %copy-start.24 = (s32[4,32]{1,0:T(4,128)S(1)}, s32[4,32]{1,0:T(4,128)}, u32[]{:S(2)}) copy-start(s32[4,32]{1,0:T(4,128)} %copy-done.23) | copy-start | bytes 1540
  217.6 32.8 %all-to-all-start.5 = ((bf16[32,128,128]{2,1,0:T(8,128)(2,1)}), bf16[32,128,128]{2,1,0:T(8,128)(2,1)}, u32[]{:S(2)}, u32[]{:S(2)}) async-start(bf16[32,128,128]{2,1,0:T(8,128)(2,1)} %get-tuple-element.38), calls=%async_computation.5 | async-start | bytes 2097152 | tf_op jit(solution)/shard_map/all_to_all | solution.py:304
  224.2 18.0 %collective-permute-start.17 = (bf16[48,128,128]{2,1,0:T(8,128)(2,1)S(1)}, bf16[48,128,128]{2,1,0:T(8,128)(2,1)S(1)}, u32[]{:S(2)}, u32[]{:S(2)}) collective-permute-start(bf16[48,128,128]{2,1,0:T(8,128)(2,1)S(1)} %copy-done.13), channel_id=1, source_target_pairs={{0,224},{32,0},{64,32},{96,64},{128,96},{160,128},{192,160},{224,1... | collective-permute-start | bytes 4718600 | tf_op jit(solution)/shard_map/ppermute | solution.py:313
  224.3 17.9 %collective-permute-start.10 = (s32[4,32]{1,0:T(4,128)S(1)}, s32[4,32]{1,0:T(4,128)S(1)}, u32[]{:S(2)}, u32[]{:S(2)}) collective-permute-start(s32[4,32]{1,0:T(4,128)S(1)} %copy-done.24), channel_id=1, source_target_pairs={{0,224},{32,0},{64,32},{96,64},{128,96},{160,128},{192,160},{224,1... | collective-permute-start | bytes 1544 | tf_op jit(solution)/shard_map/ppermute | solution.py:312
  242.2 8.2 %copy-start.25 = (s32[4,32]{1,0:T(4,128)}, s32[4,32]{1,0:T(4,128)S(1)}, u32[]{:S(2)}) copy-start(s32[4,32]{1,0:T(4,128)S(1)} %collective-permute-done.10.table.before) | copy-start | bytes 1540
  242.2 8.2 %copy-start.14 = (bf16[48,128,128]{2,1,0:T(8,128)(2,1)}, bf16[48,128,128]{2,1,0:T(8,128)(2,1)S(1)}, u32[]{:S(2)}) copy-start(bf16[48,128,128]{2,1,0:T(8,128)(2,1)S(1)} %collective-permute-done.17.blocks_ref) | copy-start | bytes 4718596
  254.8 6.6 %copy-start.15 = (bf16[48,128,128]{2,1,0:T(8,128)(2,1)S(1)}, bf16[48,128,128]{2,1,0:T(8,128)(2,1)}, u32[]{:S(2)}) copy-start(bf16[48,128,128]{2,1,0:T(8,128)(2,1)} %copy-done.14) | copy-start | bytes 4718596
  254.8 6.6 %copy-start.26 = (s32[4,32]{1,0:T(4,128)S(1)}, s32[4,32]{1,0:T(4,128)}, u32[]{:S(2)}) copy-start(s32[4,32]{1,0:T(4,128)} %copy-done.25) | copy-start | bytes 1540
  254.8 32.4 %all-to-all-start.6 = ((bf16[32,128,128]{2,1,0:T(8,128)(2,1)}), bf16[32,128,128]{2,1,0:T(8,128)(2,1)S(1)}, u32[]{:S(2)}, u32[]{:S(2)}) async-start(bf16[32,128,128]{2,1,0:T(8,128)(2,1)} %get-tuple-element.40), calls=%async_computation.6 | async-start | bytes 2097152 | tf_op jit(solution)/shard_map/all_to_all | solution.py:304
  261.4 18.0 %collective-permute-start.18 = (bf16[48,128,128]{2,1,0:T(8,128)(2,1)S(1)}, bf16[48,128,128]{2,1,0:T(8,128)(2,1)}, u32[]{:S(2)}, u32[]{:S(2)}) collective-permute-start(bf16[48,128,128]{2,1,0:T(8,128)(2,1)S(1)} %copy-done.15), channel_id=1, source_target_pairs={{0,224},{32,0},{64,32},{96,64},{128,96},{160,128},{192,160},{224,1... | collective-permute-start | bytes 4718600 | tf_op jit(solution)/shard_map/ppermute | solution.py:313
  261.5 17.9 %collective-permute-start.11 = (s32[4,32]{1,0:T(4,128)S(1)}, s32[4,32]{1,0:T(4,128)S(1)}, u32[]{:S(2)}, u32[]{:S(2)}) collective-permute-start(s32[4,32]{1,0:T(4,128)S(1)} %copy-done.26), channel_id=1, source_target_pairs={{0,224},{32,0},{64,32},{96,64},{128,96},{160,128},{192,160},{224,1... | collective-permute-start | bytes 1544 | tf_op jit(solution)/shard_map/ppermute | solution.py:312
  279.4 7.9 %copy-start.1 = (s32[4,32]{1,0:T(4,128)}, s32[4,32]{1,0:T(4,128)S(1)}, u32[]{:S(2)}) copy-start(s32[4,32]{1,0:T(4,128)S(1)} %collective-permute-done.11.table.before) | copy-start | bytes 1540
  287.3 1.0 copy-start.16
  292.7 32.0 %all-to-all-start.7 = ((bf16[32,128,128]{2,1,0:T(8,128)(2,1)}), bf16[32,128,128]{2,1,0:T(8,128)(2,1)S(1)}, u32[]{:S(2)}, u32[]{:S(2)}) async-start(bf16[32,128,128]{2,1,0:T(8,128)(2,1)} %get-tuple-element.42), calls=%async_computation.7 | async-start | bytes 2097152 | tf_op jit(solution)/shard_map/all_to_all | solution.py:304
  299.2 25.6 %copy-start.2 = (s32[4,32]{1,0:T(4,128)S(1)}, s32[4,32]{1,0:T(4,128)}, u32[]{:S(2)}) copy-start(s32[4,32]{1,0:T(4,128)} %copy-done.1) | copy-start | bytes 1540
  324.8 1.2 copy-start
  327.2 8.3 %collective-permute-start.19 = (bf16[1,128,128]{2,1,0:T(8,128)(2,1)S(1)}, bf16[1,128,128]{2,1,0:T(8,128)(2,1)S(1)}, u32[]{:S(2)}, u32[]{:S(2)}) collective-permute-start(bf16[1,128,128]{2,1,0:T(8,128)(2,1)S(1)} %get-tuple-element.51), channel_id=1, source_target_pairs={{0,1},{1,2},{2,3},{3,4},{4,5},{5,6},{6,7},{7,8},{8,9},{9,10},{10,1... | collective-permute-start | bytes 98312 | tf_op jit(solution)/shard_map/ppermute | solution.py:315
  331.5 7.9 %collective-permute-start.20 = (bf16[1,128,128]{2,1,0:T(8,128)(2,1)S(1)}, bf16[1,128,128]{2,1,0:T(8,128)(2,1)S(1)}, u32[]{:S(2)}, u32[]{:S(2)}) collective-permute-start(bf16[1,128,128]{2,1,0:T(8,128)(2,1)S(1)} %get-tuple-element.50), channel_id=1, source_target_pairs={{1,0},{2,1},{3,2},{4,3},{5,4},{6,5},{7,6},{8,7},{9,8},{10,9},{11,1... | collective-permute-start | bytes 98312 | tf_op jit(solution)/shard_map/ppermute | solution.py:316
where the time goes:
time: 343 us; the launch traced here: 341 us
  waiting for transfers between devices  170 us (50%)
  starting transfers between devices  92.7 us (27%)
  Pallas kernels  70.3 us (20%)
  local copies, waits for them, and re-layouts  5.41 us (2%)
    ppermute x7, waiting for transfers between devices, body(): table = lax.ppermute(table, 'day', shifted(ndays, -1))  78.1 us
    all_to_all x8, waiting for transfers between devices, body(): lax.all_to_all(out, 'tile', split_axis=0, concat_axis=0, tiled=True)  71.4 us
    all_to_all x8, starting transfers between devices, body(): lax.all_to_all(out, 'tile', split_axis=0, concat_axis=0, tiled=True)  60.3 us
    pallas_call x8, Pallas kernels, send(): pl.pallas_call(first_body if first else send_body, out_shape=(jax.ShapeDt...  35.3 us
    pallas_call x8, Pallas kernels, keep(): pl.pallas_call(keep_body, out_shape=jax.ShapeDtypeStruct((tiles, rows, po...  30.4 us
    ppermute x5, waiting for transfers between devices, landing_row(): lax.ppermute(known, 'tile', [(i, i ^ step) for i in range(peers)])  16.6 us
    ppermute x5, starting transfers between devices, landing_row(): lax.ppermute(known, 'tile', [(i, i ^ step) for i in range(peers)])  12.6 us
    ppermute x7, starting transfers between devices, body(): table = lax.ppermute(table, 'day', shifted(ndays, -1))  8.51 us
  transfers between devices with their start and end apart: 29, of which 20 were waited for; matrix products, arithmetic and copies ran while one was open for 0% of the time, Pallas kernels for 10%

commit v1 on v0

--- a/solution.py
+++ b/solution.py
@@ -13,7 +13,7 @@
 PARAMS = pltpu.CompilerParams(vmem_limit_bytes=56 * 1024 * 1024)
 SMALL = pltpu.CompilerParams(vmem_limit_bytes=16 * 1024 * 1024)
 PART = 8
-BLOCK, SOURCE, HOME, LANDING = range(4)
+WANTED, HOME, LANDING = range(3)
 
 
 def shifted(n, by):
@@ -24,12 +24,16 @@
     return lax.dot_general(v, block, (((1,), (1,)), ((), ())), preferred_element_type=jnp.float32)
 
 
-def send_products(table, state_ref, blocks_scr, out_ref, stage, out_sems):
-    peers = stage.shape[0]
+def send_products(wanted, state_scr, blocks_scr, out_ref, made, stage, out_sems):
+    tiles = state_scr.shape[0]
+    nnz = blocks_scr.shape[0] // tiles
+    for t in range(tiles):
+        v = state_scr[t]
+        for k in range(1, nnz):
+            made[t * (nnz - 1) + k - 1] = product(v, blocks_scr[t * nnz + k]).astype(jnp.bfloat16)
     copies = []
-    for p in range(peers):
-        v = state_ref[table[SOURCE, p]]
-        stage[p] = product(v, blocks_scr[table[BLOCK, p]]).astype(jnp.bfloat16)
+    for p in range(stage.shape[0]):
+        stage[p] = made[wanted(p)]
         if p % PART == PART - 1:
             part = pl.ds(p + 1 - PART, PART)
             copy = pltpu.make_async_copy(stage.at[part], out_ref.at[part], out_sems.at[p // PART])
@@ -39,80 +43,74 @@
         copy.wait()
 
 
-def arrival_copies(arrived_ref, arrived_scr, sems):
-    parts = [pl.ds(p, PART) for p in range(0, arrived_scr.shape[0], PART)]
-    return [
-        pltpu.make_async_copy(arrived_ref.at[part], arrived_scr.at[part], sems.at[n]) for n, part in enumerate(parts)
-    ]
-
-
-def add_arrived(table, copies, arrived_scr, gathered):
+def add_arrived(table, arrived_ref, gathered):
     gathered[...] = jnp.zeros_like(gathered)
-    for n, copy in enumerate(copies):
-        copy.wait()
-        for p in range(n * PART, (n + 1) * PART):
-            home = table[LANDING, p]
-            gathered[home] = gathered[home] + arrived_scr[p].astype(jnp.float32)
-
-
-def first_body(table, seeds_ref, blocks_ref, out_ref, state_ref, blocks_scr, stage, state_scr, sems, out_sems):
+    for p in range(arrived_ref.shape[0]):
+        home = table[LANDING, p]
+        gathered[home] = gathered[home] + arrived_ref[p].astype(jnp.float32)
+
+
+def first_body(dest, seeds_ref, blocks_ref, out_ref, state_ref, blocks_scr, made, stage, state_scr, numbers, sems, out_sems):
     load = pltpu.make_async_copy(blocks_ref, blocks_scr, sems.at[0])
     load.start()
-    for t in range(state_scr.shape[0]):
+    tiles, nnz = dest.shape[1:]
+    for t in range(tiles):
         state_scr[t] = jnp.transpose(seeds_ref[t].astype(jnp.float32)).astype(jnp.bfloat16)
     store = pltpu.make_async_copy(state_scr, state_ref, sems.at[2])
     store.start()
+    for p in range(stage.shape[0]):
+        numbers[p] = 0
+    for t in range(tiles):
+        for k in range(1, nnz):
+            numbers[dest[0, t, k] // tiles] = t * (nnz - 1) + k - 1
     load.wait()
-    send_products(table, state_scr, blocks_scr, out_ref, stage, out_sems)
+    send_products(lambda p: numbers[p], state_scr, blocks_scr, out_ref, made, stage, out_sems)
     store.wait()
 
 
 def send_body(
     before, table, arrived_ref, local_ref, blocks_ref, out_ref, state_ref,
-    blocks_scr, stage, state_scr, arrived_scr, gathered, local_scr, sems, out_sems, in_sems,
+    blocks_scr, made, stage, state_scr, gathered, local_scr, sems, out_sems,
 ):
-    arrivals = arrival_copies(arrived_ref, arrived_scr, in_sems)
     load_local = pltpu.make_async_copy(local_ref, local_scr, sems.at[1])
     load = pltpu.make_async_copy(blocks_ref, blocks_scr, sems.at[0])
-    for copy in [*arrivals, load_local, load]:
-        copy.start()
-    add_arrived(before, arrivals, arrived_scr, gathered)
+    load_local.start()
+    load.start()
+    add_arrived(before, arrived_ref, gathered)
     load_local.wait()
     for t in range(state_scr.shape[0]):
         state_scr[t] = (gathered[t] + local_scr[t]).astype(jnp.bfloat16)
     store = pltpu.make_async_copy(state_scr, state_ref, sems.at[2])
     store.start()
     load.wait()
-    send_products(table, state_scr, blocks_scr, out_ref, stage, out_sems)
+    send_products(lambda p: table[WANTED, p], state_scr, blocks_scr, out_ref, made, stage, out_sems)
     store.wait()
 
 
 def send(tables, carried, blocks, peers):
-    points = blocks.shape[1]
+    count, points = blocks.shape[:2]
     first = len(carried) == 1
     rows = points
     tiles = carried[-1].shape[0]
     scratch = [
         pltpu.VMEM(blocks.shape, jnp.bfloat16),
+        pltpu.VMEM((count - tiles, rows, points), jnp.bfloat16),
         pltpu.VMEM((peers, rows, points), jnp.bfloat16),
         pltpu.VMEM((tiles, rows, points), jnp.bfloat16),
     ]
-    if not first:
-        scratch += [
-            pltpu.VMEM((peers, rows, points), jnp.bfloat16),
-            pltpu.VMEM((tiles + 1, rows, points), jnp.float32),
-            pltpu.VMEM((tiles, rows, points), jnp.float32),
-        ]
+    if first:
+        scratch.append(pltpu.SMEM((peers,), jnp.int32))
+    else:
+        scratch.append(pltpu.VMEM((tiles + 1, rows, points), jnp.float32))
+        scratch.append(pltpu.VMEM((tiles, rows, points), jnp.float32))
     scratch += [pltpu.SemaphoreType.DMA((3,)), pltpu.SemaphoreType.DMA((peers // PART,))]
-    if not first:
-        scratch.append(pltpu.SemaphoreType.DMA((peers // PART,)))
     return pl.pallas_call(
         first_body if first else send_body,
         out_shape=(
             jax.ShapeDtypeStruct((peers, rows, points), jnp.bfloat16),
             jax.ShapeDtypeStruct((tiles, rows, points), jnp.bfloat16),
         ),
-        in_specs=[SMEM] * len(tables) + ([VMEM] if first else [HBM, HBM]) + [HBM],
+        in_specs=[SMEM] * len(tables) + ([VMEM] if first else [VMEM, HBM]) + [HBM],
         out_specs=(HBM, HBM),
         scratch_shapes=scratch,
         compiler_params=PARAMS,
@@ -151,12 +149,10 @@
     )(table, state, blocks)
 
 
-def last_body(before, arrived_ref, local_ref, final_ref, edges_ref, arrived_scr, gathered, local_scr, sem, in_sems):
-    arrivals = arrival_copies(arrived_ref, arrived_scr, in_sems)
+def last_body(before, arrived_ref, local_ref, final_ref, edges_ref, gathered, local_scr, sem):
     load_local = pltpu.make_async_copy(local_ref, local_scr, sem)
-    for copy in [*arrivals, load_local]:
-        copy.start()
-    add_arrived(before, arrivals, arrived_scr, gathered)
+    load_local.start()
+    add_arrived(before, arrived_ref, gathered)
     load_local.wait()
     tiles = final_ref.shape[0]
     for t in range(tiles):
@@ -173,14 +169,12 @@
             jax.ShapeDtypeStruct((tiles, rows, points), jnp.bfloat16),
             jax.ShapeDtypeStruct((2, rows, points), jnp.bfloat16),
         ),
-        in_specs=[SMEM, HBM, HBM],
+        in_specs=[SMEM, VMEM, HBM],
         out_specs=(VMEM, VMEM),
         scratch_shapes=[
-            pltpu.VMEM(arrived.shape, jnp.bfloat16),
             pltpu.VMEM((tiles + 1, rows, points), jnp.float32),
             pltpu.VMEM((tiles, rows, points), jnp.float32),
             pltpu.SemaphoreType.DMA,
-            pltpu.SemaphoreType.DMA((arrived.shape[0] // PART,)),
         ],
         compiler_params=SMALL,
     )(before, arrived, local)
@@ -262,13 +256,12 @@
 
 
 def own_rows(dest, me, tiles, peers, nnz):
-    flat = dest.reshape(tiles * nnz)
     off = dest[:, 1:].reshape(tiles * (nnz - 1))
     peer = jnp.arange(peers, dtype=jnp.int32)
-    order = jnp.arange(tiles * nnz, dtype=jnp.int32)
-    block = jnp.max(jnp.where(flat[None, :] // tiles == peer[:, None], order, 0), axis=1)
+    order = jnp.arange(tiles * (nnz - 1), dtype=jnp.int32)
+    wanted = jnp.max(jnp.where(off[None, :] // tiles == peer[:, None], order, 0), axis=1)
     home = jnp.where(off // tiles == me, off % tiles, tiles)
-    return block, block // nnz, home
+    return wanted, home
 
 
 def landing_row(dest, me, tiles, peers):
@@ -290,23 +283,20 @@
     ndays, peers = lax.axis_size("day"), lax.axis_size("tile")
     me = lax.axis_index("tile")
 
-    block, source, home = own_rows(dest_tiles[0], me, tiles, peers, nnz)
-    first_table = jnp.stack([block, source, home, jnp.zeros_like(home)])
-    table = first_table
     seeds = seeds.reshape(tiles, points, width)
     wblk = blocks.reshape(tiles * nnz, points, points)
 
     for step in range(ndays):
         if step == 0:
-            out, state = send((first_table,), (seeds,), wblk, peers)
+            out, state = send((dest_tiles,), (seeds,), wblk, peers)
         else:
             out, state = send((before, table), (arrived, local), wblk, peers)
         arrived = lax.all_to_all(out, "tile", split_axis=0, concat_axis=0, tiled=True)
+        if step == 0:
+            dest, state = lax.optimization_barrier((dest_tiles[0], state))
+            landing = landing_row(dest, me, tiles, peers)
+            table = jnp.stack([*own_rows(dest, me, tiles, peers, nnz), landing])
         local = keep(table, state, wblk)
-        if step == 0:
-            dest, local = lax.optimization_barrier((dest_tiles[0], local))
-            landing = landing_row(dest, me, tiles, peers)
-            table = jnp.stack([block, source, home, landing])
         before = table
         if step < ndays - 1:
             table = lax.ppermute(table, "day", shifted(ndays, -1))

time: 343 us -> 346 us (level)
  starting transfers between devices: 92.7 us -> 98.3 us
  waiting for transfers between devices: 170 us -> 165 us
  Pallas kernels: 70.3 us -> 73.8 us
    ppermute x7, waiting for transfers between devices: 78.1 us -> 72.1 us  [body(): table = lax.ppermute(table, 'day', shifted(ndays, -1))]
    ppermute x7, starting transfers between devices: 8.51 us -> 13.2 us  [body(): table = lax.ppermute(table, 'day', shifted(ndays, -1))]
    pallas_call x8, Pallas kernels: 35.3 us -> 38.9 us  [send(): pl.pallas_call(first_body if first else send_body, out_shape=(jax.ShapeDt...]
  transfers between devices with their start and end apart: 29 -> 29, of which waited for: 20 -> 19; matrix products, arithmetic and copies ran while one was open for 0% -> 0% of each run, Pallas kernels for 10% -> 9%
where the time goes in v1:
time: 346 us; the launch traced here: 344 us
  waiting for transfers between devices  165 us (48%)
  starting transfers between devices  98.3 us (28%)
  Pallas kernels  73.8 us (21%)
  local copies, waits for them, and re-layouts  5.34 us (2%)
    ppermute x7, waiting for transfers between devices, body(): table = lax.ppermute(table, 'day', shifted(ndays, -1))  72.1 us
    all_to_all x8, waiting for transfers between devices, body(): lax.all_to_all(out, 'tile', split_axis=0, concat_axis=0, tiled=True)  68.8 us
    all_to_all x8, starting transfers between devices, body(): lax.all_to_all(out, 'tile', split_axis=0, concat_axis=0, tiled=True)  61.3 us
    pallas_call x8, Pallas kernels, send(): pl.pallas_call(first_body if first else send_body, out_shape=(jax.ShapeDt...  38.9 us
    pallas_call x8, Pallas kernels, keep(): pl.pallas_call(keep_body, out_shape=jax.ShapeDtypeStruct((tiles, rows, po...  30.5 us
    ppermute x5, waiting for transfers between devices, landing_row(): lax.ppermute(known, 'tile', [(i, i ^ step) for i in range(peers)])  19.9 us
    ppermute x7, starting transfers between devices, body(): table = lax.ppermute(table, 'day', shifted(ndays, -1))  13.2 us
    ppermute x5, starting transfers between devices, landing_row(): lax.ppermute(known, 'tile', [(i, i ^ step) for i in range(peers)])  12.7 us
  transfers between devices with their start and end apart: 29, of which 19 were waited for; matrix products, arithmetic and copies ran while one was open for 0% of the time, Pallas kernels for 9%

profile of v1, /device:TPU:56, one launch (start us, length us, event | category | flops | bytes accessed | tf_op | source)
XLA Modules:
  0.0 344.1 jit_solution(14527636264013491391)
XLA Ops:
  0.6 1.4 copy.15.dest
  2.0 4.6 %shard_map.50 = (bf16[32,128,128]{2,1,0:T(8,128)(2,1)}, bf16[16,128,128]{2,1,0:T(8,128)(2,1)}) custom-call(s32[1,16,3]{2,1,0:T(8,128)} %copy.15.dest, bf16[16,128,128]{2,1,0:T(8,128)(2,1)} %bitcast.16, bf16[48,128,128]{2,1,0:T(8,128)(2,1)} %bitcast.11), custom_call_target="tpu_custom_call" | custom-call | flops 134217728 | bytes 4194304 | tf_op jit(solution)/shard_map/pallas_call | solution.py:107
  6.6 11.2 %all-to-all-start = ((bf16[32,128,128]{2,1,0:T(8,128)(2,1)}), bf16[32,128,128]{2,1,0:T(8,128)(2,1)}, u32[]{:S(2)}, u32[]{:S(2)}) async-start(bf16[32,128,128]{2,1,0:T(8,128)(2,1)} %get-tuple-element.28), calls=%async_computation | async-start | bytes 2097152 | tf_op jit(solution)/shard_map/all_to_all | solution.py:294
  17.9 1.7 collective-permute-start.12
  19.7 0.9 collective-permute-start
  20.6 2.7 collective-permute-done
  23.3 1.6 collective-permute-start.1
  25.1 3.4 collective-permute-done.1
  29.4 10.7 %collective-permute-done.2 = s32[4,48]{1,0:T(4,128)S(1)} collective-permute-done((s32[4,48]{1,0:T(4,128)S(1)}, s32[4,48]{1,0:T(4,128)S(1)}, u32[]{:S(2)}, u32[]{:S(2)}) %collective-permute-start.2) | collective-permute-done | bytes 800 | tf_op jit(solution)/shard_map/ppermute | solution.py:271
  40.1 3.5 %collective-permute-start.3 = (s32[8,48]{1,0:T(8,128)S(1)}, s32[8,48]{1,0:T(8,128)S(1)}, u32[]{:S(2)}, u32[]{:S(2)}) collective-permute-start(s32[8,48]{1,0:T(8,128)S(1)} %pad_add_fusion), channel_id=1, source_target_pairs={{0,8},{1,9},{2,10},{3,11},{4,12},{5,13},{6,14},{7,15},{8,0},{9,1},... | collective-permute-start | bytes 4616 | tf_op jit(solution)/shard_map/ppermute | solution.py:271
  43.6 1.6 collective-permute-done.3
  45.2 6.0 %collective-permute-start.4 = (s32[16,48]{1,0:T(8,128)S(1)}, s32[16,48]{1,0:T(8,128)S(1)}, u32[]{:S(2)}, u32[]{:S(2)}) collective-permute-start(s32[16,48]{1,0:T(8,128)S(1)} %concatenate.22), channel_id=1, source_target_pairs={{0,16},{1,17},{2,18},{3,19},{4,20},{5,21},{6,22},{7,23},{8,24},{9,... | collective-permute-start | bytes 9224 | tf_op jit(solution)/shard_map/ppermute | solution.py:271
  51.3 1.5 collective-permute-done.4
  53.7 3.8 %shard_map.51.local_ref = f32[16,128,128]{2,1,0:T(8,128)} custom-call(s32[3,32]{1,0:T(4,128)} %copy-done.29, bf16[16,128,128]{2,1,0:T(8,128)(2,1)} %get-tuple-element.29.state_ref, bf16[48,128,128]{2,1,0:T(8,128)(2,1)} %bitcast.12), custom_call_target="tpu_custom_call" | custom-call | flops 201326592 | bytes 4194304 | tf_op jit(solution)/shard_map/pallas_call | solution.py:139
  58.7 4.9 %shard_map.52 = (bf16[32,128,128]{2,1,0:T(8,128)(2,1)}, bf16[16,128,128]{2,1,0:T(8,128)(2,1)}) custom-call(s32[3,32]{1,0:T(4,128)} %copy-done.29, s32[3,32]{1,0:T(4,128)} %copy-done.27, bf16[32,128,128]{2,1,0:T(8,128)(2,1)} %all-to-all-done.arrived_ref, f32[16,128,128]{2,1,0:T(8,128)} %shard_map.51.local_ref, bf16[48,128,128]{2,1,0:T(8,128)(2,1)} %copy-done.3), custom_call_target="tpu_custom_call" | custom-call | flops 134217728 | bytes 4194304 | tf_op jit(solution)/shard_map/pallas_call | solution.py:107
  63.6 10.6 %all-to-all-start.1 = ((bf16[32,128,128]{2,1,0:T(8,128)(2,1)}), bf16[32,128,128]{2,1,0:T(8,128)(2,1)}, u32[]{:S(2)}, u32[]{:S(2)}) async-start(bf16[32,128,128]{2,1,0:T(8,128)(2,1)} %get-tuple-element.30), calls=%async_computation.1 | async-start | bytes 2097152 | tf_op jit(solution)/shard_map/all_to_all | solution.py:294
  74.2 1.8 collective-permute-start.13
  76.0 1.1 collective-permute-start.6
  77.1 3.8 %shard_map.53.local_ref = f32[16,128,128]{2,1,0:T(8,128)} custom-call(s32[3,32]{1,0:T(4,128)} %copy-done.27, bf16[16,128,128]{2,1,0:T(8,128)(2,1)} %get-tuple-element.31.state_ref, bf16[48,128,128]{2,1,0:T(8,128)(2,1)} %copy-done.3), custom_call_target="tpu_custom_call" | custom-call | flops 201326592 | bytes 4194304 | tf_op jit(solution)/shard_map/pallas_call | solution.py:139
  80.9 13.0 %collective-permute-done.6.table.before = s32[3,32]{1,0:T(4,128)S(1)} collective-permute-done((s32[3,32]{1,0:T(4,128)S(1)}, s32[3,32]{1,0:T(4,128)S(1)}, u32[]{:S(2)}, u32[]{:S(2)}) %collective-permute-start.6) | collective-permute-done | bytes 416 | tf_op jit(solution)/shard_map/ppermute | solution.py:302
  93.9 7.6 %all-to-all-done.1.arrived_ref = bf16[32,128,128]{2,1,0:T(8,128)(2,1)} async-done(((bf16[32,128,128]{2,1,0:T(8,128)(2,1)}), bf16[32,128,128]{2,1,0:T(8,128)(2,1)}, u32[]{:S(2)}, u32[]{:S(2)}) %all-to-all-start.1) | async-done | bytes 1048608 | tf_op jit(solution)/shard_map/all_to_all | solution.py:294
  101.6 4.9 %shard_map.54 = (bf16[32,128,128]{2,1,0:T(8,128)(2,1)}, bf16[16,128,128]{2,1,0:T(8,128)(2,1)}) custom-call(s32[3,32]{1,0:T(4,128)} %copy-done.27, s32[3,32]{1,0:T(4,128)} %copy-done.17, bf16[32,128,128]{2,1,0:T(8,128)(2,1)} %all-to-all-done.1.arrived_ref, f32[16,128,128]{2,1,0:T(8,128)} %shard_map.53.local_ref, bf16[48,128,128]{2,1,0:T(8,128)(2,1)} %copy-done.5), custom_call_target="tpu_custom_call" | custom-call | flops 134217728 | bytes 4194304 | tf_op jit(solution)/shard_map/pallas_call | solution.py:107
  106.5 6.6 %all-to-all-start.2 = ((bf16[32,128,128]{2,1,0:T(8,128)(2,1)}), bf16[32,128,128]{2,1,0:T(8,128)(2,1)}, u32[]{:S(2)}, u32[]{:S(2)}) async-start(bf16[32,128,128]{2,1,0:T(8,128)(2,1)} %get-tuple-element.32), calls=%async_computation.2 | async-start | bytes 2097152 | tf_op jit(solution)/shard_map/all_to_all | solution.py:294
  113.1 0.9 collective-permute-start.14
  114.1 1.9 collective-permute-start.7
  116.0 3.8 %shard_map.55.local_ref = f32[16,128,128]{2,1,0:T(8,128)} custom-call(s32[3,32]{1,0:T(4,128)} %copy-done.17, bf16[16,128,128]{2,1,0:T(8,128)(2,1)} %get-tuple-element.33.state_ref, bf16[48,128,128]{2,1,0:T(8,128)(2,1)} %copy-done.5), custom_call_target="tpu_custom_call" | custom-call | flops 201326592 | bytes 4194304 | tf_op jit(solution)/shard_map/pallas_call | solution.py:139
  119.9 12.2 %collective-permute-done.7.table.before = s32[3,32]{1,0:T(4,128)S(1)} collective-permute-done((s32[3,32]{1,0:T(4,128)S(1)}, s32[3,32]{1,0:T(4,128)S(1)}, u32[]{:S(2)}, u32[]{:S(2)}) %collective-permute-start.7) | collective-permute-done | bytes 416 | tf_op jit(solution)/shard_map/ppermute | solution.py:302
  132.1 7.6 %all-to-all-done.2.arrived_ref = bf16[32,128,128]{2,1,0:T(8,128)(2,1)} async-done(((bf16[32,128,128]{2,1,0:T(8,128)(2,1)}), bf16[32,128,128]{2,1,0:T(8,128)(2,1)}, u32[]{:S(2)}, u32[]{:S(2)}) %all-to-all-start.2) | async-done | bytes 1048608 | tf_op jit(solution)/shard_map/all_to_all | solution.py:294
  139.7 4.9 %shard_map.56 = (bf16[32,128,128]{2,1,0:T(8,128)(2,1)}, bf16[16,128,128]{2,1,0:T(8,128)(2,1)}) custom-call(s32[3,32]{1,0:T(4,128)} %copy-done.17, s32[3,32]{1,0:T(4,128)} %copy-done.19, bf16[32,128,128]{2,1,0:T(8,128)(2,1)} %all-to-all-done.2.arrived_ref, f32[16,128,128]{2,1,0:T(8,128)} %shard_map.55.local_ref, bf16[48,128,128]{2,1,0:T(8,128)(2,1)} %copy-done.7), custom_call_target="tpu_custom_call" | custom-call | flops 134217728 | bytes 4194304 | tf_op jit(solution)/shard_map/pallas_call | solution.py:107
  144.6 6.6 %all-to-all-start.3 = ((bf16[32,128,128]{2,1,0:T(8,128)(2,1)}), bf16[32,128,128]{2,1,0:T(8,128)(2,1)}, u32[]{:S(2)}, u32[]{:S(2)}) async-start(bf16[32,128,128]{2,1,0:T(8,128)(2,1)} %get-tuple-element.34), calls=%async_computation.3 | async-start | bytes 2097152 | tf_op jit(solution)/shard_map/all_to_all | solution.py:294
  151.6 2.6 collective-permute-start.8
  154.2 3.8 %shard_map.57.local_ref = f32[16,128,128]{2,1,0:T(8,128)} custom-call(s32[3,32]{1,0:T(4,128)} %copy-done.19, bf16[16,128,128]{2,1,0:T(8,128)(2,1)} %get-tuple-element.35.state_ref, bf16[48,128,128]{2,1,0:T(8,128)(2,1)} %copy-done.7), custom_call_target="tpu_custom_call" | custom-call | flops 201326592 | bytes 4194304 | tf_op jit(solution)/shard_map/pallas_call | solution.py:139
  158.0 11.5 %collective-permute-done.8.table.before = s32[3,32]{1,0:T(4,128)S(1)} collective-permute-done((s32[3,32]{1,0:T(4,128)S(1)}, s32[3,32]{1,0:T(4,128)S(1)}, u32[]{:S(2)}, u32[]{:S(2)}) %collective-permute-start.8) | collective-permute-done | bytes 416 | tf_op jit(solution)/shard_map/ppermute | solution.py:302
  169.6 7.6 %all-to-all-done.3.arrived_ref = bf16[32,128,128]{2,1,0:T(8,128)(2,1)} async-done(((bf16[32,128,128]{2,1,0:T(8,128)(2,1)}), bf16[32,128,128]{2,1,0:T(8,128)(2,1)}, u32[]{:S(2)}, u32[]{:S(2)}) %all-to-all-start.3) | async-done | bytes 1048608 | tf_op jit(solution)/shard_map/all_to_all | solution.py:294
  177.2 4.9 %shard_map.58 = (bf16[32,128,128]{2,1,0:T(8,128)(2,1)}, bf16[16,128,128]{2,1,0:T(8,128)(2,1)}) custom-call(s32[3,32]{1,0:T(4,128)} %copy-done.19, s32[3,32]{1,0:T(4,128)} %copy-done.21, bf16[32,128,128]{2,1,0:T(8,128)(2,1)} %all-to-all-done.3.arrived_ref, f32[16,128,128]{2,1,0:T(8,128)} %shard_map.57.local_ref, bf16[48,128,128]{2,1,0:T(8,128)(2,1)} %copy-done.9), custom_call_target="tpu_custom_call" | custom-call | flops 134217728 | bytes 4194304 | tf_op jit(solution)/shard_map/pallas_call | solution.py:107
  182.1 6.6 %all-to-all-start.4 = ((bf16[32,128,128]{2,1,0:T(8,128)(2,1)}), bf16[32,128,128]{2,1,0:T(8,128)(2,1)}, u32[]{:S(2)}, u32[]{:S(2)}) async-start(bf16[32,128,128]{2,1,0:T(8,128)(2,1)} %get-tuple-element.36), calls=%async_computation.4 | async-start | bytes 2097152 | tf_op jit(solution)/shard_map/all_to_all | solution.py:294
  188.8 2.8 collective-permute-start.9
  191.7 3.8 %shard_map.59.local_ref = f32[16,128,128]{2,1,0:T(8,128)} custom-call(s32[3,32]{1,0:T(4,128)} %copy-done.21, bf16[16,128,128]{2,1,0:T(8,128)(2,1)} %get-tuple-element.37.state_ref, bf16[48,128,128]{2,1,0:T(8,128)(2,1)} %copy-done.9), custom_call_target="tpu_custom_call" | custom-call | flops 201326592 | bytes 4194304 | tf_op jit(solution)/shard_map/pallas_call | solution.py:139
  195.5 11.3 %collective-permute-done.9.table.before = s32[3,32]{1,0:T(4,128)S(1)} collective-permute-done((s32[3,32]{1,0:T(4,128)S(1)}, s32[3,32]{1,0:T(4,128)S(1)}, u32[]{:S(2)}, u32[]{:S(2)}) %collective-permute-start.9) | collective-permute-done | bytes 416 | tf_op jit(solution)/shard_map/ppermute | solution.py:302
  206.8 8.2 %all-to-all-done.4.arrived_ref = bf16[32,128,128]{2,1,0:T(8,128)(2,1)} async-done(((bf16[32,128,128]{2,1,0:T(8,128)(2,1)}), bf16[32,128,128]{2,1,0:T(8,128)(2,1)}, u32[]{:S(2)}, u32[]{:S(2)}) %all-to-all-start.4) | async-done | bytes 1048608 | tf_op jit(solution)/shard_map/all_to_all | solution.py:294
  214.9 4.9 %shard_map.60 = (bf16[32,128,128]{2,1,0:T(8,128)(2,1)}, bf16[16,128,128]{2,1,0:T(8,128)(2,1)}) custom-call(s32[3,32]{1,0:T(4,128)} %copy-done.21, s32[3,32]{1,0:T(4,128)} %copy-done.23, bf16[32,128,128]{2,1,0:T(8,128)(2,1)} %all-to-all-done.4.arrived_ref, f32[16,128,128]{2,1,0:T(8,128)} %shard_map.59.local_ref, bf16[48,128,128]{2,1,0:T(8,128)(2,1)} %copy-done.11), custom_call_target="tpu_custom_call" | custom-call | flops 134217728 | bytes 4194304 | tf_op jit(solution)/shard_map/pallas_call | solution.py:107
  219.9 6.6 %all-to-all-start.5 = ((bf16[32,128,128]{2,1,0:T(8,128)(2,1)}), bf16[32,128,128]{2,1,0:T(8,128)(2,1)}, u32[]{:S(2)}, u32[]{:S(2)}) async-start(bf16[32,128,128]{2,1,0:T(8,128)(2,1)} %get-tuple-element.38), calls=%async_computation.5 | async-start | bytes 2097152 | tf_op jit(solution)/shard_map/all_to_all | solution.py:294
  226.6 2.3 collective-permute-start.10
  228.9 3.8 %shard_map.61.local_ref = f32[16,128,128]{2,1,0:T(8,128)} custom-call(s32[3,32]{1,0:T(4,128)} %copy-done.23, bf16[16,128,128]{2,1,0:T(8,128)(2,1)} %get-tuple-element.39.state_ref, bf16[48,128,128]{2,1,0:T(8,128)(2,1)} %copy-done.11), custom_call_target="tpu_custom_call" | custom-call | flops 201326592 | bytes 4194304 | tf_op jit(solution)/shard_map/pallas_call | solution.py:139
  232.7 11.8 %collective-permute-done.10.table.before = s32[3,32]{1,0:T(4,128)S(1)} collective-permute-done((s32[3,32]{1,0:T(4,128)S(1)}, s32[3,32]{1,0:T(4,128)S(1)}, u32[]{:S(2)}, u32[]{:S(2)}) %collective-permute-start.10) | collective-permute-done | bytes 416 | tf_op jit(solution)/shard_map/ppermute | solution.py:302
  244.5 7.9 %all-to-all-done.5.arrived_ref = bf16[32,128,128]{2,1,0:T(8,128)(2,1)} async-done(((bf16[32,128,128]{2,1,0:T(8,128)(2,1)}), bf16[32,128,128]{2,1,0:T(8,128)(2,1)}, u32[]{:S(2)}, u32[]{:S(2)}) %all-to-all-start.5) | async-done | bytes 1048608 | tf_op jit(solution)/shard_map/all_to_all | solution.py:294
  252.4 4.9 %shard_map.62 = (bf16[32,128,128]{2,1,0:T(8,128)(2,1)}, bf16[16,128,128]{2,1,0:T(8,128)(2,1)}) custom-call(s32[3,32]{1,0:T(4,128)} %copy-done.23, s32[3,32]{1,0:T(4,128)} %copy-done.25, bf16[32,128,128]{2,1,0:T(8,128)(2,1)} %all-to-all-done.5.arrived_ref, f32[16,128,128]{2,1,0:T(8,128)} %shard_map.61.local_ref, bf16[48,128,128]{2,1,0:T(8,128)(2,1)} %copy-done.13), custom_call_target="tpu_custom_call" | custom-call | flops 134217728 | bytes 4194304 | tf_op jit(solution)/shard_map/pallas_call | solution.py:107
  257.3 6.6 %all-to-all-start.6 = ((bf16[32,128,128]{2,1,0:T(8,128)(2,1)}), bf16[32,128,128]{2,1,0:T(8,128)(2,1)S(1)}, u32[]{:S(2)}, u32[]{:S(2)}) async-start(bf16[32,128,128]{2,1,0:T(8,128)(2,1)} %get-tuple-element.40), calls=%async_computation.6 | async-start | bytes 2097152 | tf_op jit(solution)/shard_map/all_to_all | solution.py:294
  264.0 1.9 collective-permute-start.11
  265.8 3.8 %shard_map.63.local_ref = f32[16,128,128]{2,1,0:T(8,128)} custom-call(s32[3,32]{1,0:T(4,128)} %copy-done.25, bf16[16,128,128]{2,1,0:T(8,128)(2,1)} %get-tuple-element.41.state_ref, bf16[48,128,128]{2,1,0:T(8,128)(2,1)} %copy-done.13), custom_call_target="tpu_custom_call" | custom-call | flops 201326592 | bytes 4194304 | tf_op jit(solution)/shard_map/pallas_call | solution.py:139
  269.6 12.3 %collective-permute-done.11.table.before = s32[3,32]{1,0:T(4,128)S(1)} collective-permute-done((s32[3,32]{1,0:T(4,128)S(1)}, s32[3,32]{1,0:T(4,128)S(1)}, u32[]{:S(2)}, u32[]{:S(2)}) %collective-permute-start.11) | collective-permute-done | bytes 416 | tf_op jit(solution)/shard_map/ppermute | solution.py:302
  281.9 8.1 %all-to-all-done.6.arrived_ref = bf16[32,128,128]{2,1,0:T(8,128)(2,1)S(1)} async-done(((bf16[32,128,128]{2,1,0:T(8,128)(2,1)}), bf16[32,128,128]{2,1,0:T(8,128)(2,1)S(1)}, u32[]{:S(2)}, u32[]{:S(2)}) %all-to-all-start.6) | async-done | bytes 1048608 | tf_op jit(solution)/shard_map/all_to_all | solution.py:294
  290.0 1.0 copy-done.16
  291.0 4.9 %shard_map.64 = (bf16[32,128,128]{2,1,0:T(8,128)(2,1)}, bf16[16,128,128]{2,1,0:T(8,128)(2,1)}) custom-call(s32[3,32]{1,0:T(4,128)} %copy-done.25, s32[3,32]{1,0:T(4,128)} %copy-done.1, bf16[32,128,128]{2,1,0:T(8,128)(2,1)} %copy-done.16, f32[16,128,128]{2,1,0:T(8,128)} %shard_map.63.local_ref, bf16[48,128,128]{2,1,0:T(8,128)(2,1)} %collective-permute-done.18.blocks_ref), custom_call_target="tpu_custom_call" | custom-call | flops 134217728 | bytes 4194304 | tf_op jit(solution)/shard_map/pallas_call | solution.py:107
  295.9 6.4 %all-to-all-start.7 = ((bf16[32,128,128]{2,1,0:T(8,128)(2,1)}), bf16[32,128,128]{2,1,0:T(8,128)(2,1)S(1)}, u32[]{:S(2)}, u32[]{:S(2)}) async-start(bf16[32,128,128]{2,1,0:T(8,128)(2,1)} %get-tuple-element.42), calls=%async_computation.7 | async-start | bytes 2097152 | tf_op jit(solution)/shard_map/all_to_all | solution.py:294
  302.4 3.8 %shard_map.65.local_ref = f32[16,128,128]{2,1,0:T(8,128)} custom-call(s32[3,32]{1,0:T(4,128)} %copy-done.1, bf16[16,128,128]{2,1,0:T(8,128)(2,1)} %get-tuple-element.43.state_ref, bf16[48,128,128]{2,1,0:T(8,128)(2,1)} %collective-permute-done.18.blocks_ref), custom_call_target="tpu_custom_call" | custom-call | flops 201326592 | bytes 4194304 | tf_op jit(solution)/shard_map/pallas_call | solution.py:139
  306.2 21.8 %all-to-all-done.7.arrived_ref = bf16[32,128,128]{2,1,0:T(8,128)(2,1)S(1)} async-done(((bf16[32,128,128]{2,1,0:T(8,128)(2,1)}), bf16[32,128,128]{2,1,0:T(8,128)(2,1)S(1)}, u32[]{:S(2)}, u32[]{:S(2)}) %all-to-all-start.7) | async-done | bytes 1048608 | tf_op jit(solution)/shard_map/all_to_all | solution.py:294
  328.0 1.2 copy-done
  329.3 1.0 shard_map.66
  330.3 4.3 %collective-permute-start.19 = (bf16[1,128,128]{2,1,0:T(8,128)(2,1)S(1)}, bf16[1,128,128]{2,1,0:T(8,128)(2,1)S(1)}, u32[]{:S(2)}, u32[]{:S(2)}) collective-permute-start(bf16[1,128,128]{2,1,0:T(8,128)(2,1)S(1)} %get-tuple-element.51), channel_id=1, source_target_pairs={{0,1},{1,2},{2,3},{3,4},{4,5},{5,6},{6,7},{7,8},{8,9},{9,10},{10,1... | collective-permute-start | bytes 98312 | tf_op jit(solution)/shard_map/ppermute | solution.py:305
  334.7 1.9 collective-permute-start.20
  336.7 2.0 shard_map.67
  338.7 3.9 %collective-permute-done.20.high_ref = bf16[1,128,128]{2,1,0:T(8,128)(2,1)S(1)} collective-permute-done((bf16[1,128,128]{2,1,0:T(8,128)(2,1)S(1)}, bf16[1,128,128]{2,1,0:T(8,128)(2,1)S(1)}, u32[]{:S(2)}, u32[]{:S(2)}) %collective-permute-start.20) | collective-permute-done | bytes 32800 | tf_op jit(solution)/shard_map/ppermute | solution.py:306
  342.6 1.4 shard_map.68
  (97 shorter events, 4.0 us)
Async XLA Ops:
  6.6 11.3 %copy-start.15 = (bf16[1,16,3,128,128]{4,3,2,1,0:T(8,128)(2,1)S(1)}, bf16[1,16,3,128,128]{4,3,2,1,0:T(8,128)(2,1)}, u32[]{:S(2)}) copy-start(bf16[1,16,3,128,128]{4,3,2,1,0:T(8,128)(2,1)} %param.4) | copy-start | bytes 4718596
  6.6 12.9 %copy-start.30 = (s32[1,16,3]{1,0,2:T(1,128)S(1)}, s32[1,16,3]{1,0,2:T(1,128)}, u32[]{:S(2)}) copy-start(s32[1,16,3]{1,0,2:T(1,128)} %param.5) | copy-start | bytes 580
  6.6 50.9 %all-to-all-start = ((bf16[32,128,128]{2,1,0:T(8,128)(2,1)}), bf16[32,128,128]{2,1,0:T(8,128)(2,1)}, u32[]{:S(2)}, u32[]{:S(2)}) async-start(bf16[32,128,128]{2,1,0:T(8,128)(2,1)} %get-tuple-element.28), calls=%async_computation | async-start | bytes 2097152 | tf_op jit(solution)/shard_map/all_to_all | solution.py:294
  17.9 39.7 %collective-permute-start.12 = (bf16[48,128,128]{2,1,0:T(8,128)(2,1)S(1)}, bf16[48,128,128]{2,1,0:T(8,128)(2,1)S(1)}, u32[]{:S(2)}, u32[]{:S(2)}) collective-permute-start(bf16[48,128,128]{2,1,0:T(8,128)(2,1)S(1)} %bitcast.13), channel_id=1, source_target_pairs={{0,224},{32,0},{64,32},{96,64},{128,96},{160,128},{192,160},{224,1... | collective-permute-start | bytes 4718600 | tf_op jit(solution)/shard_map/ppermute | solution.py:303
  19.7 3.6 %collective-permute-start = (s32[1,48]{1,0:T(1,128)S(1)}, s32[1,48]{1,0:T(1,128)S(1)}, u32[]{:S(2)}, u32[]{:S(2)}) collective-permute-start(s32[1,48]{1,0:T(1,128)S(1)} %reshape.166), channel_id=1, source_target_pairs={{0,1},{1,0},{2,3},{3,2},{4,5},{5,4},{6,7},{7,6},{8,9},{9,8},{10,11... | collective-permute-start | bytes 584 | tf_op jit(solution)/shard_map/ppermute | solution.py:271
  23.3 5.2 %collective-permute-start.1 = (s32[2,48]{1,0:T(2,128)S(1)}, s32[2,48]{1,0:T(2,128)S(1)}, u32[]{:S(2)}, u32[]{:S(2)}) collective-permute-start(s32[2,48]{1,0:T(2,128)S(1)} %pad_add_fusion.3), channel_id=1, source_target_pairs={{0,2},{1,3},{2,0},{3,1},{4,6},{5,7},{6,4},{7,5},{8,10},{9,11},{10,... | collective-permute-start | bytes 1160 | tf_op jit(solution)/shard_map/ppermute | solution.py:271
  28.5 11.5 %collective-permute-start.2 = (s32[4,48]{1,0:T(4,128)S(1)}, s32[4,48]{1,0:T(4,128)S(1)}, u32[]{:S(2)}, u32[]{:S(2)}) collective-permute-start(s32[4,48]{1,0:T(4,128)S(1)} %pad_add_fusion.1), channel_id=1, source_target_pairs={{0,4},{1,5},{2,6},{3,7},{4,0},{5,1},{6,2},{7,3},{8,12},{9,13},{10,... | collective-permute-start | bytes 2312 | tf_op jit(solution)/shard_map/ppermute | solution.py:271
  40.1 5.0 %collective-permute-start.3 = (s32[8,48]{1,0:T(8,128)S(1)}, s32[8,48]{1,0:T(8,128)S(1)}, u32[]{:S(2)}, u32[]{:S(2)}) collective-permute-start(s32[8,48]{1,0:T(8,128)S(1)} %pad_add_fusion), channel_id=1, source_target_pairs={{0,8},{1,9},{2,10},{3,11},{4,12},{5,13},{6,14},{7,15},{8,0},{9,1},... | collective-permute-start | bytes 4616 | tf_op jit(solution)/shard_map/ppermute | solution.py:271
  45.2 7.7 %collective-permute-start.4 = (s32[16,48]{1,0:T(8,128)S(1)}, s32[16,48]{1,0:T(8,128)S(1)}, u32[]{:S(2)}, u32[]{:S(2)}) collective-permute-start(s32[16,48]{1,0:T(8,128)S(1)} %concatenate.22), channel_id=1, source_target_pairs={{0,16},{1,17},{2,18},{3,19},{4,20},{5,21},{6,22},{7,23},{8,24},{9,... | collective-permute-start | bytes 9224 | tf_op jit(solution)/shard_map/ppermute | solution.py:271
  53.1 0.6 copy-start.29
  53.1 4.4 %collective-permute-start.5 = (s32[3,32]{1,0:T(4,128)S(1)}, s32[3,32]{1,0:T(4,128)S(1)}, u32[]{:S(2)}, u32[]{:S(2)}) collective-permute-start(s32[3,32]{1,0:T(4,128)S(1)} %pad_add_fusion.2.table.before), channel_id=1, source_target_pairs={{0,224},{32,0},{64,32},{96,64},{128,96},{160,128},{192,160},{224,1... | collective-permute-start | bytes 1160 | tf_op jit(solution)/shard_map/ppermute | solution.py:302
  57.5 0.6 copy-start.27
  57.5 1.1 copy-start.3
  63.6 10.6 %copy-start.4 = (bf16[48,128,128]{2,1,0:T(8,128)(2,1)S(1)}, bf16[48,128,128]{2,1,0:T(8,128)(2,1)}, u32[]{:S(2)}) copy-start(bf16[48,128,128]{2,1,0:T(8,128)(2,1)} %copy-done.3) | copy-start | bytes 4718596
  63.6 12.3 %copy-start.28 = (s32[3,32]{1,0:T(4,128)S(1)}, s32[3,32]{1,0:T(4,128)}, u32[]{:S(2)}) copy-start(s32[3,32]{1,0:T(4,128)} %copy-done.27) | copy-start | bytes 1156
  63.6 37.9 %all-to-all-start.1 = ((bf16[32,128,128]{2,1,0:T(8,128)(2,1)}), bf16[32,128,128]{2,1,0:T(8,128)(2,1)}, u32[]{:S(2)}, u32[]{:S(2)}) async-start(bf16[32,128,128]{2,1,0:T(8,128)(2,1)} %get-tuple-element.30), calls=%async_computation.1 | async-start | bytes 2097152 | tf_op jit(solution)/shard_map/all_to_all | solution.py:294
  74.2 19.7 %collective-permute-start.13 = (bf16[48,128,128]{2,1,0:T(8,128)(2,1)S(1)}, bf16[48,128,128]{2,1,0:T(8,128)(2,1)S(1)}, u32[]{:S(2)}, u32[]{:S(2)}) collective-permute-start(bf16[48,128,128]{2,1,0:T(8,128)(2,1)S(1)} %copy-done.4), channel_id=1, source_target_pairs={{0,224},{32,0},{64,32},{96,64},{128,96},{160,128},{192,160},{224,1... | collective-permute-start | bytes 4718600 | tf_op jit(solution)/shard_map/ppermute | solution.py:303
  76.0 18.0 %collective-permute-start.6 = (s32[3,32]{1,0:T(4,128)S(1)}, s32[3,32]{1,0:T(4,128)S(1)}, u32[]{:S(2)}, u32[]{:S(2)}) collective-permute-start(s32[3,32]{1,0:T(4,128)S(1)} %copy-done.28), channel_id=1, source_target_pairs={{0,224},{32,0},{64,32},{96,64},{128,96},{160,128},{192,160},{224,1... | collective-permute-start | bytes 1160 | tf_op jit(solution)/shard_map/ppermute | solution.py:302
  93.9 7.6 %copy-start.17 = (s32[3,32]{1,0:T(4,128)}, s32[3,32]{1,0:T(4,128)S(1)}, u32[]{:S(2)}) copy-start(s32[3,32]{1,0:T(4,128)S(1)} %collective-permute-done.6.table.before) | copy-start | bytes 1156
  93.9 7.6 %copy-start.5 = (bf16[48,128,128]{2,1,0:T(8,128)(2,1)}, bf16[48,128,128]{2,1,0:T(8,128)(2,1)S(1)}, u32[]{:S(2)}) copy-start(bf16[48,128,128]{2,1,0:T(8,128)(2,1)S(1)} %collective-permute-done.13.blocks_ref) | copy-start | bytes 4718596
  106.5 6.7 %copy-start.6 = (bf16[48,128,128]{2,1,0:T(8,128)(2,1)S(1)}, bf16[48,128,128]{2,1,0:T(8,128)(2,1)}, u32[]{:S(2)}) copy-start(bf16[48,128,128]{2,1,0:T(8,128)(2,1)} %copy-done.5) | copy-start | bytes 4718596
  106.5 7.6 %copy-start.18 = (s32[3,32]{1,0:T(4,128)S(1)}, s32[3,32]{1,0:T(4,128)}, u32[]{:S(2)}) copy-start(s32[3,32]{1,0:T(4,128)} %copy-done.17) | copy-start | bytes 1156
  106.5 33.2 %all-to-all-start.2 = ((bf16[32,128,128]{2,1,0:T(8,128)(2,1)}), bf16[32,128,128]{2,1,0:T(8,128)(2,1)}, u32[]{:S(2)}, u32[]{:S(2)}) async-start(bf16[32,128,128]{2,1,0:T(8,128)(2,1)} %get-tuple-element.32), calls=%async_computation.2 | async-start | bytes 2097152 | tf_op jit(solution)/shard_map/all_to_all | solution.py:294
  113.1 18.9 %collective-permute-start.14 = (bf16[48,128,128]{2,1,0:T(8,128)(2,1)S(1)}, bf16[48,128,128]{2,1,0:T(8,128)(2,1)S(1)}, u32[]{:S(2)}, u32[]{:S(2)}) collective-permute-start(bf16[48,128,128]{2,1,0:T(8,128)(2,1)S(1)} %copy-done.6), channel_id=1, source_target_pairs={{0,224},{32,0},{64,32},{96,64},{128,96},{160,128},{192,160},{224,1... | collective-permute-start | bytes 4718600 | tf_op jit(solution)/shard_map/ppermute | solution.py:303
  114.1 18.0 %collective-permute-start.7 = (s32[3,32]{1,0:T(4,128)S(1)}, s32[3,32]{1,0:T(4,128)S(1)}, u32[]{:S(2)}, u32[]{:S(2)}) collective-permute-start(s32[3,32]{1,0:T(4,128)S(1)} %copy-done.18), channel_id=1, source_target_pairs={{0,224},{32,0},{64,32},{96,64},{128,96},{160,128},{192,160},{224,1... | collective-permute-start | bytes 1160 | tf_op jit(solution)/shard_map/ppermute | solution.py:302
  132.0 7.6 %copy-start.19 = (s32[3,32]{1,0:T(4,128)}, s32[3,32]{1,0:T(4,128)S(1)}, u32[]{:S(2)}) copy-start(s32[3,32]{1,0:T(4,128)S(1)} %collective-permute-done.7.table.before) | copy-start | bytes 1156
  132.1 7.6 %copy-start.7 = (bf16[48,128,128]{2,1,0:T(8,128)(2,1)}, bf16[48,128,128]{2,1,0:T(8,128)(2,1)S(1)}, u32[]{:S(2)}) copy-start(bf16[48,128,128]{2,1,0:T(8,128)(2,1)S(1)} %collective-permute-done.14.blocks_ref) | copy-start | bytes 4718596
  144.6 6.7 %copy-start.8 = (bf16[48,128,128]{2,1,0:T(8,128)(2,1)S(1)}, bf16[48,128,128]{2,1,0:T(8,128)(2,1)}, u32[]{:S(2)}) copy-start(bf16[48,128,128]{2,1,0:T(8,128)(2,1)} %copy-done.7) | copy-start | bytes 4718596
  144.6 7.0 %copy-start.20 = (s32[3,32]{1,0:T(4,128)S(1)}, s32[3,32]{1,0:T(4,128)}, u32[]{:S(2)}) copy-start(s32[3,32]{1,0:T(4,128)} %copy-done.19) | copy-start | bytes 1156
  144.6 32.5 %all-to-all-start.3 = ((bf16[32,128,128]{2,1,0:T(8,128)(2,1)}), bf16[32,128,128]{2,1,0:T(8,128)(2,1)}, u32[]{:S(2)}, u32[]{:S(2)}) async-start(bf16[32,128,128]{2,1,0:T(8,128)(2,1)} %get-tuple-element.34), calls=%async_computation.3 | async-start | bytes 2097152 | tf_op jit(solution)/shard_map/all_to_all | solution.py:294
  151.3 18.3 %collective-permute-start.15 = (bf16[48,128,128]{2,1,0:T(8,128)(2,1)S(1)}, bf16[48,128,128]{2,1,0:T(8,128)(2,1)S(1)}, u32[]{:S(2)}, u32[]{:S(2)}) collective-permute-start(bf16[48,128,128]{2,1,0:T(8,128)(2,1)S(1)} %copy-done.8), channel_id=1, source_target_pairs={{0,224},{32,0},{64,32},{96,64},{128,96},{160,128},{192,160},{224,1... | collective-permute-start | bytes 4718600 | tf_op jit(solution)/shard_map/ppermute | solution.py:303
  151.6 18.0 %collective-permute-start.8 = (s32[3,32]{1,0:T(4,128)S(1)}, s32[3,32]{1,0:T(4,128)S(1)}, u32[]{:S(2)}, u32[]{:S(2)}) collective-permute-start(s32[3,32]{1,0:T(4,128)S(1)} %copy-done.20), channel_id=1, source_target_pairs={{0,224},{32,0},{64,32},{96,64},{128,96},{160,128},{192,160},{224,1... | collective-permute-start | bytes 1160 | tf_op jit(solution)/shard_map/ppermute | solution.py:302
  169.6 7.6 %copy-start.21 = (s32[3,32]{1,0:T(4,128)}, s32[3,32]{1,0:T(4,128)S(1)}, u32[]{:S(2)}) copy-start(s32[3,32]{1,0:T(4,128)S(1)} %collective-permute-done.8.table.before) | copy-start | bytes 1156
  169.6 7.6 %copy-start.9 = (bf16[48,128,128]{2,1,0:T(8,128)(2,1)}, bf16[48,128,128]{2,1,0:T(8,128)(2,1)S(1)}, u32[]{:S(2)}) copy-start(bf16[48,128,128]{2,1,0:T(8,128)(2,1)S(1)} %collective-permute-done.15.blocks_ref) | copy-start | bytes 4718596
  182.1 6.7 %copy-start.10 = (bf16[48,128,128]{2,1,0:T(8,128)(2,1)S(1)}, bf16[48,128,128]{2,1,0:T(8,128)(2,1)}, u32[]{:S(2)}) copy-start(bf16[48,128,128]{2,1,0:T(8,128)(2,1)} %copy-done.9) | copy-start | bytes 4718596
  182.1 6.7 %copy-start.22 = (s32[3,32]{1,0:T(4,128)S(1)}, s32[3,32]{1,0:T(4,128)}, u32[]{:S(2)}) copy-start(s32[3,32]{1,0:T(4,128)} %copy-done.21) | copy-start | bytes 1156
  182.1 32.8 %all-to-all-start.4 = ((bf16[32,128,128]{2,1,0:T(8,128)(2,1)}), bf16[32,128,128]{2,1,0:T(8,128)(2,1)}, u32[]{:S(2)}, u32[]{:S(2)}) async-start(bf16[32,128,128]{2,1,0:T(8,128)(2,1)} %get-tuple-element.36), calls=%async_computation.4 | async-start | bytes 2097152 | tf_op jit(solution)/shard_map/all_to_all | solution.py:294
  188.8 18.0 %collective-permute-start.16 = (bf16[48,128,128]{2,1,0:T(8,128)(2,1)S(1)}, bf16[48,128,128]{2,1,0:T(8,128)(2,1)S(1)}, u32[]{:S(2)}, u32[]{:S(2)}) collective-permute-start(bf16[48,128,128]{2,1,0:T(8,128)(2,1)S(1)} %copy-done.10), channel_id=1, source_target_pairs={{0,224},{32,0},{64,32},{96,64},{128,96},{160,128},{192,160},{224,1... | collective-permute-start | bytes 4718600 | tf_op jit(solution)/shard_map/ppermute | solution.py:303
  188.8 18.0 %collective-permute-start.9 = (s32[3,32]{1,0:T(4,128)S(1)}, s32[3,32]{1,0:T(4,128)S(1)}, u32[]{:S(2)}, u32[]{:S(2)}) collective-permute-start(s32[3,32]{1,0:T(4,128)S(1)} %copy-done.22), channel_id=1, source_target_pairs={{0,224},{32,0},{64,32},{96,64},{128,96},{160,128},{192,160},{224,1... | collective-permute-start | bytes 1160 | tf_op jit(solution)/shard_map/ppermute | solution.py:302
  206.8 8.2 %copy-start.23 = (s32[3,32]{1,0:T(4,128)}, s32[3,32]{1,0:T(4,128)S(1)}, u32[]{:S(2)}) copy-start(s32[3,32]{1,0:T(4,128)S(1)} %collective-permute-done.9.table.before) | copy-start | bytes 1156
  206.8 8.2 %copy-start.11 = (bf16[48,128,128]{2,1,0:T(8,128)(2,1)}, bf16[48,128,128]{2,1,0:T(8,128)(2,1)S(1)}, u32[]{:S(2)}) copy-start(bf16[48,128,128]{2,1,0:T(8,128)(2,1)S(1)} %collective-permute-done.16.blocks_ref) | copy-start | bytes 4718596
  219.9 6.7 %copy-start.12 = (bf16[48,128,128]{2,1,0:T(8,128)(2,1)S(1)}, bf16[48,128,128]{2,1,0:T(8,128)(2,1)}, u32[]{:S(2)}) copy-start(bf16[48,128,128]{2,1,0:T(8,128)(2,1)} %copy-done.11) | copy-start | bytes 4718596
  219.9 6.7 %copy-start.24 = (s32[3,32]{1,0:T(4,128)S(1)}, s32[3,32]{1,0:T(4,128)}, u32[]{:S(2)}) copy-start(s32[3,32]{1,0:T(4,128)} %copy-done.23) | copy-start | bytes 1156
  219.9 32.5 %all-to-all-start.5 = ((bf16[32,128,128]{2,1,0:T(8,128)(2,1)}), bf16[32,128,128]{2,1,0:T(8,128)(2,1)}, u32[]{:S(2)}, u32[]{:S(2)}) async-start(bf16[32,128,128]{2,1,0:T(8,128)(2,1)} %get-tuple-element.38), calls=%async_computation.5 | async-start | bytes 2097152 | tf_op jit(solution)/shard_map/all_to_all | solution.py:294
  226.5 18.0 %collective-permute-start.17 = (bf16[48,128,128]{2,1,0:T(8,128)(2,1)S(1)}, bf16[48,128,128]{2,1,0:T(8,128)(2,1)S(1)}, u32[]{:S(2)}, u32[]{:S(2)}) collective-permute-start(bf16[48,128,128]{2,1,0:T(8,128)(2,1)S(1)} %copy-done.12), channel_id=1, source_target_pairs={{0,224},{32,0},{64,32},{96,64},{128,96},{160,128},{192,160},{224,1... | collective-permute-start | bytes 4718600 | tf_op jit(solution)/shard_map/ppermute | solution.py:303
  226.6 17.9 %collective-permute-start.10 = (s32[3,32]{1,0:T(4,128)S(1)}, s32[3,32]{1,0:T(4,128)S(1)}, u32[]{:S(2)}, u32[]{:S(2)}) collective-permute-start(s32[3,32]{1,0:T(4,128)S(1)} %copy-done.24), channel_id=1, source_target_pairs={{0,224},{32,0},{64,32},{96,64},{128,96},{160,128},{192,160},{224,1... | collective-permute-start | bytes 1160 | tf_op jit(solution)/shard_map/ppermute | solution.py:302
  244.5 7.9 %copy-start.25 = (s32[3,32]{1,0:T(4,128)}, s32[3,32]{1,0:T(4,128)S(1)}, u32[]{:S(2)}) copy-start(s32[3,32]{1,0:T(4,128)S(1)} %collective-permute-done.10.table.before) | copy-start | bytes 1156
  244.5 7.9 %copy-start.13 = (bf16[48,128,128]{2,1,0:T(8,128)(2,1)}, bf16[48,128,128]{2,1,0:T(8,128)(2,1)S(1)}, u32[]{:S(2)}) copy-start(bf16[48,128,128]{2,1,0:T(8,128)(2,1)S(1)} %collective-permute-done.17.blocks_ref) | copy-start | bytes 4718596
  257.3 6.6 %copy-start.14 = (bf16[48,128,128]{2,1,0:T(8,128)(2,1)S(1)}, bf16[48,128,128]{2,1,0:T(8,128)(2,1)}, u32[]{:S(2)}) copy-start(bf16[48,128,128]{2,1,0:T(8,128)(2,1)} %copy-done.13) | copy-start | bytes 4718596
  257.3 6.6 %copy-start.26 = (s32[3,32]{1,0:T(4,128)S(1)}, s32[3,32]{1,0:T(4,128)}, u32[]{:S(2)}) copy-start(s32[3,32]{1,0:T(4,128)} %copy-done.25) | copy-start | bytes 1156
  257.3 32.7 %all-to-all-start.6 = ((bf16[32,128,128]{2,1,0:T(8,128)(2,1)}), bf16[32,128,128]{2,1,0:T(8,128)(2,1)S(1)}, u32[]{:S(2)}, u32[]{:S(2)}) async-start(bf16[32,128,128]{2,1,0:T(8,128)(2,1)} %get-tuple-element.40), calls=%async_computation.6 | async-start | bytes 2097152 | tf_op jit(solution)/shard_map/all_to_all | solution.py:294
  263.9 18.0 %collective-permute-start.18 = (bf16[48,128,128]{2,1,0:T(8,128)(2,1)S(1)}, bf16[48,128,128]{2,1,0:T(8,128)(2,1)}, u32[]{:S(2)}, u32[]{:S(2)}) collective-permute-start(bf16[48,128,128]{2,1,0:T(8,128)(2,1)S(1)} %copy-done.14), channel_id=1, source_target_pairs={{0,224},{32,0},{64,32},{96,64},{128,96},{160,128},{192,160},{224,1... | collective-permute-start | bytes 4718600 | tf_op jit(solution)/shard_map/ppermute | solution.py:303
  264.0 17.9 %collective-permute-start.11 = (s32[3,32]{1,0:T(4,128)S(1)}, s32[3,32]{1,0:T(4,128)S(1)}, u32[]{:S(2)}, u32[]{:S(2)}) collective-permute-start(s32[3,32]{1,0:T(4,128)S(1)} %copy-done.26), channel_id=1, source_target_pairs={{0,224},{32,0},{64,32},{96,64},{128,96},{160,128},{192,160},{224,1... | collective-permute-start | bytes 1160 | tf_op jit(solution)/shard_map/ppermute | solution.py:302
  281.9 8.1 %copy-start.1 = (s32[3,32]{1,0:T(4,128)}, s32[3,32]{1,0:T(4,128)S(1)}, u32[]{:S(2)}) copy-start(s32[3,32]{1,0:T(4,128)S(1)} %collective-permute-done.11.table.before) | copy-start | bytes 1156
  290.0 1.0 copy-start.16
  295.9 32.1 %all-to-all-start.7 = ((bf16[32,128,128]{2,1,0:T(8,128)(2,1)}), bf16[32,128,128]{2,1,0:T(8,128)(2,1)S(1)}, u32[]{:S(2)}, u32[]{:S(2)}) async-start(bf16[32,128,128]{2,1,0:T(8,128)(2,1)} %get-tuple-element.42), calls=%async_computation.7 | async-start | bytes 2097152 | tf_op jit(solution)/shard_map/all_to_all | solution.py:294
  302.4 25.7 %copy-start.2 = (s32[3,32]{1,0:T(4,128)S(1)}, s32[3,32]{1,0:T(4,128)}, u32[]{:S(2)}) copy-start(s32[3,32]{1,0:T(4,128)} %copy-done.1) | copy-start | bytes 1156
  328.0 1.2 copy-start
  330.3 8.3 %collective-permute-start.19 = (bf16[1,128,128]{2,1,0:T(8,128)(2,1)S(1)}, bf16[1,128,128]{2,1,0:T(8,128)(2,1)S(1)}, u32[]{:S(2)}, u32[]{:S(2)}) collective-permute-start(bf16[1,128,128]{2,1,0:T(8,128)(2,1)S(1)} %get-tuple-element.51), channel_id=1, source_target_pairs={{0,1},{1,2},{2,3},{3,4},{4,5},{5,6},{6,7},{7,8},{8,9},{9,10},{10,1... | collective-permute-start | bytes 98312 | tf_op jit(solution)/shard_map/ppermute | solution.py:305
  334.7 7.9 %collective-permute-start.20 = (bf16[1,128,128]{2,1,0:T(8,128)(2,1)S(1)}, bf16[1,128,128]{2,1,0:T(8,128)(2,1)S(1)}, u32[]{:S(2)}, u32[]{:S(2)}) collective-permute-start(bf16[1,128,128]{2,1,0:T(8,128)(2,1)S(1)} %get-tuple-element.50), channel_id=1, source_target_pairs={{1,0},{2,1},{3,2},{4,3},{5,4},{6,5},{7,6},{8,7},{9,8},{10,9},{11,1... | collective-permute-start | bytes 98312 | tf_op jit(solution)/shard_map/ppermute | solution.py:306

commit v2 on v1

--- a/solution.py
+++ b/solution.py
@@ -10,10 +10,13 @@
 VMEM = pl.BlockSpec(memory_space=pltpu.VMEM)
 SMEM = pl.BlockSpec(memory_space=pltpu.SMEM)
 HBM = pl.BlockSpec(memory_space=pltpu.HBM)
-PARAMS = pltpu.CompilerParams(vmem_limit_bytes=56 * 1024 * 1024)
+SEND_SPECS = [VMEM, VMEM, VMEM]
+SEND = pltpu.CompilerParams(vmem_limit_bytes=24 * 1024 * 1024)
+KEEP = pltpu.CompilerParams(vmem_limit_bytes=24 * 1024 * 1024)
 SMALL = pltpu.CompilerParams(vmem_limit_bytes=16 * 1024 * 1024)
-PART = 8
-WANTED, HOME, LANDING = range(3)
+PART = 4
+SAYS = 16
+WANTED, HOME, LANDED = range(3)
 
 
 def shifted(n, by):
@@ -24,16 +27,12 @@
     return lax.dot_general(v, block, (((1,), (1,)), ((), ())), preferred_element_type=jnp.float32)
 
 
-def send_products(wanted, state_scr, blocks_scr, out_ref, made, stage, out_sems):
-    tiles = state_scr.shape[0]
-    nnz = blocks_scr.shape[0] // tiles
-    for t in range(tiles):
-        v = state_scr[t]
-        for k in range(1, nnz):
-            made[t * (nnz - 1) + k - 1] = product(v, blocks_scr[t * nnz + k]).astype(jnp.bfloat16)
+def send_products(wanted, block_of, state_ref, out_ref, stage, out_sems):
+    rows, each = state_ref.shape[1], wanted.each
     copies = []
     for p in range(stage.shape[0]):
-        stage[p] = made[wanted(p)]
+        number = wanted(p)
+        stage[p, :rows] = product(state_ref[number // each], block_of(number)).astype(jnp.bfloat16)
         if p % PART == PART - 1:
             part = pl.ds(p + 1 - PART, PART)
             copy = pltpu.make_async_copy(stage.at[part], out_ref.at[part], out_sems.at[p // PART])
@@ -45,108 +44,137 @@
 
 def add_arrived(table, arrived_ref, gathered):
     gathered[...] = jnp.zeros_like(gathered)
+    rows = gathered.shape[1]
     for p in range(arrived_ref.shape[0]):
-        home = table[LANDING, p]
-        gathered[home] = gathered[home] + arrived_ref[p].astype(jnp.float32)
-
-
-def first_body(dest, seeds_ref, blocks_ref, out_ref, state_ref, blocks_scr, made, stage, state_scr, numbers, sems, out_sems):
+        home = table[LANDED, p]
+        gathered[home] = gathered[home] + arrived_ref[p, :rows].astype(jnp.float32)
+
+
+class Wanted:
+    def __init__(self, read, each):
+        self.read, self.each = read, each
+
+    def __call__(self, p):
+        return self.read(p)
+
+
+def first_body(dest, seeds_ref, blocks_ref, out_ref, state_ref, blocks_scr, stage, state_scr, lists, sems, out_sems):
     load = pltpu.make_async_copy(blocks_ref, blocks_scr, sems.at[0])
     load.start()
     tiles, nnz = dest.shape[1:]
+    each = nnz - 1
+    rows = state_scr.shape[1]
     for t in range(tiles):
         state_scr[t] = jnp.transpose(seeds_ref[t].astype(jnp.float32)).astype(jnp.bfloat16)
-    store = pltpu.make_async_copy(state_scr, state_ref, sems.at[2])
+    store = pltpu.make_async_copy(state_scr, state_ref, sems.at[1])
     store.start()
     for p in range(stage.shape[0]):
-        numbers[p] = 0
+        lists[0, p] = 0
+        lists[1, p] = tiles
     for t in range(tiles):
         for k in range(1, nnz):
-            numbers[dest[0, t, k] // tiles] = t * (nnz - 1) + k - 1
+            to = dest[0, t, k]
+            peer = to // tiles
+            lists[0, peer] = t * each + k - 1
+            lists[1, peer] = to - peer * tiles
+    for p in range(stage.shape[0]):
+        stage[p, rows:] = jnp.full((SAYS, stage.shape[2]), lists[1, p], jnp.int32).astype(jnp.float32).astype(jnp.bfloat16)
     load.wait()
-    send_products(lambda p: numbers[p], state_scr, blocks_scr, out_ref, made, stage, out_sems)
+    wanted = Wanted(lambda p: lists[0, p], each)
+    send_products(wanted, lambda n: blocks_scr[n + n // each + 1], state_scr, out_ref, stage, out_sems)
     store.wait()
 
 
-def send_body(
-    before, table, arrived_ref, local_ref, blocks_ref, out_ref, state_ref,
-    blocks_scr, made, stage, state_scr, gathered, local_scr, sems, out_sems,
-):
-    load_local = pltpu.make_async_copy(local_ref, local_scr, sems.at[1])
-    load = pltpu.make_async_copy(blocks_ref, blocks_scr, sems.at[0])
-    load_local.start()
-    load.start()
-    add_arrived(before, arrived_ref, gathered)
-    load_local.wait()
+def send_first(dest, seeds, blocks, peers):
+    count, points = blocks.shape[:2]
+    tiles, _, rows = seeds.shape
+    return pl.pallas_call(
+        first_body,
+        out_shape=(
+            jax.ShapeDtypeStruct((peers, rows + SAYS, points), jnp.bfloat16),
+            jax.ShapeDtypeStruct((tiles, rows, points), jnp.bfloat16),
+        ),
+        in_specs=[SMEM, VMEM, HBM],
+        out_specs=(HBM, HBM),
+        scratch_shapes=[
+            pltpu.VMEM(blocks.shape, jnp.bfloat16),
+            pltpu.VMEM((peers, rows + SAYS, points), jnp.bfloat16),
+            pltpu.VMEM((tiles, rows, points), jnp.bfloat16),
+            pltpu.SMEM((2, peers), jnp.int32),
+            pltpu.SemaphoreType.DMA((2,)),
+            pltpu.SemaphoreType.DMA((peers // PART,)),
+        ],
+        compiler_params=SEND,
+        cost_estimate=pl.CostEstimate(
+            flops=2 * peers * points * points * rows, bytes_accessed=4 << 20, transcendentals=0
+        ),
+    )(dest, seeds, blocks)
+
+
+def send_body(table, arrived_ref, local_ref, off_ref, out_ref, state_ref, stage, gathered, state_scr, store_sem, out_sems):
+    each = off_ref.shape[0] // state_scr.shape[0]
+    add_arrived(table, arrived_ref, gathered)
     for t in range(state_scr.shape[0]):
-        state_scr[t] = (gathered[t] + local_scr[t]).astype(jnp.bfloat16)
-    store = pltpu.make_async_copy(state_scr, state_ref, sems.at[2])
+        state_scr[t] = (gathered[t] + local_ref[t]).astype(jnp.bfloat16)
+    store = pltpu.make_async_copy(state_scr, state_ref, store_sem)
     store.start()
-    load.wait()
-    send_products(lambda p: table[WANTED, p], state_scr, blocks_scr, out_ref, made, stage, out_sems)
+    wanted = Wanted(lambda p: table[WANTED, p], each)
+    send_products(wanted, lambda n: off_ref[n], state_scr, out_ref, stage, out_sems)
     store.wait()
 
 
-def send(tables, carried, blocks, peers):
-    count, points = blocks.shape[:2]
-    first = len(carried) == 1
-    rows = points
-    tiles = carried[-1].shape[0]
-    scratch = [
-        pltpu.VMEM(blocks.shape, jnp.bfloat16),
-        pltpu.VMEM((count - tiles, rows, points), jnp.bfloat16),
-        pltpu.VMEM((peers, rows, points), jnp.bfloat16),
-        pltpu.VMEM((tiles, rows, points), jnp.bfloat16),
-    ]
-    if first:
-        scratch.append(pltpu.SMEM((peers,), jnp.int32))
-    else:
-        scratch.append(pltpu.VMEM((tiles + 1, rows, points), jnp.float32))
-        scratch.append(pltpu.VMEM((tiles, rows, points), jnp.float32))
-    scratch += [pltpu.SemaphoreType.DMA((3,)), pltpu.SemaphoreType.DMA((peers // PART,))]
-    return pl.pallas_call(
-        first_body if first else send_body,
+def send(table, arrived, local, off):
+    peers = arrived.shape[0]
+    tiles, rows, points = local.shape
+    return pl.pallas_call(
+        send_body,
         out_shape=(
             jax.ShapeDtypeStruct((peers, rows, points), jnp.bfloat16),
             jax.ShapeDtypeStruct((tiles, rows, points), jnp.bfloat16),
         ),
-        in_specs=[SMEM] * len(tables) + ([VMEM] if first else [VMEM, HBM]) + [HBM],
+        in_specs=[SMEM] + SEND_SPECS,
         out_specs=(HBM, HBM),
-        scratch_shapes=scratch,
-        compiler_params=PARAMS,
+        scratch_shapes=[
+            pltpu.VMEM((peers, rows, points), jnp.bfloat16),
+            pltpu.VMEM((tiles + 1, rows, points), jnp.float32),
+            pltpu.VMEM((tiles, rows, points), jnp.bfloat16),
+            pltpu.SemaphoreType.DMA,
+            pltpu.SemaphoreType.DMA((peers // PART,)),
+        ],
+        compiler_params=SEND,
         cost_estimate=pl.CostEstimate(
             flops=2 * peers * points * points * rows, bytes_accessed=4 << 20, transcendentals=0
         ),
-    )(*tables, *carried, blocks)
-
-
-def keep_body(table, state_ref, blocks_ref, local_ref, total, sem):
+    )(table, arrived, local, off)
+
+
+def keep_body(table, state_ref, diag_ref, off_ref, local_ref, total, sem):
     tiles = state_ref.shape[0]
-    nnz = blocks_ref.shape[0] // tiles
-    for t in range(tiles):
-        total[t] = product(state_ref[t], blocks_ref[t * nnz])
-    for t in range(tiles):
-        for k in range(nnz - 1):
-            home = table[HOME, t * (nnz - 1) + k]
-            total[home] = total[home] + product(state_ref[t], blocks_ref[t * nnz + 1 + k])
+    each = off_ref.shape[0] // tiles
+    for t in range(tiles):
+        total[t] = product(state_ref[t], diag_ref[t])
+    for t in range(tiles):
+        for k in range(each):
+            home = table[HOME, t * each + k]
+            total[home] = total[home] + product(state_ref[t], off_ref[t * each + k])
     store = pltpu.make_async_copy(total.at[pl.ds(0, tiles)], local_ref, sem)
     store.start()
     store.wait()
 
 
-def keep(table, state, blocks):
+def keep(table, state, diag, off):
     tiles, rows, points = state.shape
     return pl.pallas_call(
         keep_body,
         out_shape=jax.ShapeDtypeStruct((tiles, rows, points), jnp.float32),
-        in_specs=[SMEM, VMEM, VMEM],
+        in_specs=[SMEM, VMEM, VMEM, VMEM],
         out_specs=HBM,
         scratch_shapes=[pltpu.VMEM((tiles + 1, rows, points), jnp.float32), pltpu.SemaphoreType.DMA],
-        compiler_params=PARAMS,
+        compiler_params=KEEP,
         cost_estimate=pl.CostEstimate(
-            flops=2 * blocks.shape[0] * points * points * rows, bytes_accessed=4 << 20, transcendentals=0
-        ),
-    )(table, state, blocks)
+            flops=2 * (tiles + off.shape[0]) * points * points * rows, bytes_accessed=4 << 20, transcendentals=0
+        ),
+    )(table, state, diag, off)
 
 
 def last_body(before, arrived_ref, local_ref, final_ref, edges_ref, gathered, local_scr, sem):
@@ -264,44 +292,34 @@
     return wanted, home
 
 
-def landing_row(dest, me, tiles, peers):
-    known = dest.reshape(1, -1)
-    step = 1
-    while step < peers:
-        known = jnp.concatenate([known, lax.ppermute(known, "tile", [(i, i ^ step) for i in range(peers)])], axis=0)
-        step *= 2
-    row_of = jnp.arange(peers, dtype=jnp.int32)
-    lands = jnp.max(jnp.where(known // tiles == me, known % tiles, -1), axis=1)
-    lands = jnp.where((lands < 0) | (row_of == 0), tiles, lands)
-    match = (row_of[:, None] ^ row_of[None, :]) == me
-    return jnp.sum(jnp.where(match, lands[None, :], 0), axis=1)
-
-
 def body(seeds, blocks, dest_tiles):
     tiles, nnz, points = blocks.shape[1:4]
     width = seeds.shape[2]
     ndays, peers = lax.axis_size("day"), lax.axis_size("tile")
     me = lax.axis_index("tile")
-
     seeds = seeds.reshape(tiles, points, width)
-    wblk = blocks.reshape(tiles * nnz, points, points)
+    whole = blocks.reshape(tiles * nnz, points, points)
+    diag, off = blocks[0, :, 0], blocks[0, :, 1:].reshape(tiles * (nnz - 1), points, points)
+    onward = functools.partial(lax.ppermute, axis_name="day", perm=shifted(ndays, -1))
 
     for step in range(ndays):
         if step == 0:
-            out, state = send((dest_tiles,), (seeds,), wblk, peers)
+            out, state = send_first(dest_tiles, seeds, whole, peers)
+            dest, state = lax.optimization_barrier((dest_tiles[0], state))
+            rows = own_rows(dest, me, tiles, peers, nnz)
+            table = jnp.stack([*rows, jnp.zeros_like(rows[0])])
         else:
-            out, state = send((before, table), (arrived, local), wblk, peers)
+            out, state = send(table, arrived, local, off)
         arrived = lax.all_to_all(out, "tile", split_axis=0, concat_axis=0, tiled=True)
+        local = keep(table, state, diag, off)
+        table = onward(table)
         if step == 0:
-            dest, state = lax.optimization_barrier((dest_tiles[0], state))
-            landing = landing_row(dest, me, tiles, peers)
-            table = jnp.stack([*own_rows(dest, me, tiles, peers, nnz), landing])
-        local = keep(table, state, wblk)
-        before = table
+            own = lax.broadcasted_iota(jnp.int32, (peers,), 0) == me
+            landed = jnp.where(own, tiles, arrived[:, width, 0].astype(jnp.int32))
+            table = jnp.concatenate([table[:2], landed[None]], axis=0)
         if step < ndays - 1:
-            table = lax.ppermute(table, "day", shifted(ndays, -1))
-            wblk = lax.ppermute(wblk, "day", shifted(ndays, -1))
-    final, edges = last_sum(before, arrived, local)
+            diag, off = onward(diag), onward(off)
+    final, edges = last_sum(table, arrived, local)
     low = lax.ppermute(edges[1:], "tile", [(i, i + 1) for i in range(peers - 1)])
     high = lax.ppermute(edges[:1], "tile", [(i + 1, i) for i in range(peers - 1)])
     place = jnp.stack([me == 0, me == peers - 1]).astype(jnp.int32)

time: 346 us -> 347 us (level); the launches traced: 344 us -> 341 us
  local copies, waits for them, and re-layouts: 5.34 us -> 36.4 us
  Pallas kernels: 73.8 us -> 48.9 us
  waiting for transfers between devices: 165 us -> 159 us
  starting transfers between devices: 98.3 us -> 94.3 us
    all_to_all x8, waiting for transfers between devices: 68.8 us -> 37.6 us  [body(): lax.all_to_all(out, 'tile', split_axis=0, concat_axis=0, tiled=True)]
    unnamed x64 -> x88, local copies, waits for them, and re-layouts: 4.86 us -> 35 us
    ppermute x19 -> x22, waiting for transfers between devices: 92.1 us -> 118 us  [the longest x14 110 us: body(): diag, off = (onward(diag), onward(off))]
    pallas_call x8, Pallas kernels: 30.5 us -> 16.3 us  [keep(): pl.pallas_call(keep_body, out_shape=jax.ShapeDtypeStruct((tiles, rows, po...]
    pallas_call x8, Pallas kernels: 38.9 us -> 28.2 us  [the longest x7 23.2 us: send(): pl.pallas_call(send_body, out_shape=(jax.ShapeDtypeStruct((peers, rows, p...]
    ppermute x19 -> x22, starting transfers between devices: 30.7 us -> 24.5 us  [the longest x14 21.9 us: body(): diag, off = (onward(diag), onward(off))]
  transfers between devices with their start and end apart: 29 -> 32, of which waited for: 19 -> 17; matrix products, arithmetic and copies ran while one was open for 0% -> 1% of each run, Pallas kernels for 9% -> 5%
where the time goes in v2:
time: 347 us; the launch traced here: 341 us
  waiting for transfers between devices  159 us (46%)
  starting transfers between devices  94.3 us (27%)
  Pallas kernels  48.9 us (14%)
  local copies, waits for them, and re-layouts  36.4 us (10%)
    ppermute x14, waiting for transfers between devices, body(): diag, off = (onward(diag), onward(off))  110 us
    all_to_all x8, starting transfers between devices, body(): lax.all_to_all(out, 'tile', split_axis=0, concat_axis=0, tiled=True)  63.5 us
    all_to_all x8, waiting for transfers between devices, body(): lax.all_to_all(out, 'tile', split_axis=0, concat_axis=0, tiled=True)  37.6 us
    unnamed x88, local copies, waits for them, and re-layouts  35 us
    pallas_call x7, Pallas kernels, send(): pl.pallas_call(send_body, out_shape=(jax.ShapeDtypeStruct((peers, rows, p...  23.2 us
    ppermute x14, starting transfers between devices, body(): diag, off = (onward(diag), onward(off))  21.9 us
    pallas_call x8, Pallas kernels, keep(): pl.pallas_call(keep_body, out_shape=jax.ShapeDtypeStruct((tiles, rows, po...  16.3 us
    ppermute x8, waiting for transfers between devices, body(): table = onward(table)  7.32 us
  transfers between devices with their start and end apart: 32, of which 17 were waited for; matrix products, arithmetic and copies ran while one was open for 1% of the time, Pallas kernels for 5%

profile of v2, /device:TPU:56, one launch (start us, length us, event | category | flops | bytes accessed | tf_op | source)
XLA Modules:
  0.0 340.8 jit_solution(3573288176300991570)
XLA Ops:
  1.4 1.4 copy-done
  3.8 5.0 %shard_map.50 = (bf16[32,144,128]{2,1,0:T(8,128)(2,1)S(1)}, bf16[16,128,128]{2,1,0:T(8,128)(2,1)S(1)}) custom-call(s32[1,16,3]{2,1,0:T(8,128)S(1)} %copy.15.dest, bf16[16,128,128]{2,1,0:T(8,128)(2,1)S(1)} %bitcast.18, bf16[48,128,128]{2,1,0:T(8,128)(2,1)S(1)} %bitcast.17), custom_call_target="tpu_custom_call" | custom-call | flops 134217728 | bytes 4194304 | tf_op jit(solution)/shard_map/pallas_call | solution.py:91
  10.6 11.1 %all-to-all-start = ((bf16[32,144,128]{2,1,0:T(8,128)(2,1)}), bf16[32,144,128]{2,1,0:T(8,128)(2,1)S(1)}, u32[]{:S(2)}, u32[]{:S(2)}) async-start(bf16[32,144,128]{2,1,0:T(8,128)(2,1)} %copy-done.12), calls=%async_computation | async-start | bytes 2359296 | tf_op jit(solution)/shard_map/all_to_all | solution.py:313
  22.8 1.6 collective-permute-start.8
  24.9 1.2 collective-permute-start
  27.3 2.5 shard_map.51.local_ref
  29.8 7.3 %collective-permute-done = s32[3,32]{1,0:T(4,128)S(1)} collective-permute-done((s32[3,32]{1,0:T(4,128)S(1)}, s32[3,32]{1,0:T(4,128)S(1)}, u32[]{:S(2)}, u32[]{:S(2)}) %collective-permute-start) | collective-permute-done | bytes 416 | tf_op jit(solution)/shard_map/ppermute | solution.py:315
  37.1 14.7 %all-to-all-done.arrived_ref = bf16[32,144,128]{2,1,0:T(8,128)(2,1)S(1)} async-done(((bf16[32,144,128]{2,1,0:T(8,128)(2,1)}), bf16[32,144,128]{2,1,0:T(8,128)(2,1)S(1)}, u32[]{:S(2)}, u32[]{:S(2)}) %all-to-all-start) | async-done | bytes 1179680 | tf_op jit(solution)/shard_map/all_to_all | solution.py:313
  52.5 4.8 %shard_map.52 = (bf16[32,128,128]{2,1,0:T(8,128)(2,1)S(1)}, bf16[16,128,128]{2,1,0:T(8,128)(2,1)S(1)}) custom-call(s32[3,32]{1,0:T(4,128)S(1)} %pad_add_fusion.1.table, bf16[32,144,128]{2,1,0:T(8,128)(2,1)S(1)} %all-to-all-done.arrived_ref, f32[16,128,128]{2,1,0:T(8,128)S(1)} %shard_map.51.local_ref, bf16[32,128,128]{2,1,0:T(8,128)(2,1)} %collective-permute-done.8.off_ref), custom_call_target="tpu_custom_call" | custom-call | flops 134217728 | bytes 4194304 | tf_op jit(solution)/shard_map/pallas_call | solution.py:129
  58.2 6.4 %all-to-all-start.1 = ((bf16[32,128,128]{2,1,0:T(8,128)(2,1)}), bf16[32,128,128]{2,1,0:T(8,128)(2,1)S(1)}, u32[]{:S(2)}, u32[]{:S(2)}) async-start(bf16[32,128,128]{2,1,0:T(8,128)(2,1)} %copy-done.13), calls=%async_computation.1 | async-start | bytes 2097152 | tf_op jit(solution)/shard_map/all_to_all | solution.py:313
  65.1 2.4 collective-permute-start.9
  67.6 15.7 %collective-permute-done.9.diag_ref = bf16[16,128,128]{2,1,0:T(8,128)(2,1)S(1)} collective-permute-done((bf16[16,128,128]{2,1,0:T(8,128)(2,1)S(1)}, bf16[16,128,128]{2,1,0:T(8,128)(2,1)S(1)}, u32[]{:S(2)}, u32[]{:S(2)}) %collective-permute-start.9) | collective-permute-done | bytes 524320 | tf_op jit(solution)/shard_map/ppermute | solution.py:321
  83.2 1.2 copy-done.29
  84.5 2.5 shard_map.53.local_ref
  87.1 3.6 %all-to-all-done.1.arrived_ref = bf16[32,128,128]{2,1,0:T(8,128)(2,1)S(1)} async-done(((bf16[32,128,128]{2,1,0:T(8,128)(2,1)}), bf16[32,128,128]{2,1,0:T(8,128)(2,1)S(1)}, u32[]{:S(2)}, u32[]{:S(2)}) %all-to-all-start.1) | async-done | bytes 1048608 | tf_op jit(solution)/shard_map/all_to_all | solution.py:313
  90.6 4.1 %shard_map.54 = (bf16[32,128,128]{2,1,0:T(8,128)(2,1)S(1)}, bf16[16,128,128]{2,1,0:T(8,128)(2,1)S(1)}) custom-call(s32[3,32]{1,0:T(4,128)S(1)} %collective-permute-done.1.table, bf16[32,128,128]{2,1,0:T(8,128)(2,1)S(1)} %all-to-all-done.1.arrived_ref, f32[16,128,128]{2,1,0:T(8,128)S(1)} %shard_map.53.local_ref, ...), custom_call_target="tpu_custom_call" | custom-call | flops 134217728 | bytes 4194304 | tf_op jit(solution)/shard_map/pallas_call | solution.py:129
  96.5 6.4 %all-to-all-start.2 = ((bf16[32,128,128]{2,1,0:T(8,128)(2,1)}), bf16[32,128,128]{2,1,0:T(8,128)(2,1)S(1)}, u32[]{:S(2)}, u32[]{:S(2)}) async-start(bf16[32,128,128]{2,1,0:T(8,128)(2,1)} %copy-done.14), calls=%async_computation.2 | async-start | bytes 2097152 | tf_op jit(solution)/shard_map/all_to_all | solution.py:313
  102.9 2.6 collective-permute-start.12
  106.8 16.8 %collective-permute-done.11.diag_ref = bf16[16,128,128]{2,1,0:T(8,128)(2,1)S(1)} collective-permute-done((bf16[16,128,128]{2,1,0:T(8,128)(2,1)}, bf16[16,128,128]{2,1,0:T(8,128)(2,1)S(1)}, u32[]{:S(2)}, u32[]{:S(2)}) %collective-permute-start.11) | collective-permute-done | bytes 524320 | tf_op jit(solution)/shard_map/ppermute | solution.py:321
  123.6 1.2 copy-done.31
  124.8 1.9 shard_map.55.local_ref
  127.7 3.7 %all-to-all-done.2.arrived_ref = bf16[32,128,128]{2,1,0:T(8,128)(2,1)S(1)} async-done(((bf16[32,128,128]{2,1,0:T(8,128)(2,1)}), bf16[32,128,128]{2,1,0:T(8,128)(2,1)S(1)}, u32[]{:S(2)}, u32[]{:S(2)}) %all-to-all-start.2) | async-done | bytes 1048608 | tf_op jit(solution)/shard_map/all_to_all | solution.py:313
  131.4 1.2 copy-done.3
  132.7 2.6 shard_map.56
  136.0 6.1 %all-to-all-start.3 = ((bf16[32,128,128]{2,1,0:T(8,128)(2,1)}), bf16[32,128,128]{2,1,0:T(8,128)(2,1)S(1)}, u32[]{:S(2)}, u32[]{:S(2)}) async-start(bf16[32,128,128]{2,1,0:T(8,128)(2,1)} %get-tuple-element.34), calls=%async_computation.3 | async-start | bytes 2097152 | tf_op jit(solution)/shard_map/all_to_all | solution.py:313
  142.1 2.8 collective-permute-start.14
  145.1 17.8 %collective-permute-done.13.diag_ref = bf16[16,128,128]{2,1,0:T(8,128)(2,1)S(1)} collective-permute-done((bf16[16,128,128]{2,1,0:T(8,128)(2,1)}, bf16[16,128,128]{2,1,0:T(8,128)(2,1)S(1)}, u32[]{:S(2)}, u32[]{:S(2)}) %collective-permute-start.13) | collective-permute-done | bytes 524320 | tf_op jit(solution)/shard_map/ppermute | solution.py:321
  162.9 1.2 copy-done.33
  164.1 1.9 shard_map.57.local_ref
  167.0 2.8 all-to-all-done.3.arrived_ref
  169.8 1.2 copy-done.5
  171.0 2.6 shard_map.58
  174.4 7.0 %all-to-all-start.4 = ((bf16[32,128,128]{2,1,0:T(8,128)(2,1)}), bf16[32,128,128]{2,1,0:T(8,128)(2,1)S(1)}, u32[]{:S(2)}, u32[]{:S(2)}) async-start(bf16[32,128,128]{2,1,0:T(8,128)(2,1)} %get-tuple-element.36), calls=%async_computation.4 | async-start | bytes 2097152 | tf_op jit(solution)/shard_map/all_to_all | solution.py:313
  181.4 2.8 collective-permute-start.16
  184.4 17.8 %collective-permute-done.15.diag_ref = bf16[16,128,128]{2,1,0:T(8,128)(2,1)S(1)} collective-permute-done((bf16[16,128,128]{2,1,0:T(8,128)(2,1)}, bf16[16,128,128]{2,1,0:T(8,128)(2,1)S(1)}, u32[]{:S(2)}, u32[]{:S(2)}) %collective-permute-start.15) | collective-permute-done | bytes 524320 | tf_op jit(solution)/shard_map/ppermute | solution.py:321
  202.2 1.2 copy-done.35
  203.4 1.9 shard_map.59.local_ref
  206.3 1.6 all-to-all-done.4.arrived_ref
  207.9 1.2 copy-done.7
  209.2 2.6 shard_map.60
  212.5 8.2 %all-to-all-start.5 = ((bf16[32,128,128]{2,1,0:T(8,128)(2,1)}), bf16[32,128,128]{2,1,0:T(8,128)(2,1)S(1)}, u32[]{:S(2)}, u32[]{:S(2)}) async-start(bf16[32,128,128]{2,1,0:T(8,128)(2,1)} %get-tuple-element.38), calls=%async_computation.5 | async-start | bytes 2097152 | tf_op jit(solution)/shard_map/all_to_all | solution.py:313
  220.7 2.8 collective-permute-start.18
  223.7 17.8 %collective-permute-done.17.diag_ref = bf16[16,128,128]{2,1,0:T(8,128)(2,1)S(1)} collective-permute-done((bf16[16,128,128]{2,1,0:T(8,128)(2,1)}, bf16[16,128,128]{2,1,0:T(8,128)(2,1)S(1)}, u32[]{:S(2)}, u32[]{:S(2)}) %collective-permute-start.17) | collective-permute-done | bytes 524320 | tf_op jit(solution)/shard_map/ppermute | solution.py:321
  241.5 1.2 copy-done.37
  242.7 1.9 shard_map.61.local_ref
  246.7 1.2 copy-done.9
  247.9 2.6 shard_map.62
  251.3 8.7 %all-to-all-start.6 = ((bf16[32,128,128]{2,1,0:T(8,128)(2,1)}), bf16[32,128,128]{2,1,0:T(8,128)(2,1)S(1)}, u32[]{:S(2)}, u32[]{:S(2)}) async-start(bf16[32,128,128]{2,1,0:T(8,128)(2,1)} %get-tuple-element.40), calls=%async_computation.6 | async-start | bytes 2097152 | tf_op jit(solution)/shard_map/all_to_all | solution.py:313
  260.0 2.8 collective-permute-start.20
  263.0 17.8 %collective-permute-done.19.diag_ref = bf16[16,128,128]{2,1,0:T(8,128)(2,1)S(1)} collective-permute-done((bf16[16,128,128]{2,1,0:T(8,128)(2,1)}, bf16[16,128,128]{2,1,0:T(8,128)(2,1)S(1)}, u32[]{:S(2)}, u32[]{:S(2)}) %collective-permute-start.19) | collective-permute-done | bytes 524320 | tf_op jit(solution)/shard_map/ppermute | solution.py:321
  280.8 1.2 copy-done.39
  282.0 1.9 shard_map.63.local_ref
  285.2 1.2 copy-done.11
  286.5 4.1 %shard_map.64 = (bf16[32,128,128]{2,1,0:T(8,128)(2,1)S(1)}, bf16[16,128,128]{2,1,0:T(8,128)(2,1)S(1)}) custom-call(s32[3,32]{1,0:T(4,128)S(1)} %collective-permute-done.6.table, bf16[32,128,128]{2,1,0:T(8,128)(2,1)S(1)} %all-to-all-done.6.arrived_ref, f32[16,128,128]{2,1,0:T(8,128)S(1)} %copy-done.11, bf16[32,128,128]{2,1,0:T(8,128)(2,1)S(1)} %collective-permute-done.20.off_ref), custom_call_target="tpu_custom_call" | custom-call | flops 134217728 | bytes 4194304 | tf_op jit(solution)/shard_map/pallas_call | solution.py:129
  292.3 9.6 %all-to-all-start.7 = ((bf16[32,128,128]{2,1,0:T(8,128)(2,1)}), bf16[32,128,128]{2,1,0:T(8,128)(2,1)S(1)}, u32[]{:S(2)}, u32[]{:S(2)}) async-start(bf16[32,128,128]{2,1,0:T(8,128)(2,1)} %copy-done.15), calls=%async_computation.7 | async-start | bytes 2097152 | tf_op jit(solution)/shard_map/all_to_all | solution.py:313
  301.9 2.8 collective-permute-start.21
  304.9 6.5 %collective-permute-done.21.diag_ref = bf16[16,128,128]{2,1,0:T(8,128)(2,1)S(1)} collective-permute-done((bf16[16,128,128]{2,1,0:T(8,128)(2,1)S(1)}, bf16[16,128,128]{2,1,0:T(8,128)(2,1)S(1)}, u32[]{:S(2)}, u32[]{:S(2)}) %collective-permute-start.21) | collective-permute-done | bytes 524320 | tf_op jit(solution)/shard_map/ppermute | solution.py:321
  314.3 1.9 shard_map.65.local_ref
  316.1 9.8 %all-to-all-done.7.arrived_ref = bf16[32,128,128]{2,1,0:T(8,128)(2,1)S(1)} async-done(((bf16[32,128,128]{2,1,0:T(8,128)(2,1)}), bf16[32,128,128]{2,1,0:T(8,128)(2,1)S(1)}, u32[]{:S(2)}, u32[]{:S(2)}) %all-to-all-start.7) | async-done | bytes 1048608 | tf_op jit(solution)/shard_map/all_to_all | solution.py:313
  327.0 4.3 %collective-permute-start.22 = (bf16[1,128,128]{2,1,0:T(8,128)(2,1)S(1)}, bf16[1,128,128]{2,1,0:T(8,128)(2,1)S(1)}, u32[]{:S(2)}, u32[]{:S(2)}) collective-permute-start(bf16[1,128,128]{2,1,0:T(8,128)(2,1)S(1)} %get-tuple-element.51), channel_id=1, source_target_pairs={{0,1},{1,2},{2,3},{3,4},{4,5},{5,6},{6,7},{7,8},{8,9},{9,10},{10,1... | collective-permute-start | bytes 98312 | tf_op jit(solution)/shard_map/ppermute | solution.py:323
  331.4 1.9 collective-permute-start.23
  333.4 2.0 shard_map.67
  335.4 3.9 %collective-permute-done.23.high_ref = bf16[1,128,128]{2,1,0:T(8,128)(2,1)S(1)} collective-permute-done((bf16[1,128,128]{2,1,0:T(8,128)(2,1)S(1)}, bf16[1,128,128]{2,1,0:T(8,128)(2,1)S(1)}, u32[]{:S(2)}, u32[]{:S(2)}) %collective-permute-start.23) | collective-permute-done | bytes 32800 | tf_op jit(solution)/shard_map/ppermute | solution.py:324
  339.3 1.4 shard_map.68
  (124 shorter events, 27.6 us)
Async XLA Ops:
  1.4 1.4 copy-start
  2.8 1.0 copy-start.16
  8.8 1.0 copy-start.12
  10.6 11.2 %copy-start.1 = (bf16[1,16,3,128,128]{4,3,2,1,0:T(8,128)(2,1)S(1)}, bf16[1,16,3,128,128]{4,3,2,1,0:T(8,128)(2,1)}, u32[]{:S(2)}) copy-start(bf16[1,16,3,128,128]{4,3,2,1,0:T(8,128)(2,1)} %param.4) | copy-start | bytes 4718596
  10.6 41.2 %all-to-all-start = ((bf16[32,144,128]{2,1,0:T(8,128)(2,1)}), bf16[32,144,128]{2,1,0:T(8,128)(2,1)S(1)}, u32[]{:S(2)}, u32[]{:S(2)}) async-start(bf16[32,144,128]{2,1,0:T(8,128)(2,1)} %copy-done.12), calls=%async_computation | async-start | bytes 2359296 | tf_op jit(solution)/shard_map/all_to_all | solution.py:313
  21.8 2.7 copy-start.42
  22.8 29.6 %collective-permute-start.8 = (bf16[32,128,128]{2,1,0:T(8,128)(2,1)}, bf16[32,128,128]{2,1,0:T(8,128)(2,1)}, u32[]{:S(2)}, u32[]{:S(2)}) collective-permute-start(bf16[32,128,128]{2,1,0:T(8,128)(2,1)} %bitcast.6.off_ref), channel_id=1, source_target_pairs={{0,224},{32,0},{64,32},{96,64},{128,96},{160,128},{192,160},{224,1... | collective-permute-start | bytes 3145736 | tf_op jit(solution)/shard_map/ppermute | solution.py:321
  24.9 12.2 %collective-permute-start = (s32[3,32]{1,0:T(4,128)S(1)}, s32[3,32]{1,0:T(4,128)S(1)}, u32[]{:S(2)}, u32[]{:S(2)}) collective-permute-start(s32[3,32]{1,0:T(4,128)S(1)} %pad_add_fusion.table), channel_id=1, source_target_pairs={{0,224},{32,0},{64,32},{96,64},{128,96},{160,128},{192,160},{224,1... | collective-permute-start | bytes 1160 | tf_op jit(solution)/shard_map/ppermute | solution.py:315
  26.2 1.0 copy-start.25
  58.2 25.0 %copy-start.28 = (bf16[16,128,128]{2,1,0:T(8,128)(2,1)}, bf16[16,128,128]{2,1,0:T(8,128)(2,1)S(1)}, u32[]{:S(2)}) copy-start(bf16[16,128,128]{2,1,0:T(8,128)(2,1)S(1)} %get-tuple-element.31.state_ref) | copy-start | bytes 1572868
  58.2 32.4 %all-to-all-start.1 = ((bf16[32,128,128]{2,1,0:T(8,128)(2,1)}), bf16[32,128,128]{2,1,0:T(8,128)(2,1)S(1)}, u32[]{:S(2)}, u32[]{:S(2)}) async-start(bf16[32,128,128]{2,1,0:T(8,128)(2,1)} %copy-done.13), calls=%async_computation.1 | async-start | bytes 2097152 | tf_op jit(solution)/shard_map/all_to_all | solution.py:313
  64.7 22.4 %collective-permute-start.10 = (bf16[32,128,128]{2,1,0:T(8,128)(2,1)}, bf16[32,128,128]{2,1,0:T(8,128)(2,1)S(1)}, u32[]{:S(2)}, u32[]{:S(2)}) collective-permute-start(bf16[32,128,128]{2,1,0:T(8,128)(2,1)} %collective-permute-done.8.off_ref), channel_id=1, source_target_pairs={{0,224},{32,0},{64,32},{96,64},{128,96},{160,128},{192,160},{224,1... | collective-permute-start | bytes 3145736 | tf_op jit(solution)/shard_map/ppermute | solution.py:321
  65.1 18.1 %collective-permute-start.9 = (bf16[16,128,128]{2,1,0:T(8,128)(2,1)S(1)}, bf16[16,128,128]{2,1,0:T(8,128)(2,1)S(1)}, u32[]{:S(2)}, u32[]{:S(2)}) collective-permute-start(bf16[16,128,128]{2,1,0:T(8,128)(2,1)S(1)} %slice_bitcast_fusion.diag_ref), channel_id=1, source_target_pairs={{0,224},{32,0},{64,32},{96,64},{128,96},{160,128},{192,160},{224,1... | collective-permute-start | bytes 1572872 | tf_op jit(solution)/shard_map/ppermute | solution.py:321
  67.5 19.5 %collective-permute-start.1 = (s32[3,32]{1,0:T(4,128)S(1)}, s32[3,32]{1,0:T(4,128)S(1)}, u32[]{:S(2)}, u32[]{:S(2)}) collective-permute-start(s32[3,32]{1,0:T(4,128)S(1)} %pad_add_fusion.1.table), channel_id=1, source_target_pairs={{0,224},{32,0},{64,32},{96,64},{128,96},{160,128},{192,160},{224,1... | collective-permute-start | bytes 1160 | tf_op jit(solution)/shard_map/ppermute | solution.py:315
  83.2 3.8 %copy-start.19 = (bf16[16,128,128]{2,1,0:T(8,128)(2,1)}, bf16[16,128,128]{2,1,0:T(8,128)(2,1)S(1)}, u32[]{:S(2)}) copy-start(bf16[16,128,128]{2,1,0:T(8,128)(2,1)S(1)} %collective-permute-done.9.diag_ref) | copy-start | bytes 1572868
  83.2 1.2 copy-start.29
  96.5 34.9 %all-to-all-start.2 = ((bf16[32,128,128]{2,1,0:T(8,128)(2,1)}), bf16[32,128,128]{2,1,0:T(8,128)(2,1)S(1)}, u32[]{:S(2)}, u32[]{:S(2)}) async-start(bf16[32,128,128]{2,1,0:T(8,128)(2,1)} %copy-done.14), calls=%async_computation.2 | async-start | bytes 2097152 | tf_op jit(solution)/shard_map/all_to_all | solution.py:313
  102.9 24.8 %collective-permute-start.12 = (bf16[32,128,128]{2,1,0:T(8,128)(2,1)S(1)}, bf16[32,128,128]{2,1,0:T(8,128)(2,1)S(1)}, u32[]{:S(2)}, u32[]{:S(2)}) collective-permute-start(bf16[32,128,128]{2,1,0:T(8,128)(2,1)S(1)} %collective-permute-done.10.off_ref), channel_id=1, source_target_pairs={{0,224},{32,0},{64,32},{96,64},{128,96},{160,128},{192,160},{224,1... | collective-permute-start | bytes 3145736 | tf_op jit(solution)/shard_map/ppermute | solution.py:321
  105.6 18.0 %collective-permute-start.11 = (bf16[16,128,128]{2,1,0:T(8,128)(2,1)}, bf16[16,128,128]{2,1,0:T(8,128)(2,1)S(1)}, u32[]{:S(2)}, u32[]{:S(2)}) collective-permute-start(bf16[16,128,128]{2,1,0:T(8,128)(2,1)} %copy-done.19), channel_id=1, source_target_pairs={{0,224},{32,0},{64,32},{96,64},{128,96},{160,128},{192,160},{224,1... | collective-permute-start | bytes 1572872 | tf_op jit(solution)/shard_map/ppermute | solution.py:321
  105.8 21.9 %collective-permute-start.2 = (s32[3,32]{1,0:T(4,128)S(1)}, s32[3,32]{1,0:T(4,128)S(1)}, u32[]{:S(2)}, u32[]{:S(2)}) collective-permute-start(s32[3,32]{1,0:T(4,128)S(1)} %collective-permute-done.1.table), channel_id=1, source_target_pairs={{0,224},{32,0},{64,32},{96,64},{128,96},{160,128},{192,160},{224,1... | collective-permute-start | bytes 1160 | tf_op jit(solution)/shard_map/ppermute | solution.py:315
  123.6 3.1 copy-start.20
  123.6 1.2 copy-start.31
  126.7 1.0 copy-start.2
  131.4 1.2 copy-start.3
  136.0 33.8 %all-to-all-start.3 = ((bf16[32,128,128]{2,1,0:T(8,128)(2,1)}), bf16[32,128,128]{2,1,0:T(8,128)(2,1)S(1)}, u32[]{:S(2)}, u32[]{:S(2)}) async-start(bf16[32,128,128]{2,1,0:T(8,128)(2,1)} %get-tuple-element.34), calls=%async_computation.3 | async-start | bytes 2097152 | tf_op jit(solution)/shard_map/all_to_all | solution.py:313
  142.1 24.9 %collective-permute-start.14 = (bf16[32,128,128]{2,1,0:T(8,128)(2,1)S(1)}, bf16[32,128,128]{2,1,0:T(8,128)(2,1)S(1)}, u32[]{:S(2)}, u32[]{:S(2)}) collective-permute-start(bf16[32,128,128]{2,1,0:T(8,128)(2,1)S(1)} %collective-permute-done.12.off_ref), channel_id=1, source_target_pairs={{0,224},{32,0},{64,32},{96,64},{128,96},{160,128},{192,160},{224,1... | collective-permute-start | bytes 3145736 | tf_op jit(solution)/shard_map/ppermute | solution.py:321
  144.9 18.0 %collective-permute-start.13 = (bf16[16,128,128]{2,1,0:T(8,128)(2,1)}, bf16[16,128,128]{2,1,0:T(8,128)(2,1)S(1)}, u32[]{:S(2)}, u32[]{:S(2)}) collective-permute-start(bf16[16,128,128]{2,1,0:T(8,128)(2,1)} %copy-done.20), channel_id=1, source_target_pairs={{0,224},{32,0},{64,32},{96,64},{128,96},{160,128},{192,160},{224,1... | collective-permute-start | bytes 1572872 | tf_op jit(solution)/shard_map/ppermute | solution.py:321
  145.0 22.0 %collective-permute-start.3 = (s32[3,32]{1,0:T(4,128)S(1)}, s32[3,32]{1,0:T(4,128)S(1)}, u32[]{:S(2)}, u32[]{:S(2)}) collective-permute-start(s32[3,32]{1,0:T(4,128)S(1)} %collective-permute-done.2.table), channel_id=1, source_target_pairs={{0,224},{32,0},{64,32},{96,64},{128,96},{160,128},{192,160},{224,1... | collective-permute-start | bytes 1160 | tf_op jit(solution)/shard_map/ppermute | solution.py:315
  162.9 3.1 copy-start.21
  162.9 1.2 copy-start.33
  166.0 1.0 copy-start.4
  169.8 1.2 copy-start.5
  174.4 33.6 %all-to-all-start.4 = ((bf16[32,128,128]{2,1,0:T(8,128)(2,1)}), bf16[32,128,128]{2,1,0:T(8,128)(2,1)S(1)}, u32[]{:S(2)}, u32[]{:S(2)}) async-start(bf16[32,128,128]{2,1,0:T(8,128)(2,1)} %get-tuple-element.36), calls=%async_computation.4 | async-start | bytes 2097152 | tf_op jit(solution)/shard_map/all_to_all | solution.py:313
  181.4 24.9 %collective-permute-start.16 = (bf16[32,128,128]{2,1,0:T(8,128)(2,1)S(1)}, bf16[32,128,128]{2,1,0:T(8,128)(2,1)S(1)}, u32[]{:S(2)}, u32[]{:S(2)}) collective-permute-start(bf16[32,128,128]{2,1,0:T(8,128)(2,1)S(1)} %collective-permute-done.14.off_ref), channel_id=1, source_target_pairs={{0,224},{32,0},{64,32},{96,64},{128,96},{160,128},{192,160},{224,1... | collective-permute-start | bytes 3145736 | tf_op jit(solution)/shard_map/ppermute | solution.py:321
  184.2 18.0 %collective-permute-start.15 = (bf16[16,128,128]{2,1,0:T(8,128)(2,1)}, bf16[16,128,128]{2,1,0:T(8,128)(2,1)S(1)}, u32[]{:S(2)}, u32[]{:S(2)}) collective-permute-start(bf16[16,128,128]{2,1,0:T(8,128)(2,1)} %copy-done.21), channel_id=1, source_target_pairs={{0,224},{32,0},{64,32},{96,64},{128,96},{160,128},{192,160},{224,1... | collective-permute-start | bytes 1572872 | tf_op jit(solution)/shard_map/ppermute | solution.py:321
  184.3 22.0 %collective-permute-start.4 = (s32[3,32]{1,0:T(4,128)S(1)}, s32[3,32]{1,0:T(4,128)S(1)}, u32[]{:S(2)}, u32[]{:S(2)}) collective-permute-start(s32[3,32]{1,0:T(4,128)S(1)} %collective-permute-done.3.table), channel_id=1, source_target_pairs={{0,224},{32,0},{64,32},{96,64},{128,96},{160,128},{192,160},{224,1... | collective-permute-start | bytes 1160 | tf_op jit(solution)/shard_map/ppermute | solution.py:315
  202.2 3.1 copy-start.22
  202.2 1.2 copy-start.35
  205.3 1.0 copy-start.6
  207.9 1.2 copy-start.7
  212.5 34.2 %all-to-all-start.5 = ((bf16[32,128,128]{2,1,0:T(8,128)(2,1)}), bf16[32,128,128]{2,1,0:T(8,128)(2,1)S(1)}, u32[]{:S(2)}, u32[]{:S(2)}) async-start(bf16[32,128,128]{2,1,0:T(8,128)(2,1)} %get-tuple-element.38), calls=%async_computation.5 | async-start | bytes 2097152 | tf_op jit(solution)/shard_map/all_to_all | solution.py:313
  220.7 24.9 %collective-permute-start.18 = (bf16[32,128,128]{2,1,0:T(8,128)(2,1)S(1)}, bf16[32,128,128]{2,1,0:T(8,128)(2,1)S(1)}, u32[]{:S(2)}, u32[]{:S(2)}) collective-permute-start(bf16[32,128,128]{2,1,0:T(8,128)(2,1)S(1)} %collective-permute-done.16.off_ref), channel_id=1, source_target_pairs={{0,224},{32,0},{64,32},{96,64},{128,96},{160,128},{192,160},{224,1... | collective-permute-start | bytes 3145736 | tf_op jit(solution)/shard_map/ppermute | solution.py:321
  223.5 18.0 %collective-permute-start.17 = (bf16[16,128,128]{2,1,0:T(8,128)(2,1)}, bf16[16,128,128]{2,1,0:T(8,128)(2,1)S(1)}, u32[]{:S(2)}, u32[]{:S(2)}) collective-permute-start(bf16[16,128,128]{2,1,0:T(8,128)(2,1)} %copy-done.22), channel_id=1, source_target_pairs={{0,224},{32,0},{64,32},{96,64},{128,96},{160,128},{192,160},{224,1... | collective-permute-start | bytes 1572872 | tf_op jit(solution)/shard_map/ppermute | solution.py:321
  223.6 22.0 %collective-permute-start.5 = (s32[3,32]{1,0:T(4,128)S(1)}, s32[3,32]{1,0:T(4,128)S(1)}, u32[]{:S(2)}, u32[]{:S(2)}) collective-permute-start(s32[3,32]{1,0:T(4,128)S(1)} %collective-permute-done.4.table), channel_id=1, source_target_pairs={{0,224},{32,0},{64,32},{96,64},{128,96},{160,128},{192,160},{224,1... | collective-permute-start | bytes 1160 | tf_op jit(solution)/shard_map/ppermute | solution.py:315
  241.5 3.1 copy-start.23
  241.5 1.2 copy-start.37
  244.6 1.0 copy-start.8
  246.7 1.2 copy-start.9
  251.3 33.9 %all-to-all-start.6 = ((bf16[32,128,128]{2,1,0:T(8,128)(2,1)}), bf16[32,128,128]{2,1,0:T(8,128)(2,1)S(1)}, u32[]{:S(2)}, u32[]{:S(2)}) async-start(bf16[32,128,128]{2,1,0:T(8,128)(2,1)} %get-tuple-element.40), calls=%async_computation.6 | async-start | bytes 2097152 | tf_op jit(solution)/shard_map/all_to_all | solution.py:313
  260.0 24.9 %collective-permute-start.20 = (bf16[32,128,128]{2,1,0:T(8,128)(2,1)S(1)}, bf16[32,128,128]{2,1,0:T(8,128)(2,1)S(1)}, u32[]{:S(2)}, u32[]{:S(2)}) collective-permute-start(bf16[32,128,128]{2,1,0:T(8,128)(2,1)S(1)} %collective-permute-done.18.off_ref), channel_id=1, source_target_pairs={{0,224},{32,0},{64,32},{96,64},{128,96},{160,128},{192,160},{224,1... | collective-permute-start | bytes 3145736 | tf_op jit(solution)/shard_map/ppermute | solution.py:321
  262.8 18.0 %collective-permute-start.19 = (bf16[16,128,128]{2,1,0:T(8,128)(2,1)}, bf16[16,128,128]{2,1,0:T(8,128)(2,1)S(1)}, u32[]{:S(2)}, u32[]{:S(2)}) collective-permute-start(bf16[16,128,128]{2,1,0:T(8,128)(2,1)} %copy-done.23), channel_id=1, source_target_pairs={{0,224},{32,0},{64,32},{96,64},{128,96},{160,128},{192,160},{224,1... | collective-permute-start | bytes 1572872 | tf_op jit(solution)/shard_map/ppermute | solution.py:321
  262.9 22.0 %collective-permute-start.6 = (s32[3,32]{1,0:T(4,128)S(1)}, s32[3,32]{1,0:T(4,128)S(1)}, u32[]{:S(2)}, u32[]{:S(2)}) collective-permute-start(s32[3,32]{1,0:T(4,128)S(1)} %collective-permute-done.5.table), channel_id=1, source_target_pairs={{0,224},{32,0},{64,32},{96,64},{128,96},{160,128},{192,160},{224,1... | collective-permute-start | bytes 1160 | tf_op jit(solution)/shard_map/ppermute | solution.py:315
  280.8 3.1 copy-start.17
  280.8 1.2 copy-start.39
  283.9 1.0 copy-start.10
  285.2 1.2 copy-start.11
  292.3 9.6 %copy-start.18 = (bf16[16,128,128]{2,1,0:T(8,128)(2,1)S(1)}, bf16[16,128,128]{2,1,0:T(8,128)(2,1)}, u32[]{:S(2)}) copy-start(bf16[16,128,128]{2,1,0:T(8,128)(2,1)} %copy-done.17) | copy-start | bytes 1572868
  292.3 33.6 %all-to-all-start.7 = ((bf16[32,128,128]{2,1,0:T(8,128)(2,1)}), bf16[32,128,128]{2,1,0:T(8,128)(2,1)S(1)}, u32[]{:S(2)}, u32[]{:S(2)}) async-start(bf16[32,128,128]{2,1,0:T(8,128)(2,1)} %copy-done.15), calls=%async_computation.7 | async-start | bytes 2097152 | tf_op jit(solution)/shard_map/all_to_all | solution.py:313
  301.9 9.5 %collective-permute-start.21 = (bf16[16,128,128]{2,1,0:T(8,128)(2,1)S(1)}, bf16[16,128,128]{2,1,0:T(8,128)(2,1)S(1)}, u32[]{:S(2)}, u32[]{:S(2)}) collective-permute-start(bf16[16,128,128]{2,1,0:T(8,128)(2,1)S(1)} %copy-done.18), channel_id=1, source_target_pairs={{0,224},{32,0},{64,32},{96,64},{128,96},{160,128},{192,160},{224,1... | collective-permute-start | bytes 1572872 | tf_op jit(solution)/shard_map/ppermute | solution.py:321
  304.7 11.4 %collective-permute-start.7 = (s32[3,32]{1,0:T(4,128)S(1)}, s32[3,32]{1,0:T(4,128)S(1)}, u32[]{:S(2)}, u32[]{:S(2)}) collective-permute-start(s32[3,32]{1,0:T(4,128)S(1)} %collective-permute-done.6.table), channel_id=1, source_target_pairs={{0,224},{32,0},{64,32},{96,64},{128,96},{160,128},{192,160},{224,1... | collective-permute-start | bytes 1160 | tf_op jit(solution)/shard_map/ppermute | solution.py:315
  312.2 1.0 copy-start.27
  313.2 1.0 copy-start.41
  327.0 8.4 %collective-permute-start.22 = (bf16[1,128,128]{2,1,0:T(8,128)(2,1)S(1)}, bf16[1,128,128]{2,1,0:T(8,128)(2,1)S(1)}, u32[]{:S(2)}, u32[]{:S(2)}) collective-permute-start(bf16[1,128,128]{2,1,0:T(8,128)(2,1)S(1)} %get-tuple-element.51), channel_id=1, source_target_pairs={{0,1},{1,2},{2,3},{3,4},{4,5},{5,6},{6,7},{7,8},{8,9},{9,10},{10,1... | collective-permute-start | bytes 98312 | tf_op jit(solution)/shard_map/ppermute | solution.py:323
  331.4 7.9 %collective-permute-start.23 = (bf16[1,128,128]{2,1,0:T(8,128)(2,1)S(1)}, bf16[1,128,128]{2,1,0:T(8,128)(2,1)S(1)}, u32[]{:S(2)}, u32[]{:S(2)}) collective-permute-start(bf16[1,128,128]{2,1,0:T(8,128)(2,1)S(1)} %get-tuple-element.50), channel_id=1, source_target_pairs={{1,0},{2,1},{3,2},{4,3},{5,4},{6,5},{7,6},{8,7},{9,8},{10,9},{11,1... | collective-permute-start | bytes 98312 | tf_op jit(solution)/shard_map/ppermute | solution.py:324
  (11 other events, 9.3 us)

commit v3 on v2

--- a/solution.py
+++ b/solution.py
@@ -10,7 +10,6 @@
 VMEM = pl.BlockSpec(memory_space=pltpu.VMEM)
 SMEM = pl.BlockSpec(memory_space=pltpu.SMEM)
 HBM = pl.BlockSpec(memory_space=pltpu.HBM)
-SEND_SPECS = [VMEM, VMEM, VMEM]
 SEND = pltpu.CompilerParams(vmem_limit_bytes=24 * 1024 * 1024)
 KEEP = pltpu.CompilerParams(vmem_limit_bytes=24 * 1024 * 1024)
 SMALL = pltpu.CompilerParams(vmem_limit_bytes=16 * 1024 * 1024)
@@ -27,12 +26,12 @@
     return lax.dot_general(v, block, (((1,), (1,)), ((), ())), preferred_element_type=jnp.float32)
 
 
-def send_products(wanted, block_of, state_ref, out_ref, stage, out_sems):
-    rows, each = state_ref.shape[1], wanted.each
+def send_products(wanted, off_ref, state_ref, out_ref, stage, out_sems):
+    rows, each = state_ref.shape[1], off_ref.shape[1]
     copies = []
     for p in range(stage.shape[0]):
         number = wanted(p)
-        stage[p, :rows] = product(state_ref[number // each], block_of(number)).astype(jnp.bfloat16)
+        stage[p, :rows] = product(state_ref[lax.div(number, each)], off_ref[lax.div(number, each), lax.rem(number, each)]).astype(jnp.bfloat16)
         if p % PART == PART - 1:
             part = pl.ds(p + 1 - PART, PART)
             copy = pltpu.make_async_copy(stage.at[part], out_ref.at[part], out_sems.at[p // PART])
@@ -50,16 +49,12 @@
         gathered[home] = gathered[home] + arrived_ref[p, :rows].astype(jnp.float32)
 
 
-class Wanted:
-    def __init__(self, read, each):
-        self.read, self.each = read, each
-
-    def __call__(self, p):
-        return self.read(p)
-
-
-def first_body(dest, seeds_ref, blocks_ref, out_ref, state_ref, blocks_scr, stage, state_scr, lists, sems, out_sems):
-    load = pltpu.make_async_copy(blocks_ref, blocks_scr, sems.at[0])
+def off_copy(blocks_ref, off_scr, sem):
+    return pltpu.make_async_copy(blocks_ref.at[:, pl.ds(1, off_scr.shape[1])], off_scr, sem)
+
+
+def first_body(dest, seeds_ref, blocks_ref, out_ref, state_ref, off_scr, stage, state_scr, lists, sems, out_sems):
+    load = off_copy(blocks_ref, off_scr, sems.at[0])
     load.start()
     tiles, nnz = dest.shape[1:]
     each = nnz - 1
@@ -74,30 +69,29 @@
     for t in range(tiles):
         for k in range(1, nnz):
             to = dest[0, t, k]
-            peer = to // tiles
+            peer = lax.div(to, tiles)
             lists[0, peer] = t * each + k - 1
             lists[1, peer] = to - peer * tiles
     for p in range(stage.shape[0]):
         stage[p, rows:] = jnp.full((SAYS, stage.shape[2]), lists[1, p], jnp.int32).astype(jnp.float32).astype(jnp.bfloat16)
     load.wait()
-    wanted = Wanted(lambda p: lists[0, p], each)
-    send_products(wanted, lambda n: blocks_scr[n + n // each + 1], state_scr, out_ref, stage, out_sems)
+    send_products(lambda p: lists[0, p], off_scr, state_scr, out_ref, stage, out_sems)
     store.wait()
 
 
 def send_first(dest, seeds, blocks, peers):
-    count, points = blocks.shape[:2]
-    tiles, _, rows = seeds.shape
+    tiles, nnz, points = blocks.shape[:3]
+    rows = seeds.shape[2]
     return pl.pallas_call(
         first_body,
         out_shape=(
-            jax.ShapeDtypeStruct((peers, rows + SAYS, points), jnp.bfloat16),
-            jax.ShapeDtypeStruct((tiles, rows, points), jnp.bfloat16),
+            pltpu.HBM((peers, rows + SAYS, points), jnp.bfloat16),
+            pltpu.HBM((tiles, rows, points), jnp.bfloat16),
         ),
         in_specs=[SMEM, VMEM, HBM],
         out_specs=(HBM, HBM),
         scratch_shapes=[
-            pltpu.VMEM(blocks.shape, jnp.bfloat16),
+            pltpu.VMEM((tiles, nnz - 1, points, points), jnp.bfloat16),
             pltpu.VMEM((peers, rows + SAYS, points), jnp.bfloat16),
             pltpu.VMEM((tiles, rows, points), jnp.bfloat16),
             pltpu.SMEM((2, peers), jnp.int32),
@@ -108,73 +102,90 @@
         cost_estimate=pl.CostEstimate(
             flops=2 * peers * points * points * rows, bytes_accessed=4 << 20, transcendentals=0
         ),
-    )(dest, seeds, blocks)
-
-
-def send_body(table, arrived_ref, local_ref, off_ref, out_ref, state_ref, stage, gathered, state_scr, store_sem, out_sems):
-    each = off_ref.shape[0] // state_scr.shape[0]
+    )(dest, seeds, placed(blocks, pltpu.HBM))
+
+
+def send_body(
+    table, arrived_ref, local_ref, blocks_ref, out_ref, state_ref,
+    stage, gathered, state_scr, local_scr, off_scr, sems, out_sems,
+):
+    load_local = pltpu.make_async_copy(local_ref, local_scr, sems.at[0])
+    load = off_copy(blocks_ref, off_scr, sems.at[1])
+    load_local.start()
+    load.start()
     add_arrived(table, arrived_ref, gathered)
+    load_local.wait()
     for t in range(state_scr.shape[0]):
-        state_scr[t] = (gathered[t] + local_ref[t]).astype(jnp.bfloat16)
-    store = pltpu.make_async_copy(state_scr, state_ref, store_sem)
+        state_scr[t] = (gathered[t] + local_scr[t]).astype(jnp.bfloat16)
+    store = pltpu.make_async_copy(state_scr, state_ref, sems.at[2])
     store.start()
-    wanted = Wanted(lambda p: table[WANTED, p], each)
-    send_products(wanted, lambda n: off_ref[n], state_scr, out_ref, stage, out_sems)
+    load.wait()
+    send_products(lambda p: table[WANTED, p], off_scr, state_scr, out_ref, stage, out_sems)
     store.wait()
 
 
-def send(table, arrived, local, off):
+placed = pltpu.with_memory_space_constraint
+
+
+def send(table, arrived, local, blocks):
     peers = arrived.shape[0]
     tiles, rows, points = local.shape
+    nnz = blocks.shape[1]
     return pl.pallas_call(
         send_body,
         out_shape=(
-            jax.ShapeDtypeStruct((peers, rows, points), jnp.bfloat16),
-            jax.ShapeDtypeStruct((tiles, rows, points), jnp.bfloat16),
-        ),
-        in_specs=[SMEM] + SEND_SPECS,
+            pltpu.HBM((peers, rows, points), jnp.bfloat16),
+            pltpu.HBM((tiles, rows, points), jnp.bfloat16),
+        ),
+        in_specs=[SMEM, VMEM, HBM, HBM],
         out_specs=(HBM, HBM),
         scratch_shapes=[
             pltpu.VMEM((peers, rows, points), jnp.bfloat16),
             pltpu.VMEM((tiles + 1, rows, points), jnp.float32),
             pltpu.VMEM((tiles, rows, points), jnp.bfloat16),
-            pltpu.SemaphoreType.DMA,
+            pltpu.VMEM(local.shape, jnp.float32),
+            pltpu.VMEM((tiles, nnz - 1, points, points), jnp.bfloat16),
+            pltpu.SemaphoreType.DMA((3,)),
             pltpu.SemaphoreType.DMA((peers // PART,)),
         ],
         compiler_params=SEND,
         cost_estimate=pl.CostEstimate(
             flops=2 * peers * points * points * rows, bytes_accessed=4 << 20, transcendentals=0
         ),
-    )(table, arrived, local, off)
-
-
-def keep_body(table, state_ref, diag_ref, off_ref, local_ref, total, sem):
-    tiles = state_ref.shape[0]
-    each = off_ref.shape[0] // tiles
-    for t in range(tiles):
-        total[t] = product(state_ref[t], diag_ref[t])
-    for t in range(tiles):
-        for k in range(each):
-            home = table[HOME, t * each + k]
-            total[home] = total[home] + product(state_ref[t], off_ref[t * each + k])
-    store = pltpu.make_async_copy(total.at[pl.ds(0, tiles)], local_ref, sem)
-    store.start()
-    store.wait()
-
-
-def keep(table, state, diag, off):
+    )(table, placed(arrived, pltpu.VMEM), placed(local, pltpu.HBM), placed(blocks, pltpu.HBM))
+
+
+def keep_body(table, state_ref, blocks_ref, local_ref, total, blocks_scr, sem):
+    load = pltpu.make_async_copy(blocks_ref, blocks_scr, sem)
+    load.start()
+    load.wait()
+    tiles, nnz = blocks_scr.shape[:2]
+    for t in range(tiles):
+        total[t] = product(state_ref[t], blocks_scr[t, 0])
+    for t in range(tiles):
+        for k in range(1, nnz):
+            home = table[HOME, t * (nnz - 1) + k - 1]
+            total[home] = total[home] + product(state_ref[t], blocks_scr[t, k])
+    local_ref[...] = total[pl.ds(0, tiles)]
+
+
+def keep(table, state, blocks):
     tiles, rows, points = state.shape
     return pl.pallas_call(
         keep_body,
-        out_shape=jax.ShapeDtypeStruct((tiles, rows, points), jnp.float32),
-        in_specs=[SMEM, VMEM, VMEM, VMEM],
-        out_specs=HBM,
-        scratch_shapes=[pltpu.VMEM((tiles + 1, rows, points), jnp.float32), pltpu.SemaphoreType.DMA],
+        out_shape=pltpu.HBM((tiles, rows, points), jnp.float32),
+        in_specs=[SMEM, VMEM, HBM],
+        out_specs=VMEM,
+        scratch_shapes=[
+            pltpu.VMEM((tiles + 1, rows, points), jnp.float32),
+            pltpu.VMEM(blocks.shape, jnp.bfloat16),
+            pltpu.SemaphoreType.DMA,
+        ],
         compiler_params=KEEP,
         cost_estimate=pl.CostEstimate(
-            flops=2 * (tiles + off.shape[0]) * points * points * rows, bytes_accessed=4 << 20, transcendentals=0
-        ),
-    )(table, state, diag, off)
+            flops=2 * tiles * blocks.shape[1] * points * points * rows, bytes_accessed=4 << 20, transcendentals=0
+        ),
+    )(table, placed(state, pltpu.HBM), placed(blocks, pltpu.HBM))
 
 
 def last_body(before, arrived_ref, local_ref, final_ref, edges_ref, gathered, local_scr, sem):
@@ -298,28 +309,27 @@
     ndays, peers = lax.axis_size("day"), lax.axis_size("tile")
     me = lax.axis_index("tile")
     seeds = seeds.reshape(tiles, points, width)
-    whole = blocks.reshape(tiles * nnz, points, points)
-    diag, off = blocks[0, :, 0], blocks[0, :, 1:].reshape(tiles * (nnz - 1), points, points)
+    wblk = blocks[0]
     onward = functools.partial(lax.ppermute, axis_name="day", perm=shifted(ndays, -1))
 
     for step in range(ndays):
         if step == 0:
-            out, state = send_first(dest_tiles, seeds, whole, peers)
+            out, state = send_first(dest_tiles, seeds, wblk, peers)
             dest, state = lax.optimization_barrier((dest_tiles[0], state))
             rows = own_rows(dest, me, tiles, peers, nnz)
             table = jnp.stack([*rows, jnp.zeros_like(rows[0])])
         else:
-            out, state = send(table, arrived, local, off)
+            out, state = send(table, arrived, local, wblk)
         arrived = lax.all_to_all(out, "tile", split_axis=0, concat_axis=0, tiled=True)
-        local = keep(table, state, diag, off)
+        local = keep(table, state, wblk)
         table = onward(table)
         if step == 0:
             own = lax.broadcasted_iota(jnp.int32, (peers,), 0) == me
             landed = jnp.where(own, tiles, arrived[:, width, 0].astype(jnp.int32))
             table = jnp.concatenate([table[:2], landed[None]], axis=0)
         if step < ndays - 1:
-            diag, off = onward(diag), onward(off)
-    final, edges = last_sum(table, arrived, local)
+            wblk = onward(wblk)
+    final, edges = last_sum(table, arrived, placed(local, pltpu.HBM))
     low = lax.ppermute(edges[1:], "tile", [(i, i + 1) for i in range(peers - 1)])
     high = lax.ppermute(edges[:1], "tile", [(i + 1, i) for i in range(peers - 1)])
     place = jnp.stack([me == 0, me == peers - 1]).astype(jnp.int32)

time: 347 us -> 320 us (0.922); the launches traced: 341 us -> 319 us
  local copies, waits for them, and re-layouts: 36.4 us -> 3.26 us
  Pallas kernels: 48.9 us -> 72.9 us
  starting transfers between devices: 94.3 us -> 79.4 us
    ppermute x14 -> x7, waiting for transfers between devices: 110 us -> 0.02 us  [body(): wblk = onward(wblk)]
    ppermute x8, waiting for transfers between devices: 7.32 us -> 78.8 us  [body(): table = onward(table)]
    all_to_all x8, waiting for transfers between devices: 37.6 us -> 78.1 us  [body(): lax.all_to_all(out, 'tile', split_axis=0, concat_axis=0, tiled=True)]
    unnamed x88 -> x20, local copies, waits for them, and re-layouts: 35 us -> 2.98 us
    pallas_call x16, Pallas kernels: 44.4 us -> 67.6 us  [the longest x8 37.9 us: keep(): pl.pallas_call(keep_body, out_shape=pltpu.HBM((tiles, rows, points), jnp....]
    ppermute x14 -> x7, starting transfers between devices: 21.9 us -> 2.23 us  [body(): wblk = onward(wblk)]
    ppermute x8, starting transfers between devices: 2.6 us -> 14.4 us  [body(): table = onward(table)]
    all_to_all x8, starting transfers between devices: 63.5 us -> 56.6 us  [body(): lax.all_to_all(out, 'tile', split_axis=0, concat_axis=0, tiled=True)]
  transfers between devices with their start and end apart: 32 -> 25, of which waited for: 17 -> 16; matrix products, arithmetic and copies ran while one was open for 1% -> 0% of each run, Pallas kernels for 5% -> 13%
where the time goes in v3:
time: 320 us; the launch traced here: 319 us
  waiting for transfers between devices  161 us (50%)
  starting transfers between devices  79.4 us (25%)
  Pallas kernels  72.9 us (23%)
  local copies, waits for them, and re-layouts  3.26 us (1%)
    ppermute x8, waiting for transfers between devices, body(): table = onward(table)  78.8 us
    all_to_all x8, waiting for transfers between devices, body(): lax.all_to_all(out, 'tile', split_axis=0, concat_axis=0, tiled=True)  78.1 us
    all_to_all x8, starting transfers between devices, body(): lax.all_to_all(out, 'tile', split_axis=0, concat_axis=0, tiled=True)  56.6 us
    pallas_call x8, Pallas kernels, keep(): pl.pallas_call(keep_body, out_shape=pltpu.HBM((tiles, rows, points), jnp....  37.9 us
    pallas_call x7, Pallas kernels, send(): pl.pallas_call(send_body, out_shape=(pltpu.HBM((peers, rows, points), jnp...  25.9 us
    ppermute x8, starting transfers between devices, body(): table = onward(table)  14.4 us
  transfers between devices with their start and end apart: 25, of which 16 were waited for; matrix products, arithmetic and copies ran while one was open for 0% of the time, Pallas kernels for 13%

profile of v3, /device:TPU:56, one launch (start us, length us, event | category | flops | bytes accessed | tf_op | source)
XLA Modules:
  0.0 318.5 jit_solution(10552117850961386697)
XLA Ops:
  0.6 0.8 copy.13.dest
  1.4 1.0 copy-done
  2.4 3.8 %shard_map.50 = (bf16[32,144,128]{2,1,0:T(8,128)(2,1)}, bf16[16,128,128]{2,1,0:T(8,128)(2,1)}) custom-call(s32[1,16,3]{2,1,0:T(8,128)S(1)} %copy.13.dest, bf16[16,128,128]{2,1,0:T(8,128)(2,1)S(1)} %bitcast.12, bf16[16,3,128,128]{3,2,1,0:T(8,128)(2,1)} %bitcast.13), custom_call_target="tpu_custom_call" | custom-call | flops 134217728 | bytes 4194304 | tf_op jit(solution)/shard_map/pallas_call | solution.py:85
  6.2 11.0 %all-to-all-start = ((bf16[32,144,128]{2,1,0:T(8,128)(2,1)}), bf16[32,144,128]{2,1,0:T(8,128)(2,1)S(1)}, u32[]{:S(2)}, u32[]{:S(2)}) async-start(bf16[32,144,128]{2,1,0:T(8,128)(2,1)} %get-tuple-element.28), calls=%async_computation | async-start | bytes 2359296 | tf_op jit(solution)/shard_map/all_to_all | solution.py:323
  17.3 1.6 collective-permute-start.8
  18.9 0.1 copy.14
  19.0 0.1 broadcast_in_dim_reshape.6
  19.1 0.1 broadcast_in_dim_reshape.5
  19.2 0.1 select_reduce_fusion
  19.4 1.2 collective-permute-start
  20.6 4.7 %shard_map.51.local_ref = f32[16,128,128]{2,1,0:T(8,128)} custom-call(s32[3,32]{1,0:T(4,128)S(1)} %pad_add_fusion.table, bf16[16,128,128]{2,1,0:T(8,128)(2,1)} %get-tuple-element.29.state_ref, bf16[16,3,128,128]{3,2,1,0:T(8,128)(2,1)} %bitcast.15), custom_call_target="tpu_custom_call" | custom-call | flops 201326592 | bytes 4194304 | tf_op jit(solution)/shard_map/pallas_call | solution.py:174
  25.4 11.8 %collective-permute-done = s32[3,32]{1,0:T(4,128)S(1)} collective-permute-done((s32[3,32]{1,0:T(4,128)S(1)}, s32[3,32]{1,0:T(4,128)S(1)}, u32[]{:S(2)}, u32[]{:S(2)}) %collective-permute-start) | collective-permute-done | bytes 416 | tf_op jit(solution)/shard_map/ppermute | solution.py:325
  37.2 10.1 %all-to-all-done.arrived_ref = bf16[32,144,128]{2,1,0:T(8,128)(2,1)S(1)} async-done(((bf16[32,144,128]{2,1,0:T(8,128)(2,1)}), bf16[32,144,128]{2,1,0:T(8,128)(2,1)S(1)}, u32[]{:S(2)}, u32[]{:S(2)}) %all-to-all-start) | async-done | bytes 1179680 | tf_op jit(solution)/shard_map/all_to_all | solution.py:323
  47.3 0.7 fusion
  48.0 1.1 copy-done.1
  49.1 3.7 %shard_map.52 = (bf16[32,128,128]{2,1,0:T(8,128)(2,1)}, bf16[16,128,128]{2,1,0:T(8,128)(2,1)}) custom-call(s32[3,32]{1,0:T(4,128)S(1)} %pad_add_fusion.1.table, bf16[32,144,128]{2,1,0:T(8,128)(2,1)S(1)} %all-to-all-done.arrived_ref, f32[16,128,128]{2,1,0:T(8,128)} %shard_map.51.local_ref, bf16[16,3,128,128]{3,2,1,0:T(8,128)(2,1)} %copy-done.1), custom_call_target="tpu_custom_call" | custom-call | flops 134217728 | bytes 4194304 | tf_op jit(solution)/shard_map/pallas_call | solution.py:134
  52.9 6.6 %all-to-all-start.1 = ((bf16[32,128,128]{2,1,0:T(8,128)(2,1)}), bf16[32,128,128]{2,1,0:T(8,128)(2,1)S(1)}, u32[]{:S(2)}, u32[]{:S(2)}) async-start(bf16[32,128,128]{2,1,0:T(8,128)(2,1)} %get-tuple-element.30), calls=%async_computation.1 | async-start | bytes 2097152 | tf_op jit(solution)/shard_map/all_to_all | solution.py:323
  59.5 0.4 collective-permute-start.9
  59.9 2.4 collective-permute-start.1
  62.3 4.7 %shard_map.53.local_ref = f32[16,128,128]{2,1,0:T(8,128)} custom-call(s32[3,32]{1,0:T(4,128)S(1)} %pad_add_fusion.1.table, bf16[16,128,128]{2,1,0:T(8,128)(2,1)} %get-tuple-element.31.state_ref, bf16[16,3,128,128]{3,2,1,0:T(8,128)(2,1)} %copy-done.1), custom_call_target="tpu_custom_call" | custom-call | flops 201326592 | bytes 4194304 | tf_op jit(solution)/shard_map/pallas_call | solution.py:174
  67.1 10.8 %collective-permute-done.1.table = s32[3,32]{1,0:T(4,128)S(1)} collective-permute-done((s32[3,32]{1,0:T(4,128)S(1)}, s32[3,32]{1,0:T(4,128)S(1)}, u32[]{:S(2)}, u32[]{:S(2)}) %collective-permute-start.1) | collective-permute-done | bytes 416 | tf_op jit(solution)/shard_map/ppermute | solution.py:325
  77.9 7.6 %all-to-all-done.1.arrived_ref = bf16[32,128,128]{2,1,0:T(8,128)(2,1)S(1)} async-done(((bf16[32,128,128]{2,1,0:T(8,128)(2,1)}), bf16[32,128,128]{2,1,0:T(8,128)(2,1)S(1)}, u32[]{:S(2)}, u32[]{:S(2)}) %all-to-all-start.1) | async-done | bytes 1048608 | tf_op jit(solution)/shard_map/all_to_all | solution.py:323
  85.4 3.7 %shard_map.54 = (bf16[32,128,128]{2,1,0:T(8,128)(2,1)}, bf16[16,128,128]{2,1,0:T(8,128)(2,1)}) custom-call(s32[3,32]{1,0:T(4,128)S(1)} %collective-permute-done.1.table, bf16[32,128,128]{2,1,0:T(8,128)(2,1)S(1)} %all-to-all-done.1.arrived_ref, f32[16,128,128]{2,1,0:T(8,128)} %shard_map.53.local_ref, bf16[16,3,128,128]{3,2,1,0:T(8,128)(2,1)} %collective-permute-done.9.blocks_ref), custom_call_target="tpu_custom_call" | custom-call | flops 134217728 | bytes 4194304 | tf_op jit(solution)/shard_map/pallas_call | solution.py:134
  89.1 6.4 %all-to-all-start.2 = ((bf16[32,128,128]{2,1,0:T(8,128)(2,1)}), bf16[32,128,128]{2,1,0:T(8,128)(2,1)S(1)}, u32[]{:S(2)}, u32[]{:S(2)}) async-start(bf16[32,128,128]{2,1,0:T(8,128)(2,1)} %get-tuple-element.32), calls=%async_computation.2 | async-start | bytes 2097152 | tf_op jit(solution)/shard_map/all_to_all | solution.py:323
  95.6 0.1 collective-permute-start.10
  95.7 2.8 collective-permute-start.2
  98.5 4.7 %shard_map.55.local_ref = f32[16,128,128]{2,1,0:T(8,128)} custom-call(s32[3,32]{1,0:T(4,128)S(1)} %collective-permute-done.1.table, bf16[16,128,128]{2,1,0:T(8,128)(2,1)} %get-tuple-element.33.state_ref, bf16[16,3,128,128]{3,2,1,0:T(8,128)(2,1)} %collective-permute-done.9.blocks_ref), custom_call_target="tpu_custom_call" | custom-call | flops 201326592 | bytes 4194304 | tf_op jit(solution)/shard_map/pallas_call | solution.py:174
  103.2 10.7 %collective-permute-done.2.table = s32[3,32]{1,0:T(4,128)S(1)} collective-permute-done((s32[3,32]{1,0:T(4,128)S(1)}, s32[3,32]{1,0:T(4,128)S(1)}, u32[]{:S(2)}, u32[]{:S(2)}) %collective-permute-start.2) | collective-permute-done | bytes 416 | tf_op jit(solution)/shard_map/ppermute | solution.py:325
  113.9 7.3 %all-to-all-done.2.arrived_ref = bf16[32,128,128]{2,1,0:T(8,128)(2,1)S(1)} async-done(((bf16[32,128,128]{2,1,0:T(8,128)(2,1)}), bf16[32,128,128]{2,1,0:T(8,128)(2,1)S(1)}, u32[]{:S(2)}, u32[]{:S(2)}) %all-to-all-start.2) | async-done | bytes 1048608 | tf_op jit(solution)/shard_map/all_to_all | solution.py:323
  121.2 3.7 %shard_map.56 = (bf16[32,128,128]{2,1,0:T(8,128)(2,1)}, bf16[16,128,128]{2,1,0:T(8,128)(2,1)}) custom-call(s32[3,32]{1,0:T(4,128)S(1)} %collective-permute-done.2.table, bf16[32,128,128]{2,1,0:T(8,128)(2,1)S(1)} %all-to-all-done.2.arrived_ref, f32[16,128,128]{2,1,0:T(8,128)} %shard_map.55.local_ref, bf16[16,3,128,128]{3,2,1,0:T(8,128)(2,1)} %copy-done.3), custom_call_target="tpu_custom_call" | custom-call | flops 134217728 | bytes 4194304 | tf_op jit(solution)/shard_map/pallas_call | solution.py:134
  125.0 6.6 %all-to-all-start.3 = ((bf16[32,128,128]{2,1,0:T(8,128)(2,1)}), bf16[32,128,128]{2,1,0:T(8,128)(2,1)S(1)}, u32[]{:S(2)}, u32[]{:S(2)}) async-start(bf16[32,128,128]{2,1,0:T(8,128)(2,1)} %get-tuple-element.34), calls=%async_computation.3 | async-start | bytes 2097152 | tf_op jit(solution)/shard_map/all_to_all | solution.py:323
  131.6 2.9 collective-permute-start.3
  134.4 4.7 %shard_map.57.local_ref = f32[16,128,128]{2,1,0:T(8,128)} custom-call(s32[3,32]{1,0:T(4,128)S(1)} %collective-permute-done.2.table, bf16[16,128,128]{2,1,0:T(8,128)(2,1)} %get-tuple-element.35.state_ref, bf16[16,3,128,128]{3,2,1,0:T(8,128)(2,1)} %copy-done.3), custom_call_target="tpu_custom_call" | custom-call | flops 201326592 | bytes 4194304 | tf_op jit(solution)/shard_map/pallas_call | solution.py:174
  139.2 10.3 %collective-permute-done.3.table = s32[3,32]{1,0:T(4,128)S(1)} collective-permute-done((s32[3,32]{1,0:T(4,128)S(1)}, s32[3,32]{1,0:T(4,128)S(1)}, u32[]{:S(2)}, u32[]{:S(2)}) %collective-permute-start.3) | collective-permute-done | bytes 416 | tf_op jit(solution)/shard_map/ppermute | solution.py:325
  149.5 8.5 %all-to-all-done.3.arrived_ref = bf16[32,128,128]{2,1,0:T(8,128)(2,1)S(1)} async-done(((bf16[32,128,128]{2,1,0:T(8,128)(2,1)}), bf16[32,128,128]{2,1,0:T(8,128)(2,1)S(1)}, u32[]{:S(2)}, u32[]{:S(2)}) %all-to-all-start.3) | async-done | bytes 1048608 | tf_op jit(solution)/shard_map/all_to_all | solution.py:323
  158.0 3.7 %shard_map.58 = (bf16[32,128,128]{2,1,0:T(8,128)(2,1)}, bf16[16,128,128]{2,1,0:T(8,128)(2,1)}) custom-call(s32[3,32]{1,0:T(4,128)S(1)} %collective-permute-done.3.table, bf16[32,128,128]{2,1,0:T(8,128)(2,1)S(1)} %all-to-all-done.3.arrived_ref, f32[16,128,128]{2,1,0:T(8,128)} %shard_map.57.local_ref, bf16[16,3,128,128]{3,2,1,0:T(8,128)(2,1)} %collective-permute-done.11.blocks_ref), custom_call_target="tpu_custom_call" | custom-call | flops 134217728 | bytes 4194304 | tf_op jit(solution)/shard_map/pallas_call | solution.py:134
  161.7 6.5 %all-to-all-start.4 = ((bf16[32,128,128]{2,1,0:T(8,128)(2,1)}), bf16[32,128,128]{2,1,0:T(8,128)(2,1)S(1)}, u32[]{:S(2)}, u32[]{:S(2)}) async-start(bf16[32,128,128]{2,1,0:T(8,128)(2,1)} %get-tuple-element.36), calls=%async_computation.4 | async-start | bytes 2097152 | tf_op jit(solution)/shard_map/all_to_all | solution.py:323
  168.2 1.9 collective-permute-start.4
  170.1 4.7 %shard_map.59.local_ref = f32[16,128,128]{2,1,0:T(8,128)} custom-call(s32[3,32]{1,0:T(4,128)S(1)} %collective-permute-done.3.table, bf16[16,128,128]{2,1,0:T(8,128)(2,1)} %get-tuple-element.37.state_ref, bf16[16,3,128,128]{3,2,1,0:T(8,128)(2,1)} %collective-permute-done.11.blocks_ref), custom_call_target="tpu_custom_call" | custom-call | flops 201326592 | bytes 4194304 | tf_op jit(solution)/shard_map/pallas_call | solution.py:174
  174.9 11.6 %collective-permute-done.4.table = s32[3,32]{1,0:T(4,128)S(1)} collective-permute-done((s32[3,32]{1,0:T(4,128)S(1)}, s32[3,32]{1,0:T(4,128)S(1)}, u32[]{:S(2)}, u32[]{:S(2)}) %collective-permute-start.4) | collective-permute-done | bytes 416 | tf_op jit(solution)/shard_map/ppermute | solution.py:325
  186.5 7.6 %all-to-all-done.4.arrived_ref = bf16[32,128,128]{2,1,0:T(8,128)(2,1)S(1)} async-done(((bf16[32,128,128]{2,1,0:T(8,128)(2,1)}), bf16[32,128,128]{2,1,0:T(8,128)(2,1)S(1)}, u32[]{:S(2)}, u32[]{:S(2)}) %all-to-all-start.4) | async-done | bytes 1048608 | tf_op jit(solution)/shard_map/all_to_all | solution.py:323
  194.0 3.7 %shard_map.60 = (bf16[32,128,128]{2,1,0:T(8,128)(2,1)}, bf16[16,128,128]{2,1,0:T(8,128)(2,1)}) custom-call(s32[3,32]{1,0:T(4,128)S(1)} %collective-permute-done.4.table, bf16[32,128,128]{2,1,0:T(8,128)(2,1)S(1)} %all-to-all-done.4.arrived_ref, f32[16,128,128]{2,1,0:T(8,128)} %shard_map.59.local_ref, bf16[16,3,128,128]{3,2,1,0:T(8,128)(2,1)} %copy-done.5), custom_call_target="tpu_custom_call" | custom-call | flops 134217728 | bytes 4194304 | tf_op jit(solution)/shard_map/pallas_call | solution.py:134
  197.8 6.6 %all-to-all-start.5 = ((bf16[32,128,128]{2,1,0:T(8,128)(2,1)}), bf16[32,128,128]{2,1,0:T(8,128)(2,1)S(1)}, u32[]{:S(2)}, u32[]{:S(2)}) async-start(bf16[32,128,128]{2,1,0:T(8,128)(2,1)} %get-tuple-element.38), calls=%async_computation.5 | async-start | bytes 2097152 | tf_op jit(solution)/shard_map/all_to_all | solution.py:323
  204.4 1.2 collective-permute-start.5
  205.6 4.7 %shard_map.61.local_ref = f32[16,128,128]{2,1,0:T(8,128)} custom-call(s32[3,32]{1,0:T(4,128)S(1)} %collective-permute-done.4.table, bf16[16,128,128]{2,1,0:T(8,128)(2,1)} %get-tuple-element.39.state_ref, bf16[16,3,128,128]{3,2,1,0:T(8,128)(2,1)} %copy-done.5), custom_call_target="tpu_custom_call" | custom-call | flops 201326592 | bytes 4194304 | tf_op jit(solution)/shard_map/pallas_call | solution.py:174
  210.3 12.0 %collective-permute-done.5.table = s32[3,32]{1,0:T(4,128)S(1)} collective-permute-done((s32[3,32]{1,0:T(4,128)S(1)}, s32[3,32]{1,0:T(4,128)S(1)}, u32[]{:S(2)}, u32[]{:S(2)}) %collective-permute-start.5) | collective-permute-done | bytes 416 | tf_op jit(solution)/shard_map/ppermute | solution.py:325
  222.3 8.3 %all-to-all-done.5.arrived_ref = bf16[32,128,128]{2,1,0:T(8,128)(2,1)S(1)} async-done(((bf16[32,128,128]{2,1,0:T(8,128)(2,1)}), bf16[32,128,128]{2,1,0:T(8,128)(2,1)S(1)}, u32[]{:S(2)}, u32[]{:S(2)}) %all-to-all-start.5) | async-done | bytes 1048608 | tf_op jit(solution)/shard_map/all_to_all | solution.py:323
  230.6 3.7 %shard_map.62 = (bf16[32,128,128]{2,1,0:T(8,128)(2,1)}, bf16[16,128,128]{2,1,0:T(8,128)(2,1)}) custom-call(s32[3,32]{1,0:T(4,128)S(1)} %collective-permute-done.5.table, bf16[32,128,128]{2,1,0:T(8,128)(2,1)S(1)} %all-to-all-done.5.arrived_ref, f32[16,128,128]{2,1,0:T(8,128)} %shard_map.61.local_ref, bf16[16,3,128,128]{3,2,1,0:T(8,128)(2,1)} %collective-permute-done.13.blocks_ref), custom_call_target="tpu_custom_call" | custom-call | flops 134217728 | bytes 4194304 | tf_op jit(solution)/shard_map/pallas_call | solution.py:134
  234.3 6.4 %all-to-all-start.6 = ((bf16[32,128,128]{2,1,0:T(8,128)(2,1)}), bf16[32,128,128]{2,1,0:T(8,128)(2,1)S(1)}, u32[]{:S(2)}, u32[]{:S(2)}) async-start(bf16[32,128,128]{2,1,0:T(8,128)(2,1)} %get-tuple-element.40), calls=%async_computation.6 | async-start | bytes 2097152 | tf_op jit(solution)/shard_map/all_to_all | solution.py:323
  240.8 1.9 collective-permute-start.6
  242.6 4.8 %shard_map.63.local_ref = f32[16,128,128]{2,1,0:T(8,128)} custom-call(s32[3,32]{1,0:T(4,128)S(1)} %collective-permute-done.5.table, bf16[16,128,128]{2,1,0:T(8,128)(2,1)} %get-tuple-element.41.state_ref, bf16[16,3,128,128]{3,2,1,0:T(8,128)(2,1)} %collective-permute-done.13.blocks_ref), custom_call_target="tpu_custom_call" | custom-call | flops 201326592 | bytes 4194304 | tf_op jit(solution)/shard_map/pallas_call | solution.py:174
  247.4 11.6 %collective-permute-done.6.table = s32[3,32]{1,0:T(4,128)S(1)} collective-permute-done((s32[3,32]{1,0:T(4,128)S(1)}, s32[3,32]{1,0:T(4,128)S(1)}, u32[]{:S(2)}, u32[]{:S(2)}) %collective-permute-start.6) | collective-permute-done | bytes 416 | tf_op jit(solution)/shard_map/ppermute | solution.py:325
  259.0 7.5 %all-to-all-done.6.arrived_ref = bf16[32,128,128]{2,1,0:T(8,128)(2,1)S(1)} async-done(((bf16[32,128,128]{2,1,0:T(8,128)(2,1)}), bf16[32,128,128]{2,1,0:T(8,128)(2,1)S(1)}, u32[]{:S(2)}, u32[]{:S(2)}) %all-to-all-start.6) | async-done | bytes 1048608 | tf_op jit(solution)/shard_map/all_to_all | solution.py:323
  266.6 3.7 %shard_map.64 = (bf16[32,128,128]{2,1,0:T(8,128)(2,1)}, bf16[16,128,128]{2,1,0:T(8,128)(2,1)}) custom-call(s32[3,32]{1,0:T(4,128)S(1)} %collective-permute-done.6.table, bf16[32,128,128]{2,1,0:T(8,128)(2,1)S(1)} %all-to-all-done.6.arrived_ref, f32[16,128,128]{2,1,0:T(8,128)} %shard_map.63.local_ref, bf16[16,3,128,128]{3,2,1,0:T(8,128)(2,1)} %copy-done.7), custom_call_target="tpu_custom_call" | custom-call | flops 134217728 | bytes 4194304 | tf_op jit(solution)/shard_map/pallas_call | solution.py:134
  270.3 6.4 %all-to-all-start.7 = ((bf16[32,128,128]{2,1,0:T(8,128)(2,1)}), bf16[32,128,128]{2,1,0:T(8,128)(2,1)S(1)}, u32[]{:S(2)}, u32[]{:S(2)}) async-start(bf16[32,128,128]{2,1,0:T(8,128)(2,1)} %get-tuple-element.42), calls=%async_computation.7 | async-start | bytes 2097152 | tf_op jit(solution)/shard_map/all_to_all | solution.py:323
  276.8 4.8 %shard_map.65.local_ref = f32[16,128,128]{2,1,0:T(8,128)} custom-call(s32[3,32]{1,0:T(4,128)S(1)} %collective-permute-done.6.table, bf16[16,128,128]{2,1,0:T(8,128)(2,1)} %get-tuple-element.43.state_ref, bf16[16,3,128,128]{3,2,1,0:T(8,128)(2,1)} %copy-done.7), custom_call_target="tpu_custom_call" | custom-call | flops 201326592 | bytes 4194304 | tf_op jit(solution)/shard_map/pallas_call | solution.py:174
  281.5 21.2 %all-to-all-done.7.arrived_ref = bf16[32,128,128]{2,1,0:T(8,128)(2,1)S(1)} async-done(((bf16[32,128,128]{2,1,0:T(8,128)(2,1)}), bf16[32,128,128]{2,1,0:T(8,128)(2,1)S(1)}, u32[]{:S(2)}, u32[]{:S(2)}) %all-to-all-start.7) | async-done | bytes 1048608 | tf_op jit(solution)/shard_map/all_to_all | solution.py:323
  302.8 1.9 shard_map.66
  304.7 4.3 %collective-permute-start.15 = (bf16[1,128,128]{2,1,0:T(8,128)(2,1)S(1)}, bf16[1,128,128]{2,1,0:T(8,128)(2,1)S(1)}, u32[]{:S(2)}, u32[]{:S(2)}) collective-permute-start(bf16[1,128,128]{2,1,0:T(8,128)(2,1)S(1)} %get-tuple-element.51), channel_id=1, source_target_pairs={{0,1},{1,2},{2,3},{3,4},{4,5},{5,6},{6,7},{7,8},{8,9},{9,10},{10,1... | collective-permute-start | bytes 98312 | tf_op jit(solution)/shard_map/ppermute | solution.py:333
  309.0 1.9 collective-permute-start.16
  311.0 0.1 add_convert_fusion.place
  311.0 2.0 shard_map.67
  313.0 3.9 %collective-permute-done.16.high_ref = bf16[1,128,128]{2,1,0:T(8,128)(2,1)S(1)} collective-permute-done((bf16[1,128,128]{2,1,0:T(8,128)(2,1)S(1)}, bf16[1,128,128]{2,1,0:T(8,128)(2,1)S(1)}, u32[]{:S(2)}, u32[]{:S(2)}) %collective-permute-start.16) | collective-permute-done | bytes 32800 | tf_op jit(solution)/shard_map/ppermute | solution.py:334
  316.9 1.4 shard_map.68
  (40 shorter events, 0.2 us)
Async XLA Ops:
  1.4 1.0 copy-start
  6.2 12.7 %copy-start.8 = (s32[1,16,3]{1,0,2:T(1,128)S(1)}, s32[1,16,3]{1,0,2:T(1,128)}, u32[]{:S(2)}) copy-start(s32[1,16,3]{1,0,2:T(1,128)} %param.5) | copy-start | bytes 580
  6.2 41.0 %all-to-all-start = ((bf16[32,144,128]{2,1,0:T(8,128)(2,1)}), bf16[32,144,128]{2,1,0:T(8,128)(2,1)S(1)}, u32[]{:S(2)}, u32[]{:S(2)}) async-start(bf16[32,144,128]{2,1,0:T(8,128)(2,1)} %get-tuple-element.28), calls=%async_computation | async-start | bytes 2359296 | tf_op jit(solution)/shard_map/all_to_all | solution.py:323
  17.3 30.7 %collective-permute-start.8 = (bf16[16,3,128,128]{3,2,1,0:T(8,128)(2,1)}, bf16[16,3,128,128]{3,2,1,0:T(8,128)(2,1)S(1)}, u32[]{:S(2)}, u32[]{:S(2)}) collective-permute-start(bf16[16,3,128,128]{3,2,1,0:T(8,128)(2,1)} %bitcast.14), channel_id=1, source_target_pairs={{0,224},{32,0},{64,32},{96,64},{128,96},{160,128},{192,160},{224,1... | collective-permute-start | bytes 4718600 | tf_op jit(solution)/shard_map/ppermute | solution.py:331
  19.4 17.8 %collective-permute-start = (s32[3,32]{1,0:T(4,128)S(1)}, s32[3,32]{1,0:T(4,128)S(1)}, u32[]{:S(2)}, u32[]{:S(2)}) collective-permute-start(s32[3,32]{1,0:T(4,128)S(1)} %pad_add_fusion.table), channel_id=1, source_target_pairs={{0,224},{32,0},{64,32},{96,64},{128,96},{160,128},{192,160},{224,1... | collective-permute-start | bytes 1160 | tf_op jit(solution)/shard_map/ppermute | solution.py:325
  48.0 1.2 copy-start.1
  52.9 6.6 %copy-start.2 = (bf16[16,3,128,128]{3,2,1,0:T(8,128)(2,1)S(1)}, bf16[16,3,128,128]{3,2,1,0:T(8,128)(2,1)}, u32[]{:S(2)}) copy-start(bf16[16,3,128,128]{3,2,1,0:T(8,128)(2,1)} %copy-done.1) | copy-start | bytes 4718596
  52.9 32.6 %all-to-all-start.1 = ((bf16[32,128,128]{2,1,0:T(8,128)(2,1)}), bf16[32,128,128]{2,1,0:T(8,128)(2,1)S(1)}, u32[]{:S(2)}, u32[]{:S(2)}) async-start(bf16[32,128,128]{2,1,0:T(8,128)(2,1)} %get-tuple-element.30), calls=%async_computation.1 | async-start | bytes 2097152 | tf_op jit(solution)/shard_map/all_to_all | solution.py:323
  59.5 18.4 %collective-permute-start.9 = (bf16[16,3,128,128]{3,2,1,0:T(8,128)(2,1)S(1)}, bf16[16,3,128,128]{3,2,1,0:T(8,128)(2,1)}, u32[]{:S(2)}, u32[]{:S(2)}) collective-permute-start(bf16[16,3,128,128]{3,2,1,0:T(8,128)(2,1)S(1)} %copy-done.2), channel_id=1, source_target_pairs={{0,224},{32,0},{64,32},{96,64},{128,96},{160,128},{192,160},{224,1... | collective-permute-start | bytes 4718600 | tf_op jit(solution)/shard_map/ppermute | solution.py:331
  59.9 18.0 %collective-permute-start.1 = (s32[3,32]{1,0:T(4,128)S(1)}, s32[3,32]{1,0:T(4,128)S(1)}, u32[]{:S(2)}, u32[]{:S(2)}) collective-permute-start(s32[3,32]{1,0:T(4,128)S(1)} %pad_add_fusion.1.table), channel_id=1, source_target_pairs={{0,224},{32,0},{64,32},{96,64},{128,96},{160,128},{192,160},{224,1... | collective-permute-start | bytes 1160 | tf_op jit(solution)/shard_map/ppermute | solution.py:325
  89.1 32.1 %all-to-all-start.2 = ((bf16[32,128,128]{2,1,0:T(8,128)(2,1)}), bf16[32,128,128]{2,1,0:T(8,128)(2,1)S(1)}, u32[]{:S(2)}, u32[]{:S(2)}) async-start(bf16[32,128,128]{2,1,0:T(8,128)(2,1)} %get-tuple-element.32), calls=%async_computation.2 | async-start | bytes 2097152 | tf_op jit(solution)/shard_map/all_to_all | solution.py:323
  95.6 18.3 %collective-permute-start.10 = (bf16[16,3,128,128]{3,2,1,0:T(8,128)(2,1)}, bf16[16,3,128,128]{3,2,1,0:T(8,128)(2,1)S(1)}, u32[]{:S(2)}, u32[]{:S(2)}) collective-permute-start(bf16[16,3,128,128]{3,2,1,0:T(8,128)(2,1)} %collective-permute-done.9.blocks_ref), channel_id=1, source_target_pairs={{0,224},{32,0},{64,32},{96,64},{128,96},{160,128},{192,160},{224,1... | collective-permute-start | bytes 4718600 | tf_op jit(solution)/shard_map/ppermute | solution.py:331
  95.7 18.3 %collective-permute-start.2 = (s32[3,32]{1,0:T(4,128)S(1)}, s32[3,32]{1,0:T(4,128)S(1)}, u32[]{:S(2)}, u32[]{:S(2)}) collective-permute-start(s32[3,32]{1,0:T(4,128)S(1)} %collective-permute-done.1.table), channel_id=1, source_target_pairs={{0,224},{32,0},{64,32},{96,64},{128,96},{160,128},{192,160},{224,1... | collective-permute-start | bytes 1160 | tf_op jit(solution)/shard_map/ppermute | solution.py:325
  113.9 7.3 %copy-start.3 = (bf16[16,3,128,128]{3,2,1,0:T(8,128)(2,1)}, bf16[16,3,128,128]{3,2,1,0:T(8,128)(2,1)S(1)}, u32[]{:S(2)}) copy-start(bf16[16,3,128,128]{3,2,1,0:T(8,128)(2,1)S(1)} %collective-permute-done.10.blocks_ref) | copy-start | bytes 4718596
  124.9 6.6 %copy-start.4 = (bf16[16,3,128,128]{3,2,1,0:T(8,128)(2,1)S(1)}, bf16[16,3,128,128]{3,2,1,0:T(8,128)(2,1)}, u32[]{:S(2)}) copy-start(bf16[16,3,128,128]{3,2,1,0:T(8,128)(2,1)} %copy-done.3) | copy-start | bytes 4718596
  125.0 33.1 %all-to-all-start.3 = ((bf16[32,128,128]{2,1,0:T(8,128)(2,1)}), bf16[32,128,128]{2,1,0:T(8,128)(2,1)S(1)}, u32[]{:S(2)}, u32[]{:S(2)}) async-start(bf16[32,128,128]{2,1,0:T(8,128)(2,1)} %get-tuple-element.34), calls=%async_computation.3 | async-start | bytes 2097152 | tf_op jit(solution)/shard_map/all_to_all | solution.py:323
  131.5 18.0 %collective-permute-start.11 = (bf16[16,3,128,128]{3,2,1,0:T(8,128)(2,1)S(1)}, bf16[16,3,128,128]{3,2,1,0:T(8,128)(2,1)}, u32[]{:S(2)}, u32[]{:S(2)}) collective-permute-start(bf16[16,3,128,128]{3,2,1,0:T(8,128)(2,1)S(1)} %copy-done.4), channel_id=1, source_target_pairs={{0,224},{32,0},{64,32},{96,64},{128,96},{160,128},{192,160},{224,1... | collective-permute-start | bytes 4718600 | tf_op jit(solution)/shard_map/ppermute | solution.py:331
  131.6 17.9 %collective-permute-start.3 = (s32[3,32]{1,0:T(4,128)S(1)}, s32[3,32]{1,0:T(4,128)S(1)}, u32[]{:S(2)}, u32[]{:S(2)}) collective-permute-start(s32[3,32]{1,0:T(4,128)S(1)} %collective-permute-done.2.table), channel_id=1, source_target_pairs={{0,224},{32,0},{64,32},{96,64},{128,96},{160,128},{192,160},{224,1... | collective-permute-start | bytes 1160 | tf_op jit(solution)/shard_map/ppermute | solution.py:325
  161.7 32.3 %all-to-all-start.4 = ((bf16[32,128,128]{2,1,0:T(8,128)(2,1)}), bf16[32,128,128]{2,1,0:T(8,128)(2,1)S(1)}, u32[]{:S(2)}, u32[]{:S(2)}) async-start(bf16[32,128,128]{2,1,0:T(8,128)(2,1)} %get-tuple-element.36), calls=%async_computation.4 | async-start | bytes 2097152 | tf_op jit(solution)/shard_map/all_to_all | solution.py:323
  168.2 18.3 %collective-permute-start.12 = (bf16[16,3,128,128]{3,2,1,0:T(8,128)(2,1)}, bf16[16,3,128,128]{3,2,1,0:T(8,128)(2,1)S(1)}, u32[]{:S(2)}, u32[]{:S(2)}) collective-permute-start(bf16[16,3,128,128]{3,2,1,0:T(8,128)(2,1)} %collective-permute-done.11.blocks_ref), channel_id=1, source_target_pairs={{0,224},{32,0},{64,32},{96,64},{128,96},{160,128},{192,160},{224,1... | collective-permute-start | bytes 4718600 | tf_op jit(solution)/shard_map/ppermute | solution.py:331
  168.2 18.2 %collective-permute-start.4 = (s32[3,32]{1,0:T(4,128)S(1)}, s32[3,32]{1,0:T(4,128)S(1)}, u32[]{:S(2)}, u32[]{:S(2)}) collective-permute-start(s32[3,32]{1,0:T(4,128)S(1)} %collective-permute-done.3.table), channel_id=1, source_target_pairs={{0,224},{32,0},{64,32},{96,64},{128,96},{160,128},{192,160},{224,1... | collective-permute-start | bytes 1160 | tf_op jit(solution)/shard_map/ppermute | solution.py:325
  186.5 7.6 %copy-start.5 = (bf16[16,3,128,128]{3,2,1,0:T(8,128)(2,1)}, bf16[16,3,128,128]{3,2,1,0:T(8,128)(2,1)S(1)}, u32[]{:S(2)}) copy-start(bf16[16,3,128,128]{3,2,1,0:T(8,128)(2,1)S(1)} %collective-permute-done.12.blocks_ref) | copy-start | bytes 4718596
  197.8 6.6 %copy-start.6 = (bf16[16,3,128,128]{3,2,1,0:T(8,128)(2,1)S(1)}, bf16[16,3,128,128]{3,2,1,0:T(8,128)(2,1)}, u32[]{:S(2)}) copy-start(bf16[16,3,128,128]{3,2,1,0:T(8,128)(2,1)} %copy-done.5) | copy-start | bytes 4718596
  197.8 32.8 %all-to-all-start.5 = ((bf16[32,128,128]{2,1,0:T(8,128)(2,1)}), bf16[32,128,128]{2,1,0:T(8,128)(2,1)S(1)}, u32[]{:S(2)}, u32[]{:S(2)}) async-start(bf16[32,128,128]{2,1,0:T(8,128)(2,1)} %get-tuple-element.38), calls=%async_computation.5 | async-start | bytes 2097152 | tf_op jit(solution)/shard_map/all_to_all | solution.py:323
  204.4 18.0 %collective-permute-start.13 = (bf16[16,3,128,128]{3,2,1,0:T(8,128)(2,1)S(1)}, bf16[16,3,128,128]{3,2,1,0:T(8,128)(2,1)}, u32[]{:S(2)}, u32[]{:S(2)}) collective-permute-start(bf16[16,3,128,128]{3,2,1,0:T(8,128)(2,1)S(1)} %copy-done.6), channel_id=1, source_target_pairs={{0,224},{32,0},{64,32},{96,64},{128,96},{160,128},{192,160},{224,1... | collective-permute-start | bytes 4718600 | tf_op jit(solution)/shard_map/ppermute | solution.py:331
  204.4 17.9 %collective-permute-start.5 = (s32[3,32]{1,0:T(4,128)S(1)}, s32[3,32]{1,0:T(4,128)S(1)}, u32[]{:S(2)}, u32[]{:S(2)}) collective-permute-start(s32[3,32]{1,0:T(4,128)S(1)} %collective-permute-done.4.table), channel_id=1, source_target_pairs={{0,224},{32,0},{64,32},{96,64},{128,96},{160,128},{192,160},{224,1... | collective-permute-start | bytes 1160 | tf_op jit(solution)/shard_map/ppermute | solution.py:325
  234.3 32.3 %all-to-all-start.6 = ((bf16[32,128,128]{2,1,0:T(8,128)(2,1)}), bf16[32,128,128]{2,1,0:T(8,128)(2,1)S(1)}, u32[]{:S(2)}, u32[]{:S(2)}) async-start(bf16[32,128,128]{2,1,0:T(8,128)(2,1)} %get-tuple-element.40), calls=%async_computation.6 | async-start | bytes 2097152 | tf_op jit(solution)/shard_map/all_to_all | solution.py:323
  240.8 18.3 %collective-permute-start.14 = (bf16[16,3,128,128]{3,2,1,0:T(8,128)(2,1)}, bf16[16,3,128,128]{3,2,1,0:T(8,128)(2,1)S(1)}, u32[]{:S(2)}, u32[]{:S(2)}) collective-permute-start(bf16[16,3,128,128]{3,2,1,0:T(8,128)(2,1)} %collective-permute-done.13.blocks_ref), channel_id=1, source_target_pairs={{0,224},{32,0},{64,32},{96,64},{128,96},{160,128},{192,160},{224,1... | collective-permute-start | bytes 4718600 | tf_op jit(solution)/shard_map/ppermute | solution.py:331
  240.8 18.2 %collective-permute-start.6 = (s32[3,32]{1,0:T(4,128)S(1)}, s32[3,32]{1,0:T(4,128)S(1)}, u32[]{:S(2)}, u32[]{:S(2)}) collective-permute-start(s32[3,32]{1,0:T(4,128)S(1)} %collective-permute-done.5.table), channel_id=1, source_target_pairs={{0,224},{32,0},{64,32},{96,64},{128,96},{160,128},{192,160},{224,1... | collective-permute-start | bytes 1160 | tf_op jit(solution)/shard_map/ppermute | solution.py:325
  259.0 7.5 %copy-start.7 = (bf16[16,3,128,128]{3,2,1,0:T(8,128)(2,1)}, bf16[16,3,128,128]{3,2,1,0:T(8,128)(2,1)S(1)}, u32[]{:S(2)}) copy-start(bf16[16,3,128,128]{3,2,1,0:T(8,128)(2,1)S(1)} %collective-permute-done.14.blocks_ref) | copy-start | bytes 4718596
  270.3 32.5 %all-to-all-start.7 = ((bf16[32,128,128]{2,1,0:T(8,128)(2,1)}), bf16[32,128,128]{2,1,0:T(8,128)(2,1)S(1)}, u32[]{:S(2)}, u32[]{:S(2)}) async-start(bf16[32,128,128]{2,1,0:T(8,128)(2,1)} %get-tuple-element.42), calls=%async_computation.7 | async-start | bytes 2097152 | tf_op jit(solution)/shard_map/all_to_all | solution.py:323
  276.7 4.8 %collective-permute-start.7 = (s32[3,32]{1,0:T(4,128)S(1)}, s32[3,32]{1,0:T(4,128)S(1)}, u32[]{:S(2)}, u32[]{:S(2)}) collective-permute-start(s32[3,32]{1,0:T(4,128)S(1)} %collective-permute-done.6.table), channel_id=1, source_target_pairs={{0,224},{32,0},{64,32},{96,64},{128,96},{160,128},{192,160},{224,1... | collective-permute-start | bytes 1160 | tf_op jit(solution)/shard_map/ppermute | solution.py:325
  304.7 8.3 %collective-permute-start.15 = (bf16[1,128,128]{2,1,0:T(8,128)(2,1)S(1)}, bf16[1,128,128]{2,1,0:T(8,128)(2,1)S(1)}, u32[]{:S(2)}, u32[]{:S(2)}) collective-permute-start(bf16[1,128,128]{2,1,0:T(8,128)(2,1)S(1)} %get-tuple-element.51), channel_id=1, source_target_pairs={{0,1},{1,2},{2,3},{3,4},{4,5},{5,6},{6,7},{7,8},{8,9},{9,10},{10,1... | collective-permute-start | bytes 98312 | tf_op jit(solution)/shard_map/ppermute | solution.py:333
  309.0 7.9 %collective-permute-start.16 = (bf16[1,128,128]{2,1,0:T(8,128)(2,1)S(1)}, bf16[1,128,128]{2,1,0:T(8,128)(2,1)S(1)}, u32[]{:S(2)}, u32[]{:S(2)}) collective-permute-start(bf16[1,128,128]{2,1,0:T(8,128)(2,1)S(1)} %get-tuple-element.50), channel_id=1, source_target_pairs={{1,0},{2,1},{3,2},{4,3},{5,4},{6,5},{7,6},{8,7},{9,8},{10,9},{11,1... | collective-permute-start | bytes 98312 | tf_op jit(solution)/shard_map/ppermute | solution.py:334

commit v4 on v3

--- a/solution.py
+++ b/solution.py
@@ -53,14 +53,21 @@
     return pltpu.make_async_copy(blocks_ref.at[:, pl.ds(1, off_scr.shape[1])], off_scr, sem)
 
 
-def first_body(dest, seeds_ref, blocks_ref, out_ref, state_ref, off_scr, stage, state_scr, lists, sems, out_sems):
-    load = off_copy(blocks_ref, off_scr, sems.at[0])
-    load.start()
-    tiles, nnz = dest.shape[1:]
+def first_body(
+    dest, seeds_ref, blocks_ref, out_ref, state_ref, seeds_scr, off_scr, stage, state_scr, lists, sems, out_sems, in_sems
+):
+    nnz, tiles = dest.shape
     each = nnz - 1
     rows = state_scr.shape[1]
-    for t in range(tiles):
-        state_scr[t] = jnp.transpose(seeds_ref[t].astype(jnp.float32)).astype(jnp.bfloat16)
+    parts = [pl.ds(t, PART) for t in range(0, tiles, PART)]
+    seeding = [pltpu.make_async_copy(seeds_ref.at[p], seeds_scr.at[p], in_sems.at[n]) for n, p in enumerate(parts)]
+    load = off_copy(blocks_ref, off_scr, sems.at[0])
+    for copy in [*seeding, load]:
+        copy.start()
+    for t in range(tiles):
+        if t % PART == 0:
+            seeding[t // PART].wait()
+        state_scr[t] = jnp.transpose(seeds_scr[t].astype(jnp.float32)).astype(jnp.bfloat16)
     store = pltpu.make_async_copy(state_scr, state_ref, sems.at[1])
     store.start()
     for p in range(stage.shape[0]):
@@ -68,7 +75,7 @@
         lists[1, p] = tiles
     for t in range(tiles):
         for k in range(1, nnz):
-            to = dest[0, t, k]
+            to = dest[k, t]
             peer = lax.div(to, tiles)
             lists[0, peer] = t * each + k - 1
             lists[1, peer] = to - peer * tiles
@@ -88,71 +95,82 @@
             pltpu.HBM((peers, rows + SAYS, points), jnp.bfloat16),
             pltpu.HBM((tiles, rows, points), jnp.bfloat16),
         ),
-        in_specs=[SMEM, VMEM, HBM],
+        in_specs=[SMEM, HBM, HBM],
         out_specs=(HBM, HBM),
         scratch_shapes=[
+            pltpu.VMEM(seeds.shape, jnp.bfloat16),
             pltpu.VMEM((tiles, nnz - 1, points, points), jnp.bfloat16),
             pltpu.VMEM((peers, rows + SAYS, points), jnp.bfloat16),
             pltpu.VMEM((tiles, rows, points), jnp.bfloat16),
             pltpu.SMEM((2, peers), jnp.int32),
             pltpu.SemaphoreType.DMA((2,)),
             pltpu.SemaphoreType.DMA((peers // PART,)),
+            pltpu.SemaphoreType.DMA((tiles // PART,)),
         ],
         compiler_params=SEND,
         cost_estimate=pl.CostEstimate(
             flops=2 * peers * points * points * rows, bytes_accessed=4 << 20, transcendentals=0
         ),
-    )(dest, seeds, placed(blocks, pltpu.HBM))
+    )(dest, placed(seeds, pltpu.HBM), placed(blocks, pltpu.HBM))
+
+
+def fetch_body(blocks_ref, off_ref, sem):
+    load = off_copy(blocks_ref, off_ref, sem)
+    load.start()
+    load.wait()
+
+
+def fetch(blocks):
+    tiles, nnz, points = blocks.shape[:3]
+    return pl.pallas_call(
+        fetch_body,
+        out_shape=pltpu.VMEM((tiles, nnz - 1, points, points), jnp.bfloat16),
+        in_specs=[HBM],
+        out_specs=VMEM,
+        scratch_shapes=[pltpu.SemaphoreType.DMA],
+        compiler_params=SMALL,
+        cost_estimate=pl.CostEstimate(flops=0, bytes_accessed=2 << 20, transcendentals=0),
+    )(placed(blocks, pltpu.HBM))
 
 
 def send_body(
-    table, arrived_ref, local_ref, blocks_ref, out_ref, state_ref,
-    stage, gathered, state_scr, local_scr, off_scr, sems, out_sems,
+    table, arrived_ref, local_ref, off_ref, out_ref, state_ref, stage, gathered, state_scr, store_sem, out_sems,
 ):
-    load_local = pltpu.make_async_copy(local_ref, local_scr, sems.at[0])
-    load = off_copy(blocks_ref, off_scr, sems.at[1])
-    load_local.start()
-    load.start()
     add_arrived(table, arrived_ref, gathered)
-    load_local.wait()
     for t in range(state_scr.shape[0]):
-        state_scr[t] = (gathered[t] + local_scr[t]).astype(jnp.bfloat16)
-    store = pltpu.make_async_copy(state_scr, state_ref, sems.at[2])
+        state_scr[t] = (gathered[t] + local_ref[t]).astype(jnp.bfloat16)
+    store = pltpu.make_async_copy(state_scr, state_ref, store_sem)
     store.start()
-    load.wait()
-    send_products(lambda p: table[WANTED, p], off_scr, state_scr, out_ref, stage, out_sems)
+    send_products(lambda p: table[WANTED, p], off_ref, state_scr, out_ref, stage, out_sems)
     store.wait()
 
 
 placed = pltpu.with_memory_space_constraint
 
 
-def send(table, arrived, local, blocks):
+def send(table, arrived, local, off):
     peers = arrived.shape[0]
     tiles, rows, points = local.shape
-    nnz = blocks.shape[1]
     return pl.pallas_call(
         send_body,
         out_shape=(
             pltpu.HBM((peers, rows, points), jnp.bfloat16),
             pltpu.HBM((tiles, rows, points), jnp.bfloat16),
         ),
-        in_specs=[SMEM, VMEM, HBM, HBM],
+        in_specs=[SMEM, VMEM, VMEM, VMEM],
         out_specs=(HBM, HBM),
         scratch_shapes=[
             pltpu.VMEM((peers, rows, points), jnp.bfloat16),
             pltpu.VMEM((tiles + 1, rows, points), jnp.float32),
             pltpu.VMEM((tiles, rows, points), jnp.bfloat16),
-            pltpu.VMEM(local.shape, jnp.float32),
-            pltpu.VMEM((tiles, nnz - 1, points, points), jnp.bfloat16),
-            pltpu.SemaphoreType.DMA((3,)),
+            pltpu.SemaphoreType.DMA,
             pltpu.SemaphoreType.DMA((peers // PART,)),
         ],
         compiler_params=SEND,
         cost_estimate=pl.CostEstimate(
             flops=2 * peers * points * points * rows, bytes_accessed=4 << 20, transcendentals=0
         ),
-    )(table, placed(arrived, pltpu.VMEM), placed(local, pltpu.HBM), placed(blocks, pltpu.HBM))
+    )(table, placed(arrived, pltpu.VMEM), placed(local, pltpu.VMEM), placed(off, pltpu.VMEM))
 
 
 def keep_body(table, state_ref, blocks_ref, local_ref, total, blocks_scr, sem):
@@ -173,7 +191,7 @@
     tiles, rows, points = state.shape
     return pl.pallas_call(
         keep_body,
-        out_shape=pltpu.HBM((tiles, rows, points), jnp.float32),
+        out_shape=pltpu.VMEM((tiles, rows, points), jnp.float32),
         in_specs=[SMEM, VMEM, HBM],
         out_specs=VMEM,
         scratch_shapes=[
@@ -188,16 +206,13 @@
     )(table, placed(state, pltpu.HBM), placed(blocks, pltpu.HBM))
 
 
-def last_body(before, arrived_ref, local_ref, final_ref, edges_ref, gathered, local_scr, sem):
-    load_local = pltpu.make_async_copy(local_ref, local_scr, sem)
-    load_local.start()
+def last_body(before, arrived_ref, local_ref, final_ref, low_ref, high_ref, gathered):
     add_arrived(before, arrived_ref, gathered)
-    load_local.wait()
     tiles = final_ref.shape[0]
     for t in range(tiles):
-        final_ref[t] = (gathered[t] + local_scr[t]).astype(jnp.bfloat16)
-    edges_ref[0] = final_ref[0]
-    edges_ref[1] = final_ref[tiles - 1]
+        final_ref[t] = (gathered[t] + local_ref[t]).astype(jnp.bfloat16)
+    low_ref[0] = final_ref[0]
+    high_ref[0] = final_ref[tiles - 1]
 
 
 def last_sum(before, arrived, local):
@@ -206,17 +221,16 @@
         last_body,
         out_shape=(
             jax.ShapeDtypeStruct((tiles, rows, points), jnp.bfloat16),
-            jax.ShapeDtypeStruct((2, rows, points), jnp.bfloat16),
-        ),
-        in_specs=[SMEM, VMEM, HBM],
-        out_specs=(VMEM, VMEM),
+            jax.ShapeDtypeStruct((1, rows, points), jnp.bfloat16),
+            jax.ShapeDtypeStruct((1, rows, points), jnp.bfloat16),
+        ),
+        in_specs=[SMEM, VMEM, VMEM],
+        out_specs=(VMEM, VMEM, VMEM),
         scratch_shapes=[
             pltpu.VMEM((tiles + 1, rows, points), jnp.float32),
-            pltpu.VMEM((tiles, rows, points), jnp.float32),
-            pltpu.SemaphoreType.DMA,
         ],
         compiler_params=SMALL,
-    )(before, arrived, local)
+    )(before, placed(arrived, pltpu.VMEM), placed(local, pltpu.VMEM))
 
 
 def stretch_tile(ndays, here, dy):
@@ -314,12 +328,12 @@
 
     for step in range(ndays):
         if step == 0:
-            out, state = send_first(dest_tiles, seeds, wblk, peers)
+            out, state = send_first(dest_tiles.transpose(2, 0, 1).reshape(nnz, tiles), seeds, wblk, peers)
             dest, state = lax.optimization_barrier((dest_tiles[0], state))
             rows = own_rows(dest, me, tiles, peers, nnz)
             table = jnp.stack([*rows, jnp.zeros_like(rows[0])])
         else:
-            out, state = send(table, arrived, local, wblk)
+            out, state = send(table, arrived, local, off)
         arrived = lax.all_to_all(out, "tile", split_axis=0, concat_axis=0, tiled=True)
         local = keep(table, state, wblk)
         table = onward(table)
@@ -329,9 +343,10 @@
             table = jnp.concatenate([table[:2], landed[None]], axis=0)
         if step < ndays - 1:
             wblk = onward(wblk)
-    final, edges = last_sum(table, arrived, placed(local, pltpu.HBM))
-    low = lax.ppermute(edges[1:], "tile", [(i, i + 1) for i in range(peers - 1)])
-    high = lax.ppermute(edges[:1], "tile", [(i + 1, i) for i in range(peers - 1)])
+            off = fetch(wblk)
+    final, lowest, highest = last_sum(table, arrived, local)
+    low = lax.ppermute(highest, "tile", [(i, i + 1) for i in range(peers - 1)])
+    high = lax.ppermute(lowest, "tile", [(i + 1, i) for i in range(peers - 1)])
     place = jnp.stack([me == 0, me == peers - 1]).astype(jnp.int32)
     inner = stretch_inner(final, ndays)
     ftle, minor = stretch_edges(place, final, low, high, inner, ndays)

time: 320 us -> 325 us (1.016)
  starting transfers between devices: 79.4 us -> 93.8 us
  Pallas kernels: 72.9 us -> 65.6 us
  waiting for transfers between devices: 161 us -> 154 us
  local copies, waits for them, and re-layouts: 3.26 us -> 6.8 us
    ppermute x7, waiting for transfers between devices: 0.02 us -> 93.7 us  [body(): wblk = onward(wblk)]
    ppermute x8, waiting for transfers between devices: 78.8 us -> 12.8 us  [body(): table = onward(table)]
    all_to_all x8, waiting for transfers between devices: 78.1 us -> 43.9 us  [body(): lax.all_to_all(out, 'tile', split_axis=0, concat_axis=0, tiled=True)]
    all_to_all x8, starting transfers between devices: 56.6 us -> 65.6 us  [body(): lax.all_to_all(out, 'tile', split_axis=0, concat_axis=0, tiled=True)]
    ppermute x7, starting transfers between devices: 2.23 us -> 11.1 us  [body(): wblk = onward(wblk)]
    pallas_call x7, Pallas kernels: 25.9 us -> 18.9 us  [send(): pl.pallas_call(send_body, out_shape=(pltpu.HBM((peers, rows, points), jnp...]
    unnamed x20 -> x22, local copies, waits for them, and re-layouts: 2.98 us -> 6.52 us
    ppermute x8, starting transfers between devices: 14.4 us -> 10.8 us  [body(): table = onward(table)]
  transfers between devices with their start and end apart: 25 -> 25, of which waited for: 16 -> 15; matrix products, arithmetic and copies ran while one was open for 0% -> 0% of each run, Pallas kernels for 13% -> 13%
where the time goes in v4:
time: 325 us; the launch traced here: 323 us
  waiting for transfers between devices  154 us (47%)
  starting transfers between devices  93.8 us (29%)
  Pallas kernels  65.6 us (20%)
  local copies, waits for them, and re-layouts  6.8 us (2%)
    ppermute x7, waiting for transfers between devices, body(): wblk = onward(wblk)  93.7 us
    all_to_all x8, starting transfers between devices, body(): lax.all_to_all(out, 'tile', split_axis=0, concat_axis=0, tiled=True)  65.6 us
    all_to_all x8, waiting for transfers between devices, body(): lax.all_to_all(out, 'tile', split_axis=0, concat_axis=0, tiled=True)  43.9 us
    pallas_call x8, Pallas kernels, keep(): pl.pallas_call(keep_body, out_shape=pltpu.VMEM((tiles, rows, points), jnp...  30 us
    pallas_call x7, Pallas kernels, send(): pl.pallas_call(send_body, out_shape=(pltpu.HBM((peers, rows, points), jnp...  18.9 us
    ppermute x8, waiting for transfers between devices, body(): table = onward(table)  12.8 us
    ppermute x7, starting transfers between devices, body(): wblk = onward(wblk)  11.1 us
    ppermute x8, starting transfers between devices, body(): table = onward(table)  10.8 us
  transfers between devices with their start and end apart: 25, of which 15 were waited for; matrix products, arithmetic and copies ran while one was open for 0% of the time, Pallas kernels for 13%

profile of v4, /device:TPU:56, one launch (start us, length us, event | category | flops | bytes accessed | tf_op | source)
XLA Modules:
  0.0 322.8 jit_solution(13709767484660797634)
XLA Ops:
  1.3 3.7 %shard_map.50 = (bf16[32,144,128]{2,1,0:T(8,128)(2,1)}, bf16[16,128,128]{2,1,0:T(8,128)(2,1)}) custom-call(s32[3,16]{1,0:T(4,128)S(1)} %bitcast.16, bf16[16,128,128]{2,1,0:T(8,128)(2,1)} %bitcast.17, bf16[16,3,128,128]{3,2,1,0:T(8,128)(2,1)} %bitcast.4.blocks_ref), custom_call_target="tpu_custom_call" | custom-call | flops 134217728 | bytes 4194304 | tf_op jit(solution)/shard_map/pallas_call | solution.py:92
  5.0 11.0 %all-to-all-start = ((bf16[32,144,128]{2,1,0:T(8,128)(2,1)}), bf16[32,144,128]{2,1,0:T(8,128)(2,1)S(1)}, u32[]{:S(2)}, u32[]{:S(2)}) async-start(bf16[32,144,128]{2,1,0:T(8,128)(2,1)} %get-tuple-element.29), calls=%async_computation | async-start | bytes 2359296 | tf_op jit(solution)/shard_map/all_to_all | solution.py:337
  16.1 1.6 collective-permute-start.8
  18.2 1.2 collective-permute-start
  19.4 3.7 %shard_map.51.local_ref = f32[16,128,128]{2,1,0:T(8,128)S(1)} custom-call(s32[3,32]{1,0:T(4,128)S(1)} %pad_add_fusion.table, bf16[16,128,128]{2,1,0:T(8,128)(2,1)} %get-tuple-element.30.state_ref, bf16[16,3,128,128]{3,2,1,0:T(8,128)(2,1)} %bitcast.4.blocks_ref), custom_call_target="tpu_custom_call" | custom-call | flops 201326592 | bytes 4194304 | tf_op jit(solution)/shard_map/pallas_call | solution.py:192
  23.2 12.8 %collective-permute-done = s32[3,32]{1,0:T(4,128)S(1)} collective-permute-done((s32[3,32]{1,0:T(4,128)S(1)}, s32[3,32]{1,0:T(4,128)S(1)}, u32[]{:S(2)}, u32[]{:S(2)}) %collective-permute-start) | collective-permute-done | bytes 416 | tf_op jit(solution)/shard_map/ppermute | solution.py:339
  36.0 1.2 shard_map.52.off_ref
  37.2 8.9 %all-to-all-done.arrived_ref = bf16[32,144,128]{2,1,0:T(8,128)(2,1)S(1)} async-done(((bf16[32,144,128]{2,1,0:T(8,128)(2,1)}), bf16[32,144,128]{2,1,0:T(8,128)(2,1)S(1)}, u32[]{:S(2)}, u32[]{:S(2)}) %all-to-all-start) | async-done | bytes 1179680 | tf_op jit(solution)/shard_map/all_to_all | solution.py:337
  46.8 2.7 shard_map.53
  49.5 6.4 %all-to-all-start.1 = ((bf16[32,128,128]{2,1,0:T(8,128)(2,1)}), bf16[32,128,128]{2,1,0:T(8,128)(2,1)S(1)}, u32[]{:S(2)}, u32[]{:S(2)}) async-start(bf16[32,128,128]{2,1,0:T(8,128)(2,1)} %get-tuple-element.31), calls=%async_computation.1 | async-start | bytes 2097152 | tf_op jit(solution)/shard_map/all_to_all | solution.py:337
  56.4 2.4 collective-permute-start.1
  58.8 3.7 %shard_map.54.local_ref = f32[16,128,128]{2,1,0:T(8,128)S(1)} custom-call(s32[3,32]{1,0:T(4,128)S(1)} %pad_add_fusion.1.table, bf16[16,128,128]{2,1,0:T(8,128)(2,1)} %get-tuple-element.32.state_ref, bf16[16,3,128,128]{3,2,1,0:T(8,128)(2,1)} %collective-permute-done.8.blocks_ref), custom_call_target="tpu_custom_call" | custom-call | flops 201326592 | bytes 4194304 | tf_op jit(solution)/shard_map/pallas_call | solution.py:192
  62.6 12.0 %collective-permute-done.9.blocks_ref = bf16[16,3,128,128]{3,2,1,0:T(8,128)(2,1)} collective-permute-done((bf16[16,3,128,128]{3,2,1,0:T(8,128)(2,1)}, bf16[16,3,128,128]{3,2,1,0:T(8,128)(2,1)}, u32[]{:S(2)}, u32[]{:S(2)}) %collective-permute-start.9) | collective-permute-done | bytes 1572896 | tf_op jit(solution)/shard_map/ppermute | solution.py:345
  74.6 1.2 shard_map.55.off_ref
  75.9 6.0 %all-to-all-done.1.arrived_ref = bf16[32,128,128]{2,1,0:T(8,128)(2,1)S(1)} async-done(((bf16[32,128,128]{2,1,0:T(8,128)(2,1)}), bf16[32,128,128]{2,1,0:T(8,128)(2,1)S(1)}, u32[]{:S(2)}, u32[]{:S(2)}) %all-to-all-start.1) | async-done | bytes 1048608 | tf_op jit(solution)/shard_map/all_to_all | solution.py:337
  81.9 2.7 shard_map.56
  84.6 6.4 %all-to-all-start.2 = ((bf16[32,128,128]{2,1,0:T(8,128)(2,1)}), bf16[32,128,128]{2,1,0:T(8,128)(2,1)S(1)}, u32[]{:S(2)}, u32[]{:S(2)}) async-start(bf16[32,128,128]{2,1,0:T(8,128)(2,1)} %get-tuple-element.33), calls=%async_computation.2 | async-start | bytes 2097152 | tf_op jit(solution)/shard_map/all_to_all | solution.py:337
  91.2 2.8 collective-permute-start.2
  94.0 3.7 %shard_map.57.local_ref = f32[16,128,128]{2,1,0:T(8,128)S(1)} custom-call(s32[3,32]{1,0:T(4,128)S(1)} %collective-permute-done.1.table, bf16[16,128,128]{2,1,0:T(8,128)(2,1)} %get-tuple-element.34.state_ref, bf16[16,3,128,128]{3,2,1,0:T(8,128)(2,1)} %collective-permute-done.9.blocks_ref), custom_call_target="tpu_custom_call" | custom-call | flops 201326592 | bytes 4194304 | tf_op jit(solution)/shard_map/pallas_call | solution.py:192
  97.7 11.7 %collective-permute-done.10.blocks_ref = bf16[16,3,128,128]{3,2,1,0:T(8,128)(2,1)S(1)} collective-permute-done((bf16[16,3,128,128]{3,2,1,0:T(8,128)(2,1)}, bf16[16,3,128,128]{3,2,1,0:T(8,128)(2,1)S(1)}, u32[]{:S(2)}, u32[]{:S(2)}) %collective-permute-start.10) | collective-permute-done | bytes 1572896 | tf_op jit(solution)/shard_map/ppermute | solution.py:345
  109.4 1.2 copy-done
  110.6 1.2 shard_map.58.off_ref
  111.8 5.5 %all-to-all-done.2.arrived_ref = bf16[32,128,128]{2,1,0:T(8,128)(2,1)S(1)} async-done(((bf16[32,128,128]{2,1,0:T(8,128)(2,1)}), bf16[32,128,128]{2,1,0:T(8,128)(2,1)S(1)}, u32[]{:S(2)}, u32[]{:S(2)}) %all-to-all-start.2) | async-done | bytes 1048608 | tf_op jit(solution)/shard_map/all_to_all | solution.py:337
  117.3 2.7 shard_map.59
  120.0 6.6 %all-to-all-start.3 = ((bf16[32,128,128]{2,1,0:T(8,128)(2,1)}), bf16[32,128,128]{2,1,0:T(8,128)(2,1)S(1)}, u32[]{:S(2)}, u32[]{:S(2)}) async-start(bf16[32,128,128]{2,1,0:T(8,128)(2,1)} %get-tuple-element.35), calls=%async_computation.3 | async-start | bytes 2097152 | tf_op jit(solution)/shard_map/all_to_all | solution.py:337
  127.3 1.7 collective-permute-start.3
  128.9 16.3 %collective-permute-done.11.blocks_ref = bf16[16,3,128,128]{3,2,1,0:T(8,128)(2,1)S(1)} collective-permute-done((bf16[16,3,128,128]{3,2,1,0:T(8,128)(2,1)S(1)}, bf16[16,3,128,128]{3,2,1,0:T(8,128)(2,1)S(1)}, u32[]{:S(2)}, u32[]{:S(2)}) %collective-permute-start.11) | collective-permute-done | bytes 1572896 | tf_op jit(solution)/shard_map/ppermute | solution.py:345
  145.2 1.2 copy-done.2
  146.4 1.2 shard_map.61.off_ref
  147.6 3.8 %shard_map.60.local_ref = f32[16,128,128]{2,1,0:T(8,128)S(1)} custom-call(s32[3,32]{1,0:T(4,128)S(1)} %collective-permute-done.2.table, bf16[16,128,128]{2,1,0:T(8,128)(2,1)} %get-tuple-element.36.state_ref, bf16[16,3,128,128]{3,2,1,0:T(8,128)(2,1)} %copy-done), custom_call_target="tpu_custom_call" | custom-call | flops 201326592 | bytes 4194304 | tf_op jit(solution)/shard_map/pallas_call | solution.py:192
  151.4 2.4 all-to-all-done.3.arrived_ref
  153.7 2.7 shard_map.62
  156.5 7.6 %all-to-all-start.4 = ((bf16[32,128,128]{2,1,0:T(8,128)(2,1)}), bf16[32,128,128]{2,1,0:T(8,128)(2,1)S(1)}, u32[]{:S(2)}, u32[]{:S(2)}) async-start(bf16[32,128,128]{2,1,0:T(8,128)(2,1)} %get-tuple-element.37), calls=%async_computation.4 | async-start | bytes 2097152 | tf_op jit(solution)/shard_map/all_to_all | solution.py:337
  164.0 2.9 collective-permute-start.12
  167.0 17.9 %collective-permute-done.12.blocks_ref = bf16[16,3,128,128]{3,2,1,0:T(8,128)(2,1)S(1)} collective-permute-done((bf16[16,3,128,128]{3,2,1,0:T(8,128)(2,1)S(1)}, bf16[16,3,128,128]{3,2,1,0:T(8,128)(2,1)S(1)}, u32[]{:S(2)}, u32[]{:S(2)}) %collective-permute-start.12) | collective-permute-done | bytes 1572896 | tf_op jit(solution)/shard_map/ppermute | solution.py:345
  184.9 1.2 copy-done.4
  186.0 1.2 shard_map.64.off_ref
  187.3 3.7 %shard_map.63.local_ref = f32[16,128,128]{2,1,0:T(8,128)S(1)} custom-call(s32[3,32]{1,0:T(4,128)S(1)} %collective-permute-done.3.table, bf16[16,128,128]{2,1,0:T(8,128)(2,1)} %get-tuple-element.38.state_ref, bf16[16,3,128,128]{3,2,1,0:T(8,128)(2,1)} %copy-done.2), custom_call_target="tpu_custom_call" | custom-call | flops 201326592 | bytes 4194304 | tf_op jit(solution)/shard_map/pallas_call | solution.py:192
  191.0 1.5 all-to-all-done.4.arrived_ref
  192.5 2.7 shard_map.65
  195.2 8.4 %all-to-all-start.5 = ((bf16[32,128,128]{2,1,0:T(8,128)(2,1)}), bf16[32,128,128]{2,1,0:T(8,128)(2,1)S(1)}, u32[]{:S(2)}, u32[]{:S(2)}) async-start(bf16[32,128,128]{2,1,0:T(8,128)(2,1)} %get-tuple-element.39), calls=%async_computation.5 | async-start | bytes 2097152 | tf_op jit(solution)/shard_map/all_to_all | solution.py:337
  203.7 2.9 collective-permute-start.13
  206.6 17.9 %collective-permute-done.13.blocks_ref = bf16[16,3,128,128]{3,2,1,0:T(8,128)(2,1)S(1)} collective-permute-done((bf16[16,3,128,128]{3,2,1,0:T(8,128)(2,1)S(1)}, bf16[16,3,128,128]{3,2,1,0:T(8,128)(2,1)S(1)}, u32[]{:S(2)}, u32[]{:S(2)}) %collective-permute-start.13) | collective-permute-done | bytes 1572896 | tf_op jit(solution)/shard_map/ppermute | solution.py:345
  224.5 1.2 copy-done.6
  225.7 1.2 shard_map.67.off_ref
  226.9 3.8 %shard_map.66.local_ref = f32[16,128,128]{2,1,0:T(8,128)S(1)} custom-call(s32[3,32]{1,0:T(4,128)S(1)} %collective-permute-done.4.table, bf16[16,128,128]{2,1,0:T(8,128)(2,1)} %get-tuple-element.40.state_ref, bf16[16,3,128,128]{3,2,1,0:T(8,128)(2,1)} %copy-done.4), custom_call_target="tpu_custom_call" | custom-call | flops 201326592 | bytes 4194304 | tf_op jit(solution)/shard_map/pallas_call | solution.py:192
  231.3 2.7 shard_map.68
  234.0 9.3 %all-to-all-start.6 = ((bf16[32,128,128]{2,1,0:T(8,128)(2,1)}), bf16[32,128,128]{2,1,0:T(8,128)(2,1)S(1)}, u32[]{:S(2)}, u32[]{:S(2)}) async-start(bf16[32,128,128]{2,1,0:T(8,128)(2,1)} %get-tuple-element.41), calls=%async_computation.6 | async-start | bytes 2097152 | tf_op jit(solution)/shard_map/all_to_all | solution.py:337
  243.3 2.6 collective-permute-start.14
  246.0 17.9 %collective-permute-done.14.blocks_ref = bf16[16,3,128,128]{3,2,1,0:T(8,128)(2,1)S(1)} collective-permute-done((bf16[16,3,128,128]{3,2,1,0:T(8,128)(2,1)S(1)}, bf16[16,3,128,128]{3,2,1,0:T(8,128)(2,1)S(1)}, u32[]{:S(2)}, u32[]{:S(2)}) %collective-permute-start.14) | collective-permute-done | bytes 1572896 | tf_op jit(solution)/shard_map/ppermute | solution.py:345
  263.9 1.2 copy-done.8
  265.0 1.2 shard_map.70.off_ref
  266.2 3.7 %shard_map.69.local_ref = f32[16,128,128]{2,1,0:T(8,128)S(1)} custom-call(s32[3,32]{1,0:T(4,128)S(1)} %collective-permute-done.5.table, bf16[16,128,128]{2,1,0:T(8,128)(2,1)} %get-tuple-element.42.state_ref, bf16[16,3,128,128]{3,2,1,0:T(8,128)(2,1)} %copy-done.6), custom_call_target="tpu_custom_call" | custom-call | flops 201326592 | bytes 4194304 | tf_op jit(solution)/shard_map/pallas_call | solution.py:192
  270.0 2.7 shard_map.71
  272.7 9.8 %all-to-all-start.7 = ((bf16[32,128,128]{2,1,0:T(8,128)(2,1)}), bf16[32,128,128]{2,1,0:T(8,128)(2,1)S(1)}, u32[]{:S(2)}, u32[]{:S(2)}) async-start(bf16[32,128,128]{2,1,0:T(8,128)(2,1)} %get-tuple-element.43), calls=%async_computation.7 | async-start | bytes 2097152 | tf_op jit(solution)/shard_map/all_to_all | solution.py:337
  282.5 2.6 collective-permute-start.7
  285.1 3.7 %shard_map.72.local_ref = f32[16,128,128]{2,1,0:T(8,128)S(1)} custom-call(s32[3,32]{1,0:T(4,128)S(1)} %collective-permute-done.6.table, bf16[16,128,128]{2,1,0:T(8,128)(2,1)} %get-tuple-element.44.state_ref, bf16[16,3,128,128]{3,2,1,0:T(8,128)(2,1)} %copy-done.8), custom_call_target="tpu_custom_call" | custom-call | flops 201326592 | bytes 4194304 | tf_op jit(solution)/shard_map/pallas_call | solution.py:192
  288.9 19.1 %all-to-all-done.7.arrived_ref = bf16[32,128,128]{2,1,0:T(8,128)(2,1)S(1)} async-done(((bf16[32,128,128]{2,1,0:T(8,128)(2,1)}), bf16[32,128,128]{2,1,0:T(8,128)(2,1)S(1)}, u32[]{:S(2)}, u32[]{:S(2)}) %all-to-all-start.7) | async-done | bytes 1048608 | tf_op jit(solution)/shard_map/all_to_all | solution.py:337
  308.0 1.0 shard_map.73
  309.0 4.3 %collective-permute-start.15 = (bf16[1,128,128]{2,1,0:T(8,128)(2,1)S(1)}, bf16[1,128,128]{2,1,0:T(8,128)(2,1)S(1)}, u32[]{:S(2)}, u32[]{:S(2)}) collective-permute-start(bf16[1,128,128]{2,1,0:T(8,128)(2,1)S(1)} %get-tuple-element.46), channel_id=1, source_target_pairs={{0,1},{1,2},{2,3},{3,4},{4,5},{5,6},{6,7},{7,8},{8,9},{9,10},{10,1... | collective-permute-start | bytes 98312 | tf_op jit(solution)/shard_map/ppermute | solution.py:348
  313.3 1.9 collective-permute-start.16
  315.3 2.0 shard_map.74
  317.3 3.9 %collective-permute-done.16.high_ref = bf16[1,128,128]{2,1,0:T(8,128)(2,1)S(1)} collective-permute-done((bf16[1,128,128]{2,1,0:T(8,128)(2,1)S(1)}, bf16[1,128,128]{2,1,0:T(8,128)(2,1)S(1)}, u32[]{:S(2)}, u32[]{:S(2)}) %collective-permute-start.16) | collective-permute-done | bytes 32800 | tf_op jit(solution)/shard_map/ppermute | solution.py:349
  321.3 1.4 shard_map.75
  (48 shorter events, 3.8 us)
Async XLA Ops:
  5.0 12.7 %copy-start.9 = (s32[1,16,3]{1,0,2:T(1,128)S(1)}, s32[1,16,3]{1,0,2:T(1,128)}, u32[]{:S(2)}) copy-start(s32[1,16,3]{1,0,2:T(1,128)} %param.5) | copy-start | bytes 580
  5.0 41.0 %all-to-all-start = ((bf16[32,144,128]{2,1,0:T(8,128)(2,1)}), bf16[32,144,128]{2,1,0:T(8,128)(2,1)S(1)}, u32[]{:S(2)}, u32[]{:S(2)}) async-start(bf16[32,144,128]{2,1,0:T(8,128)(2,1)} %get-tuple-element.29), calls=%async_computation | async-start | bytes 2359296 | tf_op jit(solution)/shard_map/all_to_all | solution.py:337
  16.1 19.9 %collective-permute-start.8 = (bf16[16,3,128,128]{3,2,1,0:T(8,128)(2,1)}, bf16[16,3,128,128]{3,2,1,0:T(8,128)(2,1)}, u32[]{:S(2)}, u32[]{:S(2)}) collective-permute-start(bf16[16,3,128,128]{3,2,1,0:T(8,128)(2,1)} %bitcast.4.blocks_ref), channel_id=1, source_target_pairs={{0,224},{32,0},{64,32},{96,64},{128,96},{160,128},{192,160},{224,1... | collective-permute-start | bytes 4718600 | tf_op jit(solution)/shard_map/ppermute | solution.py:345
  18.2 17.8 %collective-permute-start = (s32[3,32]{1,0:T(4,128)S(1)}, s32[3,32]{1,0:T(4,128)S(1)}, u32[]{:S(2)}, u32[]{:S(2)}) collective-permute-start(s32[3,32]{1,0:T(4,128)S(1)} %pad_add_fusion.table), channel_id=1, source_target_pairs={{0,224},{32,0},{64,32},{96,64},{128,96},{160,128},{192,160},{224,1... | collective-permute-start | bytes 1160 | tf_op jit(solution)/shard_map/ppermute | solution.py:339
  49.5 32.4 %all-to-all-start.1 = ((bf16[32,128,128]{2,1,0:T(8,128)(2,1)}), bf16[32,128,128]{2,1,0:T(8,128)(2,1)S(1)}, u32[]{:S(2)}, u32[]{:S(2)}) async-start(bf16[32,128,128]{2,1,0:T(8,128)(2,1)} %get-tuple-element.31), calls=%async_computation.1 | async-start | bytes 2097152 | tf_op jit(solution)/shard_map/all_to_all | solution.py:337
  55.9 18.7 %collective-permute-start.9 = (bf16[16,3,128,128]{3,2,1,0:T(8,128)(2,1)}, bf16[16,3,128,128]{3,2,1,0:T(8,128)(2,1)}, u32[]{:S(2)}, u32[]{:S(2)}) collective-permute-start(bf16[16,3,128,128]{3,2,1,0:T(8,128)(2,1)} %collective-permute-done.8.blocks_ref), channel_id=1, source_target_pairs={{0,224},{32,0},{64,32},{96,64},{128,96},{160,128},{192,160},{224,1... | collective-permute-start | bytes 4718600 | tf_op jit(solution)/shard_map/ppermute | solution.py:345
  56.4 19.5 %collective-permute-start.1 = (s32[3,32]{1,0:T(4,128)S(1)}, s32[3,32]{1,0:T(4,128)S(1)}, u32[]{:S(2)}, u32[]{:S(2)}) collective-permute-start(s32[3,32]{1,0:T(4,128)S(1)} %pad_add_fusion.1.table), channel_id=1, source_target_pairs={{0,224},{32,0},{64,32},{96,64},{128,96},{160,128},{192,160},{224,1... | collective-permute-start | bytes 1160 | tf_op jit(solution)/shard_map/ppermute | solution.py:339
  84.6 32.7 %all-to-all-start.2 = ((bf16[32,128,128]{2,1,0:T(8,128)(2,1)}), bf16[32,128,128]{2,1,0:T(8,128)(2,1)S(1)}, u32[]{:S(2)}, u32[]{:S(2)}) async-start(bf16[32,128,128]{2,1,0:T(8,128)(2,1)} %get-tuple-element.33), calls=%async_computation.2 | async-start | bytes 2097152 | tf_op jit(solution)/shard_map/all_to_all | solution.py:337
  91.1 18.3 %collective-permute-start.10 = (bf16[16,3,128,128]{3,2,1,0:T(8,128)(2,1)}, bf16[16,3,128,128]{3,2,1,0:T(8,128)(2,1)S(1)}, u32[]{:S(2)}, u32[]{:S(2)}) collective-permute-start(bf16[16,3,128,128]{3,2,1,0:T(8,128)(2,1)} %collective-permute-done.9.blocks_ref), channel_id=1, source_target_pairs={{0,224},{32,0},{64,32},{96,64},{128,96},{160,128},{192,160},{224,1... | collective-permute-start | bytes 4718600 | tf_op jit(solution)/shard_map/ppermute | solution.py:345
  91.2 20.7 %collective-permute-start.2 = (s32[3,32]{1,0:T(4,128)S(1)}, s32[3,32]{1,0:T(4,128)S(1)}, u32[]{:S(2)}, u32[]{:S(2)}) collective-permute-start(s32[3,32]{1,0:T(4,128)S(1)} %collective-permute-done.1.table), channel_id=1, source_target_pairs={{0,224},{32,0},{64,32},{96,64},{128,96},{160,128},{192,160},{224,1... | collective-permute-start | bytes 1160 | tf_op jit(solution)/shard_map/ppermute | solution.py:339
  109.4 1.2 copy-start
  120.0 6.6 %copy-start.1 = (bf16[16,3,128,128]{3,2,1,0:T(8,128)(2,1)S(1)}, bf16[16,3,128,128]{3,2,1,0:T(8,128)(2,1)}, u32[]{:S(2)}) copy-start(bf16[16,3,128,128]{3,2,1,0:T(8,128)(2,1)} %copy-done) | copy-start | bytes 4718596
  120.0 33.7 %all-to-all-start.3 = ((bf16[32,128,128]{2,1,0:T(8,128)(2,1)}), bf16[32,128,128]{2,1,0:T(8,128)(2,1)S(1)}, u32[]{:S(2)}, u32[]{:S(2)}) async-start(bf16[32,128,128]{2,1,0:T(8,128)(2,1)} %get-tuple-element.35), calls=%async_computation.3 | async-start | bytes 2097152 | tf_op jit(solution)/shard_map/all_to_all | solution.py:337
  126.6 18.6 %collective-permute-start.11 = (bf16[16,3,128,128]{3,2,1,0:T(8,128)(2,1)S(1)}, bf16[16,3,128,128]{3,2,1,0:T(8,128)(2,1)S(1)}, u32[]{:S(2)}, u32[]{:S(2)}) collective-permute-start(bf16[16,3,128,128]{3,2,1,0:T(8,128)(2,1)S(1)} %copy-done.1), channel_id=1, source_target_pairs={{0,224},{32,0},{64,32},{96,64},{128,96},{160,128},{192,160},{224,1... | collective-permute-start | bytes 4718600 | tf_op jit(solution)/shard_map/ppermute | solution.py:345
  127.3 24.1 %collective-permute-start.3 = (s32[3,32]{1,0:T(4,128)S(1)}, s32[3,32]{1,0:T(4,128)S(1)}, u32[]{:S(2)}, u32[]{:S(2)}) collective-permute-start(s32[3,32]{1,0:T(4,128)S(1)} %collective-permute-done.2.table), channel_id=1, source_target_pairs={{0,224},{32,0},{64,32},{96,64},{128,96},{160,128},{192,160},{224,1... | collective-permute-start | bytes 1160 | tf_op jit(solution)/shard_map/ppermute | solution.py:339
  145.2 1.2 copy-start.2
  156.5 7.6 %copy-start.3 = (bf16[16,3,128,128]{3,2,1,0:T(8,128)(2,1)S(1)}, bf16[16,3,128,128]{3,2,1,0:T(8,128)(2,1)}, u32[]{:S(2)}) copy-start(bf16[16,3,128,128]{3,2,1,0:T(8,128)(2,1)} %copy-done.2) | copy-start | bytes 4718596
  156.5 36.1 %all-to-all-start.4 = ((bf16[32,128,128]{2,1,0:T(8,128)(2,1)}), bf16[32,128,128]{2,1,0:T(8,128)(2,1)S(1)}, u32[]{:S(2)}, u32[]{:S(2)}) async-start(bf16[32,128,128]{2,1,0:T(8,128)(2,1)} %get-tuple-element.37), calls=%async_computation.4 | async-start | bytes 2097152 | tf_op jit(solution)/shard_map/all_to_all | solution.py:337
  164.0 20.8 %collective-permute-start.12 = (bf16[16,3,128,128]{3,2,1,0:T(8,128)(2,1)S(1)}, bf16[16,3,128,128]{3,2,1,0:T(8,128)(2,1)S(1)}, u32[]{:S(2)}, u32[]{:S(2)}) collective-permute-start(bf16[16,3,128,128]{3,2,1,0:T(8,128)(2,1)S(1)} %copy-done.3), channel_id=1, source_target_pairs={{0,224},{32,0},{64,32},{96,64},{128,96},{160,128},{192,160},{224,1... | collective-permute-start | bytes 4718600 | tf_op jit(solution)/shard_map/ppermute | solution.py:345
  166.9 24.1 %collective-permute-start.4 = (s32[3,32]{1,0:T(4,128)S(1)}, s32[3,32]{1,0:T(4,128)S(1)}, u32[]{:S(2)}, u32[]{:S(2)}) collective-permute-start(s32[3,32]{1,0:T(4,128)S(1)} %collective-permute-done.3.table), channel_id=1, source_target_pairs={{0,224},{32,0},{64,32},{96,64},{128,96},{160,128},{192,160},{224,1... | collective-permute-start | bytes 1160 | tf_op jit(solution)/shard_map/ppermute | solution.py:339
  184.9 1.2 copy-start.4
  195.2 8.4 %copy-start.5 = (bf16[16,3,128,128]{3,2,1,0:T(8,128)(2,1)S(1)}, bf16[16,3,128,128]{3,2,1,0:T(8,128)(2,1)}, u32[]{:S(2)}) copy-start(bf16[16,3,128,128]{3,2,1,0:T(8,128)(2,1)} %copy-done.4) | copy-start | bytes 4718596
  195.2 36.0 %all-to-all-start.5 = ((bf16[32,128,128]{2,1,0:T(8,128)(2,1)}), bf16[32,128,128]{2,1,0:T(8,128)(2,1)S(1)}, u32[]{:S(2)}, u32[]{:S(2)}) async-start(bf16[32,128,128]{2,1,0:T(8,128)(2,1)} %get-tuple-element.39), calls=%async_computation.5 | async-start | bytes 2097152 | tf_op jit(solution)/shard_map/all_to_all | solution.py:337
  203.7 20.8 %collective-permute-start.13 = (bf16[16,3,128,128]{3,2,1,0:T(8,128)(2,1)S(1)}, bf16[16,3,128,128]{3,2,1,0:T(8,128)(2,1)S(1)}, u32[]{:S(2)}, u32[]{:S(2)}) collective-permute-start(bf16[16,3,128,128]{3,2,1,0:T(8,128)(2,1)S(1)} %copy-done.5), channel_id=1, source_target_pairs={{0,224},{32,0},{64,32},{96,64},{128,96},{160,128},{192,160},{224,1... | collective-permute-start | bytes 4718600 | tf_op jit(solution)/shard_map/ppermute | solution.py:345
  206.6 24.1 %collective-permute-start.5 = (s32[3,32]{1,0:T(4,128)S(1)}, s32[3,32]{1,0:T(4,128)S(1)}, u32[]{:S(2)}, u32[]{:S(2)}) collective-permute-start(s32[3,32]{1,0:T(4,128)S(1)} %collective-permute-done.4.table), channel_id=1, source_target_pairs={{0,224},{32,0},{64,32},{96,64},{128,96},{160,128},{192,160},{224,1... | collective-permute-start | bytes 1160 | tf_op jit(solution)/shard_map/ppermute | solution.py:339
  224.5 1.2 copy-start.6
  234.0 9.4 %copy-start.7 = (bf16[16,3,128,128]{3,2,1,0:T(8,128)(2,1)S(1)}, bf16[16,3,128,128]{3,2,1,0:T(8,128)(2,1)}, u32[]{:S(2)}) copy-start(bf16[16,3,128,128]{3,2,1,0:T(8,128)(2,1)} %copy-done.6) | copy-start | bytes 4718596
  234.0 36.0 %all-to-all-start.6 = ((bf16[32,128,128]{2,1,0:T(8,128)(2,1)}), bf16[32,128,128]{2,1,0:T(8,128)(2,1)S(1)}, u32[]{:S(2)}, u32[]{:S(2)}) async-start(bf16[32,128,128]{2,1,0:T(8,128)(2,1)} %get-tuple-element.41), calls=%async_computation.6 | async-start | bytes 2097152 | tf_op jit(solution)/shard_map/all_to_all | solution.py:337
  243.3 20.5 %collective-permute-start.14 = (bf16[16,3,128,128]{3,2,1,0:T(8,128)(2,1)S(1)}, bf16[16,3,128,128]{3,2,1,0:T(8,128)(2,1)S(1)}, u32[]{:S(2)}, u32[]{:S(2)}) collective-permute-start(bf16[16,3,128,128]{3,2,1,0:T(8,128)(2,1)S(1)} %copy-done.7), channel_id=1, source_target_pairs={{0,224},{32,0},{64,32},{96,64},{128,96},{160,128},{192,160},{224,1... | collective-permute-start | bytes 4718600 | tf_op jit(solution)/shard_map/ppermute | solution.py:345
  245.9 24.1 %collective-permute-start.6 = (s32[3,32]{1,0:T(4,128)S(1)}, s32[3,32]{1,0:T(4,128)S(1)}, u32[]{:S(2)}, u32[]{:S(2)}) collective-permute-start(s32[3,32]{1,0:T(4,128)S(1)} %collective-permute-done.5.table), channel_id=1, source_target_pairs={{0,224},{32,0},{64,32},{96,64},{128,96},{160,128},{192,160},{224,1... | collective-permute-start | bytes 1160 | tf_op jit(solution)/shard_map/ppermute | solution.py:339
  263.9 1.2 copy-start.8
  272.7 35.2 %all-to-all-start.7 = ((bf16[32,128,128]{2,1,0:T(8,128)(2,1)}), bf16[32,128,128]{2,1,0:T(8,128)(2,1)S(1)}, u32[]{:S(2)}, u32[]{:S(2)}) async-start(bf16[32,128,128]{2,1,0:T(8,128)(2,1)} %get-tuple-element.43), calls=%async_computation.7 | async-start | bytes 2097152 | tf_op jit(solution)/shard_map/all_to_all | solution.py:337
  282.5 6.3 %collective-permute-start.7 = (s32[3,32]{1,0:T(4,128)S(1)}, s32[3,32]{1,0:T(4,128)S(1)}, u32[]{:S(2)}, u32[]{:S(2)}) collective-permute-start(s32[3,32]{1,0:T(4,128)S(1)} %collective-permute-done.6.table), channel_id=1, source_target_pairs={{0,224},{32,0},{64,32},{96,64},{128,96},{160,128},{192,160},{224,1... | collective-permute-start | bytes 1160 | tf_op jit(solution)/shard_map/ppermute | solution.py:339
  309.0 8.3 %collective-permute-start.15 = (bf16[1,128,128]{2,1,0:T(8,128)(2,1)S(1)}, bf16[1,128,128]{2,1,0:T(8,128)(2,1)S(1)}, u32[]{:S(2)}, u32[]{:S(2)}) collective-permute-start(bf16[1,128,128]{2,1,0:T(8,128)(2,1)S(1)} %get-tuple-element.46), channel_id=1, source_target_pairs={{0,1},{1,2},{2,3},{3,4},{4,5},{5,6},{6,7},{7,8},{8,9},{9,10},{10,1... | collective-permute-start | bytes 98312 | tf_op jit(solution)/shard_map/ppermute | solution.py:348
  313.3 7.9 %collective-permute-start.16 = (bf16[1,128,128]{2,1,0:T(8,128)(2,1)S(1)}, bf16[1,128,128]{2,1,0:T(8,128)(2,1)S(1)}, u32[]{:S(2)}, u32[]{:S(2)}) collective-permute-start(bf16[1,128,128]{2,1,0:T(8,128)(2,1)S(1)} %get-tuple-element.47), channel_id=1, source_target_pairs={{1,0},{2,1},{3,2},{4,3},{5,4},{6,5},{7,6},{8,7},{9,8},{10,9},{11,1... | collective-permute-start | bytes 98312 | tf_op jit(solution)/shard_map/ppermute | solution.py:349

commit v5 on v4

--- a/solution.py
+++ b/solution.py
@@ -343,6 +343,7 @@
             table = jnp.concatenate([table[:2], landed[None]], axis=0)
         if step < ndays - 1:
             wblk = onward(wblk)
+            wblk, local = lax.optimization_barrier((wblk, local))
             off = fetch(wblk)
     final, lowest, highest = last_sum(table, arrived, local)
     low = lax.ppermute(highest, "tile", [(i, i + 1) for i in range(peers - 1)])

time: 325 us -> 311 us (0.957)
  starting transfers between devices: 93.8 us -> 79.9 us
  waiting for transfers between devices: 154 us -> 159 us
  local copies, waits for them, and re-layouts: 6.8 us -> 2.15 us
    all_to_all x8, waiting for transfers between devices: 43.9 us -> 68.8 us  [body(): lax.all_to_all(out, 'tile', split_axis=0, concat_axis=0, tiled=True)]
    ppermute x7, waiting for transfers between devices: 93.7 us -> 73.9 us  [body(): wblk = onward(wblk)]
    all_to_all x8, starting transfers between devices: 65.6 us -> 56.2 us  [body(): lax.all_to_all(out, 'tile', split_axis=0, concat_axis=0, tiled=True)]
    ppermute x7, starting transfers between devices: 11.1 us -> 2.23 us  [body(): wblk = onward(wblk)]
    unnamed x22 -> x6, local copies, waits for them, and re-layouts: 6.52 us -> 1.88 us
    ppermute x8, starting transfers between devices: 10.8 us -> 15.3 us  [body(): table = onward(table)]
  transfers between devices with their start and end apart: 25 -> 25, of which waited for: 15 -> 16; matrix products, arithmetic and copies ran while one was open for 0% -> 0% of each run, Pallas kernels for 13% -> 13%
where the time goes in v5:
time: 311 us; the launch traced here: 309 us
  waiting for transfers between devices  159 us (51%)
  starting transfers between devices  79.9 us (26%)
  Pallas kernels  65.6 us (21%)
    ppermute x7, waiting for transfers between devices, body(): wblk = onward(wblk)  73.9 us
    all_to_all x8, waiting for transfers between devices, body(): lax.all_to_all(out, 'tile', split_axis=0, concat_axis=0, tiled=True)  68.8 us
    all_to_all x8, starting transfers between devices, body(): lax.all_to_all(out, 'tile', split_axis=0, concat_axis=0, tiled=True)  56.2 us
    pallas_call x8, Pallas kernels, keep(): pl.pallas_call(keep_body, out_shape=pltpu.VMEM((tiles, rows, points), jnp...  29.9 us
    pallas_call x7, Pallas kernels, send(): pl.pallas_call(send_body, out_shape=(pltpu.HBM((peers, rows, points), jnp...  19 us
    ppermute x8, starting transfers between devices, body(): table = onward(table)  15.3 us
    ppermute x8, waiting for transfers between devices, body(): table = onward(table)  12.8 us
    pallas_call x7, Pallas kernels, fetch(): pl.pallas_call(fetch_body, out_shape=pltpu.VMEM((tiles, nnz - 1, points,...  8.63 us
  transfers between devices with their start and end apart: 25, of which 16 were waited for; matrix products, arithmetic and copies ran while one was open for 0% of the time, Pallas kernels for 13%

profile of v5, /device:TPU:56, one launch (start us, length us, event | category | flops | bytes accessed | tf_op | source)
XLA Modules:
  0.0 309.3 jit_solution(4927112999222891016)
XLA Ops:
  0.6 0.7 copy.17
  1.3 3.7 %shard_map.50 = (bf16[32,144,128]{2,1,0:T(8,128)(2,1)}, bf16[16,128,128]{2,1,0:T(8,128)(2,1)}) custom-call(s32[3,16]{1,0:T(4,128)S(1)} %bitcast.16, bf16[16,128,128]{2,1,0:T(8,128)(2,1)} %bitcast.17, bf16[16,3,128,128]{3,2,1,0:T(8,128)(2,1)} %bitcast.4.blocks_ref), custom_call_target="tpu_custom_call" | custom-call | flops 134217728 | bytes 4194304 | tf_op jit(solution)/shard_map/pallas_call | solution.py:92
  5.0 11.0 %all-to-all-start = ((bf16[32,144,128]{2,1,0:T(8,128)(2,1)}), bf16[32,144,128]{2,1,0:T(8,128)(2,1)S(1)}, u32[]{:S(2)}, u32[]{:S(2)}) async-start(bf16[32,144,128]{2,1,0:T(8,128)(2,1)} %get-tuple-element.43), calls=%async_computation | async-start | bytes 2359296 | tf_op jit(solution)/shard_map/all_to_all | solution.py:337
  16.1 1.6 collective-permute-start.8
  18.2 1.2 collective-permute-start
  19.4 3.7 %shard_map.51.local_ref = f32[16,128,128]{2,1,0:T(8,128)S(1)} custom-call(s32[3,32]{1,0:T(4,128)S(1)} %pad_add_fusion.table, bf16[16,128,128]{2,1,0:T(8,128)(2,1)} %get-tuple-element.44.state_ref, bf16[16,3,128,128]{3,2,1,0:T(8,128)(2,1)} %bitcast.4.blocks_ref), custom_call_target="tpu_custom_call" | custom-call | flops 201326592 | bytes 4194304 | tf_op jit(solution)/shard_map/pallas_call | solution.py:192
  23.2 12.8 %collective-permute-done = s32[3,32]{1,0:T(4,128)S(1)} collective-permute-done((s32[3,32]{1,0:T(4,128)S(1)}, s32[3,32]{1,0:T(4,128)S(1)}, u32[]{:S(2)}, u32[]{:S(2)}) %collective-permute-start) | collective-permute-done | bytes 416 | tf_op jit(solution)/shard_map/ppermute | solution.py:339
  36.0 1.2 shard_map.52.off_ref
  37.2 8.9 %all-to-all-done.arrived_ref = bf16[32,144,128]{2,1,0:T(8,128)(2,1)S(1)} async-done(((bf16[32,144,128]{2,1,0:T(8,128)(2,1)}), bf16[32,144,128]{2,1,0:T(8,128)(2,1)S(1)}, u32[]{:S(2)}, u32[]{:S(2)}) %all-to-all-start) | async-done | bytes 1179680 | tf_op jit(solution)/shard_map/all_to_all | solution.py:337
  46.1 0.7 fusion
  46.8 2.7 shard_map.53
  49.5 6.5 %all-to-all-start.1 = ((bf16[32,128,128]{2,1,0:T(8,128)(2,1)}), bf16[32,128,128]{2,1,0:T(8,128)(2,1)S(1)}, u32[]{:S(2)}, u32[]{:S(2)}) async-start(bf16[32,128,128]{2,1,0:T(8,128)(2,1)} %get-tuple-element.47), calls=%async_computation.1 | async-start | bytes 2097152 | tf_op jit(solution)/shard_map/all_to_all | solution.py:337
  56.4 2.5 collective-permute-start.1
  58.8 3.7 %shard_map.54.local_ref = f32[16,128,128]{2,1,0:T(8,128)S(1)} custom-call(s32[3,32]{1,0:T(4,128)S(1)} %pad_add_fusion.1.table, bf16[16,128,128]{2,1,0:T(8,128)(2,1)} %get-tuple-element.48.state_ref, bf16[16,3,128,128]{3,2,1,0:T(8,128)(2,1)} %collective-permute-done.8.blocks_ref), custom_call_target="tpu_custom_call" | custom-call | flops 201326592 | bytes 4194304 | tf_op jit(solution)/shard_map/pallas_call | solution.py:192
  62.6 12.0 %collective-permute-done.9.blocks_ref = bf16[16,3,128,128]{3,2,1,0:T(8,128)(2,1)} collective-permute-done((bf16[16,3,128,128]{3,2,1,0:T(8,128)(2,1)}, bf16[16,3,128,128]{3,2,1,0:T(8,128)(2,1)}, u32[]{:S(2)}, u32[]{:S(2)}) %collective-permute-start.9) | collective-permute-done | bytes 1572896 | tf_op jit(solution)/shard_map/ppermute | solution.py:345
  74.6 1.2 shard_map.55.off_ref
  75.9 6.0 %all-to-all-done.1.arrived_ref = bf16[32,128,128]{2,1,0:T(8,128)(2,1)S(1)} async-done(((bf16[32,128,128]{2,1,0:T(8,128)(2,1)}), bf16[32,128,128]{2,1,0:T(8,128)(2,1)S(1)}, u32[]{:S(2)}, u32[]{:S(2)}) %all-to-all-start.1) | async-done | bytes 1048608 | tf_op jit(solution)/shard_map/all_to_all | solution.py:337
  81.9 2.7 shard_map.56
  84.6 6.4 %all-to-all-start.2 = ((bf16[32,128,128]{2,1,0:T(8,128)(2,1)}), bf16[32,128,128]{2,1,0:T(8,128)(2,1)S(1)}, u32[]{:S(2)}, u32[]{:S(2)}) async-start(bf16[32,128,128]{2,1,0:T(8,128)(2,1)} %get-tuple-element.51), calls=%async_computation.2 | async-start | bytes 2097152 | tf_op jit(solution)/shard_map/all_to_all | solution.py:337
  91.2 2.8 collective-permute-start.2
  94.0 3.7 %shard_map.57.local_ref = f32[16,128,128]{2,1,0:T(8,128)S(1)} custom-call(s32[3,32]{1,0:T(4,128)S(1)} %collective-permute-done.1.table, bf16[16,128,128]{2,1,0:T(8,128)(2,1)} %get-tuple-element.52.state_ref, bf16[16,3,128,128]{3,2,1,0:T(8,128)(2,1)} %collective-permute-done.9.blocks_ref), custom_call_target="tpu_custom_call" | custom-call | flops 201326592 | bytes 4194304 | tf_op jit(solution)/shard_map/pallas_call | solution.py:192
  97.7 11.7 %collective-permute-done.10.blocks_ref = bf16[16,3,128,128]{3,2,1,0:T(8,128)(2,1)} collective-permute-done((bf16[16,3,128,128]{3,2,1,0:T(8,128)(2,1)}, bf16[16,3,128,128]{3,2,1,0:T(8,128)(2,1)}, u32[]{:S(2)}, u32[]{:S(2)}) %collective-permute-start.10) | collective-permute-done | bytes 1572896 | tf_op jit(solution)/shard_map/ppermute | solution.py:345
  109.4 1.2 shard_map.58.off_ref
  110.7 6.6 %all-to-all-done.2.arrived_ref = bf16[32,128,128]{2,1,0:T(8,128)(2,1)S(1)} async-done(((bf16[32,128,128]{2,1,0:T(8,128)(2,1)}), bf16[32,128,128]{2,1,0:T(8,128)(2,1)S(1)}, u32[]{:S(2)}, u32[]{:S(2)}) %all-to-all-start.2) | async-done | bytes 1048608 | tf_op jit(solution)/shard_map/all_to_all | solution.py:337
  117.3 2.7 shard_map.59
  120.0 6.4 %all-to-all-start.3 = ((bf16[32,128,128]{2,1,0:T(8,128)(2,1)}), bf16[32,128,128]{2,1,0:T(8,128)(2,1)S(1)}, u32[]{:S(2)}, u32[]{:S(2)}) async-start(bf16[32,128,128]{2,1,0:T(8,128)(2,1)} %get-tuple-element.55), calls=%async_computation.3 | async-start | bytes 2097152 | tf_op jit(solution)/shard_map/all_to_all | solution.py:337
  126.5 2.3 collective-permute-start.3
  128.8 3.8 %shard_map.60.local_ref = f32[16,128,128]{2,1,0:T(8,128)S(1)} custom-call(s32[3,32]{1,0:T(4,128)S(1)} %collective-permute-done.2.table, bf16[16,128,128]{2,1,0:T(8,128)(2,1)} %get-tuple-element.56.state_ref, bf16[16,3,128,128]{3,2,1,0:T(8,128)(2,1)} %collective-permute-done.10.blocks_ref), custom_call_target="tpu_custom_call" | custom-call | flops 201326592 | bytes 4194304 | tf_op jit(solution)/shard_map/pallas_call | solution.py:192
  132.5 12.2 %collective-permute-done.11.blocks_ref = bf16[16,3,128,128]{3,2,1,0:T(8,128)(2,1)} collective-permute-done((bf16[16,3,128,128]{3,2,1,0:T(8,128)(2,1)}, bf16[16,3,128,128]{3,2,1,0:T(8,128)(2,1)}, u32[]{:S(2)}, u32[]{:S(2)}) %collective-permute-start.11) | collective-permute-done | bytes 1572896 | tf_op jit(solution)/shard_map/ppermute | solution.py:345
  144.7 1.2 shard_map.61.off_ref
  146.0 6.5 %all-to-all-done.3.arrived_ref = bf16[32,128,128]{2,1,0:T(8,128)(2,1)S(1)} async-done(((bf16[32,128,128]{2,1,0:T(8,128)(2,1)}), bf16[32,128,128]{2,1,0:T(8,128)(2,1)S(1)}, u32[]{:S(2)}, u32[]{:S(2)}) %all-to-all-start.3) | async-done | bytes 1048608 | tf_op jit(solution)/shard_map/all_to_all | solution.py:337
  152.5 2.7 shard_map.62
  155.2 6.5 %all-to-all-start.4 = ((bf16[32,128,128]{2,1,0:T(8,128)(2,1)}), bf16[32,128,128]{2,1,0:T(8,128)(2,1)S(1)}, u32[]{:S(2)}, u32[]{:S(2)}) async-start(bf16[32,128,128]{2,1,0:T(8,128)(2,1)} %get-tuple-element.59), calls=%async_computation.4 | async-start | bytes 2097152 | tf_op jit(solution)/shard_map/all_to_all | solution.py:337
  161.7 1.9 collective-permute-start.4
  163.6 3.7 %shard_map.63.local_ref = f32[16,128,128]{2,1,0:T(8,128)S(1)} custom-call(s32[3,32]{1,0:T(4,128)S(1)} %collective-permute-done.3.table, bf16[16,128,128]{2,1,0:T(8,128)(2,1)} %get-tuple-element.60.state_ref, bf16[16,3,128,128]{3,2,1,0:T(8,128)(2,1)} %collective-permute-done.11.blocks_ref), custom_call_target="tpu_custom_call" | custom-call | flops 201326592 | bytes 4194304 | tf_op jit(solution)/shard_map/pallas_call | solution.py:192
  167.3 12.6 %collective-permute-done.12.blocks_ref = bf16[16,3,128,128]{3,2,1,0:T(8,128)(2,1)} collective-permute-done((bf16[16,3,128,128]{3,2,1,0:T(8,128)(2,1)}, bf16[16,3,128,128]{3,2,1,0:T(8,128)(2,1)}, u32[]{:S(2)}, u32[]{:S(2)}) %collective-permute-start.12) | collective-permute-done | bytes 1572896 | tf_op jit(solution)/shard_map/ppermute | solution.py:345
  179.9 1.2 shard_map.64.off_ref
  181.2 6.7 %all-to-all-done.4.arrived_ref = bf16[32,128,128]{2,1,0:T(8,128)(2,1)S(1)} async-done(((bf16[32,128,128]{2,1,0:T(8,128)(2,1)}), bf16[32,128,128]{2,1,0:T(8,128)(2,1)S(1)}, u32[]{:S(2)}, u32[]{:S(2)}) %all-to-all-start.4) | async-done | bytes 1048608 | tf_op jit(solution)/shard_map/all_to_all | solution.py:337
  187.9 2.7 shard_map.65
  190.6 6.4 %all-to-all-start.5 = ((bf16[32,128,128]{2,1,0:T(8,128)(2,1)}), bf16[32,128,128]{2,1,0:T(8,128)(2,1)S(1)}, u32[]{:S(2)}, u32[]{:S(2)}) async-start(bf16[32,128,128]{2,1,0:T(8,128)(2,1)} %get-tuple-element.63), calls=%async_computation.5 | async-start | bytes 2097152 | tf_op jit(solution)/shard_map/all_to_all | solution.py:337
  197.1 1.8 collective-permute-start.5
  198.9 3.7 %shard_map.66.local_ref = f32[16,128,128]{2,1,0:T(8,128)S(1)} custom-call(s32[3,32]{1,0:T(4,128)S(1)} %collective-permute-done.4.table, bf16[16,128,128]{2,1,0:T(8,128)(2,1)} %get-tuple-element.64.state_ref, bf16[16,3,128,128]{3,2,1,0:T(8,128)(2,1)} %collective-permute-done.12.blocks_ref), custom_call_target="tpu_custom_call" | custom-call | flops 201326592 | bytes 4194304 | tf_op jit(solution)/shard_map/pallas_call | solution.py:192
  202.7 12.7 %collective-permute-done.13.blocks_ref = bf16[16,3,128,128]{3,2,1,0:T(8,128)(2,1)} collective-permute-done((bf16[16,3,128,128]{3,2,1,0:T(8,128)(2,1)}, bf16[16,3,128,128]{3,2,1,0:T(8,128)(2,1)}, u32[]{:S(2)}, u32[]{:S(2)}) %collective-permute-start.13) | collective-permute-done | bytes 1572896 | tf_op jit(solution)/shard_map/ppermute | solution.py:345
  215.3 1.2 shard_map.67.off_ref
  216.6 6.5 %all-to-all-done.5.arrived_ref = bf16[32,128,128]{2,1,0:T(8,128)(2,1)S(1)} async-done(((bf16[32,128,128]{2,1,0:T(8,128)(2,1)}), bf16[32,128,128]{2,1,0:T(8,128)(2,1)S(1)}, u32[]{:S(2)}, u32[]{:S(2)}) %all-to-all-start.5) | async-done | bytes 1048608 | tf_op jit(solution)/shard_map/all_to_all | solution.py:337
  223.0 2.7 shard_map.68
  225.7 6.4 %all-to-all-start.6 = ((bf16[32,128,128]{2,1,0:T(8,128)(2,1)}), bf16[32,128,128]{2,1,0:T(8,128)(2,1)S(1)}, u32[]{:S(2)}, u32[]{:S(2)}) async-start(bf16[32,128,128]{2,1,0:T(8,128)(2,1)} %get-tuple-element.67), calls=%async_computation.6 | async-start | bytes 2097152 | tf_op jit(solution)/shard_map/all_to_all | solution.py:337
  232.2 1.8 collective-permute-start.6
  234.1 3.7 %shard_map.69.local_ref = f32[16,128,128]{2,1,0:T(8,128)S(1)} custom-call(s32[3,32]{1,0:T(4,128)S(1)} %collective-permute-done.5.table, bf16[16,128,128]{2,1,0:T(8,128)(2,1)} %get-tuple-element.68.state_ref, bf16[16,3,128,128]{3,2,1,0:T(8,128)(2,1)} %collective-permute-done.13.blocks_ref), custom_call_target="tpu_custom_call" | custom-call | flops 201326592 | bytes 4194304 | tf_op jit(solution)/shard_map/pallas_call | solution.py:192
  237.8 12.7 %collective-permute-done.14.blocks_ref = bf16[16,3,128,128]{3,2,1,0:T(8,128)(2,1)S(1)} collective-permute-done((bf16[16,3,128,128]{3,2,1,0:T(8,128)(2,1)}, bf16[16,3,128,128]{3,2,1,0:T(8,128)(2,1)S(1)}, u32[]{:S(2)}, u32[]{:S(2)}) %collective-permute-start.14) | collective-permute-done | bytes 1572896 | tf_op jit(solution)/shard_map/ppermute | solution.py:345
  250.5 1.2 copy-done
  251.7 1.2 shard_map.70.off_ref
  252.9 5.2 %all-to-all-done.6.arrived_ref = bf16[32,128,128]{2,1,0:T(8,128)(2,1)S(1)} async-done(((bf16[32,128,128]{2,1,0:T(8,128)(2,1)}), bf16[32,128,128]{2,1,0:T(8,128)(2,1)S(1)}, u32[]{:S(2)}, u32[]{:S(2)}) %all-to-all-start.6) | async-done | bytes 1048608 | tf_op jit(solution)/shard_map/all_to_all | solution.py:337
  258.1 2.7 shard_map.71
  260.8 6.5 %all-to-all-start.7 = ((bf16[32,128,128]{2,1,0:T(8,128)(2,1)}), bf16[32,128,128]{2,1,0:T(8,128)(2,1)S(1)}, u32[]{:S(2)}, u32[]{:S(2)}) async-start(bf16[32,128,128]{2,1,0:T(8,128)(2,1)} %get-tuple-element.71), calls=%async_computation.7 | async-start | bytes 2097152 | tf_op jit(solution)/shard_map/all_to_all | solution.py:337
  267.3 0.9 collective-permute-start.7
  268.2 3.7 %shard_map.72.local_ref = f32[16,128,128]{2,1,0:T(8,128)S(1)} custom-call(s32[3,32]{1,0:T(4,128)S(1)} %collective-permute-done.6.table, bf16[16,128,128]{2,1,0:T(8,128)(2,1)} %get-tuple-element.72.state_ref, bf16[16,3,128,128]{3,2,1,0:T(8,128)(2,1)} %copy-done), custom_call_target="tpu_custom_call" | custom-call | flops 201326592 | bytes 4194304 | tf_op jit(solution)/shard_map/pallas_call | solution.py:192
  272.0 22.5 %all-to-all-done.7.arrived_ref = bf16[32,128,128]{2,1,0:T(8,128)(2,1)S(1)} async-done(((bf16[32,128,128]{2,1,0:T(8,128)(2,1)}), bf16[32,128,128]{2,1,0:T(8,128)(2,1)S(1)}, u32[]{:S(2)}, u32[]{:S(2)}) %all-to-all-start.7) | async-done | bytes 1048608 | tf_op jit(solution)/shard_map/all_to_all | solution.py:337
  294.4 1.0 shard_map.73
  295.4 4.3 %collective-permute-start.15 = (bf16[1,128,128]{2,1,0:T(8,128)(2,1)S(1)}, bf16[1,128,128]{2,1,0:T(8,128)(2,1)S(1)}, u32[]{:S(2)}, u32[]{:S(2)}) collective-permute-start(bf16[1,128,128]{2,1,0:T(8,128)(2,1)S(1)} %get-tuple-element.74), channel_id=1, source_target_pairs={{0,1},{1,2},{2,3},{3,4},{4,5},{5,6},{6,7},{7,8},{8,9},{9,10},{10,1... | collective-permute-start | bytes 98312 | tf_op jit(solution)/shard_map/ppermute | solution.py:349
  299.8 1.9 collective-permute-start.16
  301.8 2.0 shard_map.74
  303.8 3.9 %collective-permute-done.16.high_ref = bf16[1,128,128]{2,1,0:T(8,128)(2,1)S(1)} collective-permute-done((bf16[1,128,128]{2,1,0:T(8,128)(2,1)S(1)}, bf16[1,128,128]{2,1,0:T(8,128)(2,1)S(1)}, u32[]{:S(2)}, u32[]{:S(2)}) %collective-permute-start.16) | collective-permute-done | bytes 32800 | tf_op jit(solution)/shard_map/ppermute | solution.py:350
  307.7 1.4 shard_map.75
  (32 shorter events, 1.1 us)
Async XLA Ops:
  5.0 12.7 %copy-start.1 = (s32[1,16,3]{1,0,2:T(1,128)S(1)}, s32[1,16,3]{1,0,2:T(1,128)}, u32[]{:S(2)}) copy-start(s32[1,16,3]{1,0,2:T(1,128)} %param.5) | copy-start | bytes 580
  5.0 41.0 %all-to-all-start = ((bf16[32,144,128]{2,1,0:T(8,128)(2,1)}), bf16[32,144,128]{2,1,0:T(8,128)(2,1)S(1)}, u32[]{:S(2)}, u32[]{:S(2)}) async-start(bf16[32,144,128]{2,1,0:T(8,128)(2,1)} %get-tuple-element.43), calls=%async_computation | async-start | bytes 2359296 | tf_op jit(solution)/shard_map/all_to_all | solution.py:337
  16.1 19.9 %collective-permute-start.8 = (bf16[16,3,128,128]{3,2,1,0:T(8,128)(2,1)}, bf16[16,3,128,128]{3,2,1,0:T(8,128)(2,1)}, u32[]{:S(2)}, u32[]{:S(2)}) collective-permute-start(bf16[16,3,128,128]{3,2,1,0:T(8,128)(2,1)} %bitcast.4.blocks_ref), channel_id=1, source_target_pairs={{0,224},{32,0},{64,32},{96,64},{128,96},{160,128},{192,160},{224,1... | collective-permute-start | bytes 4718600 | tf_op jit(solution)/shard_map/ppermute | solution.py:345
  18.2 17.8 %collective-permute-start = (s32[3,32]{1,0:T(4,128)S(1)}, s32[3,32]{1,0:T(4,128)S(1)}, u32[]{:S(2)}, u32[]{:S(2)}) collective-permute-start(s32[3,32]{1,0:T(4,128)S(1)} %pad_add_fusion.table), channel_id=1, source_target_pairs={{0,224},{32,0},{64,32},{96,64},{128,96},{160,128},{192,160},{224,1... | collective-permute-start | bytes 1160 | tf_op jit(solution)/shard_map/ppermute | solution.py:339
  49.5 32.4 %all-to-all-start.1 = ((bf16[32,128,128]{2,1,0:T(8,128)(2,1)}), bf16[32,128,128]{2,1,0:T(8,128)(2,1)S(1)}, u32[]{:S(2)}, u32[]{:S(2)}) async-start(bf16[32,128,128]{2,1,0:T(8,128)(2,1)} %get-tuple-element.47), calls=%async_computation.1 | async-start | bytes 2097152 | tf_op jit(solution)/shard_map/all_to_all | solution.py:337
  55.9 18.7 %collective-permute-start.9 = (bf16[16,3,128,128]{3,2,1,0:T(8,128)(2,1)}, bf16[16,3,128,128]{3,2,1,0:T(8,128)(2,1)}, u32[]{:S(2)}, u32[]{:S(2)}) collective-permute-start(bf16[16,3,128,128]{3,2,1,0:T(8,128)(2,1)} %collective-permute-done.8.blocks_ref), channel_id=1, source_target_pairs={{0,224},{32,0},{64,32},{96,64},{128,96},{160,128},{192,160},{224,1... | collective-permute-start | bytes 4718600 | tf_op jit(solution)/shard_map/ppermute | solution.py:345
  56.4 19.5 %collective-permute-start.1 = (s32[3,32]{1,0:T(4,128)S(1)}, s32[3,32]{1,0:T(4,128)S(1)}, u32[]{:S(2)}, u32[]{:S(2)}) collective-permute-start(s32[3,32]{1,0:T(4,128)S(1)} %pad_add_fusion.1.table), channel_id=1, source_target_pairs={{0,224},{32,0},{64,32},{96,64},{128,96},{160,128},{192,160},{224,1... | collective-permute-start | bytes 1160 | tf_op jit(solution)/shard_map/ppermute | solution.py:339
  84.6 32.7 %all-to-all-start.2 = ((bf16[32,128,128]{2,1,0:T(8,128)(2,1)}), bf16[32,128,128]{2,1,0:T(8,128)(2,1)S(1)}, u32[]{:S(2)}, u32[]{:S(2)}) async-start(bf16[32,128,128]{2,1,0:T(8,128)(2,1)} %get-tuple-element.51), calls=%async_computation.2 | async-start | bytes 2097152 | tf_op jit(solution)/shard_map/all_to_all | solution.py:337
  91.1 18.3 %collective-permute-start.10 = (bf16[16,3,128,128]{3,2,1,0:T(8,128)(2,1)}, bf16[16,3,128,128]{3,2,1,0:T(8,128)(2,1)}, u32[]{:S(2)}, u32[]{:S(2)}) collective-permute-start(bf16[16,3,128,128]{3,2,1,0:T(8,128)(2,1)} %collective-permute-done.9.blocks_ref), channel_id=1, source_target_pairs={{0,224},{32,0},{64,32},{96,64},{128,96},{160,128},{192,160},{224,1... | collective-permute-start | bytes 4718600 | tf_op jit(solution)/shard_map/ppermute | solution.py:345
  91.2 19.5 %collective-permute-start.2 = (s32[3,32]{1,0:T(4,128)S(1)}, s32[3,32]{1,0:T(4,128)S(1)}, u32[]{:S(2)}, u32[]{:S(2)}) collective-permute-start(s32[3,32]{1,0:T(4,128)S(1)} %collective-permute-done.1.table), channel_id=1, source_target_pairs={{0,224},{32,0},{64,32},{96,64},{128,96},{160,128},{192,160},{224,1... | collective-permute-start | bytes 1160 | tf_op jit(solution)/shard_map/ppermute | solution.py:339
  120.0 32.4 %all-to-all-start.3 = ((bf16[32,128,128]{2,1,0:T(8,128)(2,1)}), bf16[32,128,128]{2,1,0:T(8,128)(2,1)S(1)}, u32[]{:S(2)}, u32[]{:S(2)}) async-start(bf16[32,128,128]{2,1,0:T(8,128)(2,1)} %get-tuple-element.55), calls=%async_computation.3 | async-start | bytes 2097152 | tf_op jit(solution)/shard_map/all_to_all | solution.py:337
  126.5 18.3 %collective-permute-start.11 = (bf16[16,3,128,128]{3,2,1,0:T(8,128)(2,1)}, bf16[16,3,128,128]{3,2,1,0:T(8,128)(2,1)}, u32[]{:S(2)}, u32[]{:S(2)}) collective-permute-start(bf16[16,3,128,128]{3,2,1,0:T(8,128)(2,1)} %collective-permute-done.10.blocks_ref), channel_id=1, source_target_pairs={{0,224},{32,0},{64,32},{96,64},{128,96},{160,128},{192,160},{224,1... | collective-permute-start | bytes 4718600 | tf_op jit(solution)/shard_map/ppermute | solution.py:345
  126.5 19.5 %collective-permute-start.3 = (s32[3,32]{1,0:T(4,128)S(1)}, s32[3,32]{1,0:T(4,128)S(1)}, u32[]{:S(2)}, u32[]{:S(2)}) collective-permute-start(s32[3,32]{1,0:T(4,128)S(1)} %collective-permute-done.2.table), channel_id=1, source_target_pairs={{0,224},{32,0},{64,32},{96,64},{128,96},{160,128},{192,160},{224,1... | collective-permute-start | bytes 1160 | tf_op jit(solution)/shard_map/ppermute | solution.py:339
  155.2 32.7 %all-to-all-start.4 = ((bf16[32,128,128]{2,1,0:T(8,128)(2,1)}), bf16[32,128,128]{2,1,0:T(8,128)(2,1)S(1)}, u32[]{:S(2)}, u32[]{:S(2)}) async-start(bf16[32,128,128]{2,1,0:T(8,128)(2,1)} %get-tuple-element.59), calls=%async_computation.4 | async-start | bytes 2097152 | tf_op jit(solution)/shard_map/all_to_all | solution.py:337
  161.7 18.3 %collective-permute-start.12 = (bf16[16,3,128,128]{3,2,1,0:T(8,128)(2,1)}, bf16[16,3,128,128]{3,2,1,0:T(8,128)(2,1)}, u32[]{:S(2)}, u32[]{:S(2)}) collective-permute-start(bf16[16,3,128,128]{3,2,1,0:T(8,128)(2,1)} %collective-permute-done.11.blocks_ref), channel_id=1, source_target_pairs={{0,224},{32,0},{64,32},{96,64},{128,96},{160,128},{192,160},{224,1... | collective-permute-start | bytes 4718600 | tf_op jit(solution)/shard_map/ppermute | solution.py:345
  161.7 19.5 %collective-permute-start.4 = (s32[3,32]{1,0:T(4,128)S(1)}, s32[3,32]{1,0:T(4,128)S(1)}, u32[]{:S(2)}, u32[]{:S(2)}) collective-permute-start(s32[3,32]{1,0:T(4,128)S(1)} %collective-permute-done.3.table), channel_id=1, source_target_pairs={{0,224},{32,0},{64,32},{96,64},{128,96},{160,128},{192,160},{224,1... | collective-permute-start | bytes 1160 | tf_op jit(solution)/shard_map/ppermute | solution.py:339
  190.6 32.5 %all-to-all-start.5 = ((bf16[32,128,128]{2,1,0:T(8,128)(2,1)}), bf16[32,128,128]{2,1,0:T(8,128)(2,1)S(1)}, u32[]{:S(2)}, u32[]{:S(2)}) async-start(bf16[32,128,128]{2,1,0:T(8,128)(2,1)} %get-tuple-element.63), calls=%async_computation.5 | async-start | bytes 2097152 | tf_op jit(solution)/shard_map/all_to_all | solution.py:337
  197.0 18.3 %collective-permute-start.13 = (bf16[16,3,128,128]{3,2,1,0:T(8,128)(2,1)}, bf16[16,3,128,128]{3,2,1,0:T(8,128)(2,1)}, u32[]{:S(2)}, u32[]{:S(2)}) collective-permute-start(bf16[16,3,128,128]{3,2,1,0:T(8,128)(2,1)} %collective-permute-done.12.blocks_ref), channel_id=1, source_target_pairs={{0,224},{32,0},{64,32},{96,64},{128,96},{160,128},{192,160},{224,1... | collective-permute-start | bytes 4718600 | tf_op jit(solution)/shard_map/ppermute | solution.py:345
  197.1 19.5 %collective-permute-start.5 = (s32[3,32]{1,0:T(4,128)S(1)}, s32[3,32]{1,0:T(4,128)S(1)}, u32[]{:S(2)}, u32[]{:S(2)}) collective-permute-start(s32[3,32]{1,0:T(4,128)S(1)} %collective-permute-done.4.table), channel_id=1, source_target_pairs={{0,224},{32,0},{64,32},{96,64},{128,96},{160,128},{192,160},{224,1... | collective-permute-start | bytes 1160 | tf_op jit(solution)/shard_map/ppermute | solution.py:339
  225.7 32.4 %all-to-all-start.6 = ((bf16[32,128,128]{2,1,0:T(8,128)(2,1)}), bf16[32,128,128]{2,1,0:T(8,128)(2,1)S(1)}, u32[]{:S(2)}, u32[]{:S(2)}) async-start(bf16[32,128,128]{2,1,0:T(8,128)(2,1)} %get-tuple-element.67), calls=%async_computation.6 | async-start | bytes 2097152 | tf_op jit(solution)/shard_map/all_to_all | solution.py:337
  232.2 18.3 %collective-permute-start.14 = (bf16[16,3,128,128]{3,2,1,0:T(8,128)(2,1)}, bf16[16,3,128,128]{3,2,1,0:T(8,128)(2,1)S(1)}, u32[]{:S(2)}, u32[]{:S(2)}) collective-permute-start(bf16[16,3,128,128]{3,2,1,0:T(8,128)(2,1)} %collective-permute-done.13.blocks_ref), channel_id=1, source_target_pairs={{0,224},{32,0},{64,32},{96,64},{128,96},{160,128},{192,160},{224,1... | collective-permute-start | bytes 4718600 | tf_op jit(solution)/shard_map/ppermute | solution.py:345
  232.2 20.7 %collective-permute-start.6 = (s32[3,32]{1,0:T(4,128)S(1)}, s32[3,32]{1,0:T(4,128)S(1)}, u32[]{:S(2)}, u32[]{:S(2)}) collective-permute-start(s32[3,32]{1,0:T(4,128)S(1)} %collective-permute-done.5.table), channel_id=1, source_target_pairs={{0,224},{32,0},{64,32},{96,64},{128,96},{160,128},{192,160},{224,1... | collective-permute-start | bytes 1160 | tf_op jit(solution)/shard_map/ppermute | solution.py:339
  250.5 1.2 copy-start
  260.8 33.6 %all-to-all-start.7 = ((bf16[32,128,128]{2,1,0:T(8,128)(2,1)}), bf16[32,128,128]{2,1,0:T(8,128)(2,1)S(1)}, u32[]{:S(2)}, u32[]{:S(2)}) async-start(bf16[32,128,128]{2,1,0:T(8,128)(2,1)} %get-tuple-element.71), calls=%async_computation.7 | async-start | bytes 2097152 | tf_op jit(solution)/shard_map/all_to_all | solution.py:337
  267.3 4.7 %collective-permute-start.7 = (s32[3,32]{1,0:T(4,128)S(1)}, s32[3,32]{1,0:T(4,128)S(1)}, u32[]{:S(2)}, u32[]{:S(2)}) collective-permute-start(s32[3,32]{1,0:T(4,128)S(1)} %collective-permute-done.6.table), channel_id=1, source_target_pairs={{0,224},{32,0},{64,32},{96,64},{128,96},{160,128},{192,160},{224,1... | collective-permute-start | bytes 1160 | tf_op jit(solution)/shard_map/ppermute | solution.py:339
  295.4 8.3 %collective-permute-start.15 = (bf16[1,128,128]{2,1,0:T(8,128)(2,1)S(1)}, bf16[1,128,128]{2,1,0:T(8,128)(2,1)S(1)}, u32[]{:S(2)}, u32[]{:S(2)}) collective-permute-start(bf16[1,128,128]{2,1,0:T(8,128)(2,1)S(1)} %get-tuple-element.74), channel_id=1, source_target_pairs={{0,1},{1,2},{2,3},{3,4},{4,5},{5,6},{6,7},{7,8},{8,9},{9,10},{10,1... | collective-permute-start | bytes 98312 | tf_op jit(solution)/shard_map/ppermute | solution.py:349
  299.8 7.9 %collective-permute-start.16 = (bf16[1,128,128]{2,1,0:T(8,128)(2,1)S(1)}, bf16[1,128,128]{2,1,0:T(8,128)(2,1)S(1)}, u32[]{:S(2)}, u32[]{:S(2)}) collective-permute-start(bf16[1,128,128]{2,1,0:T(8,128)(2,1)S(1)} %get-tuple-element.75), channel_id=1, source_target_pairs={{1,0},{2,1},{3,2},{4,3},{5,4},{6,5},{7,6},{8,7},{9,8},{10,9},{11,1... | collective-permute-start | bytes 98312 | tf_op jit(solution)/shard_map/ppermute | solution.py:350

commit v6 on v5

--- a/solution.py
+++ b/solution.py
@@ -56,7 +56,7 @@
 def first_body(
     dest, seeds_ref, blocks_ref, out_ref, state_ref, seeds_scr, off_scr, stage, state_scr, lists, sems, out_sems, in_sems
 ):
-    nnz, tiles = dest.shape
+    nnz, _, tiles = dest.shape
     each = nnz - 1
     rows = state_scr.shape[1]
     parts = [pl.ds(t, PART) for t in range(0, tiles, PART)]
@@ -67,7 +67,7 @@
     for t in range(tiles):
         if t % PART == 0:
             seeding[t // PART].wait()
-        state_scr[t] = jnp.transpose(seeds_scr[t].astype(jnp.float32)).astype(jnp.bfloat16)
+        state_scr[t] = jnp.transpose(seeds_scr[t])
     store = pltpu.make_async_copy(state_scr, state_ref, sems.at[1])
     store.start()
     for p in range(stage.shape[0]):
@@ -75,7 +75,7 @@
         lists[1, p] = tiles
     for t in range(tiles):
         for k in range(1, nnz):
-            to = dest[k, t]
+            to = dest[k, 0, t]
             peer = lax.div(to, tiles)
             lists[0, peer] = t * each + k - 1
             lists[1, peer] = to - peer * tiles
@@ -111,26 +111,49 @@
         cost_estimate=pl.CostEstimate(
             flops=2 * peers * points * points * rows, bytes_accessed=4 << 20, transcendentals=0
         ),
-    )(dest, placed(seeds, pltpu.HBM), placed(blocks, pltpu.HBM))
-
-
-def fetch_body(blocks_ref, off_ref, sem):
-    load = off_copy(blocks_ref, off_ref, sem)
+    )(placed(dest, pltpu.HBM), placed(seeds, pltpu.HBM), placed(blocks, pltpu.HBM))
+
+
+def fetch_body(blocks_ref, table_ref, off_ref, read_ref, sems):
+    loads = [off_copy(blocks_ref, off_ref, sems.at[0]), pltpu.make_async_copy(table_ref, read_ref, sems.at[1])]
+    for load in loads:
+        load.start()
+    for load in loads:
+        load.wait()
+
+
+def fetch(blocks, table):
+    tiles, nnz, points = blocks.shape[:3]
+    return pl.pallas_call(
+        fetch_body,
+        out_shape=(
+            pltpu.VMEM((tiles, nnz - 1, points, points), jnp.bfloat16),
+            pltpu.SMEM(table.shape, jnp.int32),
+        ),
+        in_specs=[HBM, HBM],
+        out_specs=(VMEM, SMEM),
+        scratch_shapes=[pltpu.SemaphoreType.DMA((2,))],
+        compiler_params=SMALL,
+        cost_estimate=pl.CostEstimate(flops=0, bytes_accessed=2 << 20, transcendentals=0),
+    )(placed(blocks, pltpu.HBM), placed(table, pltpu.HBM))
+
+
+def hold_body(table_ref, read_ref, sem):
+    load = pltpu.make_async_copy(table_ref, read_ref, sem)
     load.start()
     load.wait()
 
 
-def fetch(blocks):
-    tiles, nnz, points = blocks.shape[:3]
-    return pl.pallas_call(
-        fetch_body,
-        out_shape=pltpu.VMEM((tiles, nnz - 1, points, points), jnp.bfloat16),
+def hold(table):
+    return pl.pallas_call(
+        hold_body,
+        out_shape=pltpu.SMEM(table.shape, jnp.int32),
         in_specs=[HBM],
-        out_specs=VMEM,
+        out_specs=SMEM,
         scratch_shapes=[pltpu.SemaphoreType.DMA],
         compiler_params=SMALL,
-        cost_estimate=pl.CostEstimate(flops=0, bytes_accessed=2 << 20, transcendentals=0),
-    )(placed(blocks, pltpu.HBM))
+        cost_estimate=pl.CostEstimate(flops=0, bytes_accessed=1 << 10, transcendentals=0),
+    )(placed(table, pltpu.HBM))
 
 
 def send_body(
@@ -148,7 +171,7 @@
 placed = pltpu.with_memory_space_constraint
 
 
-def send(table, arrived, local, off):
+def send(table, arrived, local, off, ready):
     peers = arrived.shape[0]
     tiles, rows, points = local.shape
     return pl.pallas_call(
@@ -170,7 +193,7 @@
         cost_estimate=pl.CostEstimate(
             flops=2 * peers * points * points * rows, bytes_accessed=4 << 20, transcendentals=0
         ),
-    )(table, placed(arrived, pltpu.VMEM), placed(local, pltpu.VMEM), placed(off, pltpu.VMEM))
+    )(placed(table, pltpu.SMEM) if ready else table, placed(arrived, pltpu.VMEM), placed(local, pltpu.VMEM), placed(off, pltpu.VMEM))
 
 
 def keep_body(table, state_ref, blocks_ref, local_ref, total, blocks_scr, sem):
@@ -230,7 +253,7 @@
             pltpu.VMEM((tiles + 1, rows, points), jnp.float32),
         ],
         compiler_params=SMALL,
-    )(before, placed(arrived, pltpu.VMEM), placed(local, pltpu.VMEM))
+    )(placed(before, pltpu.SMEM), placed(arrived, pltpu.VMEM), placed(local, pltpu.VMEM))
 
 
 def stretch_tile(ndays, here, dy):
@@ -261,7 +284,7 @@
         ftle_ref[:, at], minor_ref[:, at] = stretch_tile(ndays, here, dy)
 
 
-def edge_body(ndays, place, final_ref, low_ref, high_ref, ftle_in, minor_in, ftle_ref, minor_ref, ftle_scr, minor_scr, sems):
+def edge_body(ndays, final_ref, low_ref, high_ref, ftle_in, minor_in, ftle_ref, minor_ref, ftle_scr, minor_scr, sems):
     tiles, rows, points = final_ref.shape
     copies = []
     for i, t in enumerate((0, tiles - 1)):
@@ -269,7 +292,8 @@
         below = (final_ref[t - 1] if t > 0 else low_ref[0]).astype(jnp.float32)
         above = (final_ref[t + 1] if t < tiles - 1 else high_ref[0]).astype(jnp.float32)
         one_sided = above - here if t == 0 else here - below
-        dy = jnp.where(place[i] == 1, one_sided, (above - below) * 0.5)
+        at_end = lax.axis_index("tile") == (0 if t == 0 else lax.axis_size("tile") - 1)
+        dy = jnp.where(at_end, one_sided, (above - below) * 0.5)
         ftle_scr[i], minor_scr[i] = stretch_tile(ndays, here, dy)
         at = pl.ds(t * points, points)
         for n, (scr, ref) in enumerate(((ftle_scr, ftle_ref), (minor_scr, minor_ref))):
@@ -293,19 +317,19 @@
     )(final)
 
 
-def stretch_edges(place, final, low, high, inner, ndays):
+def stretch_edges(final, low, high, inner, ndays):
     tiles, rows, points = final.shape
     shape = jax.ShapeDtypeStruct((rows // 2, tiles * points), jnp.float32)
     scr = pltpu.VMEM((2, rows // 2, points), jnp.float32)
     return pl.pallas_call(
         functools.partial(edge_body, float(ndays)),
         out_shape=(shape, shape),
-        in_specs=[SMEM, VMEM, VMEM, VMEM, HBM, HBM],
+        in_specs=[VMEM, VMEM, VMEM, HBM, HBM],
         out_specs=(HBM, HBM),
         scratch_shapes=[scr, scr, pltpu.SemaphoreType.DMA((4,))],
-        input_output_aliases={4: 0, 5: 1},
-        compiler_params=SMALL,
-    )(place, final, low, high, *inner)
+        input_output_aliases={3: 0, 4: 1},
+        compiler_params=SMALL,
+    )(final, low, high, *inner)
 
 
 def own_rows(dest, me, tiles, peers, nnz):
@@ -328,15 +352,15 @@
 
     for step in range(ndays):
         if step == 0:
-            out, state = send_first(dest_tiles.transpose(2, 0, 1).reshape(nnz, tiles), seeds, wblk, peers)
+            out, state = send_first(dest_tiles.transpose(2, 0, 1), seeds, wblk, peers)
             dest, state = lax.optimization_barrier((dest_tiles[0], state))
             rows = own_rows(dest, me, tiles, peers, nnz)
             table = jnp.stack([*rows, jnp.zeros_like(rows[0])])
         else:
-            out, state = send(table, arrived, local, off)
+            out, state = send(table if step == 1 else quick, arrived, local, off, step > 1)
         arrived = lax.all_to_all(out, "tile", split_axis=0, concat_axis=0, tiled=True)
         local = keep(table, state, wblk)
-        table = onward(table)
+        given = table = onward(table)
         if step == 0:
             own = lax.broadcasted_iota(jnp.int32, (peers,), 0) == me
             landed = jnp.where(own, tiles, arrived[:, width, 0].astype(jnp.int32))
@@ -344,13 +368,12 @@
         if step < ndays - 1:
             wblk = onward(wblk)
             wblk, local = lax.optimization_barrier((wblk, local))
-            off = fetch(wblk)
-    final, lowest, highest = last_sum(table, arrived, local)
+            off, quick = fetch(wblk, table if step else given)
+    final, lowest, highest = last_sum(hold(table), arrived, local)
     low = lax.ppermute(highest, "tile", [(i, i + 1) for i in range(peers - 1)])
     high = lax.ppermute(lowest, "tile", [(i + 1, i) for i in range(peers - 1)])
-    place = jnp.stack([me == 0, me == peers - 1]).astype(jnp.int32)
     inner = stretch_inner(final, ndays)
-    ftle, minor = stretch_edges(place, final, low, high, inner, ndays)
+    ftle, minor = stretch_edges(final, low, high, inner, ndays)
     return ftle[None], minor[None]
 
 

time: 311 us -> 308 us (level)
  waiting for transfers between devices: 159 us -> 155 us
  local copies, waits for them, and re-layouts: 2.15 us -> 6.11 us
  Pallas kernels: 65.6 us -> 61.9 us
    all_to_all x8, waiting for transfers between devices: 68.8 us -> 62.6 us  [body(): lax.all_to_all(out, 'tile', split_axis=0, concat_axis=0, tiled=True)]
    unnamed x6 -> x33, local copies, waits for them, and re-layouts: 1.88 us -> 5.83 us
    pallas_call x7, Pallas kernels: 19 us -> 15.4 us  [send(): pl.pallas_call(send_body, out_shape=(pltpu.HBM((peers, rows, points), jnp...]
    pallas_call x7 -> x8, Pallas kernels: 8.63 us -> 9.44 us  [the longest x7 8.75 us: fetch(): pl.pallas_call(fetch_body, out_shape=(pltpu.VMEM((tiles, nnz - 1, points,...]
  transfers between devices with their start and end apart: 25 -> 25, of which waited for: 16 -> 17; matrix products, arithmetic and copies ran while one was open for 0% -> 0% of each run, Pallas kernels for 13% -> 14%
where the time goes in v6:
time: 308 us; the launch traced here: 306 us
  waiting for transfers between devices  155 us (50%)
  starting transfers between devices  81.1 us (26%)
  Pallas kernels  61.9 us (20%)
  local copies, waits for them, and re-layouts  6.11 us (2%)
    ppermute x7, waiting for transfers between devices, body(): wblk = onward(wblk)  74.1 us
    all_to_all x8, waiting for transfers between devices, body(): lax.all_to_all(out, 'tile', split_axis=0, concat_axis=0, tiled=True)  62.6 us
    all_to_all x8, starting transfers between devices, body(): lax.all_to_all(out, 'tile', split_axis=0, concat_axis=0, tiled=True)  56.2 us
    pallas_call x8, Pallas kernels, keep(): pl.pallas_call(keep_body, out_shape=pltpu.VMEM((tiles, rows, points), jnp...  29.9 us
    pallas_call x7, Pallas kernels, send(): pl.pallas_call(send_body, out_shape=(pltpu.HBM((peers, rows, points), jnp...  15.4 us
    ppermute x8, starting transfers between devices, body(): given = table = onward(table)  15.2 us
    ppermute x8, waiting for transfers between devices, body(): given = table = onward(table)  14.1 us
    pallas_call x7, Pallas kernels, fetch(): pl.pallas_call(fetch_body, out_shape=(pltpu.VMEM((tiles, nnz - 1, points,...  8.75 us
  transfers between devices with their start and end apart: 25, of which 17 were waited for; matrix products, arithmetic and copies ran while one was open for 0% of the time, Pallas kernels for 14%

profile of v6, /device:TPU:56, one launch (start us, length us, event | category | flops | bytes accessed | tf_op | source)
XLA Modules:
  0.0 305.9 jit_solution(11771568072109390439)
XLA Ops:
  0.6 3.8 %shard_map.50 = (bf16[32,144,128]{2,1,0:T(8,128)(2,1)}, bf16[16,128,128]{2,1,0:T(8,128)(2,1)}) custom-call(s32[3,1,16]{2,1,0:T(1,128)} %bitcast.14, bf16[16,128,128]{2,1,0:T(8,128)(2,1)} %bitcast.13, bf16[16,3,128,128]{3,2,1,0:T(8,128)(2,1)} %bitcast.2.blocks_ref), custom_call_target="tpu_custom_call" | custom-call | flops 134217728 | bytes 4194304 | tf_op jit(solution)/shard_map/pallas_call | solution.py:92
  4.5 11.0 %all-to-all-start = ((bf16[32,144,128]{2,1,0:T(8,128)(2,1)}), bf16[32,144,128]{2,1,0:T(8,128)(2,1)S(1)}, u32[]{:S(2)}, u32[]{:S(2)}) async-start(bf16[32,144,128]{2,1,0:T(8,128)(2,1)} %get-tuple-element.56), calls=%async_computation | async-start | bytes 2359296 | tf_op jit(solution)/shard_map/all_to_all | solution.py:361
  15.5 1.6 collective-permute-start.8
  17.6 1.2 collective-permute-start
  18.9 3.7 %shard_map.52.local_ref = f32[16,128,128]{2,1,0:T(8,128)S(1)} custom-call(s32[3,32]{1,0:T(4,128)S(1)} %pad_add_fusion.table, bf16[16,128,128]{2,1,0:T(8,128)(2,1)} %get-tuple-element.57.state_ref, bf16[16,3,128,128]{3,2,1,0:T(8,128)(2,1)} %bitcast.2.blocks_ref), custom_call_target="tpu_custom_call" | custom-call | flops 201326592 | bytes 4194304 | tf_op jit(solution)/shard_map/pallas_call | solution.py:215
  22.6 12.8 %collective-permute-done.table_ref = s32[3,32]{1,0:T(4,128)S(1)} collective-permute-done((s32[3,32]{1,0:T(4,128)S(1)}, s32[3,32]{1,0:T(4,128)S(1)}, u32[]{:S(2)}, u32[]{:S(2)}) %collective-permute-start) | collective-permute-done | bytes 416 | tf_op jit(solution)/shard_map/ppermute | solution.py:363
  36.0 1.2 shard_map.53
  37.2 8.3 %all-to-all-done.arrived_ref = bf16[32,144,128]{2,1,0:T(8,128)(2,1)S(1)} async-done(((bf16[32,144,128]{2,1,0:T(8,128)(2,1)}), bf16[32,144,128]{2,1,0:T(8,128)(2,1)S(1)}, u32[]{:S(2)}, u32[]{:S(2)}) %all-to-all-start) | async-done | bytes 1179680 | tf_op jit(solution)/shard_map/all_to_all | solution.py:361
  46.2 2.7 shard_map.54
  48.9 6.4 %all-to-all-start.1 = ((bf16[32,128,128]{2,1,0:T(8,128)(2,1)}), bf16[32,128,128]{2,1,0:T(8,128)(2,1)S(1)}, u32[]{:S(2)}, u32[]{:S(2)}) async-start(bf16[32,128,128]{2,1,0:T(8,128)(2,1)} %get-tuple-element.64), calls=%async_computation.1 | async-start | bytes 2097152 | tf_op jit(solution)/shard_map/all_to_all | solution.py:361
  55.8 2.5 collective-permute-start.1
  58.2 3.7 %shard_map.55.local_ref = f32[16,128,128]{2,1,0:T(8,128)S(1)} custom-call(s32[3,32]{1,0:T(4,128)S(1)} %pad_add_fusion.1.table, bf16[16,128,128]{2,1,0:T(8,128)(2,1)} %get-tuple-element.61.state_ref, bf16[16,3,128,128]{3,2,1,0:T(8,128)(2,1)} %collective-permute-done.8.blocks_ref), custom_call_target="tpu_custom_call" | custom-call | flops 201326592 | bytes 4194304 | tf_op jit(solution)/shard_map/pallas_call | solution.py:215
  62.0 12.0 %collective-permute-done.9.blocks_ref = bf16[16,3,128,128]{3,2,1,0:T(8,128)(2,1)} collective-permute-done((bf16[16,3,128,128]{3,2,1,0:T(8,128)(2,1)}, bf16[16,3,128,128]{3,2,1,0:T(8,128)(2,1)}, u32[]{:S(2)}, u32[]{:S(2)}) %collective-permute-start.9) | collective-permute-done | bytes 1572896 | tf_op jit(solution)/shard_map/ppermute | solution.py:369
  74.6 1.2 shard_map.56
  75.9 5.5 %all-to-all-done.1.arrived_ref = bf16[32,128,128]{2,1,0:T(8,128)(2,1)S(1)} async-done(((bf16[32,128,128]{2,1,0:T(8,128)(2,1)}), bf16[32,128,128]{2,1,0:T(8,128)(2,1)S(1)}, u32[]{:S(2)}, u32[]{:S(2)}) %all-to-all-start.1) | async-done | bytes 1048608 | tf_op jit(solution)/shard_map/all_to_all | solution.py:361
  81.3 2.1 shard_map.57
  83.5 6.4 %all-to-all-start.2 = ((bf16[32,128,128]{2,1,0:T(8,128)(2,1)}), bf16[32,128,128]{2,1,0:T(8,128)(2,1)S(1)}, u32[]{:S(2)}, u32[]{:S(2)}) async-start(bf16[32,128,128]{2,1,0:T(8,128)(2,1)} %get-tuple-element.70), calls=%async_computation.2 | async-start | bytes 2097152 | tf_op jit(solution)/shard_map/all_to_all | solution.py:361
  89.9 0.7 collective-permute-start.10
  90.6 2.2 collective-permute-start.2
  92.8 3.7 %shard_map.58.local_ref = f32[16,128,128]{2,1,0:T(8,128)S(1)} custom-call(s32[3,32]{1,0:T(4,128)S(1)} %copy-done.1, bf16[16,128,128]{2,1,0:T(8,128)(2,1)} %get-tuple-element.67.state_ref, bf16[16,3,128,128]{3,2,1,0:T(8,128)(2,1)} %collective-permute-done.9.blocks_ref), custom_call_target="tpu_custom_call" | custom-call | flops 201326592 | bytes 4194304 | tf_op jit(solution)/shard_map/pallas_call | solution.py:215
  96.6 12.3 %collective-permute-done.10.blocks_ref = bf16[16,3,128,128]{3,2,1,0:T(8,128)(2,1)} collective-permute-done((bf16[16,3,128,128]{3,2,1,0:T(8,128)(2,1)}, bf16[16,3,128,128]{3,2,1,0:T(8,128)(2,1)}, u32[]{:S(2)}, u32[]{:S(2)}) %collective-permute-start.10) | collective-permute-done | bytes 1572896 | tf_op jit(solution)/shard_map/ppermute | solution.py:369
  109.4 1.2 shard_map.59
  110.7 6.1 %all-to-all-done.2.arrived_ref = bf16[32,128,128]{2,1,0:T(8,128)(2,1)S(1)} async-done(((bf16[32,128,128]{2,1,0:T(8,128)(2,1)}), bf16[32,128,128]{2,1,0:T(8,128)(2,1)S(1)}, u32[]{:S(2)}, u32[]{:S(2)}) %all-to-all-start.2) | async-done | bytes 1048608 | tf_op jit(solution)/shard_map/all_to_all | solution.py:361
  116.8 2.1 shard_map.60
  118.9 6.4 %all-to-all-start.3 = ((bf16[32,128,128]{2,1,0:T(8,128)(2,1)}), bf16[32,128,128]{2,1,0:T(8,128)(2,1)S(1)}, u32[]{:S(2)}, u32[]{:S(2)}) async-start(bf16[32,128,128]{2,1,0:T(8,128)(2,1)} %get-tuple-element.76), calls=%async_computation.3 | async-start | bytes 2097152 | tf_op jit(solution)/shard_map/all_to_all | solution.py:361
  125.4 2.2 collective-permute-start.3
  127.6 3.7 %shard_map.61.local_ref = f32[16,128,128]{2,1,0:T(8,128)S(1)} custom-call(s32[3,32]{1,0:T(4,128)S(1)} %copy-done.3, bf16[16,128,128]{2,1,0:T(8,128)(2,1)} %get-tuple-element.73.state_ref, bf16[16,3,128,128]{3,2,1,0:T(8,128)(2,1)} %collective-permute-done.10.blocks_ref), custom_call_target="tpu_custom_call" | custom-call | flops 201326592 | bytes 4194304 | tf_op jit(solution)/shard_map/pallas_call | solution.py:215
  131.4 12.3 %collective-permute-done.11.blocks_ref = bf16[16,3,128,128]{3,2,1,0:T(8,128)(2,1)} collective-permute-done((bf16[16,3,128,128]{3,2,1,0:T(8,128)(2,1)}, bf16[16,3,128,128]{3,2,1,0:T(8,128)(2,1)}, u32[]{:S(2)}, u32[]{:S(2)}) %collective-permute-start.11) | collective-permute-done | bytes 1572896 | tf_op jit(solution)/shard_map/ppermute | solution.py:369
  144.3 1.2 shard_map.62
  145.5 5.8 %all-to-all-done.3.arrived_ref = bf16[32,128,128]{2,1,0:T(8,128)(2,1)S(1)} async-done(((bf16[32,128,128]{2,1,0:T(8,128)(2,1)}), bf16[32,128,128]{2,1,0:T(8,128)(2,1)S(1)}, u32[]{:S(2)}, u32[]{:S(2)}) %all-to-all-start.3) | async-done | bytes 1048608 | tf_op jit(solution)/shard_map/all_to_all | solution.py:361
  151.3 2.1 shard_map.63
  153.5 6.5 %all-to-all-start.4 = ((bf16[32,128,128]{2,1,0:T(8,128)(2,1)}), bf16[32,128,128]{2,1,0:T(8,128)(2,1)S(1)}, u32[]{:S(2)}, u32[]{:S(2)}) async-start(bf16[32,128,128]{2,1,0:T(8,128)(2,1)} %get-tuple-element.82), calls=%async_computation.4 | async-start | bytes 2097152 | tf_op jit(solution)/shard_map/all_to_all | solution.py:361
  160.3 2.2 collective-permute-start.4
  162.5 3.7 %shard_map.64.local_ref = f32[16,128,128]{2,1,0:T(8,128)S(1)} custom-call(s32[3,32]{1,0:T(4,128)S(1)} %copy-done.5, bf16[16,128,128]{2,1,0:T(8,128)(2,1)} %get-tuple-element.79.state_ref, bf16[16,3,128,128]{3,2,1,0:T(8,128)(2,1)} %collective-permute-done.11.blocks_ref), custom_call_target="tpu_custom_call" | custom-call | flops 201326592 | bytes 4194304 | tf_op jit(solution)/shard_map/pallas_call | solution.py:215
  166.2 12.3 %collective-permute-done.12.blocks_ref = bf16[16,3,128,128]{3,2,1,0:T(8,128)(2,1)} collective-permute-done((bf16[16,3,128,128]{3,2,1,0:T(8,128)(2,1)}, bf16[16,3,128,128]{3,2,1,0:T(8,128)(2,1)}, u32[]{:S(2)}, u32[]{:S(2)}) %collective-permute-start.12) | collective-permute-done | bytes 1572896 | tf_op jit(solution)/shard_map/ppermute | solution.py:369
  179.1 1.2 shard_map.65
  180.3 6.4 %all-to-all-done.4.arrived_ref = bf16[32,128,128]{2,1,0:T(8,128)(2,1)S(1)} async-done(((bf16[32,128,128]{2,1,0:T(8,128)(2,1)}), bf16[32,128,128]{2,1,0:T(8,128)(2,1)S(1)}, u32[]{:S(2)}, u32[]{:S(2)}) %all-to-all-start.4) | async-done | bytes 1048608 | tf_op jit(solution)/shard_map/all_to_all | solution.py:361
  186.8 2.1 shard_map.66
  188.9 6.4 %all-to-all-start.5 = ((bf16[32,128,128]{2,1,0:T(8,128)(2,1)}), bf16[32,128,128]{2,1,0:T(8,128)(2,1)S(1)}, u32[]{:S(2)}, u32[]{:S(2)}) async-start(bf16[32,128,128]{2,1,0:T(8,128)(2,1)} %get-tuple-element.88), calls=%async_computation.5 | async-start | bytes 2097152 | tf_op jit(solution)/shard_map/all_to_all | solution.py:361
  195.4 1.9 collective-permute-start.5
  197.3 3.8 %shard_map.67.local_ref = f32[16,128,128]{2,1,0:T(8,128)S(1)} custom-call(s32[3,32]{1,0:T(4,128)S(1)} %copy-done.7, bf16[16,128,128]{2,1,0:T(8,128)(2,1)} %get-tuple-element.85.state_ref, bf16[16,3,128,128]{3,2,1,0:T(8,128)(2,1)} %collective-permute-done.12.blocks_ref), custom_call_target="tpu_custom_call" | custom-call | flops 201326592 | bytes 4194304 | tf_op jit(solution)/shard_map/pallas_call | solution.py:215
  201.0 12.6 %collective-permute-done.13.blocks_ref = bf16[16,3,128,128]{3,2,1,0:T(8,128)(2,1)} collective-permute-done((bf16[16,3,128,128]{3,2,1,0:T(8,128)(2,1)}, bf16[16,3,128,128]{3,2,1,0:T(8,128)(2,1)}, u32[]{:S(2)}, u32[]{:S(2)}) %collective-permute-start.13) | collective-permute-done | bytes 1572896 | tf_op jit(solution)/shard_map/ppermute | solution.py:369
  214.2 1.2 shard_map.68
  215.5 5.9 %all-to-all-done.5.arrived_ref = bf16[32,128,128]{2,1,0:T(8,128)(2,1)S(1)} async-done(((bf16[32,128,128]{2,1,0:T(8,128)(2,1)}), bf16[32,128,128]{2,1,0:T(8,128)(2,1)S(1)}, u32[]{:S(2)}, u32[]{:S(2)}) %all-to-all-start.5) | async-done | bytes 1048608 | tf_op jit(solution)/shard_map/all_to_all | solution.py:361
  221.4 2.1 shard_map.69
  223.5 6.4 %all-to-all-start.6 = ((bf16[32,128,128]{2,1,0:T(8,128)(2,1)}), bf16[32,128,128]{2,1,0:T(8,128)(2,1)S(1)}, u32[]{:S(2)}, u32[]{:S(2)}) async-start(bf16[32,128,128]{2,1,0:T(8,128)(2,1)} %get-tuple-element.94), calls=%async_computation.6 | async-start | bytes 2097152 | tf_op jit(solution)/shard_map/all_to_all | solution.py:361
  230.2 1.9 collective-permute-start.6
  232.1 3.7 %shard_map.70.local_ref = f32[16,128,128]{2,1,0:T(8,128)S(1)} custom-call(s32[3,32]{1,0:T(4,128)S(1)} %copy-done.9, bf16[16,128,128]{2,1,0:T(8,128)(2,1)} %get-tuple-element.91.state_ref, bf16[16,3,128,128]{3,2,1,0:T(8,128)(2,1)} %collective-permute-done.13.blocks_ref), custom_call_target="tpu_custom_call" | custom-call | flops 201326592 | bytes 4194304 | tf_op jit(solution)/shard_map/pallas_call | solution.py:215
  235.9 12.6 %collective-permute-done.14.blocks_ref = bf16[16,3,128,128]{3,2,1,0:T(8,128)(2,1)S(1)} collective-permute-done((bf16[16,3,128,128]{3,2,1,0:T(8,128)(2,1)}, bf16[16,3,128,128]{3,2,1,0:T(8,128)(2,1)S(1)}, u32[]{:S(2)}, u32[]{:S(2)}) %collective-permute-start.14) | collective-permute-done | bytes 1572896 | tf_op jit(solution)/shard_map/ppermute | solution.py:369
  248.5 1.2 copy-done.12
  250.2 1.2 shard_map.71
  251.5 5.0 %all-to-all-done.6.arrived_ref = bf16[32,128,128]{2,1,0:T(8,128)(2,1)S(1)} async-done(((bf16[32,128,128]{2,1,0:T(8,128)(2,1)}), bf16[32,128,128]{2,1,0:T(8,128)(2,1)S(1)}, u32[]{:S(2)}, u32[]{:S(2)}) %all-to-all-start.6) | async-done | bytes 1048608 | tf_op jit(solution)/shard_map/all_to_all | solution.py:361
  256.5 2.1 shard_map.72
  258.6 6.4 %all-to-all-start.7 = ((bf16[32,128,128]{2,1,0:T(8,128)(2,1)}), bf16[32,128,128]{2,1,0:T(8,128)(2,1)S(1)}, u32[]{:S(2)}, u32[]{:S(2)}) async-start(bf16[32,128,128]{2,1,0:T(8,128)(2,1)} %get-tuple-element.97), calls=%async_computation.7 | async-start | bytes 2097152 | tf_op jit(solution)/shard_map/all_to_all | solution.py:361
  265.1 1.1 collective-permute-start.7
  266.2 1.3 collective-permute-done.7.table_ref
  268.1 0.7 shard_map.51.before
  268.8 3.7 %shard_map.73.local_ref = f32[16,128,128]{2,1,0:T(8,128)S(1)} custom-call(s32[3,32]{1,0:T(4,128)S(1)} %copy-done.11, bf16[16,128,128]{2,1,0:T(8,128)(2,1)} %get-tuple-element.98.state_ref, bf16[16,3,128,128]{3,2,1,0:T(8,128)(2,1)} %copy-done.12), custom_call_target="tpu_custom_call" | custom-call | flops 201326592 | bytes 4194304 | tf_op jit(solution)/shard_map/pallas_call | solution.py:215
  272.5 19.7 %all-to-all-done.7.arrived_ref = bf16[32,128,128]{2,1,0:T(8,128)(2,1)S(1)} async-done(((bf16[32,128,128]{2,1,0:T(8,128)(2,1)}), bf16[32,128,128]{2,1,0:T(8,128)(2,1)S(1)}, u32[]{:S(2)}, u32[]{:S(2)}) %all-to-all-start.7) | async-done | bytes 1048608 | tf_op jit(solution)/shard_map/all_to_all | solution.py:361
  292.6 4.3 %collective-permute-start.15 = (bf16[1,128,128]{2,1,0:T(8,128)(2,1)S(1)}, bf16[1,128,128]{2,1,0:T(8,128)(2,1)S(1)}, u32[]{:S(2)}, u32[]{:S(2)}) collective-permute-start(bf16[1,128,128]{2,1,0:T(8,128)(2,1)S(1)} %get-tuple-element.100), channel_id=1, source_target_pairs={{0,1},{1,2},{2,3},{3,4},{4,5},{5,6},{6,7},{7,8},{8,9},{9,10},{10,1... | collective-permute-start | bytes 98312 | tf_op jit(solution)/shard_map/ppermute | solution.py:373
  297.0 1.9 collective-permute-start.16
  298.9 2.0 shard_map.75
  300.9 4.0 %collective-permute-done.16.high_ref = bf16[1,128,128]{2,1,0:T(8,128)(2,1)S(1)} collective-permute-done((bf16[1,128,128]{2,1,0:T(8,128)(2,1)S(1)}, bf16[1,128,128]{2,1,0:T(8,128)(2,1)S(1)}, u32[]{:S(2)}, u32[]{:S(2)}) %collective-permute-start.16) | collective-permute-done | bytes 32800 | tf_op jit(solution)/shard_map/ppermute | solution.py:374
  304.9 0.9 shard_map.76
  (59 shorter events, 7.3 us)
Async XLA Ops:
  4.5 12.7 %copy-start.13 = (s32[1,16,3]{1,0,2:T(1,128)S(1)}, s32[1,16,3]{1,0,2:T(1,128)}, u32[]{:S(2)}) copy-start(s32[1,16,3]{1,0,2:T(1,128)} %param.5) | copy-start | bytes 580
  4.5 41.0 %all-to-all-start = ((bf16[32,144,128]{2,1,0:T(8,128)(2,1)}), bf16[32,144,128]{2,1,0:T(8,128)(2,1)S(1)}, u32[]{:S(2)}, u32[]{:S(2)}) async-start(bf16[32,144,128]{2,1,0:T(8,128)(2,1)} %get-tuple-element.56), calls=%async_computation | async-start | bytes 2359296 | tf_op jit(solution)/shard_map/all_to_all | solution.py:361
  15.5 19.9 %collective-permute-start.8 = (bf16[16,3,128,128]{3,2,1,0:T(8,128)(2,1)}, bf16[16,3,128,128]{3,2,1,0:T(8,128)(2,1)}, u32[]{:S(2)}, u32[]{:S(2)}) collective-permute-start(bf16[16,3,128,128]{3,2,1,0:T(8,128)(2,1)} %bitcast.2.blocks_ref), channel_id=1, source_target_pairs={{0,224},{32,0},{64,32},{96,64},{128,96},{160,128},{192,160},{224,1... | collective-permute-start | bytes 4718600 | tf_op jit(solution)/shard_map/ppermute | solution.py:369
  17.6 17.8 %collective-permute-start = (s32[3,32]{1,0:T(4,128)S(1)}, s32[3,32]{1,0:T(4,128)S(1)}, u32[]{:S(2)}, u32[]{:S(2)}) collective-permute-start(s32[3,32]{1,0:T(4,128)S(1)} %pad_add_fusion.table), channel_id=1, source_target_pairs={{0,224},{32,0},{64,32},{96,64},{128,96},{160,128},{192,160},{224,1... | collective-permute-start | bytes 1160 | tf_op jit(solution)/shard_map/ppermute | solution.py:363
  35.4 0.6 copy-start.14
  48.9 32.4 %all-to-all-start.1 = ((bf16[32,128,128]{2,1,0:T(8,128)(2,1)}), bf16[32,128,128]{2,1,0:T(8,128)(2,1)S(1)}, u32[]{:S(2)}, u32[]{:S(2)}) async-start(bf16[32,128,128]{2,1,0:T(8,128)(2,1)} %get-tuple-element.64), calls=%async_computation.1 | async-start | bytes 2097152 | tf_op jit(solution)/shard_map/all_to_all | solution.py:361
  55.3 18.7 %collective-permute-start.9 = (bf16[16,3,128,128]{3,2,1,0:T(8,128)(2,1)}, bf16[16,3,128,128]{3,2,1,0:T(8,128)(2,1)}, u32[]{:S(2)}, u32[]{:S(2)}) collective-permute-start(bf16[16,3,128,128]{3,2,1,0:T(8,128)(2,1)} %collective-permute-done.8.blocks_ref), channel_id=1, source_target_pairs={{0,224},{32,0},{64,32},{96,64},{128,96},{160,128},{192,160},{224,1... | collective-permute-start | bytes 4718600 | tf_op jit(solution)/shard_map/ppermute | solution.py:369
  55.8 18.3 %collective-permute-start.1 = (s32[3,32]{1,0:T(4,128)S(1)}, s32[3,32]{1,0:T(4,128)S(1)}, u32[]{:S(2)}, u32[]{:S(2)}) collective-permute-start(s32[3,32]{1,0:T(4,128)S(1)} %pad_add_fusion.1.table), channel_id=1, source_target_pairs={{0,224},{32,0},{64,32},{96,64},{128,96},{160,128},{192,160},{224,1... | collective-permute-start | bytes 1160 | tf_op jit(solution)/shard_map/ppermute | solution.py:363
  74.0 0.6 copy-start
  83.5 7.1 %copy-start.1 = (s32[3,32]{1,0:T(4,128)S(1)}, s32[3,32]{1,0:T(4,128)}, u32[]{:S(2)}) copy-start(s32[3,32]{1,0:T(4,128)} %copy-done) | copy-start | bytes 1156
  83.5 33.3 %all-to-all-start.2 = ((bf16[32,128,128]{2,1,0:T(8,128)(2,1)}), bf16[32,128,128]{2,1,0:T(8,128)(2,1)S(1)}, u32[]{:S(2)}, u32[]{:S(2)}) async-start(bf16[32,128,128]{2,1,0:T(8,128)(2,1)} %get-tuple-element.70), calls=%async_computation.2 | async-start | bytes 2097152 | tf_op jit(solution)/shard_map/all_to_all | solution.py:361
  89.9 18.9 %collective-permute-start.10 = (bf16[16,3,128,128]{3,2,1,0:T(8,128)(2,1)}, bf16[16,3,128,128]{3,2,1,0:T(8,128)(2,1)}, u32[]{:S(2)}, u32[]{:S(2)}) collective-permute-start(bf16[16,3,128,128]{3,2,1,0:T(8,128)(2,1)} %collective-permute-done.9.blocks_ref), channel_id=1, source_target_pairs={{0,224},{32,0},{64,32},{96,64},{128,96},{160,128},{192,160},{224,1... | collective-permute-start | bytes 4718600 | tf_op jit(solution)/shard_map/ppermute | solution.py:369
  90.6 18.3 %collective-permute-start.2 = (s32[3,32]{1,0:T(4,128)S(1)}, s32[3,32]{1,0:T(4,128)S(1)}, u32[]{:S(2)}, u32[]{:S(2)}) collective-permute-start(s32[3,32]{1,0:T(4,128)S(1)} %copy-done.1), channel_id=1, source_target_pairs={{0,224},{32,0},{64,32},{96,64},{128,96},{160,128},{192,160},{224,1... | collective-permute-start | bytes 1160 | tf_op jit(solution)/shard_map/ppermute | solution.py:363
  108.9 0.6 copy-start.2
  118.9 6.5 %copy-start.3 = (s32[3,32]{1,0:T(4,128)S(1)}, s32[3,32]{1,0:T(4,128)}, u32[]{:S(2)}) copy-start(s32[3,32]{1,0:T(4,128)} %copy-done.2) | copy-start | bytes 1156
  118.9 32.4 %all-to-all-start.3 = ((bf16[32,128,128]{2,1,0:T(8,128)(2,1)}), bf16[32,128,128]{2,1,0:T(8,128)(2,1)S(1)}, u32[]{:S(2)}, u32[]{:S(2)}) async-start(bf16[32,128,128]{2,1,0:T(8,128)(2,1)} %get-tuple-element.76), calls=%async_computation.3 | async-start | bytes 2097152 | tf_op jit(solution)/shard_map/all_to_all | solution.py:361
  125.4 18.3 %collective-permute-start.11 = (bf16[16,3,128,128]{3,2,1,0:T(8,128)(2,1)}, bf16[16,3,128,128]{3,2,1,0:T(8,128)(2,1)}, u32[]{:S(2)}, u32[]{:S(2)}) collective-permute-start(bf16[16,3,128,128]{3,2,1,0:T(8,128)(2,1)} %collective-permute-done.10.blocks_ref), channel_id=1, source_target_pairs={{0,224},{32,0},{64,32},{96,64},{128,96},{160,128},{192,160},{224,1... | collective-permute-start | bytes 4718600 | tf_op jit(solution)/shard_map/ppermute | solution.py:369
  125.4 18.3 %collective-permute-start.3 = (s32[3,32]{1,0:T(4,128)S(1)}, s32[3,32]{1,0:T(4,128)S(1)}, u32[]{:S(2)}, u32[]{:S(2)}) collective-permute-start(s32[3,32]{1,0:T(4,128)S(1)} %copy-done.3), channel_id=1, source_target_pairs={{0,224},{32,0},{64,32},{96,64},{128,96},{160,128},{192,160},{224,1... | collective-permute-start | bytes 1160 | tf_op jit(solution)/shard_map/ppermute | solution.py:363
  143.7 0.6 copy-start.4
  153.5 6.8 %copy-start.5 = (s32[3,32]{1,0:T(4,128)S(1)}, s32[3,32]{1,0:T(4,128)}, u32[]{:S(2)}) copy-start(s32[3,32]{1,0:T(4,128)} %copy-done.4) | copy-start | bytes 1156
  153.5 33.3 %all-to-all-start.4 = ((bf16[32,128,128]{2,1,0:T(8,128)(2,1)}), bf16[32,128,128]{2,1,0:T(8,128)(2,1)S(1)}, u32[]{:S(2)}, u32[]{:S(2)}) async-start(bf16[32,128,128]{2,1,0:T(8,128)(2,1)} %get-tuple-element.82), calls=%async_computation.4 | async-start | bytes 2097152 | tf_op jit(solution)/shard_map/all_to_all | solution.py:361
  159.9 18.6 %collective-permute-start.12 = (bf16[16,3,128,128]{3,2,1,0:T(8,128)(2,1)}, bf16[16,3,128,128]{3,2,1,0:T(8,128)(2,1)}, u32[]{:S(2)}, u32[]{:S(2)}) collective-permute-start(bf16[16,3,128,128]{3,2,1,0:T(8,128)(2,1)} %collective-permute-done.11.blocks_ref), channel_id=1, source_target_pairs={{0,224},{32,0},{64,32},{96,64},{128,96},{160,128},{192,160},{224,1... | collective-permute-start | bytes 4718600 | tf_op jit(solution)/shard_map/ppermute | solution.py:369
  160.3 18.3 %collective-permute-start.4 = (s32[3,32]{1,0:T(4,128)S(1)}, s32[3,32]{1,0:T(4,128)S(1)}, u32[]{:S(2)}, u32[]{:S(2)}) collective-permute-start(s32[3,32]{1,0:T(4,128)S(1)} %copy-done.5), channel_id=1, source_target_pairs={{0,224},{32,0},{64,32},{96,64},{128,96},{160,128},{192,160},{224,1... | collective-permute-start | bytes 1160 | tf_op jit(solution)/shard_map/ppermute | solution.py:363
  178.5 0.6 copy-start.6
  188.9 6.5 %copy-start.7 = (s32[3,32]{1,0:T(4,128)S(1)}, s32[3,32]{1,0:T(4,128)}, u32[]{:S(2)}) copy-start(s32[3,32]{1,0:T(4,128)} %copy-done.6) | copy-start | bytes 1156
  188.9 32.4 %all-to-all-start.5 = ((bf16[32,128,128]{2,1,0:T(8,128)(2,1)}), bf16[32,128,128]{2,1,0:T(8,128)(2,1)S(1)}, u32[]{:S(2)}, u32[]{:S(2)}) async-start(bf16[32,128,128]{2,1,0:T(8,128)(2,1)} %get-tuple-element.88), calls=%async_computation.5 | async-start | bytes 2097152 | tf_op jit(solution)/shard_map/all_to_all | solution.py:361
  195.4 18.3 %collective-permute-start.13 = (bf16[16,3,128,128]{3,2,1,0:T(8,128)(2,1)}, bf16[16,3,128,128]{3,2,1,0:T(8,128)(2,1)}, u32[]{:S(2)}, u32[]{:S(2)}) collective-permute-start(bf16[16,3,128,128]{3,2,1,0:T(8,128)(2,1)} %collective-permute-done.12.blocks_ref), channel_id=1, source_target_pairs={{0,224},{32,0},{64,32},{96,64},{128,96},{160,128},{192,160},{224,1... | collective-permute-start | bytes 4718600 | tf_op jit(solution)/shard_map/ppermute | solution.py:369
  195.4 18.2 %collective-permute-start.5 = (s32[3,32]{1,0:T(4,128)S(1)}, s32[3,32]{1,0:T(4,128)S(1)}, u32[]{:S(2)}, u32[]{:S(2)}) collective-permute-start(s32[3,32]{1,0:T(4,128)S(1)} %copy-done.7), channel_id=1, source_target_pairs={{0,224},{32,0},{64,32},{96,64},{128,96},{160,128},{192,160},{224,1... | collective-permute-start | bytes 1160 | tf_op jit(solution)/shard_map/ppermute | solution.py:363
  213.6 0.6 copy-start.8
  223.5 6.7 %copy-start.9 = (s32[3,32]{1,0:T(4,128)S(1)}, s32[3,32]{1,0:T(4,128)}, u32[]{:S(2)}) copy-start(s32[3,32]{1,0:T(4,128)} %copy-done.8) | copy-start | bytes 1156
  223.5 33.0 %all-to-all-start.6 = ((bf16[32,128,128]{2,1,0:T(8,128)(2,1)}), bf16[32,128,128]{2,1,0:T(8,128)(2,1)S(1)}, u32[]{:S(2)}, u32[]{:S(2)}) async-start(bf16[32,128,128]{2,1,0:T(8,128)(2,1)} %get-tuple-element.94), calls=%async_computation.6 | async-start | bytes 2097152 | tf_op jit(solution)/shard_map/all_to_all | solution.py:361
  229.9 18.5 %collective-permute-start.14 = (bf16[16,3,128,128]{3,2,1,0:T(8,128)(2,1)}, bf16[16,3,128,128]{3,2,1,0:T(8,128)(2,1)S(1)}, u32[]{:S(2)}, u32[]{:S(2)}) collective-permute-start(bf16[16,3,128,128]{3,2,1,0:T(8,128)(2,1)} %collective-permute-done.13.blocks_ref), channel_id=1, source_target_pairs={{0,224},{32,0},{64,32},{96,64},{128,96},{160,128},{192,160},{224,1... | collective-permute-start | bytes 4718600 | tf_op jit(solution)/shard_map/ppermute | solution.py:369
  230.2 18.3 %collective-permute-start.6 = (s32[3,32]{1,0:T(4,128)S(1)}, s32[3,32]{1,0:T(4,128)S(1)}, u32[]{:S(2)}, u32[]{:S(2)}) collective-permute-start(s32[3,32]{1,0:T(4,128)S(1)} %copy-done.9), channel_id=1, source_target_pairs={{0,224},{32,0},{64,32},{96,64},{128,96},{160,128},{192,160},{224,1... | collective-permute-start | bytes 1160 | tf_op jit(solution)/shard_map/ppermute | solution.py:363
  248.4 1.2 copy-start.12
  249.6 0.6 copy-start.10
  258.6 6.5 %copy-start.11 = (s32[3,32]{1,0:T(4,128)S(1)}, s32[3,32]{1,0:T(4,128)}, u32[]{:S(2)}) copy-start(s32[3,32]{1,0:T(4,128)} %copy-done.10) | copy-start | bytes 1156
  258.6 33.6 %all-to-all-start.7 = ((bf16[32,128,128]{2,1,0:T(8,128)(2,1)}), bf16[32,128,128]{2,1,0:T(8,128)(2,1)S(1)}, u32[]{:S(2)}, u32[]{:S(2)}) async-start(bf16[32,128,128]{2,1,0:T(8,128)(2,1)} %get-tuple-element.97), calls=%async_computation.7 | async-start | bytes 2097152 | tf_op jit(solution)/shard_map/all_to_all | solution.py:361
  265.1 2.4 collective-permute-start.7
  267.5 0.6 copy-start.15
  292.6 8.3 %collective-permute-start.15 = (bf16[1,128,128]{2,1,0:T(8,128)(2,1)S(1)}, bf16[1,128,128]{2,1,0:T(8,128)(2,1)S(1)}, u32[]{:S(2)}, u32[]{:S(2)}) collective-permute-start(bf16[1,128,128]{2,1,0:T(8,128)(2,1)S(1)} %get-tuple-element.100), channel_id=1, source_target_pairs={{0,1},{1,2},{2,3},{3,4},{4,5},{5,6},{6,7},{7,8},{8,9},{9,10},{10,1... | collective-permute-start | bytes 98312 | tf_op jit(solution)/shard_map/ppermute | solution.py:373
  297.0 7.9 %collective-permute-start.16 = (bf16[1,128,128]{2,1,0:T(8,128)(2,1)S(1)}, bf16[1,128,128]{2,1,0:T(8,128)(2,1)S(1)}, u32[]{:S(2)}, u32[]{:S(2)}) collective-permute-start(bf16[1,128,128]{2,1,0:T(8,128)(2,1)S(1)} %get-tuple-element.101), channel_id=1, source_target_pairs={{1,0},{2,1},{3,2},{4,3},{5,4},{6,5},{7,6},{8,7},{9,8},{10,9},{11,1... | collective-permute-start | bytes 98312 | tf_op jit(solution)/shard_map/ppermute | solution.py:374

commit v7 on v6

--- a/solution.py
+++ b/solution.py
@@ -41,11 +41,11 @@
         copy.wait()
 
 
-def add_arrived(table, arrived_ref, gathered):
+def add_arrived(landed, arrived_ref, gathered):
     gathered[...] = jnp.zeros_like(gathered)
     rows = gathered.shape[1]
     for p in range(arrived_ref.shape[0]):
-        home = table[LANDED, p]
+        home = landed(p)
         gathered[home] = gathered[home] + arrived_ref[p, :rows].astype(jnp.float32)
 
 
@@ -54,9 +54,11 @@
 
 
 def first_body(
-    dest, seeds_ref, blocks_ref, out_ref, state_ref, seeds_scr, off_scr, stage, state_scr, lists, sems, out_sems, in_sems
+    dest_ref, seeds_ref, blocks_ref, out_ref, state_ref, seeds_scr, off_scr, stage, state_scr, dest, lists, sems, out_sems, in_sems
 ):
     nnz, _, tiles = dest.shape
+    read = pltpu.make_async_copy(dest_ref, dest, sems.at[2])
+    read.start()
     each = nnz - 1
     rows = state_scr.shape[1]
     parts = [pl.ds(t, PART) for t in range(0, tiles, PART)]
@@ -70,6 +72,7 @@
         state_scr[t] = jnp.transpose(seeds_scr[t])
     store = pltpu.make_async_copy(state_scr, state_ref, sems.at[1])
     store.start()
+    read.wait()
     for p in range(stage.shape[0]):
         lists[0, p] = 0
         lists[1, p] = tiles
@@ -95,15 +98,16 @@
             pltpu.HBM((peers, rows + SAYS, points), jnp.bfloat16),
             pltpu.HBM((tiles, rows, points), jnp.bfloat16),
         ),
-        in_specs=[SMEM, HBM, HBM],
+        in_specs=[HBM, HBM, HBM],
         out_specs=(HBM, HBM),
         scratch_shapes=[
             pltpu.VMEM(seeds.shape, jnp.bfloat16),
             pltpu.VMEM((tiles, nnz - 1, points, points), jnp.bfloat16),
             pltpu.VMEM((peers, rows + SAYS, points), jnp.bfloat16),
             pltpu.VMEM((tiles, rows, points), jnp.bfloat16),
+            pltpu.SMEM(dest.shape, jnp.int32),
             pltpu.SMEM((2, peers), jnp.int32),
-            pltpu.SemaphoreType.DMA((2,)),
+            pltpu.SemaphoreType.DMA((3,)),
             pltpu.SemaphoreType.DMA((peers // PART,)),
             pltpu.SemaphoreType.DMA((tiles // PART,)),
         ],
@@ -157,9 +161,18 @@
 
 
 def send_body(
-    table, arrived_ref, local_ref, off_ref, out_ref, state_ref, stage, gathered, state_scr, store_sem, out_sems,
+    table, arrived_ref, local_ref, off_ref, out_ref, state_ref, stage, gathered, state_scr, store_sem, out_sems, *told,
 ):
-    add_arrived(table, arrived_ref, gathered)
+    landed = lambda p: table[LANDED, p]
+    if told:
+        said, read, sem = told
+        said[...] = arrived_ref[:, state_scr.shape[1], :].astype(jnp.float32).astype(jnp.int32)
+        copy = pltpu.make_async_copy(said, read, sem)
+        copy.start()
+        copy.wait()
+        me = lax.axis_index("tile")
+        landed = lambda p: jnp.where(me == p, state_scr.shape[0], read[p, 0])
+    add_arrived(landed, arrived_ref, gathered)
     for t in range(state_scr.shape[0]):
         state_scr[t] = (gathered[t] + local_ref[t]).astype(jnp.bfloat16)
     store = pltpu.make_async_copy(state_scr, state_ref, store_sem)
@@ -171,9 +184,12 @@
 placed = pltpu.with_memory_space_constraint
 
 
-def send(table, arrived, local, off, ready):
+def send(table, arrived, local, off):
     peers = arrived.shape[0]
     tiles, rows, points = local.shape
+    told = []
+    if arrived.shape[1] > rows:
+        told = [pltpu.VMEM((peers, points), jnp.int32), pltpu.SMEM((peers, points), jnp.int32), pltpu.SemaphoreType.DMA]
     return pl.pallas_call(
         send_body,
         out_shape=(
@@ -188,12 +204,13 @@
             pltpu.VMEM((tiles, rows, points), jnp.bfloat16),
             pltpu.SemaphoreType.DMA,
             pltpu.SemaphoreType.DMA((peers // PART,)),
+            *told,
         ],
         compiler_params=SEND,
         cost_estimate=pl.CostEstimate(
             flops=2 * peers * points * points * rows, bytes_accessed=4 << 20, transcendentals=0
         ),
-    )(placed(table, pltpu.SMEM) if ready else table, placed(arrived, pltpu.VMEM), placed(local, pltpu.VMEM), placed(off, pltpu.VMEM))
+    )(placed(table, pltpu.SMEM), placed(arrived, pltpu.VMEM), placed(local, pltpu.VMEM), placed(off, pltpu.VMEM))
 
 
 def keep_body(table, state_ref, blocks_ref, local_ref, total, blocks_scr, sem):
@@ -230,7 +247,7 @@
 
 
 def last_body(before, arrived_ref, local_ref, final_ref, low_ref, high_ref, gathered):
-    add_arrived(before, arrived_ref, gathered)
+    add_arrived(lambda p: before[LANDED, p], arrived_ref, gathered)
     tiles = final_ref.shape[0]
     for t in range(tiles):
         final_ref[t] = (gathered[t] + local_ref[t]).astype(jnp.bfloat16)
@@ -357,7 +374,7 @@
             rows = own_rows(dest, me, tiles, peers, nnz)
             table = jnp.stack([*rows, jnp.zeros_like(rows[0])])
         else:
-            out, state = send(table if step == 1 else quick, arrived, local, off, step > 1)
+            out, state = send(quick, arrived, local, off)
         arrived = lax.all_to_all(out, "tile", split_axis=0, concat_axis=0, tiled=True)
         local = keep(table, state, wblk)
         given = table = onward(table)

time: 308 us -> 307 us (level)
    ppermute x8, waiting for transfers between devices: 14.1 us -> 1.33 us  [body(): given = table = onward(table)]
    ppermute x7, waiting for transfers between devices: 74.1 us -> 86.1 us  [body(): wblk = onward(wblk)]
where the time goes in v7:
time: 307 us; the launch traced here: 305 us
  waiting for transfers between devices  154 us (50%)
  starting transfers between devices  81.1 us (26%)
  Pallas kernels  61.4 us (20%)
  local copies, waits for them, and re-layouts  6.12 us (2%)
    ppermute x7, waiting for transfers between devices, body(): wblk = onward(wblk)  86.1 us
    all_to_all x8, waiting for transfers between devices, body(): lax.all_to_all(out, 'tile', split_axis=0, concat_axis=0, tiled=True)  62.5 us
    all_to_all x8, starting transfers between devices, body(): lax.all_to_all(out, 'tile', split_axis=0, concat_axis=0, tiled=True)  56.2 us
    pallas_call x8, Pallas kernels, keep(): pl.pallas_call(keep_body, out_shape=pltpu.VMEM((tiles, rows, points), jnp...  30 us
    pallas_call x7, Pallas kernels, send(): pl.pallas_call(send_body, out_shape=(pltpu.HBM((peers, rows, points), jnp...  15.6 us
    ppermute x8, starting transfers between devices, body(): given = table = onward(table)  15.3 us
    pallas_call x7, Pallas kernels, fetch(): pl.pallas_call(fetch_body, out_shape=(pltpu.VMEM((tiles, nnz - 1, points,...  8.75 us
  transfers between devices with their start and end apart: 25, of which 17 were waited for; matrix products, arithmetic and copies ran while one was open for 0% of the time, Pallas kernels for 14%

profile of v7, /device:TPU:56, one launch (start us, length us, event | category | flops | bytes accessed | tf_op | source)
XLA Modules:
  0.0 304.7 jit_solution(1108907313274199273)
XLA Ops:
  0.6 3.1 %shard_map.50 = (bf16[32,144,128]{2,1,0:T(8,128)(2,1)}, bf16[16,128,128]{2,1,0:T(8,128)(2,1)}) custom-call(s32[3,1,16]{2,1,0:T(1,128)} %bitcast.14, bf16[16,128,128]{2,1,0:T(8,128)(2,1)} %bitcast.13, bf16[16,3,128,128]{3,2,1,0:T(8,128)(2,1)} %bitcast.2.blocks_ref), custom_call_target="tpu_custom_call" | custom-call | flops 134217728 | bytes 4194304 | tf_op jit(solution)/shard_map/pallas_call | solution.py:95
  3.8 11.0 %all-to-all-start = ((bf16[32,144,128]{2,1,0:T(8,128)(2,1)}), bf16[32,144,128]{2,1,0:T(8,128)(2,1)S(1)}, u32[]{:S(2)}, u32[]{:S(2)}) async-start(bf16[32,144,128]{2,1,0:T(8,128)(2,1)} %get-tuple-element.57), calls=%async_computation | async-start | bytes 2359296 | tf_op jit(solution)/shard_map/all_to_all | solution.py:378
  14.8 1.6 collective-permute-start.8
  16.9 1.2 collective-permute-start
  18.2 3.7 %shard_map.52.local_ref = f32[16,128,128]{2,1,0:T(8,128)S(1)} custom-call(s32[3,32]{1,0:T(4,128)S(1)} %pad_add_fusion.table, bf16[16,128,128]{2,1,0:T(8,128)(2,1)} %get-tuple-element.58.state_ref, bf16[16,3,128,128]{3,2,1,0:T(8,128)(2,1)} %bitcast.2.blocks_ref), custom_call_target="tpu_custom_call" | custom-call | flops 201326592 | bytes 4194304 | tf_op jit(solution)/shard_map/pallas_call | solution.py:232
  21.9 12.8 %collective-permute-done.8.blocks_ref = bf16[16,3,128,128]{3,2,1,0:T(8,128)(2,1)} collective-permute-done((bf16[16,3,128,128]{3,2,1,0:T(8,128)(2,1)}, bf16[16,3,128,128]{3,2,1,0:T(8,128)(2,1)}, u32[]{:S(2)}, u32[]{:S(2)}) %collective-permute-start.8) | collective-permute-done | bytes 1572896 | tf_op jit(solution)/shard_map/ppermute | solution.py:386
  35.3 1.2 shard_map.53
  36.6 8.3 %all-to-all-done.arrived_ref = bf16[32,144,128]{2,1,0:T(8,128)(2,1)S(1)} async-done(((bf16[32,144,128]{2,1,0:T(8,128)(2,1)}), bf16[32,144,128]{2,1,0:T(8,128)(2,1)S(1)}, u32[]{:S(2)}, u32[]{:S(2)}) %all-to-all-start) | async-done | bytes 1179680 | tf_op jit(solution)/shard_map/all_to_all | solution.py:378
  44.8 2.9 shard_map.54
  47.7 6.5 %all-to-all-start.1 = ((bf16[32,128,128]{2,1,0:T(8,128)(2,1)}), bf16[32,128,128]{2,1,0:T(8,128)(2,1)S(1)}, u32[]{:S(2)}, u32[]{:S(2)}) async-start(bf16[32,128,128]{2,1,0:T(8,128)(2,1)} %get-tuple-element.66), calls=%async_computation.1 | async-start | bytes 2097152 | tf_op jit(solution)/shard_map/all_to_all | solution.py:378
  55.3 2.5 collective-permute-start.1
  57.8 3.7 %shard_map.55.local_ref = f32[16,128,128]{2,1,0:T(8,128)S(1)} custom-call(s32[3,32]{1,0:T(4,128)S(1)} %pad_add_fusion.1.table, bf16[16,128,128]{2,1,0:T(8,128)(2,1)} %get-tuple-element.63.state_ref, bf16[16,3,128,128]{3,2,1,0:T(8,128)(2,1)} %collective-permute-done.8.blocks_ref), custom_call_target="tpu_custom_call" | custom-call | flops 201326592 | bytes 4194304 | tf_op jit(solution)/shard_map/pallas_call | solution.py:232
  61.5 11.3 %collective-permute-done.9.blocks_ref = bf16[16,3,128,128]{3,2,1,0:T(8,128)(2,1)} collective-permute-done((bf16[16,3,128,128]{3,2,1,0:T(8,128)(2,1)}, bf16[16,3,128,128]{3,2,1,0:T(8,128)(2,1)}, u32[]{:S(2)}, u32[]{:S(2)}) %collective-permute-start.9) | collective-permute-done | bytes 1572896 | tf_op jit(solution)/shard_map/ppermute | solution.py:386
  73.4 1.2 shard_map.56
  74.7 5.5 %all-to-all-done.1.arrived_ref = bf16[32,128,128]{2,1,0:T(8,128)(2,1)S(1)} async-done(((bf16[32,128,128]{2,1,0:T(8,128)(2,1)}), bf16[32,128,128]{2,1,0:T(8,128)(2,1)S(1)}, u32[]{:S(2)}, u32[]{:S(2)}) %all-to-all-start.1) | async-done | bytes 1048608 | tf_op jit(solution)/shard_map/all_to_all | solution.py:378
  80.2 2.1 shard_map.57
  82.3 6.4 %all-to-all-start.2 = ((bf16[32,128,128]{2,1,0:T(8,128)(2,1)}), bf16[32,128,128]{2,1,0:T(8,128)(2,1)S(1)}, u32[]{:S(2)}, u32[]{:S(2)}) async-start(bf16[32,128,128]{2,1,0:T(8,128)(2,1)} %get-tuple-element.72), calls=%async_computation.2 | async-start | bytes 2097152 | tf_op jit(solution)/shard_map/all_to_all | solution.py:378
  88.7 0.7 collective-permute-start.10
  89.4 2.2 collective-permute-start.2
  91.6 3.7 %shard_map.58.local_ref = f32[16,128,128]{2,1,0:T(8,128)S(1)} custom-call(s32[3,32]{1,0:T(4,128)S(1)} %copy-done.1, bf16[16,128,128]{2,1,0:T(8,128)(2,1)} %get-tuple-element.69.state_ref, bf16[16,3,128,128]{3,2,1,0:T(8,128)(2,1)} %collective-permute-done.9.blocks_ref), custom_call_target="tpu_custom_call" | custom-call | flops 201326592 | bytes 4194304 | tf_op jit(solution)/shard_map/pallas_call | solution.py:232
  95.4 12.3 %collective-permute-done.10.blocks_ref = bf16[16,3,128,128]{3,2,1,0:T(8,128)(2,1)} collective-permute-done((bf16[16,3,128,128]{3,2,1,0:T(8,128)(2,1)}, bf16[16,3,128,128]{3,2,1,0:T(8,128)(2,1)}, u32[]{:S(2)}, u32[]{:S(2)}) %collective-permute-start.10) | collective-permute-done | bytes 1572896 | tf_op jit(solution)/shard_map/ppermute | solution.py:386
  108.2 1.2 shard_map.59
  109.5 6.1 %all-to-all-done.2.arrived_ref = bf16[32,128,128]{2,1,0:T(8,128)(2,1)S(1)} async-done(((bf16[32,128,128]{2,1,0:T(8,128)(2,1)}), bf16[32,128,128]{2,1,0:T(8,128)(2,1)S(1)}, u32[]{:S(2)}, u32[]{:S(2)}) %all-to-all-start.2) | async-done | bytes 1048608 | tf_op jit(solution)/shard_map/all_to_all | solution.py:378
  115.5 2.1 shard_map.60
  117.7 6.4 %all-to-all-start.3 = ((bf16[32,128,128]{2,1,0:T(8,128)(2,1)}), bf16[32,128,128]{2,1,0:T(8,128)(2,1)S(1)}, u32[]{:S(2)}, u32[]{:S(2)}) async-start(bf16[32,128,128]{2,1,0:T(8,128)(2,1)} %get-tuple-element.78), calls=%async_computation.3 | async-start | bytes 2097152 | tf_op jit(solution)/shard_map/all_to_all | solution.py:378
  124.2 2.2 collective-permute-start.3
  126.4 3.8 %shard_map.61.local_ref = f32[16,128,128]{2,1,0:T(8,128)S(1)} custom-call(s32[3,32]{1,0:T(4,128)S(1)} %copy-done.3, bf16[16,128,128]{2,1,0:T(8,128)(2,1)} %get-tuple-element.75.state_ref, bf16[16,3,128,128]{3,2,1,0:T(8,128)(2,1)} %collective-permute-done.10.blocks_ref), custom_call_target="tpu_custom_call" | custom-call | flops 201326592 | bytes 4194304 | tf_op jit(solution)/shard_map/pallas_call | solution.py:232
  130.2 12.3 %collective-permute-done.11.blocks_ref = bf16[16,3,128,128]{3,2,1,0:T(8,128)(2,1)} collective-permute-done((bf16[16,3,128,128]{3,2,1,0:T(8,128)(2,1)}, bf16[16,3,128,128]{3,2,1,0:T(8,128)(2,1)}, u32[]{:S(2)}, u32[]{:S(2)}) %collective-permute-start.11) | collective-permute-done | bytes 1572896 | tf_op jit(solution)/shard_map/ppermute | solution.py:386
  143.1 1.2 shard_map.62
  144.3 5.8 %all-to-all-done.3.arrived_ref = bf16[32,128,128]{2,1,0:T(8,128)(2,1)S(1)} async-done(((bf16[32,128,128]{2,1,0:T(8,128)(2,1)}), bf16[32,128,128]{2,1,0:T(8,128)(2,1)S(1)}, u32[]{:S(2)}, u32[]{:S(2)}) %all-to-all-start.3) | async-done | bytes 1048608 | tf_op jit(solution)/shard_map/all_to_all | solution.py:378
  150.1 2.1 shard_map.63
  152.3 6.5 %all-to-all-start.4 = ((bf16[32,128,128]{2,1,0:T(8,128)(2,1)}), bf16[32,128,128]{2,1,0:T(8,128)(2,1)S(1)}, u32[]{:S(2)}, u32[]{:S(2)}) async-start(bf16[32,128,128]{2,1,0:T(8,128)(2,1)} %get-tuple-element.84), calls=%async_computation.4 | async-start | bytes 2097152 | tf_op jit(solution)/shard_map/all_to_all | solution.py:378
  159.1 2.2 collective-permute-start.4
  161.3 3.8 %shard_map.64.local_ref = f32[16,128,128]{2,1,0:T(8,128)S(1)} custom-call(s32[3,32]{1,0:T(4,128)S(1)} %copy-done.5, bf16[16,128,128]{2,1,0:T(8,128)(2,1)} %get-tuple-element.81.state_ref, bf16[16,3,128,128]{3,2,1,0:T(8,128)(2,1)} %collective-permute-done.11.blocks_ref), custom_call_target="tpu_custom_call" | custom-call | flops 201326592 | bytes 4194304 | tf_op jit(solution)/shard_map/pallas_call | solution.py:232
  165.0 12.3 %collective-permute-done.12.blocks_ref = bf16[16,3,128,128]{3,2,1,0:T(8,128)(2,1)} collective-permute-done((bf16[16,3,128,128]{3,2,1,0:T(8,128)(2,1)}, bf16[16,3,128,128]{3,2,1,0:T(8,128)(2,1)}, u32[]{:S(2)}, u32[]{:S(2)}) %collective-permute-start.12) | collective-permute-done | bytes 1572896 | tf_op jit(solution)/shard_map/ppermute | solution.py:386
  177.9 1.2 shard_map.65
  179.2 6.4 %all-to-all-done.4.arrived_ref = bf16[32,128,128]{2,1,0:T(8,128)(2,1)S(1)} async-done(((bf16[32,128,128]{2,1,0:T(8,128)(2,1)}), bf16[32,128,128]{2,1,0:T(8,128)(2,1)S(1)}, u32[]{:S(2)}, u32[]{:S(2)}) %all-to-all-start.4) | async-done | bytes 1048608 | tf_op jit(solution)/shard_map/all_to_all | solution.py:378
  185.6 2.1 shard_map.66
  187.7 6.4 %all-to-all-start.5 = ((bf16[32,128,128]{2,1,0:T(8,128)(2,1)}), bf16[32,128,128]{2,1,0:T(8,128)(2,1)S(1)}, u32[]{:S(2)}, u32[]{:S(2)}) async-start(bf16[32,128,128]{2,1,0:T(8,128)(2,1)} %get-tuple-element.90), calls=%async_computation.5 | async-start | bytes 2097152 | tf_op jit(solution)/shard_map/all_to_all | solution.py:378
  194.2 1.9 collective-permute-start.5
  196.1 3.7 %shard_map.67.local_ref = f32[16,128,128]{2,1,0:T(8,128)S(1)} custom-call(s32[3,32]{1,0:T(4,128)S(1)} %copy-done.7, bf16[16,128,128]{2,1,0:T(8,128)(2,1)} %get-tuple-element.87.state_ref, bf16[16,3,128,128]{3,2,1,0:T(8,128)(2,1)} %collective-permute-done.12.blocks_ref), custom_call_target="tpu_custom_call" | custom-call | flops 201326592 | bytes 4194304 | tf_op jit(solution)/shard_map/pallas_call | solution.py:232
  199.9 12.6 %collective-permute-done.13.blocks_ref = bf16[16,3,128,128]{3,2,1,0:T(8,128)(2,1)} collective-permute-done((bf16[16,3,128,128]{3,2,1,0:T(8,128)(2,1)}, bf16[16,3,128,128]{3,2,1,0:T(8,128)(2,1)}, u32[]{:S(2)}, u32[]{:S(2)}) %collective-permute-start.13) | collective-permute-done | bytes 1572896 | tf_op jit(solution)/shard_map/ppermute | solution.py:386
  213.0 1.2 shard_map.68
  214.3 5.9 %all-to-all-done.5.arrived_ref = bf16[32,128,128]{2,1,0:T(8,128)(2,1)S(1)} async-done(((bf16[32,128,128]{2,1,0:T(8,128)(2,1)}), bf16[32,128,128]{2,1,0:T(8,128)(2,1)S(1)}, u32[]{:S(2)}, u32[]{:S(2)}) %all-to-all-start.5) | async-done | bytes 1048608 | tf_op jit(solution)/shard_map/all_to_all | solution.py:378
  220.1 2.1 shard_map.69
  222.3 6.5 %all-to-all-start.6 = ((bf16[32,128,128]{2,1,0:T(8,128)(2,1)}), bf16[32,128,128]{2,1,0:T(8,128)(2,1)S(1)}, u32[]{:S(2)}, u32[]{:S(2)}) async-start(bf16[32,128,128]{2,1,0:T(8,128)(2,1)} %get-tuple-element.96), calls=%async_computation.6 | async-start | bytes 2097152 | tf_op jit(solution)/shard_map/all_to_all | solution.py:378
  229.0 1.9 collective-permute-start.6
  230.9 3.7 %shard_map.70.local_ref = f32[16,128,128]{2,1,0:T(8,128)S(1)} custom-call(s32[3,32]{1,0:T(4,128)S(1)} %copy-done.9, bf16[16,128,128]{2,1,0:T(8,128)(2,1)} %get-tuple-element.93.state_ref, bf16[16,3,128,128]{3,2,1,0:T(8,128)(2,1)} %collective-permute-done.13.blocks_ref), custom_call_target="tpu_custom_call" | custom-call | flops 201326592 | bytes 4194304 | tf_op jit(solution)/shard_map/pallas_call | solution.py:232
  234.7 12.6 %collective-permute-done.14.blocks_ref = bf16[16,3,128,128]{3,2,1,0:T(8,128)(2,1)S(1)} collective-permute-done((bf16[16,3,128,128]{3,2,1,0:T(8,128)(2,1)}, bf16[16,3,128,128]{3,2,1,0:T(8,128)(2,1)S(1)}, u32[]{:S(2)}, u32[]{:S(2)}) %collective-permute-start.14) | collective-permute-done | bytes 1572896 | tf_op jit(solution)/shard_map/ppermute | solution.py:386
  247.3 1.2 copy-done.12
  249.0 1.2 shard_map.71
  250.3 5.0 %all-to-all-done.6.arrived_ref = bf16[32,128,128]{2,1,0:T(8,128)(2,1)S(1)} async-done(((bf16[32,128,128]{2,1,0:T(8,128)(2,1)}), bf16[32,128,128]{2,1,0:T(8,128)(2,1)S(1)}, u32[]{:S(2)}, u32[]{:S(2)}) %all-to-all-start.6) | async-done | bytes 1048608 | tf_op jit(solution)/shard_map/all_to_all | solution.py:378
  255.3 2.1 shard_map.72
  257.4 6.4 %all-to-all-start.7 = ((bf16[32,128,128]{2,1,0:T(8,128)(2,1)}), bf16[32,128,128]{2,1,0:T(8,128)(2,1)S(1)}, u32[]{:S(2)}, u32[]{:S(2)}) async-start(bf16[32,128,128]{2,1,0:T(8,128)(2,1)} %get-tuple-element.99), calls=%async_computation.7 | async-start | bytes 2097152 | tf_op jit(solution)/shard_map/all_to_all | solution.py:378
  263.9 1.1 collective-permute-start.7
  265.0 1.3 collective-permute-done.7.table_ref
  266.9 0.7 shard_map.51.before
  267.6 3.7 %shard_map.73.local_ref = f32[16,128,128]{2,1,0:T(8,128)S(1)} custom-call(s32[3,32]{1,0:T(4,128)S(1)} %copy-done.11, bf16[16,128,128]{2,1,0:T(8,128)(2,1)} %get-tuple-element.100.state_ref, bf16[16,3,128,128]{3,2,1,0:T(8,128)(2,1)} %copy-done.12), custom_call_target="tpu_custom_call" | custom-call | flops 201326592 | bytes 4194304 | tf_op jit(solution)/shard_map/pallas_call | solution.py:232
  271.3 19.7 %all-to-all-done.7.arrived_ref = bf16[32,128,128]{2,1,0:T(8,128)(2,1)S(1)} async-done(((bf16[32,128,128]{2,1,0:T(8,128)(2,1)}), bf16[32,128,128]{2,1,0:T(8,128)(2,1)S(1)}, u32[]{:S(2)}, u32[]{:S(2)}) %all-to-all-start.7) | async-done | bytes 1048608 | tf_op jit(solution)/shard_map/all_to_all | solution.py:378
  291.5 4.3 %collective-permute-start.15 = (bf16[1,128,128]{2,1,0:T(8,128)(2,1)S(1)}, bf16[1,128,128]{2,1,0:T(8,128)(2,1)S(1)}, u32[]{:S(2)}, u32[]{:S(2)}) collective-permute-start(bf16[1,128,128]{2,1,0:T(8,128)(2,1)S(1)} %get-tuple-element.102), channel_id=1, source_target_pairs={{0,1},{1,2},{2,3},{3,4},{4,5},{5,6},{6,7},{7,8},{8,9},{9,10},{10,1... | collective-permute-start | bytes 98312 | tf_op jit(solution)/shard_map/ppermute | solution.py:390
  295.8 1.9 collective-permute-start.16
  297.7 2.0 shard_map.75
  299.7 4.0 %collective-permute-done.16.high_ref = bf16[1,128,128]{2,1,0:T(8,128)(2,1)S(1)} collective-permute-done((bf16[1,128,128]{2,1,0:T(8,128)(2,1)S(1)}, bf16[1,128,128]{2,1,0:T(8,128)(2,1)S(1)}, u32[]{:S(2)}, u32[]{:S(2)}) %collective-permute-start.16) | collective-permute-done | bytes 32800 | tf_op jit(solution)/shard_map/ppermute | solution.py:391
  303.7 0.9 shard_map.76
  (60 shorter events, 7.3 us)
Async XLA Ops:
  3.8 12.7 %copy-start.13 = (s32[1,16,3]{1,0,2:T(1,128)S(1)}, s32[1,16,3]{1,0,2:T(1,128)}, u32[]{:S(2)}) copy-start(s32[1,16,3]{1,0,2:T(1,128)} %param.5) | copy-start | bytes 580
  3.8 41.0 %all-to-all-start = ((bf16[32,144,128]{2,1,0:T(8,128)(2,1)}), bf16[32,144,128]{2,1,0:T(8,128)(2,1)S(1)}, u32[]{:S(2)}, u32[]{:S(2)}) async-start(bf16[32,144,128]{2,1,0:T(8,128)(2,1)} %get-tuple-element.57), calls=%async_computation | async-start | bytes 2359296 | tf_op jit(solution)/shard_map/all_to_all | solution.py:378
  14.8 19.9 %collective-permute-start.8 = (bf16[16,3,128,128]{3,2,1,0:T(8,128)(2,1)}, bf16[16,3,128,128]{3,2,1,0:T(8,128)(2,1)}, u32[]{:S(2)}, u32[]{:S(2)}) collective-permute-start(bf16[16,3,128,128]{3,2,1,0:T(8,128)(2,1)} %bitcast.2.blocks_ref), channel_id=1, source_target_pairs={{0,224},{32,0},{64,32},{96,64},{128,96},{160,128},{192,160},{224,1... | collective-permute-start | bytes 4718600 | tf_op jit(solution)/shard_map/ppermute | solution.py:386
  16.9 17.8 %collective-permute-start = (s32[3,32]{1,0:T(4,128)S(1)}, s32[3,32]{1,0:T(4,128)S(1)}, u32[]{:S(2)}, u32[]{:S(2)}) collective-permute-start(s32[3,32]{1,0:T(4,128)S(1)} %pad_add_fusion.table), channel_id=1, source_target_pairs={{0,224},{32,0},{64,32},{96,64},{128,96},{160,128},{192,160},{224,1... | collective-permute-start | bytes 1160 | tf_op jit(solution)/shard_map/ppermute | solution.py:380
  34.7 0.6 copy-start.14
  47.7 7.6 %slice-start = ((s32[3,32]{1,0:T(4,128)}), s32[2,32]{1,0:T(2,128)S(1)}, s32[]{:S(2)}) async-start(s32[3,32]{1,0:T(4,128)} %copy-done.14), calls=%async_computation.8 | async-start | bytes 2048 | tf_op jit(solution)/shard_map/slice | solution.py:384
  47.7 32.5 %all-to-all-start.1 = ((bf16[32,128,128]{2,1,0:T(8,128)(2,1)}), bf16[32,128,128]{2,1,0:T(8,128)(2,1)S(1)}, u32[]{:S(2)}, u32[]{:S(2)}) async-start(bf16[32,128,128]{2,1,0:T(8,128)(2,1)} %get-tuple-element.66), calls=%async_computation.1 | async-start | bytes 2097152 | tf_op jit(solution)/shard_map/all_to_all | solution.py:378
  54.2 18.7 %collective-permute-start.9 = (bf16[16,3,128,128]{3,2,1,0:T(8,128)(2,1)}, bf16[16,3,128,128]{3,2,1,0:T(8,128)(2,1)}, u32[]{:S(2)}, u32[]{:S(2)}) collective-permute-start(bf16[16,3,128,128]{3,2,1,0:T(8,128)(2,1)} %collective-permute-done.8.blocks_ref), channel_id=1, source_target_pairs={{0,224},{32,0},{64,32},{96,64},{128,96},{160,128},{192,160},{224,1... | collective-permute-start | bytes 4718600 | tf_op jit(solution)/shard_map/ppermute | solution.py:386
  55.3 17.6 %collective-permute-start.1 = (s32[3,32]{1,0:T(4,128)S(1)}, s32[3,32]{1,0:T(4,128)S(1)}, u32[]{:S(2)}, u32[]{:S(2)}) collective-permute-start(s32[3,32]{1,0:T(4,128)S(1)} %pad_add_fusion.1.table), channel_id=1, source_target_pairs={{0,224},{32,0},{64,32},{96,64},{128,96},{160,128},{192,160},{224,1... | collective-permute-start | bytes 1160 | tf_op jit(solution)/shard_map/ppermute | solution.py:380
  72.9 0.6 copy-start
  82.3 7.1 %copy-start.1 = (s32[3,32]{1,0:T(4,128)S(1)}, s32[3,32]{1,0:T(4,128)}, u32[]{:S(2)}) copy-start(s32[3,32]{1,0:T(4,128)} %copy-done) | copy-start | bytes 1156
  82.3 33.3 %all-to-all-start.2 = ((bf16[32,128,128]{2,1,0:T(8,128)(2,1)}), bf16[32,128,128]{2,1,0:T(8,128)(2,1)S(1)}, u32[]{:S(2)}, u32[]{:S(2)}) async-start(bf16[32,128,128]{2,1,0:T(8,128)(2,1)} %get-tuple-element.72), calls=%async_computation.2 | async-start | bytes 2097152 | tf_op jit(solution)/shard_map/all_to_all | solution.py:378
  88.7 18.9 %collective-permute-start.10 = (bf16[16,3,128,128]{3,2,1,0:T(8,128)(2,1)}, bf16[16,3,128,128]{3,2,1,0:T(8,128)(2,1)}, u32[]{:S(2)}, u32[]{:S(2)}) collective-permute-start(bf16[16,3,128,128]{3,2,1,0:T(8,128)(2,1)} %collective-permute-done.9.blocks_ref), channel_id=1, source_target_pairs={{0,224},{32,0},{64,32},{96,64},{128,96},{160,128},{192,160},{224,1... | collective-permute-start | bytes 4718600 | tf_op jit(solution)/shard_map/ppermute | solution.py:386
  89.4 18.3 %collective-permute-start.2 = (s32[3,32]{1,0:T(4,128)S(1)}, s32[3,32]{1,0:T(4,128)S(1)}, u32[]{:S(2)}, u32[]{:S(2)}) collective-permute-start(s32[3,32]{1,0:T(4,128)S(1)} %copy-done.1), channel_id=1, source_target_pairs={{0,224},{32,0},{64,32},{96,64},{128,96},{160,128},{192,160},{224,1... | collective-permute-start | bytes 1160 | tf_op jit(solution)/shard_map/ppermute | solution.py:380
  107.7 0.6 copy-start.2
  117.7 6.5 %copy-start.3 = (s32[3,32]{1,0:T(4,128)S(1)}, s32[3,32]{1,0:T(4,128)}, u32[]{:S(2)}) copy-start(s32[3,32]{1,0:T(4,128)} %copy-done.2) | copy-start | bytes 1156
  117.7 32.4 %all-to-all-start.3 = ((bf16[32,128,128]{2,1,0:T(8,128)(2,1)}), bf16[32,128,128]{2,1,0:T(8,128)(2,1)S(1)}, u32[]{:S(2)}, u32[]{:S(2)}) async-start(bf16[32,128,128]{2,1,0:T(8,128)(2,1)} %get-tuple-element.78), calls=%async_computation.3 | async-start | bytes 2097152 | tf_op jit(solution)/shard_map/all_to_all | solution.py:378
  124.2 18.3 %collective-permute-start.11 = (bf16[16,3,128,128]{3,2,1,0:T(8,128)(2,1)}, bf16[16,3,128,128]{3,2,1,0:T(8,128)(2,1)}, u32[]{:S(2)}, u32[]{:S(2)}) collective-permute-start(bf16[16,3,128,128]{3,2,1,0:T(8,128)(2,1)} %collective-permute-done.10.blocks_ref), channel_id=1, source_target_pairs={{0,224},{32,0},{64,32},{96,64},{128,96},{160,128},{192,160},{224,1... | collective-permute-start | bytes 4718600 | tf_op jit(solution)/shard_map/ppermute | solution.py:386
  124.2 18.3 %collective-permute-start.3 = (s32[3,32]{1,0:T(4,128)S(1)}, s32[3,32]{1,0:T(4,128)S(1)}, u32[]{:S(2)}, u32[]{:S(2)}) collective-permute-start(s32[3,32]{1,0:T(4,128)S(1)} %copy-done.3), channel_id=1, source_target_pairs={{0,224},{32,0},{64,32},{96,64},{128,96},{160,128},{192,160},{224,1... | collective-permute-start | bytes 1160 | tf_op jit(solution)/shard_map/ppermute | solution.py:380
  142.5 0.6 copy-start.4
  152.3 6.8 %copy-start.5 = (s32[3,32]{1,0:T(4,128)S(1)}, s32[3,32]{1,0:T(4,128)}, u32[]{:S(2)}) copy-start(s32[3,32]{1,0:T(4,128)} %copy-done.4) | copy-start | bytes 1156
  152.3 33.3 %all-to-all-start.4 = ((bf16[32,128,128]{2,1,0:T(8,128)(2,1)}), bf16[32,128,128]{2,1,0:T(8,128)(2,1)S(1)}, u32[]{:S(2)}, u32[]{:S(2)}) async-start(bf16[32,128,128]{2,1,0:T(8,128)(2,1)} %get-tuple-element.84), calls=%async_computation.4 | async-start | bytes 2097152 | tf_op jit(solution)/shard_map/all_to_all | solution.py:378
  158.7 18.6 %collective-permute-start.12 = (bf16[16,3,128,128]{3,2,1,0:T(8,128)(2,1)}, bf16[16,3,128,128]{3,2,1,0:T(8,128)(2,1)}, u32[]{:S(2)}, u32[]{:S(2)}) collective-permute-start(bf16[16,3,128,128]{3,2,1,0:T(8,128)(2,1)} %collective-permute-done.11.blocks_ref), channel_id=1, source_target_pairs={{0,224},{32,0},{64,32},{96,64},{128,96},{160,128},{192,160},{224,1... | collective-permute-start | bytes 4718600 | tf_op jit(solution)/shard_map/ppermute | solution.py:386
  159.1 18.3 %collective-permute-start.4 = (s32[3,32]{1,0:T(4,128)S(1)}, s32[3,32]{1,0:T(4,128)S(1)}, u32[]{:S(2)}, u32[]{:S(2)}) collective-permute-start(s32[3,32]{1,0:T(4,128)S(1)} %copy-done.5), channel_id=1, source_target_pairs={{0,224},{32,0},{64,32},{96,64},{128,96},{160,128},{192,160},{224,1... | collective-permute-start | bytes 1160 | tf_op jit(solution)/shard_map/ppermute | solution.py:380
  177.3 0.6 copy-start.6
  187.7 6.5 %copy-start.7 = (s32[3,32]{1,0:T(4,128)S(1)}, s32[3,32]{1,0:T(4,128)}, u32[]{:S(2)}) copy-start(s32[3,32]{1,0:T(4,128)} %copy-done.6) | copy-start | bytes 1156
  187.7 32.4 %all-to-all-start.5 = ((bf16[32,128,128]{2,1,0:T(8,128)(2,1)}), bf16[32,128,128]{2,1,0:T(8,128)(2,1)S(1)}, u32[]{:S(2)}, u32[]{:S(2)}) async-start(bf16[32,128,128]{2,1,0:T(8,128)(2,1)} %get-tuple-element.90), calls=%async_computation.5 | async-start | bytes 2097152 | tf_op jit(solution)/shard_map/all_to_all | solution.py:378
  194.2 18.3 %collective-permute-start.13 = (bf16[16,3,128,128]{3,2,1,0:T(8,128)(2,1)}, bf16[16,3,128,128]{3,2,1,0:T(8,128)(2,1)}, u32[]{:S(2)}, u32[]{:S(2)}) collective-permute-start(bf16[16,3,128,128]{3,2,1,0:T(8,128)(2,1)} %collective-permute-done.12.blocks_ref), channel_id=1, source_target_pairs={{0,224},{32,0},{64,32},{96,64},{128,96},{160,128},{192,160},{224,1... | collective-permute-start | bytes 4718600 | tf_op jit(solution)/shard_map/ppermute | solution.py:386
  194.2 18.2 %collective-permute-start.5 = (s32[3,32]{1,0:T(4,128)S(1)}, s32[3,32]{1,0:T(4,128)S(1)}, u32[]{:S(2)}, u32[]{:S(2)}) collective-permute-start(s32[3,32]{1,0:T(4,128)S(1)} %copy-done.7), channel_id=1, source_target_pairs={{0,224},{32,0},{64,32},{96,64},{128,96},{160,128},{192,160},{224,1... | collective-permute-start | bytes 1160 | tf_op jit(solution)/shard_map/ppermute | solution.py:380
  212.4 0.6 copy-start.8
  222.3 6.7 %copy-start.9 = (s32[3,32]{1,0:T(4,128)S(1)}, s32[3,32]{1,0:T(4,128)}, u32[]{:S(2)}) copy-start(s32[3,32]{1,0:T(4,128)} %copy-done.8) | copy-start | bytes 1156
  222.3 33.0 %all-to-all-start.6 = ((bf16[32,128,128]{2,1,0:T(8,128)(2,1)}), bf16[32,128,128]{2,1,0:T(8,128)(2,1)S(1)}, u32[]{:S(2)}, u32[]{:S(2)}) async-start(bf16[32,128,128]{2,1,0:T(8,128)(2,1)} %get-tuple-element.96), calls=%async_computation.6 | async-start | bytes 2097152 | tf_op jit(solution)/shard_map/all_to_all | solution.py:378
  228.7 18.5 %collective-permute-start.14 = (bf16[16,3,128,128]{3,2,1,0:T(8,128)(2,1)}, bf16[16,3,128,128]{3,2,1,0:T(8,128)(2,1)S(1)}, u32[]{:S(2)}, u32[]{:S(2)}) collective-permute-start(bf16[16,3,128,128]{3,2,1,0:T(8,128)(2,1)} %collective-permute-done.13.blocks_ref), channel_id=1, source_target_pairs={{0,224},{32,0},{64,32},{96,64},{128,96},{160,128},{192,160},{224,1... | collective-permute-start | bytes 4718600 | tf_op jit(solution)/shard_map/ppermute | solution.py:386
  229.0 18.3 %collective-permute-start.6 = (s32[3,32]{1,0:T(4,128)S(1)}, s32[3,32]{1,0:T(4,128)S(1)}, u32[]{:S(2)}, u32[]{:S(2)}) collective-permute-start(s32[3,32]{1,0:T(4,128)S(1)} %copy-done.9), channel_id=1, source_target_pairs={{0,224},{32,0},{64,32},{96,64},{128,96},{160,128},{192,160},{224,1... | collective-permute-start | bytes 1160 | tf_op jit(solution)/shard_map/ppermute | solution.py:380
  247.3 1.2 copy-start.12
  248.4 0.6 copy-start.10
  257.4 6.5 %copy-start.11 = (s32[3,32]{1,0:T(4,128)S(1)}, s32[3,32]{1,0:T(4,128)}, u32[]{:S(2)}) copy-start(s32[3,32]{1,0:T(4,128)} %copy-done.10) | copy-start | bytes 1156
  257.4 33.6 %all-to-all-start.7 = ((bf16[32,128,128]{2,1,0:T(8,128)(2,1)}), bf16[32,128,128]{2,1,0:T(8,128)(2,1)S(1)}, u32[]{:S(2)}, u32[]{:S(2)}) async-start(bf16[32,128,128]{2,1,0:T(8,128)(2,1)} %get-tuple-element.99), calls=%async_computation.7 | async-start | bytes 2097152 | tf_op jit(solution)/shard_map/all_to_all | solution.py:378
  263.9 2.4 collective-permute-start.7
  266.3 0.6 copy-start.15
  291.5 8.3 %collective-permute-start.15 = (bf16[1,128,128]{2,1,0:T(8,128)(2,1)S(1)}, bf16[1,128,128]{2,1,0:T(8,128)(2,1)S(1)}, u32[]{:S(2)}, u32[]{:S(2)}) collective-permute-start(bf16[1,128,128]{2,1,0:T(8,128)(2,1)S(1)} %get-tuple-element.102), channel_id=1, source_target_pairs={{0,1},{1,2},{2,3},{3,4},{4,5},{5,6},{6,7},{7,8},{8,9},{9,10},{10,1... | collective-permute-start | bytes 98312 | tf_op jit(solution)/shard_map/ppermute | solution.py:390
  295.8 7.9 %collective-permute-start.16 = (bf16[1,128,128]{2,1,0:T(8,128)(2,1)S(1)}, bf16[1,128,128]{2,1,0:T(8,128)(2,1)S(1)}, u32[]{:S(2)}, u32[]{:S(2)}) collective-permute-start(bf16[1,128,128]{2,1,0:T(8,128)(2,1)S(1)} %get-tuple-element.103), channel_id=1, source_target_pairs={{1,0},{2,1},{3,2},{4,3},{5,4},{6,5},{7,6},{8,7},{9,8},{10,9},{11,1... | collective-permute-start | bytes 98312 | tf_op jit(solution)/shard_map/ppermute | solution.py:391

commit v8 on v7

--- a/solution.py
+++ b/solution.py
@@ -15,7 +15,7 @@
 SMALL = pltpu.CompilerParams(vmem_limit_bytes=16 * 1024 * 1024)
 PART = 4
 SAYS = 16
-WANTED, HOME, LANDED = range(3)
+SLOT, HOME, LANDED = range(3)
 
 
 def shifted(n, by):
@@ -177,7 +177,18 @@
         state_scr[t] = (gathered[t] + local_ref[t]).astype(jnp.bfloat16)
     store = pltpu.make_async_copy(state_scr, state_ref, store_sem)
     store.start()
-    send_products(lambda p: table[WANTED, p], off_ref, state_scr, out_ref, stage, out_sems)
+    each, points = off_ref.shape[1:3]
+    copies = []
+    for t in range(state_scr.shape[0]):
+        both = product(state_scr[t], off_ref[t].reshape(each * points, off_ref.shape[3])).astype(jnp.bfloat16)
+        for k in range(each):
+            n = t * each + k
+            stage[n] = both[:, k * points : (k + 1) * points]
+            copy = pltpu.make_async_copy(stage.at[n], out_ref.at[table[SLOT, n]], out_sems.at[n])
+            copy.start()
+            copies.append(copy)
+    for copy in copies:
+        copy.wait()
     store.wait()
 
 
@@ -203,7 +214,7 @@
             pltpu.VMEM((tiles + 1, rows, points), jnp.float32),
             pltpu.VMEM((tiles, rows, points), jnp.bfloat16),
             pltpu.SemaphoreType.DMA,
-            pltpu.SemaphoreType.DMA((peers // PART,)),
+            pltpu.SemaphoreType.DMA((peers,)),
             *told,
         ],
         compiler_params=SEND,
@@ -351,11 +362,17 @@
 
 def own_rows(dest, me, tiles, peers, nnz):
     off = dest[:, 1:].reshape(tiles * (nnz - 1))
+    dev = off // tiles
+    stays = dev == me
+    home = jnp.where(stays, off % tiles, tiles)
     peer = jnp.arange(peers, dtype=jnp.int32)
-    order = jnp.arange(tiles * (nnz - 1), dtype=jnp.int32)
-    wanted = jnp.max(jnp.where(off[None, :] // tiles == peer[:, None], order, 0), axis=1)
-    home = jnp.where(off // tiles == me, off % tiles, tiles)
-    return wanted, home
+    order = jnp.arange(off.shape[0], dtype=jnp.int32)
+    free = jnp.logical_not(jnp.any((dev[None, :] == peer[:, None]) & jnp.logical_not(stays)[None, :], axis=1))
+    stayed = jnp.sum(jnp.where(order[None, :] < order[:, None], stays[None, :], False).astype(jnp.int32), axis=1)
+    frees = jnp.sum(jnp.where(peer[None, :] < peer[:, None], free[None, :], False).astype(jnp.int32), axis=1)
+    taken = (stayed[:, None] == frees[None, :]) & free[None, :]
+    slot = jnp.where(stays, jnp.sum(jnp.where(taken, peer[None, :], 0), axis=1), dev)
+    return slot, home
 
 
 def body(seeds, blocks, dest_tiles):

time: 307 us -> 305 us (level)
  no operation moved by 1% of the time
where the time goes in v8:
time: 305 us; the launch traced here: 303 us
  waiting for transfers between devices  154 us (50%)
  starting transfers between devices  81.1 us (27%)
  Pallas kernels  60.1 us (20%)
  local copies, waits for them, and re-layouts  6.12 us (2%)
    ppermute x7, waiting for transfers between devices, body(): wblk = onward(wblk)  85.8 us
    all_to_all x8, waiting for transfers between devices, body(): lax.all_to_all(out, 'tile', split_axis=0, concat_axis=0, tiled=True)  62.5 us
    all_to_all x8, starting transfers between devices, body(): lax.all_to_all(out, 'tile', split_axis=0, concat_axis=0, tiled=True)  56.2 us
    pallas_call x8, Pallas kernels, keep(): pl.pallas_call(keep_body, out_shape=pltpu.VMEM((tiles, rows, points), jnp...  30 us
    ppermute x8, starting transfers between devices, body(): given = table = onward(table)  15.3 us
    pallas_call x7, Pallas kernels, send(): pl.pallas_call(send_body, out_shape=(pltpu.HBM((peers, rows, points), jnp...  14.3 us
    pallas_call x7, Pallas kernels, fetch(): pl.pallas_call(fetch_body, out_shape=(pltpu.VMEM((tiles, nnz - 1, points,...  8.75 us
  transfers between devices with their start and end apart: 25, of which 17 were waited for; matrix products, arithmetic and copies ran while one was open for 0% of the time, Pallas kernels for 14%

profile of v8, /device:TPU:56, one launch (start us, length us, event | category | flops | bytes accessed | tf_op | source)
XLA Modules:
  0.0 303.4 jit_solution(4697388644860790683)
XLA Ops:
  0.6 3.1 %shard_map.50 = (bf16[32,144,128]{2,1,0:T(8,128)(2,1)}, bf16[16,128,128]{2,1,0:T(8,128)(2,1)}) custom-call(s32[3,1,16]{2,1,0:T(1,128)} %bitcast.15, bf16[16,128,128]{2,1,0:T(8,128)(2,1)} %bitcast.14, bf16[16,3,128,128]{3,2,1,0:T(8,128)(2,1)} %bitcast.2.blocks_ref), custom_call_target="tpu_custom_call" | custom-call | flops 134217728 | bytes 4194304 | tf_op jit(solution)/shard_map/pallas_call | solution.py:95
  3.8 11.0 %all-to-all-start = ((bf16[32,144,128]{2,1,0:T(8,128)(2,1)}), bf16[32,144,128]{2,1,0:T(8,128)(2,1)S(1)}, u32[]{:S(2)}, u32[]{:S(2)}) async-start(bf16[32,144,128]{2,1,0:T(8,128)(2,1)} %get-tuple-element.57), calls=%async_computation | async-start | bytes 2359296 | tf_op jit(solution)/shard_map/all_to_all | solution.py:395
  14.8 1.6 collective-permute-start.8
  17.3 1.2 collective-permute-start
  18.5 3.7 %shard_map.52.local_ref = f32[16,128,128]{2,1,0:T(8,128)S(1)} custom-call(s32[3,32]{1,0:T(4,128)S(1)} %pad_add_fusion.table, bf16[16,128,128]{2,1,0:T(8,128)(2,1)} %get-tuple-element.58.state_ref, bf16[16,3,128,128]{3,2,1,0:T(8,128)(2,1)} %bitcast.2.blocks_ref), custom_call_target="tpu_custom_call" | custom-call | flops 201326592 | bytes 4194304 | tf_op jit(solution)/shard_map/pallas_call | solution.py:243
  22.3 12.4 %collective-permute-done.8.blocks_ref = bf16[16,3,128,128]{3,2,1,0:T(8,128)(2,1)} collective-permute-done((bf16[16,3,128,128]{3,2,1,0:T(8,128)(2,1)}, bf16[16,3,128,128]{3,2,1,0:T(8,128)(2,1)}, u32[]{:S(2)}, u32[]{:S(2)}) %collective-permute-start.8) | collective-permute-done | bytes 1572896 | tf_op jit(solution)/shard_map/ppermute | solution.py:403
  35.3 1.2 shard_map.53
  36.6 8.3 %all-to-all-done.arrived_ref = bf16[32,144,128]{2,1,0:T(8,128)(2,1)S(1)} async-done(((bf16[32,144,128]{2,1,0:T(8,128)(2,1)}), bf16[32,144,128]{2,1,0:T(8,128)(2,1)S(1)}, u32[]{:S(2)}, u32[]{:S(2)}) %all-to-all-start) | async-done | bytes 1179680 | tf_op jit(solution)/shard_map/all_to_all | solution.py:395
  44.8 2.7 shard_map.54
  47.6 6.4 %all-to-all-start.1 = ((bf16[32,128,128]{2,1,0:T(8,128)(2,1)}), bf16[32,128,128]{2,1,0:T(8,128)(2,1)S(1)}, u32[]{:S(2)}, u32[]{:S(2)}) async-start(bf16[32,128,128]{2,1,0:T(8,128)(2,1)} %get-tuple-element.66), calls=%async_computation.1 | async-start | bytes 2097152 | tf_op jit(solution)/shard_map/all_to_all | solution.py:395
  55.2 2.5 collective-permute-start.1
  57.6 3.7 %shard_map.55.local_ref = f32[16,128,128]{2,1,0:T(8,128)S(1)} custom-call(s32[3,32]{1,0:T(4,128)S(1)} %pad_add_fusion.1.table, bf16[16,128,128]{2,1,0:T(8,128)(2,1)} %get-tuple-element.63.state_ref, bf16[16,3,128,128]{3,2,1,0:T(8,128)(2,1)} %collective-permute-done.8.blocks_ref), custom_call_target="tpu_custom_call" | custom-call | flops 201326592 | bytes 4194304 | tf_op jit(solution)/shard_map/pallas_call | solution.py:243
  61.4 11.3 %collective-permute-done.9.blocks_ref = bf16[16,3,128,128]{3,2,1,0:T(8,128)(2,1)} collective-permute-done((bf16[16,3,128,128]{3,2,1,0:T(8,128)(2,1)}, bf16[16,3,128,128]{3,2,1,0:T(8,128)(2,1)}, u32[]{:S(2)}, u32[]{:S(2)}) %collective-permute-start.9) | collective-permute-done | bytes 1572896 | tf_op jit(solution)/shard_map/ppermute | solution.py:403
  73.3 1.2 shard_map.56
  74.5 5.5 %all-to-all-done.1.arrived_ref = bf16[32,128,128]{2,1,0:T(8,128)(2,1)S(1)} async-done(((bf16[32,128,128]{2,1,0:T(8,128)(2,1)}), bf16[32,128,128]{2,1,0:T(8,128)(2,1)S(1)}, u32[]{:S(2)}, u32[]{:S(2)}) %all-to-all-start.1) | async-done | bytes 1048608 | tf_op jit(solution)/shard_map/all_to_all | solution.py:395
  80.0 1.9 shard_map.57
  81.9 6.5 %all-to-all-start.2 = ((bf16[32,128,128]{2,1,0:T(8,128)(2,1)}), bf16[32,128,128]{2,1,0:T(8,128)(2,1)S(1)}, u32[]{:S(2)}, u32[]{:S(2)}) async-start(bf16[32,128,128]{2,1,0:T(8,128)(2,1)} %get-tuple-element.72), calls=%async_computation.2 | async-start | bytes 2097152 | tf_op jit(solution)/shard_map/all_to_all | solution.py:395
  88.4 0.7 collective-permute-start.10
  89.1 2.2 collective-permute-start.2
  91.3 3.7 %shard_map.58.local_ref = f32[16,128,128]{2,1,0:T(8,128)S(1)} custom-call(s32[3,32]{1,0:T(4,128)S(1)} %copy-done.1, bf16[16,128,128]{2,1,0:T(8,128)(2,1)} %get-tuple-element.69.state_ref, bf16[16,3,128,128]{3,2,1,0:T(8,128)(2,1)} %collective-permute-done.9.blocks_ref), custom_call_target="tpu_custom_call" | custom-call | flops 201326592 | bytes 4194304 | tf_op jit(solution)/shard_map/pallas_call | solution.py:243
  95.0 12.3 %collective-permute-done.10.blocks_ref = bf16[16,3,128,128]{3,2,1,0:T(8,128)(2,1)} collective-permute-done((bf16[16,3,128,128]{3,2,1,0:T(8,128)(2,1)}, bf16[16,3,128,128]{3,2,1,0:T(8,128)(2,1)}, u32[]{:S(2)}, u32[]{:S(2)}) %collective-permute-start.10) | collective-permute-done | bytes 1572896 | tf_op jit(solution)/shard_map/ppermute | solution.py:403
  107.9 1.2 shard_map.59
  109.2 6.1 %all-to-all-done.2.arrived_ref = bf16[32,128,128]{2,1,0:T(8,128)(2,1)S(1)} async-done(((bf16[32,128,128]{2,1,0:T(8,128)(2,1)}), bf16[32,128,128]{2,1,0:T(8,128)(2,1)S(1)}, u32[]{:S(2)}, u32[]{:S(2)}) %all-to-all-start.2) | async-done | bytes 1048608 | tf_op jit(solution)/shard_map/all_to_all | solution.py:395
  115.2 1.9 shard_map.60
  117.2 6.5 %all-to-all-start.3 = ((bf16[32,128,128]{2,1,0:T(8,128)(2,1)}), bf16[32,128,128]{2,1,0:T(8,128)(2,1)S(1)}, u32[]{:S(2)}, u32[]{:S(2)}) async-start(bf16[32,128,128]{2,1,0:T(8,128)(2,1)} %get-tuple-element.78), calls=%async_computation.3 | async-start | bytes 2097152 | tf_op jit(solution)/shard_map/all_to_all | solution.py:395
  123.7 2.2 collective-permute-start.3
  125.9 3.7 %shard_map.61.local_ref = f32[16,128,128]{2,1,0:T(8,128)S(1)} custom-call(s32[3,32]{1,0:T(4,128)S(1)} %copy-done.3, bf16[16,128,128]{2,1,0:T(8,128)(2,1)} %get-tuple-element.75.state_ref, bf16[16,3,128,128]{3,2,1,0:T(8,128)(2,1)} %collective-permute-done.10.blocks_ref), custom_call_target="tpu_custom_call" | custom-call | flops 201326592 | bytes 4194304 | tf_op jit(solution)/shard_map/pallas_call | solution.py:243
  129.7 12.3 %collective-permute-done.11.blocks_ref = bf16[16,3,128,128]{3,2,1,0:T(8,128)(2,1)} collective-permute-done((bf16[16,3,128,128]{3,2,1,0:T(8,128)(2,1)}, bf16[16,3,128,128]{3,2,1,0:T(8,128)(2,1)}, u32[]{:S(2)}, u32[]{:S(2)}) %collective-permute-start.11) | collective-permute-done | bytes 1572896 | tf_op jit(solution)/shard_map/ppermute | solution.py:403
  142.5 1.2 shard_map.62
  143.8 5.8 %all-to-all-done.3.arrived_ref = bf16[32,128,128]{2,1,0:T(8,128)(2,1)S(1)} async-done(((bf16[32,128,128]{2,1,0:T(8,128)(2,1)}), bf16[32,128,128]{2,1,0:T(8,128)(2,1)S(1)}, u32[]{:S(2)}, u32[]{:S(2)}) %all-to-all-start.3) | async-done | bytes 1048608 | tf_op jit(solution)/shard_map/all_to_all | solution.py:395
  149.6 1.9 shard_map.63
  151.6 6.5 %all-to-all-start.4 = ((bf16[32,128,128]{2,1,0:T(8,128)(2,1)}), bf16[32,128,128]{2,1,0:T(8,128)(2,1)S(1)}, u32[]{:S(2)}, u32[]{:S(2)}) async-start(bf16[32,128,128]{2,1,0:T(8,128)(2,1)} %get-tuple-element.84), calls=%async_computation.4 | async-start | bytes 2097152 | tf_op jit(solution)/shard_map/all_to_all | solution.py:395
  158.4 2.2 collective-permute-start.4
  160.6 3.8 %shard_map.64.local_ref = f32[16,128,128]{2,1,0:T(8,128)S(1)} custom-call(s32[3,32]{1,0:T(4,128)S(1)} %copy-done.5, bf16[16,128,128]{2,1,0:T(8,128)(2,1)} %get-tuple-element.81.state_ref, bf16[16,3,128,128]{3,2,1,0:T(8,128)(2,1)} %collective-permute-done.11.blocks_ref), custom_call_target="tpu_custom_call" | custom-call | flops 201326592 | bytes 4194304 | tf_op jit(solution)/shard_map/pallas_call | solution.py:243
  164.3 12.3 %collective-permute-done.12.blocks_ref = bf16[16,3,128,128]{3,2,1,0:T(8,128)(2,1)} collective-permute-done((bf16[16,3,128,128]{3,2,1,0:T(8,128)(2,1)}, bf16[16,3,128,128]{3,2,1,0:T(8,128)(2,1)}, u32[]{:S(2)}, u32[]{:S(2)}) %collective-permute-start.12) | collective-permute-done | bytes 1572896 | tf_op jit(solution)/shard_map/ppermute | solution.py:403
  177.2 1.2 shard_map.65
  178.4 6.4 %all-to-all-done.4.arrived_ref = bf16[32,128,128]{2,1,0:T(8,128)(2,1)S(1)} async-done(((bf16[32,128,128]{2,1,0:T(8,128)(2,1)}), bf16[32,128,128]{2,1,0:T(8,128)(2,1)S(1)}, u32[]{:S(2)}, u32[]{:S(2)}) %all-to-all-start.4) | async-done | bytes 1048608 | tf_op jit(solution)/shard_map/all_to_all | solution.py:395
  184.9 1.9 shard_map.66
  186.8 6.5 %all-to-all-start.5 = ((bf16[32,128,128]{2,1,0:T(8,128)(2,1)}), bf16[32,128,128]{2,1,0:T(8,128)(2,1)S(1)}, u32[]{:S(2)}, u32[]{:S(2)}) async-start(bf16[32,128,128]{2,1,0:T(8,128)(2,1)} %get-tuple-element.90), calls=%async_computation.5 | async-start | bytes 2097152 | tf_op jit(solution)/shard_map/all_to_all | solution.py:395
  193.3 1.9 collective-permute-start.5
  195.2 3.7 %shard_map.67.local_ref = f32[16,128,128]{2,1,0:T(8,128)S(1)} custom-call(s32[3,32]{1,0:T(4,128)S(1)} %copy-done.7, bf16[16,128,128]{2,1,0:T(8,128)(2,1)} %get-tuple-element.87.state_ref, bf16[16,3,128,128]{3,2,1,0:T(8,128)(2,1)} %collective-permute-done.12.blocks_ref), custom_call_target="tpu_custom_call" | custom-call | flops 201326592 | bytes 4194304 | tf_op jit(solution)/shard_map/pallas_call | solution.py:243
  199.0 12.6 %collective-permute-done.13.blocks_ref = bf16[16,3,128,128]{3,2,1,0:T(8,128)(2,1)} collective-permute-done((bf16[16,3,128,128]{3,2,1,0:T(8,128)(2,1)}, bf16[16,3,128,128]{3,2,1,0:T(8,128)(2,1)}, u32[]{:S(2)}, u32[]{:S(2)}) %collective-permute-start.13) | collective-permute-done | bytes 1572896 | tf_op jit(solution)/shard_map/ppermute | solution.py:403
  212.1 1.2 shard_map.68
  213.4 5.9 %all-to-all-done.5.arrived_ref = bf16[32,128,128]{2,1,0:T(8,128)(2,1)S(1)} async-done(((bf16[32,128,128]{2,1,0:T(8,128)(2,1)}), bf16[32,128,128]{2,1,0:T(8,128)(2,1)S(1)}, u32[]{:S(2)}, u32[]{:S(2)}) %all-to-all-start.5) | async-done | bytes 1048608 | tf_op jit(solution)/shard_map/all_to_all | solution.py:395
  219.3 1.9 shard_map.69
  221.2 6.4 %all-to-all-start.6 = ((bf16[32,128,128]{2,1,0:T(8,128)(2,1)}), bf16[32,128,128]{2,1,0:T(8,128)(2,1)S(1)}, u32[]{:S(2)}, u32[]{:S(2)}) async-start(bf16[32,128,128]{2,1,0:T(8,128)(2,1)} %get-tuple-element.96), calls=%async_computation.6 | async-start | bytes 2097152 | tf_op jit(solution)/shard_map/all_to_all | solution.py:395
  227.9 1.9 collective-permute-start.6
  229.8 3.7 %shard_map.70.local_ref = f32[16,128,128]{2,1,0:T(8,128)S(1)} custom-call(s32[3,32]{1,0:T(4,128)S(1)} %copy-done.9, bf16[16,128,128]{2,1,0:T(8,128)(2,1)} %get-tuple-element.93.state_ref, bf16[16,3,128,128]{3,2,1,0:T(8,128)(2,1)} %collective-permute-done.13.blocks_ref), custom_call_target="tpu_custom_call" | custom-call | flops 201326592 | bytes 4194304 | tf_op jit(solution)/shard_map/pallas_call | solution.py:243
  233.6 12.6 %collective-permute-done.14.blocks_ref = bf16[16,3,128,128]{3,2,1,0:T(8,128)(2,1)S(1)} collective-permute-done((bf16[16,3,128,128]{3,2,1,0:T(8,128)(2,1)}, bf16[16,3,128,128]{3,2,1,0:T(8,128)(2,1)S(1)}, u32[]{:S(2)}, u32[]{:S(2)}) %collective-permute-start.14) | collective-permute-done | bytes 1572896 | tf_op jit(solution)/shard_map/ppermute | solution.py:403
  246.2 1.2 copy-done.12
  247.9 1.2 shard_map.71
  249.2 5.0 %all-to-all-done.6.arrived_ref = bf16[32,128,128]{2,1,0:T(8,128)(2,1)S(1)} async-done(((bf16[32,128,128]{2,1,0:T(8,128)(2,1)}), bf16[32,128,128]{2,1,0:T(8,128)(2,1)S(1)}, u32[]{:S(2)}, u32[]{:S(2)}) %all-to-all-start.6) | async-done | bytes 1048608 | tf_op jit(solution)/shard_map/all_to_all | solution.py:395
  254.2 1.9 shard_map.72
  256.1 6.4 %all-to-all-start.7 = ((bf16[32,128,128]{2,1,0:T(8,128)(2,1)}), bf16[32,128,128]{2,1,0:T(8,128)(2,1)S(1)}, u32[]{:S(2)}, u32[]{:S(2)}) async-start(bf16[32,128,128]{2,1,0:T(8,128)(2,1)} %get-tuple-element.99), calls=%async_computation.7 | async-start | bytes 2097152 | tf_op jit(solution)/shard_map/all_to_all | solution.py:395
  262.6 1.1 collective-permute-start.7
  263.7 1.3 collective-permute-done.7.table_ref
  265.6 0.7 shard_map.51.before
  266.3 3.8 %shard_map.73.local_ref = f32[16,128,128]{2,1,0:T(8,128)S(1)} custom-call(s32[3,32]{1,0:T(4,128)S(1)} %copy-done.11, bf16[16,128,128]{2,1,0:T(8,128)(2,1)} %get-tuple-element.100.state_ref, bf16[16,3,128,128]{3,2,1,0:T(8,128)(2,1)} %copy-done.12), custom_call_target="tpu_custom_call" | custom-call | flops 201326592 | bytes 4194304 | tf_op jit(solution)/shard_map/pallas_call | solution.py:243
  270.1 19.6 %all-to-all-done.7.arrived_ref = bf16[32,128,128]{2,1,0:T(8,128)(2,1)S(1)} async-done(((bf16[32,128,128]{2,1,0:T(8,128)(2,1)}), bf16[32,128,128]{2,1,0:T(8,128)(2,1)S(1)}, u32[]{:S(2)}, u32[]{:S(2)}) %all-to-all-start.7) | async-done | bytes 1048608 | tf_op jit(solution)/shard_map/all_to_all | solution.py:395
  290.1 4.3 %collective-permute-start.15 = (bf16[1,128,128]{2,1,0:T(8,128)(2,1)S(1)}, bf16[1,128,128]{2,1,0:T(8,128)(2,1)S(1)}, u32[]{:S(2)}, u32[]{:S(2)}) collective-permute-start(bf16[1,128,128]{2,1,0:T(8,128)(2,1)S(1)} %get-tuple-element.102), channel_id=1, source_target_pairs={{0,1},{1,2},{2,3},{3,4},{4,5},{5,6},{6,7},{7,8},{8,9},{9,10},{10,1... | collective-permute-start | bytes 98312 | tf_op jit(solution)/shard_map/ppermute | solution.py:407
  294.5 1.9 collective-permute-start.16
  296.4 2.0 shard_map.75
  298.4 4.0 %collective-permute-done.16.high_ref = bf16[1,128,128]{2,1,0:T(8,128)(2,1)S(1)} collective-permute-done((bf16[1,128,128]{2,1,0:T(8,128)(2,1)S(1)}, bf16[1,128,128]{2,1,0:T(8,128)(2,1)S(1)}, u32[]{:S(2)}, u32[]{:S(2)}) %collective-permute-start.16) | collective-permute-done | bytes 32800 | tf_op jit(solution)/shard_map/ppermute | solution.py:408
  302.4 0.9 shard_map.76
  (64 shorter events, 7.6 us)
Async XLA Ops:
  3.8 12.7 %copy-start.13 = (s32[1,16,3]{1,0,2:T(1,128)S(1)}, s32[1,16,3]{1,0,2:T(1,128)}, u32[]{:S(2)}) copy-start(s32[1,16,3]{1,0,2:T(1,128)} %param.5) | copy-start | bytes 580
  3.8 41.0 %all-to-all-start = ((bf16[32,144,128]{2,1,0:T(8,128)(2,1)}), bf16[32,144,128]{2,1,0:T(8,128)(2,1)S(1)}, u32[]{:S(2)}, u32[]{:S(2)}) async-start(bf16[32,144,128]{2,1,0:T(8,128)(2,1)} %get-tuple-element.57), calls=%async_computation | async-start | bytes 2359296 | tf_op jit(solution)/shard_map/all_to_all | solution.py:395
  14.8 19.9 %collective-permute-start.8 = (bf16[16,3,128,128]{3,2,1,0:T(8,128)(2,1)}, bf16[16,3,128,128]{3,2,1,0:T(8,128)(2,1)}, u32[]{:S(2)}, u32[]{:S(2)}) collective-permute-start(bf16[16,3,128,128]{3,2,1,0:T(8,128)(2,1)} %bitcast.2.blocks_ref), channel_id=1, source_target_pairs={{0,224},{32,0},{64,32},{96,64},{128,96},{160,128},{192,160},{224,1... | collective-permute-start | bytes 4718600 | tf_op jit(solution)/shard_map/ppermute | solution.py:403
  17.3 17.5 %collective-permute-start = (s32[3,32]{1,0:T(4,128)S(1)}, s32[3,32]{1,0:T(4,128)S(1)}, u32[]{:S(2)}, u32[]{:S(2)}) collective-permute-start(s32[3,32]{1,0:T(4,128)S(1)} %pad_add_fusion.table), channel_id=1, source_target_pairs={{0,224},{32,0},{64,32},{96,64},{128,96},{160,128},{192,160},{224,1... | collective-permute-start | bytes 1160 | tf_op jit(solution)/shard_map/ppermute | solution.py:397
  34.7 0.6 copy-start.14
  47.6 7.6 %slice-start = ((s32[3,32]{1,0:T(4,128)}), s32[2,32]{1,0:T(2,128)S(1)}, s32[]{:S(2)}) async-start(s32[3,32]{1,0:T(4,128)} %copy-done.14), calls=%async_computation.8 | async-start | bytes 2048 | tf_op jit(solution)/shard_map/slice | solution.py:401
  47.6 32.4 %all-to-all-start.1 = ((bf16[32,128,128]{2,1,0:T(8,128)(2,1)}), bf16[32,128,128]{2,1,0:T(8,128)(2,1)S(1)}, u32[]{:S(2)}, u32[]{:S(2)}) async-start(bf16[32,128,128]{2,1,0:T(8,128)(2,1)} %get-tuple-element.66), calls=%async_computation.1 | async-start | bytes 2097152 | tf_op jit(solution)/shard_map/all_to_all | solution.py:395
  54.0 18.7 %collective-permute-start.9 = (bf16[16,3,128,128]{3,2,1,0:T(8,128)(2,1)}, bf16[16,3,128,128]{3,2,1,0:T(8,128)(2,1)}, u32[]{:S(2)}, u32[]{:S(2)}) collective-permute-start(bf16[16,3,128,128]{3,2,1,0:T(8,128)(2,1)} %collective-permute-done.8.blocks_ref), channel_id=1, source_target_pairs={{0,224},{32,0},{64,32},{96,64},{128,96},{160,128},{192,160},{224,1... | collective-permute-start | bytes 4718600 | tf_op jit(solution)/shard_map/ppermute | solution.py:403
  55.2 17.6 %collective-permute-start.1 = (s32[3,32]{1,0:T(4,128)S(1)}, s32[3,32]{1,0:T(4,128)S(1)}, u32[]{:S(2)}, u32[]{:S(2)}) collective-permute-start(s32[3,32]{1,0:T(4,128)S(1)} %pad_add_fusion.1.table), channel_id=1, source_target_pairs={{0,224},{32,0},{64,32},{96,64},{128,96},{160,128},{192,160},{224,1... | collective-permute-start | bytes 1160 | tf_op jit(solution)/shard_map/ppermute | solution.py:397
  72.7 0.6 copy-start
  81.9 7.1 %copy-start.1 = (s32[3,32]{1,0:T(4,128)S(1)}, s32[3,32]{1,0:T(4,128)}, u32[]{:S(2)}) copy-start(s32[3,32]{1,0:T(4,128)} %copy-done) | copy-start | bytes 1156
  81.9 33.3 %all-to-all-start.2 = ((bf16[32,128,128]{2,1,0:T(8,128)(2,1)}), bf16[32,128,128]{2,1,0:T(8,128)(2,1)S(1)}, u32[]{:S(2)}, u32[]{:S(2)}) async-start(bf16[32,128,128]{2,1,0:T(8,128)(2,1)} %get-tuple-element.72), calls=%async_computation.2 | async-start | bytes 2097152 | tf_op jit(solution)/shard_map/all_to_all | solution.py:395
  88.4 18.9 %collective-permute-start.10 = (bf16[16,3,128,128]{3,2,1,0:T(8,128)(2,1)}, bf16[16,3,128,128]{3,2,1,0:T(8,128)(2,1)}, u32[]{:S(2)}, u32[]{:S(2)}) collective-permute-start(bf16[16,3,128,128]{3,2,1,0:T(8,128)(2,1)} %collective-permute-done.9.blocks_ref), channel_id=1, source_target_pairs={{0,224},{32,0},{64,32},{96,64},{128,96},{160,128},{192,160},{224,1... | collective-permute-start | bytes 4718600 | tf_op jit(solution)/shard_map/ppermute | solution.py:403
  89.1 18.3 %collective-permute-start.2 = (s32[3,32]{1,0:T(4,128)S(1)}, s32[3,32]{1,0:T(4,128)S(1)}, u32[]{:S(2)}, u32[]{:S(2)}) collective-permute-start(s32[3,32]{1,0:T(4,128)S(1)} %copy-done.1), channel_id=1, source_target_pairs={{0,224},{32,0},{64,32},{96,64},{128,96},{160,128},{192,160},{224,1... | collective-permute-start | bytes 1160 | tf_op jit(solution)/shard_map/ppermute | solution.py:397
  107.3 0.6 copy-start.2
  117.2 6.5 %copy-start.3 = (s32[3,32]{1,0:T(4,128)S(1)}, s32[3,32]{1,0:T(4,128)}, u32[]{:S(2)}) copy-start(s32[3,32]{1,0:T(4,128)} %copy-done.2) | copy-start | bytes 1156
  117.2 32.4 %all-to-all-start.3 = ((bf16[32,128,128]{2,1,0:T(8,128)(2,1)}), bf16[32,128,128]{2,1,0:T(8,128)(2,1)S(1)}, u32[]{:S(2)}, u32[]{:S(2)}) async-start(bf16[32,128,128]{2,1,0:T(8,128)(2,1)} %get-tuple-element.78), calls=%async_computation.3 | async-start | bytes 2097152 | tf_op jit(solution)/shard_map/all_to_all | solution.py:395
  123.6 18.3 %collective-permute-start.11 = (bf16[16,3,128,128]{3,2,1,0:T(8,128)(2,1)}, bf16[16,3,128,128]{3,2,1,0:T(8,128)(2,1)}, u32[]{:S(2)}, u32[]{:S(2)}) collective-permute-start(bf16[16,3,128,128]{3,2,1,0:T(8,128)(2,1)} %collective-permute-done.10.blocks_ref), channel_id=1, source_target_pairs={{0,224},{32,0},{64,32},{96,64},{128,96},{160,128},{192,160},{224,1... | collective-permute-start | bytes 4718600 | tf_op jit(solution)/shard_map/ppermute | solution.py:403
  123.7 18.3 %collective-permute-start.3 = (s32[3,32]{1,0:T(4,128)S(1)}, s32[3,32]{1,0:T(4,128)S(1)}, u32[]{:S(2)}, u32[]{:S(2)}) collective-permute-start(s32[3,32]{1,0:T(4,128)S(1)} %copy-done.3), channel_id=1, source_target_pairs={{0,224},{32,0},{64,32},{96,64},{128,96},{160,128},{192,160},{224,1... | collective-permute-start | bytes 1160 | tf_op jit(solution)/shard_map/ppermute | solution.py:397
  142.0 0.6 copy-start.4
  151.5 6.8 %copy-start.5 = (s32[3,32]{1,0:T(4,128)S(1)}, s32[3,32]{1,0:T(4,128)}, u32[]{:S(2)}) copy-start(s32[3,32]{1,0:T(4,128)} %copy-done.4) | copy-start | bytes 1156
  151.6 33.3 %all-to-all-start.4 = ((bf16[32,128,128]{2,1,0:T(8,128)(2,1)}), bf16[32,128,128]{2,1,0:T(8,128)(2,1)S(1)}, u32[]{:S(2)}, u32[]{:S(2)}) async-start(bf16[32,128,128]{2,1,0:T(8,128)(2,1)} %get-tuple-element.84), calls=%async_computation.4 | async-start | bytes 2097152 | tf_op jit(solution)/shard_map/all_to_all | solution.py:395
  158.0 18.6 %collective-permute-start.12 = (bf16[16,3,128,128]{3,2,1,0:T(8,128)(2,1)}, bf16[16,3,128,128]{3,2,1,0:T(8,128)(2,1)}, u32[]{:S(2)}, u32[]{:S(2)}) collective-permute-start(bf16[16,3,128,128]{3,2,1,0:T(8,128)(2,1)} %collective-permute-done.11.blocks_ref), channel_id=1, source_target_pairs={{0,224},{32,0},{64,32},{96,64},{128,96},{160,128},{192,160},{224,1... | collective-permute-start | bytes 4718600 | tf_op jit(solution)/shard_map/ppermute | solution.py:403
  158.4 18.3 %collective-permute-start.4 = (s32[3,32]{1,0:T(4,128)S(1)}, s32[3,32]{1,0:T(4,128)S(1)}, u32[]{:S(2)}, u32[]{:S(2)}) collective-permute-start(s32[3,32]{1,0:T(4,128)S(1)} %copy-done.5), channel_id=1, source_target_pairs={{0,224},{32,0},{64,32},{96,64},{128,96},{160,128},{192,160},{224,1... | collective-permute-start | bytes 1160 | tf_op jit(solution)/shard_map/ppermute | solution.py:397
  176.6 0.6 copy-start.6
  186.8 6.5 %copy-start.7 = (s32[3,32]{1,0:T(4,128)S(1)}, s32[3,32]{1,0:T(4,128)}, u32[]{:S(2)}) copy-start(s32[3,32]{1,0:T(4,128)} %copy-done.6) | copy-start | bytes 1156
  186.8 32.4 %all-to-all-start.5 = ((bf16[32,128,128]{2,1,0:T(8,128)(2,1)}), bf16[32,128,128]{2,1,0:T(8,128)(2,1)S(1)}, u32[]{:S(2)}, u32[]{:S(2)}) async-start(bf16[32,128,128]{2,1,0:T(8,128)(2,1)} %get-tuple-element.90), calls=%async_computation.5 | async-start | bytes 2097152 | tf_op jit(solution)/shard_map/all_to_all | solution.py:395
  193.3 18.3 %collective-permute-start.13 = (bf16[16,3,128,128]{3,2,1,0:T(8,128)(2,1)}, bf16[16,3,128,128]{3,2,1,0:T(8,128)(2,1)}, u32[]{:S(2)}, u32[]{:S(2)}) collective-permute-start(bf16[16,3,128,128]{3,2,1,0:T(8,128)(2,1)} %collective-permute-done.12.blocks_ref), channel_id=1, source_target_pairs={{0,224},{32,0},{64,32},{96,64},{128,96},{160,128},{192,160},{224,1... | collective-permute-start | bytes 4718600 | tf_op jit(solution)/shard_map/ppermute | solution.py:403
  193.3 18.2 %collective-permute-start.5 = (s32[3,32]{1,0:T(4,128)S(1)}, s32[3,32]{1,0:T(4,128)S(1)}, u32[]{:S(2)}, u32[]{:S(2)}) collective-permute-start(s32[3,32]{1,0:T(4,128)S(1)} %copy-done.7), channel_id=1, source_target_pairs={{0,224},{32,0},{64,32},{96,64},{128,96},{160,128},{192,160},{224,1... | collective-permute-start | bytes 1160 | tf_op jit(solution)/shard_map/ppermute | solution.py:397
  211.5 0.6 copy-start.8
  221.2 6.7 %copy-start.9 = (s32[3,32]{1,0:T(4,128)S(1)}, s32[3,32]{1,0:T(4,128)}, u32[]{:S(2)}) copy-start(s32[3,32]{1,0:T(4,128)} %copy-done.8) | copy-start | bytes 1156
  221.2 33.0 %all-to-all-start.6 = ((bf16[32,128,128]{2,1,0:T(8,128)(2,1)}), bf16[32,128,128]{2,1,0:T(8,128)(2,1)S(1)}, u32[]{:S(2)}, u32[]{:S(2)}) async-start(bf16[32,128,128]{2,1,0:T(8,128)(2,1)} %get-tuple-element.96), calls=%async_computation.6 | async-start | bytes 2097152 | tf_op jit(solution)/shard_map/all_to_all | solution.py:395
  227.7 18.5 %collective-permute-start.14 = (bf16[16,3,128,128]{3,2,1,0:T(8,128)(2,1)}, bf16[16,3,128,128]{3,2,1,0:T(8,128)(2,1)S(1)}, u32[]{:S(2)}, u32[]{:S(2)}) collective-permute-start(bf16[16,3,128,128]{3,2,1,0:T(8,128)(2,1)} %collective-permute-done.13.blocks_ref), channel_id=1, source_target_pairs={{0,224},{32,0},{64,32},{96,64},{128,96},{160,128},{192,160},{224,1... | collective-permute-start | bytes 4718600 | tf_op jit(solution)/shard_map/ppermute | solution.py:403
  227.9 18.3 %collective-permute-start.6 = (s32[3,32]{1,0:T(4,128)S(1)}, s32[3,32]{1,0:T(4,128)S(1)}, u32[]{:S(2)}, u32[]{:S(2)}) collective-permute-start(s32[3,32]{1,0:T(4,128)S(1)} %copy-done.9), channel_id=1, source_target_pairs={{0,224},{32,0},{64,32},{96,64},{128,96},{160,128},{192,160},{224,1... | collective-permute-start | bytes 1160 | tf_op jit(solution)/shard_map/ppermute | solution.py:397
  246.2 1.2 copy-start.12
  247.4 0.6 copy-start.10
  256.1 6.5 %copy-start.11 = (s32[3,32]{1,0:T(4,128)S(1)}, s32[3,32]{1,0:T(4,128)}, u32[]{:S(2)}) copy-start(s32[3,32]{1,0:T(4,128)} %copy-done.10) | copy-start | bytes 1156
  256.1 33.6 %all-to-all-start.7 = ((bf16[32,128,128]{2,1,0:T(8,128)(2,1)}), bf16[32,128,128]{2,1,0:T(8,128)(2,1)S(1)}, u32[]{:S(2)}, u32[]{:S(2)}) async-start(bf16[32,128,128]{2,1,0:T(8,128)(2,1)} %get-tuple-element.99), calls=%async_computation.7 | async-start | bytes 2097152 | tf_op jit(solution)/shard_map/all_to_all | solution.py:395
  262.6 2.4 collective-permute-start.7
  265.0 0.6 copy-start.15
  290.1 8.3 %collective-permute-start.15 = (bf16[1,128,128]{2,1,0:T(8,128)(2,1)S(1)}, bf16[1,128,128]{2,1,0:T(8,128)(2,1)S(1)}, u32[]{:S(2)}, u32[]{:S(2)}) collective-permute-start(bf16[1,128,128]{2,1,0:T(8,128)(2,1)S(1)} %get-tuple-element.102), channel_id=1, source_target_pairs={{0,1},{1,2},{2,3},{3,4},{4,5},{5,6},{6,7},{7,8},{8,9},{9,10},{10,1... | collective-permute-start | bytes 98312 | tf_op jit(solution)/shard_map/ppermute | solution.py:407
  294.5 7.9 %collective-permute-start.16 = (bf16[1,128,128]{2,1,0:T(8,128)(2,1)S(1)}, bf16[1,128,128]{2,1,0:T(8,128)(2,1)S(1)}, u32[]{:S(2)}, u32[]{:S(2)}) collective-permute-start(bf16[1,128,128]{2,1,0:T(8,128)(2,1)S(1)} %get-tuple-element.103), channel_id=1, source_target_pairs={{1,0},{2,1},{3,2},{4,3},{5,4},{6,5},{7,6},{8,7},{9,8},{10,9},{11,1... | collective-permute-start | bytes 98312 | tf_op jit(solution)/shard_map/ppermute | solution.py:408

commit v9 on v8

--- a/solution.py
+++ b/solution.py
@@ -166,7 +166,8 @@
     landed = lambda p: table[LANDED, p]
     if told:
         said, read, sem = told
-        said[...] = arrived_ref[:, state_scr.shape[1], :].astype(jnp.float32).astype(jnp.int32)
+        says = arrived_ref[:, state_scr.shape[1] :].astype(jnp.float32)
+        said[...] = jnp.max(says, axis=1).astype(jnp.int32)
         copy = pltpu.make_async_copy(said, read, sem)
         copy.start()
         copy.wait()

time: 305 us -> 305 us (level)
  no operation moved by 1% of the time
where the time goes in v9:
time: 305 us; the launch traced here: 303 us
  waiting for transfers between devices  154 us (50%)
  starting transfers between devices  81 us (27%)
  Pallas kernels  60.2 us (20%)
  local copies, waits for them, and re-layouts  6.12 us (2%)
    ppermute x7, waiting for transfers between devices, body(): wblk = onward(wblk)  85.8 us
    all_to_all x8, waiting for transfers between devices, body(): lax.all_to_all(out, 'tile', split_axis=0, concat_axis=0, tiled=True)  62.6 us
    all_to_all x8, starting transfers between devices, body(): lax.all_to_all(out, 'tile', split_axis=0, concat_axis=0, tiled=True)  56.2 us
    pallas_call x8, Pallas kernels, keep(): pl.pallas_call(keep_body, out_shape=pltpu.VMEM((tiles, rows, points), jnp...  30 us
    ppermute x8, starting transfers between devices, body(): given = table = onward(table)  15.2 us
    pallas_call x7, Pallas kernels, send(): pl.pallas_call(send_body, out_shape=(pltpu.HBM((peers, rows, points), jnp...  14.4 us
    pallas_call x7, Pallas kernels, fetch(): pl.pallas_call(fetch_body, out_shape=(pltpu.VMEM((tiles, nnz - 1, points,...  8.75 us
  transfers between devices with their start and end apart: 25, of which 17 were waited for; matrix products, arithmetic and copies ran while one was open for 0% of the time, Pallas kernels for 14%

profile of v9, /device:TPU:56, one launch (start us, length us, event | category | flops | bytes accessed | tf_op | source)
XLA Modules:
  0.0 303.5 jit_solution(9500286716357044059)
XLA Ops:
  0.6 3.1 %shard_map.50 = (bf16[32,144,128]{2,1,0:T(8,128)(2,1)}, bf16[16,128,128]{2,1,0:T(8,128)(2,1)}) custom-call(s32[3,1,16]{2,1,0:T(1,128)} %bitcast.15, bf16[16,128,128]{2,1,0:T(8,128)(2,1)} %bitcast.14, bf16[16,3,128,128]{3,2,1,0:T(8,128)(2,1)} %bitcast.2.blocks_ref), custom_call_target="tpu_custom_call" | custom-call | flops 134217728 | bytes 4194304 | tf_op jit(solution)/shard_map/pallas_call | solution.py:95
  3.8 11.0 %all-to-all-start = ((bf16[32,144,128]{2,1,0:T(8,128)(2,1)}), bf16[32,144,128]{2,1,0:T(8,128)(2,1)S(1)}, u32[]{:S(2)}, u32[]{:S(2)}) async-start(bf16[32,144,128]{2,1,0:T(8,128)(2,1)} %get-tuple-element.57), calls=%async_computation | async-start | bytes 2359296 | tf_op jit(solution)/shard_map/all_to_all | solution.py:396
  14.8 1.6 collective-permute-start.8
  17.3 1.2 collective-permute-start
  18.5 3.8 %shard_map.52.local_ref = f32[16,128,128]{2,1,0:T(8,128)S(1)} custom-call(s32[3,32]{1,0:T(4,128)S(1)} %pad_add_fusion.table, bf16[16,128,128]{2,1,0:T(8,128)(2,1)} %get-tuple-element.58.state_ref, bf16[16,3,128,128]{3,2,1,0:T(8,128)(2,1)} %bitcast.2.blocks_ref), custom_call_target="tpu_custom_call" | custom-call | flops 201326592 | bytes 4194304 | tf_op jit(solution)/shard_map/pallas_call | solution.py:244
  22.3 12.4 %collective-permute-done.8.blocks_ref = bf16[16,3,128,128]{3,2,1,0:T(8,128)(2,1)} collective-permute-done((bf16[16,3,128,128]{3,2,1,0:T(8,128)(2,1)}, bf16[16,3,128,128]{3,2,1,0:T(8,128)(2,1)}, u32[]{:S(2)}, u32[]{:S(2)}) %collective-permute-start.8) | collective-permute-done | bytes 1572896 | tf_op jit(solution)/shard_map/ppermute | solution.py:404
  35.3 1.2 shard_map.53
  36.6 8.3 %all-to-all-done.arrived_ref = bf16[32,144,128]{2,1,0:T(8,128)(2,1)S(1)} async-done(((bf16[32,144,128]{2,1,0:T(8,128)(2,1)}), bf16[32,144,128]{2,1,0:T(8,128)(2,1)S(1)}, u32[]{:S(2)}, u32[]{:S(2)}) %all-to-all-start) | async-done | bytes 1179680 | tf_op jit(solution)/shard_map/all_to_all | solution.py:396
  44.8 2.8 shard_map.54
  47.6 6.4 %all-to-all-start.1 = ((bf16[32,128,128]{2,1,0:T(8,128)(2,1)}), bf16[32,128,128]{2,1,0:T(8,128)(2,1)S(1)}, u32[]{:S(2)}, u32[]{:S(2)}) async-start(bf16[32,128,128]{2,1,0:T(8,128)(2,1)} %get-tuple-element.66), calls=%async_computation.1 | async-start | bytes 2097152 | tf_op jit(solution)/shard_map/all_to_all | solution.py:396
  55.2 2.5 collective-permute-start.1
  57.7 3.7 %shard_map.55.local_ref = f32[16,128,128]{2,1,0:T(8,128)S(1)} custom-call(s32[3,32]{1,0:T(4,128)S(1)} %pad_add_fusion.1.table, bf16[16,128,128]{2,1,0:T(8,128)(2,1)} %get-tuple-element.63.state_ref, bf16[16,3,128,128]{3,2,1,0:T(8,128)(2,1)} %collective-permute-done.8.blocks_ref), custom_call_target="tpu_custom_call" | custom-call | flops 201326592 | bytes 4194304 | tf_op jit(solution)/shard_map/pallas_call | solution.py:244
  61.4 11.3 %collective-permute-done.9.blocks_ref = bf16[16,3,128,128]{3,2,1,0:T(8,128)(2,1)} collective-permute-done((bf16[16,3,128,128]{3,2,1,0:T(8,128)(2,1)}, bf16[16,3,128,128]{3,2,1,0:T(8,128)(2,1)}, u32[]{:S(2)}, u32[]{:S(2)}) %collective-permute-start.9) | collective-permute-done | bytes 1572896 | tf_op jit(solution)/shard_map/ppermute | solution.py:404
  73.3 1.2 shard_map.56
  74.6 5.5 %all-to-all-done.1.arrived_ref = bf16[32,128,128]{2,1,0:T(8,128)(2,1)S(1)} async-done(((bf16[32,128,128]{2,1,0:T(8,128)(2,1)}), bf16[32,128,128]{2,1,0:T(8,128)(2,1)S(1)}, u32[]{:S(2)}, u32[]{:S(2)}) %all-to-all-start.1) | async-done | bytes 1048608 | tf_op jit(solution)/shard_map/all_to_all | solution.py:396
  80.0 1.9 shard_map.57
  82.0 6.5 %all-to-all-start.2 = ((bf16[32,128,128]{2,1,0:T(8,128)(2,1)}), bf16[32,128,128]{2,1,0:T(8,128)(2,1)S(1)}, u32[]{:S(2)}, u32[]{:S(2)}) async-start(bf16[32,128,128]{2,1,0:T(8,128)(2,1)} %get-tuple-element.72), calls=%async_computation.2 | async-start | bytes 2097152 | tf_op jit(solution)/shard_map/all_to_all | solution.py:396
  88.4 0.7 collective-permute-start.10
  89.1 2.2 collective-permute-start.2
  91.3 3.7 %shard_map.58.local_ref = f32[16,128,128]{2,1,0:T(8,128)S(1)} custom-call(s32[3,32]{1,0:T(4,128)S(1)} %copy-done.1, bf16[16,128,128]{2,1,0:T(8,128)(2,1)} %get-tuple-element.69.state_ref, bf16[16,3,128,128]{3,2,1,0:T(8,128)(2,1)} %collective-permute-done.9.blocks_ref), custom_call_target="tpu_custom_call" | custom-call | flops 201326592 | bytes 4194304 | tf_op jit(solution)/shard_map/pallas_call | solution.py:244
  95.1 12.3 %collective-permute-done.10.blocks_ref = bf16[16,3,128,128]{3,2,1,0:T(8,128)(2,1)} collective-permute-done((bf16[16,3,128,128]{3,2,1,0:T(8,128)(2,1)}, bf16[16,3,128,128]{3,2,1,0:T(8,128)(2,1)}, u32[]{:S(2)}, u32[]{:S(2)}) %collective-permute-start.10) | collective-permute-done | bytes 1572896 | tf_op jit(solution)/shard_map/ppermute | solution.py:404
  107.9 1.2 shard_map.59
  109.2 6.0 %all-to-all-done.2.arrived_ref = bf16[32,128,128]{2,1,0:T(8,128)(2,1)S(1)} async-done(((bf16[32,128,128]{2,1,0:T(8,128)(2,1)}), bf16[32,128,128]{2,1,0:T(8,128)(2,1)S(1)}, u32[]{:S(2)}, u32[]{:S(2)}) %all-to-all-start.2) | async-done | bytes 1048608 | tf_op jit(solution)/shard_map/all_to_all | solution.py:396
  115.2 1.9 shard_map.60
  117.2 6.4 %all-to-all-start.3 = ((bf16[32,128,128]{2,1,0:T(8,128)(2,1)}), bf16[32,128,128]{2,1,0:T(8,128)(2,1)S(1)}, u32[]{:S(2)}, u32[]{:S(2)}) async-start(bf16[32,128,128]{2,1,0:T(8,128)(2,1)} %get-tuple-element.78), calls=%async_computation.3 | async-start | bytes 2097152 | tf_op jit(solution)/shard_map/all_to_all | solution.py:396
  123.7 2.2 collective-permute-start.3
  126.0 3.8 %shard_map.61.local_ref = f32[16,128,128]{2,1,0:T(8,128)S(1)} custom-call(s32[3,32]{1,0:T(4,128)S(1)} %copy-done.3, bf16[16,128,128]{2,1,0:T(8,128)(2,1)} %get-tuple-element.75.state_ref, bf16[16,3,128,128]{3,2,1,0:T(8,128)(2,1)} %collective-permute-done.10.blocks_ref), custom_call_target="tpu_custom_call" | custom-call | flops 201326592 | bytes 4194304 | tf_op jit(solution)/shard_map/pallas_call | solution.py:244
  129.7 12.3 %collective-permute-done.11.blocks_ref = bf16[16,3,128,128]{3,2,1,0:T(8,128)(2,1)} collective-permute-done((bf16[16,3,128,128]{3,2,1,0:T(8,128)(2,1)}, bf16[16,3,128,128]{3,2,1,0:T(8,128)(2,1)}, u32[]{:S(2)}, u32[]{:S(2)}) %collective-permute-start.11) | collective-permute-done | bytes 1572896 | tf_op jit(solution)/shard_map/ppermute | solution.py:404
  142.6 1.2 shard_map.62
  143.8 5.8 %all-to-all-done.3.arrived_ref = bf16[32,128,128]{2,1,0:T(8,128)(2,1)S(1)} async-done(((bf16[32,128,128]{2,1,0:T(8,128)(2,1)}), bf16[32,128,128]{2,1,0:T(8,128)(2,1)S(1)}, u32[]{:S(2)}, u32[]{:S(2)}) %all-to-all-start.3) | async-done | bytes 1048608 | tf_op jit(solution)/shard_map/all_to_all | solution.py:396
  149.6 1.9 shard_map.63
  151.6 6.5 %all-to-all-start.4 = ((bf16[32,128,128]{2,1,0:T(8,128)(2,1)}), bf16[32,128,128]{2,1,0:T(8,128)(2,1)S(1)}, u32[]{:S(2)}, u32[]{:S(2)}) async-start(bf16[32,128,128]{2,1,0:T(8,128)(2,1)} %get-tuple-element.84), calls=%async_computation.4 | async-start | bytes 2097152 | tf_op jit(solution)/shard_map/all_to_all | solution.py:396
  158.4 2.2 collective-permute-start.4
  160.6 3.7 %shard_map.64.local_ref = f32[16,128,128]{2,1,0:T(8,128)S(1)} custom-call(s32[3,32]{1,0:T(4,128)S(1)} %copy-done.5, bf16[16,128,128]{2,1,0:T(8,128)(2,1)} %get-tuple-element.81.state_ref, bf16[16,3,128,128]{3,2,1,0:T(8,128)(2,1)} %collective-permute-done.11.blocks_ref), custom_call_target="tpu_custom_call" | custom-call | flops 201326592 | bytes 4194304 | tf_op jit(solution)/shard_map/pallas_call | solution.py:244
  164.3 12.3 %collective-permute-done.12.blocks_ref = bf16[16,3,128,128]{3,2,1,0:T(8,128)(2,1)} collective-permute-done((bf16[16,3,128,128]{3,2,1,0:T(8,128)(2,1)}, bf16[16,3,128,128]{3,2,1,0:T(8,128)(2,1)}, u32[]{:S(2)}, u32[]{:S(2)}) %collective-permute-start.12) | collective-permute-done | bytes 1572896 | tf_op jit(solution)/shard_map/ppermute | solution.py:404
  177.2 1.2 shard_map.65
  178.5 6.4 %all-to-all-done.4.arrived_ref = bf16[32,128,128]{2,1,0:T(8,128)(2,1)S(1)} async-done(((bf16[32,128,128]{2,1,0:T(8,128)(2,1)}), bf16[32,128,128]{2,1,0:T(8,128)(2,1)S(1)}, u32[]{:S(2)}, u32[]{:S(2)}) %all-to-all-start.4) | async-done | bytes 1048608 | tf_op jit(solution)/shard_map/all_to_all | solution.py:396
  184.9 1.9 shard_map.66
  186.8 6.4 %all-to-all-start.5 = ((bf16[32,128,128]{2,1,0:T(8,128)(2,1)}), bf16[32,128,128]{2,1,0:T(8,128)(2,1)S(1)}, u32[]{:S(2)}, u32[]{:S(2)}) async-start(bf16[32,128,128]{2,1,0:T(8,128)(2,1)} %get-tuple-element.90), calls=%async_computation.5 | async-start | bytes 2097152 | tf_op jit(solution)/shard_map/all_to_all | solution.py:396
  193.3 1.9 collective-permute-start.5
  195.2 3.7 %shard_map.67.local_ref = f32[16,128,128]{2,1,0:T(8,128)S(1)} custom-call(s32[3,32]{1,0:T(4,128)S(1)} %copy-done.7, bf16[16,128,128]{2,1,0:T(8,128)(2,1)} %get-tuple-element.87.state_ref, bf16[16,3,128,128]{3,2,1,0:T(8,128)(2,1)} %collective-permute-done.12.blocks_ref), custom_call_target="tpu_custom_call" | custom-call | flops 201326592 | bytes 4194304 | tf_op jit(solution)/shard_map/pallas_call | solution.py:244
  199.0 12.6 %collective-permute-done.13.blocks_ref = bf16[16,3,128,128]{3,2,1,0:T(8,128)(2,1)} collective-permute-done((bf16[16,3,128,128]{3,2,1,0:T(8,128)(2,1)}, bf16[16,3,128,128]{3,2,1,0:T(8,128)(2,1)}, u32[]{:S(2)}, u32[]{:S(2)}) %collective-permute-start.13) | collective-permute-done | bytes 1572896 | tf_op jit(solution)/shard_map/ppermute | solution.py:404
  212.1 1.2 shard_map.68
  213.4 5.9 %all-to-all-done.5.arrived_ref = bf16[32,128,128]{2,1,0:T(8,128)(2,1)S(1)} async-done(((bf16[32,128,128]{2,1,0:T(8,128)(2,1)}), bf16[32,128,128]{2,1,0:T(8,128)(2,1)S(1)}, u32[]{:S(2)}, u32[]{:S(2)}) %all-to-all-start.5) | async-done | bytes 1048608 | tf_op jit(solution)/shard_map/all_to_all | solution.py:396
  219.3 1.9 shard_map.69
  221.2 6.4 %all-to-all-start.6 = ((bf16[32,128,128]{2,1,0:T(8,128)(2,1)}), bf16[32,128,128]{2,1,0:T(8,128)(2,1)S(1)}, u32[]{:S(2)}, u32[]{:S(2)}) async-start(bf16[32,128,128]{2,1,0:T(8,128)(2,1)} %get-tuple-element.96), calls=%async_computation.6 | async-start | bytes 2097152 | tf_op jit(solution)/shard_map/all_to_all | solution.py:396
  227.9 1.9 collective-permute-start.6
  229.9 3.7 %shard_map.70.local_ref = f32[16,128,128]{2,1,0:T(8,128)S(1)} custom-call(s32[3,32]{1,0:T(4,128)S(1)} %copy-done.9, bf16[16,128,128]{2,1,0:T(8,128)(2,1)} %get-tuple-element.93.state_ref, bf16[16,3,128,128]{3,2,1,0:T(8,128)(2,1)} %collective-permute-done.13.blocks_ref), custom_call_target="tpu_custom_call" | custom-call | flops 201326592 | bytes 4194304 | tf_op jit(solution)/shard_map/pallas_call | solution.py:244
  233.6 12.6 %collective-permute-done.14.blocks_ref = bf16[16,3,128,128]{3,2,1,0:T(8,128)(2,1)S(1)} collective-permute-done((bf16[16,3,128,128]{3,2,1,0:T(8,128)(2,1)}, bf16[16,3,128,128]{3,2,1,0:T(8,128)(2,1)S(1)}, u32[]{:S(2)}, u32[]{:S(2)}) %collective-permute-start.14) | collective-permute-done | bytes 1572896 | tf_op jit(solution)/shard_map/ppermute | solution.py:404
  246.2 1.2 copy-done.12
  247.9 1.2 shard_map.71
  249.2 5.1 %all-to-all-done.6.arrived_ref = bf16[32,128,128]{2,1,0:T(8,128)(2,1)S(1)} async-done(((bf16[32,128,128]{2,1,0:T(8,128)(2,1)}), bf16[32,128,128]{2,1,0:T(8,128)(2,1)S(1)}, u32[]{:S(2)}, u32[]{:S(2)}) %all-to-all-start.6) | async-done | bytes 1048608 | tf_op jit(solution)/shard_map/all_to_all | solution.py:396
  254.3 2.0 shard_map.72
  256.3 6.4 %all-to-all-start.7 = ((bf16[32,128,128]{2,1,0:T(8,128)(2,1)}), bf16[32,128,128]{2,1,0:T(8,128)(2,1)S(1)}, u32[]{:S(2)}, u32[]{:S(2)}) async-start(bf16[32,128,128]{2,1,0:T(8,128)(2,1)} %get-tuple-element.99), calls=%async_computation.7 | async-start | bytes 2097152 | tf_op jit(solution)/shard_map/all_to_all | solution.py:396
  262.7 1.0 collective-permute-start.7
  263.7 1.3 collective-permute-done.7.table_ref
  265.6 0.7 shard_map.51.before
  266.3 3.8 %shard_map.73.local_ref = f32[16,128,128]{2,1,0:T(8,128)S(1)} custom-call(s32[3,32]{1,0:T(4,128)S(1)} %copy-done.11, bf16[16,128,128]{2,1,0:T(8,128)(2,1)} %get-tuple-element.100.state_ref, bf16[16,3,128,128]{3,2,1,0:T(8,128)(2,1)} %copy-done.12), custom_call_target="tpu_custom_call" | custom-call | flops 201326592 | bytes 4194304 | tf_op jit(solution)/shard_map/pallas_call | solution.py:244
  270.1 19.7 %all-to-all-done.7.arrived_ref = bf16[32,128,128]{2,1,0:T(8,128)(2,1)S(1)} async-done(((bf16[32,128,128]{2,1,0:T(8,128)(2,1)}), bf16[32,128,128]{2,1,0:T(8,128)(2,1)S(1)}, u32[]{:S(2)}, u32[]{:S(2)}) %all-to-all-start.7) | async-done | bytes 1048608 | tf_op jit(solution)/shard_map/all_to_all | solution.py:396
  290.2 4.3 %collective-permute-start.15 = (bf16[1,128,128]{2,1,0:T(8,128)(2,1)S(1)}, bf16[1,128,128]{2,1,0:T(8,128)(2,1)S(1)}, u32[]{:S(2)}, u32[]{:S(2)}) collective-permute-start(bf16[1,128,128]{2,1,0:T(8,128)(2,1)S(1)} %get-tuple-element.102), channel_id=1, source_target_pairs={{0,1},{1,2},{2,3},{3,4},{4,5},{5,6},{6,7},{7,8},{8,9},{9,10},{10,1... | collective-permute-start | bytes 98312 | tf_op jit(solution)/shard_map/ppermute | solution.py:408
  294.5 1.9 collective-permute-start.16
  296.4 2.0 shard_map.75
  298.4 4.0 %collective-permute-done.16.high_ref = bf16[1,128,128]{2,1,0:T(8,128)(2,1)S(1)} collective-permute-done((bf16[1,128,128]{2,1,0:T(8,128)(2,1)S(1)}, bf16[1,128,128]{2,1,0:T(8,128)(2,1)S(1)}, u32[]{:S(2)}, u32[]{:S(2)}) %collective-permute-start.16) | collective-permute-done | bytes 32800 | tf_op jit(solution)/shard_map/ppermute | solution.py:409
  302.4 0.9 shard_map.76
  (64 shorter events, 7.6 us)
Async XLA Ops:
  3.8 12.7 %copy-start.13 = (s32[1,16,3]{1,0,2:T(1,128)S(1)}, s32[1,16,3]{1,0,2:T(1,128)}, u32[]{:S(2)}) copy-start(s32[1,16,3]{1,0,2:T(1,128)} %param.5) | copy-start | bytes 580
  3.8 41.0 %all-to-all-start = ((bf16[32,144,128]{2,1,0:T(8,128)(2,1)}), bf16[32,144,128]{2,1,0:T(8,128)(2,1)S(1)}, u32[]{:S(2)}, u32[]{:S(2)}) async-start(bf16[32,144,128]{2,1,0:T(8,128)(2,1)} %get-tuple-element.57), calls=%async_computation | async-start | bytes 2359296 | tf_op jit(solution)/shard_map/all_to_all | solution.py:396
  14.8 19.9 %collective-permute-start.8 = (bf16[16,3,128,128]{3,2,1,0:T(8,128)(2,1)}, bf16[16,3,128,128]{3,2,1,0:T(8,128)(2,1)}, u32[]{:S(2)}, u32[]{:S(2)}) collective-permute-start(bf16[16,3,128,128]{3,2,1,0:T(8,128)(2,1)} %bitcast.2.blocks_ref), channel_id=1, source_target_pairs={{0,224},{32,0},{64,32},{96,64},{128,96},{160,128},{192,160},{224,1... | collective-permute-start | bytes 4718600 | tf_op jit(solution)/shard_map/ppermute | solution.py:404
  17.3 17.5 %collective-permute-start = (s32[3,32]{1,0:T(4,128)S(1)}, s32[3,32]{1,0:T(4,128)S(1)}, u32[]{:S(2)}, u32[]{:S(2)}) collective-permute-start(s32[3,32]{1,0:T(4,128)S(1)} %pad_add_fusion.table), channel_id=1, source_target_pairs={{0,224},{32,0},{64,32},{96,64},{128,96},{160,128},{192,160},{224,1... | collective-permute-start | bytes 1160 | tf_op jit(solution)/shard_map/ppermute | solution.py:398
  34.7 0.6 copy-start.14
  47.6 7.6 %slice-start = ((s32[3,32]{1,0:T(4,128)}), s32[2,32]{1,0:T(2,128)S(1)}, s32[]{:S(2)}) async-start(s32[3,32]{1,0:T(4,128)} %copy-done.14), calls=%async_computation.8 | async-start | bytes 2048 | tf_op jit(solution)/shard_map/slice | solution.py:402
  47.6 32.4 %all-to-all-start.1 = ((bf16[32,128,128]{2,1,0:T(8,128)(2,1)}), bf16[32,128,128]{2,1,0:T(8,128)(2,1)S(1)}, u32[]{:S(2)}, u32[]{:S(2)}) async-start(bf16[32,128,128]{2,1,0:T(8,128)(2,1)} %get-tuple-element.66), calls=%async_computation.1 | async-start | bytes 2097152 | tf_op jit(solution)/shard_map/all_to_all | solution.py:396
  54.1 18.7 %collective-permute-start.9 = (bf16[16,3,128,128]{3,2,1,0:T(8,128)(2,1)}, bf16[16,3,128,128]{3,2,1,0:T(8,128)(2,1)}, u32[]{:S(2)}, u32[]{:S(2)}) collective-permute-start(bf16[16,3,128,128]{3,2,1,0:T(8,128)(2,1)} %collective-permute-done.8.blocks_ref), channel_id=1, source_target_pairs={{0,224},{32,0},{64,32},{96,64},{128,96},{160,128},{192,160},{224,1... | collective-permute-start | bytes 4718600 | tf_op jit(solution)/shard_map/ppermute | solution.py:404
  55.2 17.6 %collective-permute-start.1 = (s32[3,32]{1,0:T(4,128)S(1)}, s32[3,32]{1,0:T(4,128)S(1)}, u32[]{:S(2)}, u32[]{:S(2)}) collective-permute-start(s32[3,32]{1,0:T(4,128)S(1)} %pad_add_fusion.1.table), channel_id=1, source_target_pairs={{0,224},{32,0},{64,32},{96,64},{128,96},{160,128},{192,160},{224,1... | collective-permute-start | bytes 1160 | tf_op jit(solution)/shard_map/ppermute | solution.py:398
  72.7 0.6 copy-start
  82.0 7.2 %copy-start.1 = (s32[3,32]{1,0:T(4,128)S(1)}, s32[3,32]{1,0:T(4,128)}, u32[]{:S(2)}) copy-start(s32[3,32]{1,0:T(4,128)} %copy-done) | copy-start | bytes 1156
  82.0 33.3 %all-to-all-start.2 = ((bf16[32,128,128]{2,1,0:T(8,128)(2,1)}), bf16[32,128,128]{2,1,0:T(8,128)(2,1)S(1)}, u32[]{:S(2)}, u32[]{:S(2)}) async-start(bf16[32,128,128]{2,1,0:T(8,128)(2,1)} %get-tuple-element.72), calls=%async_computation.2 | async-start | bytes 2097152 | tf_op jit(solution)/shard_map/all_to_all | solution.py:396
  88.4 18.9 %collective-permute-start.10 = (bf16[16,3,128,128]{3,2,1,0:T(8,128)(2,1)}, bf16[16,3,128,128]{3,2,1,0:T(8,128)(2,1)}, u32[]{:S(2)}, u32[]{:S(2)}) collective-permute-start(bf16[16,3,128,128]{3,2,1,0:T(8,128)(2,1)} %collective-permute-done.9.blocks_ref), channel_id=1, source_target_pairs={{0,224},{32,0},{64,32},{96,64},{128,96},{160,128},{192,160},{224,1... | collective-permute-start | bytes 4718600 | tf_op jit(solution)/shard_map/ppermute | solution.py:404
  89.1 18.3 %collective-permute-start.2 = (s32[3,32]{1,0:T(4,128)S(1)}, s32[3,32]{1,0:T(4,128)S(1)}, u32[]{:S(2)}, u32[]{:S(2)}) collective-permute-start(s32[3,32]{1,0:T(4,128)S(1)} %copy-done.1), channel_id=1, source_target_pairs={{0,224},{32,0},{64,32},{96,64},{128,96},{160,128},{192,160},{224,1... | collective-permute-start | bytes 1160 | tf_op jit(solution)/shard_map/ppermute | solution.py:398
  107.4 0.6 copy-start.2
  117.2 6.5 %copy-start.3 = (s32[3,32]{1,0:T(4,128)S(1)}, s32[3,32]{1,0:T(4,128)}, u32[]{:S(2)}) copy-start(s32[3,32]{1,0:T(4,128)} %copy-done.2) | copy-start | bytes 1156
  117.2 32.4 %all-to-all-start.3 = ((bf16[32,128,128]{2,1,0:T(8,128)(2,1)}), bf16[32,128,128]{2,1,0:T(8,128)(2,1)S(1)}, u32[]{:S(2)}, u32[]{:S(2)}) async-start(bf16[32,128,128]{2,1,0:T(8,128)(2,1)} %get-tuple-element.78), calls=%async_computation.3 | async-start | bytes 2097152 | tf_op jit(solution)/shard_map/all_to_all | solution.py:396
  123.7 18.3 %collective-permute-start.11 = (bf16[16,3,128,128]{3,2,1,0:T(8,128)(2,1)}, bf16[16,3,128,128]{3,2,1,0:T(8,128)(2,1)}, u32[]{:S(2)}, u32[]{:S(2)}) collective-permute-start(bf16[16,3,128,128]{3,2,1,0:T(8,128)(2,1)} %collective-permute-done.10.blocks_ref), channel_id=1, source_target_pairs={{0,224},{32,0},{64,32},{96,64},{128,96},{160,128},{192,160},{224,1... | collective-permute-start | bytes 4718600 | tf_op jit(solution)/shard_map/ppermute | solution.py:404
  123.7 18.3 %collective-permute-start.3 = (s32[3,32]{1,0:T(4,128)S(1)}, s32[3,32]{1,0:T(4,128)S(1)}, u32[]{:S(2)}, u32[]{:S(2)}) collective-permute-start(s32[3,32]{1,0:T(4,128)S(1)} %copy-done.3), channel_id=1, source_target_pairs={{0,224},{32,0},{64,32},{96,64},{128,96},{160,128},{192,160},{224,1... | collective-permute-start | bytes 1160 | tf_op jit(solution)/shard_map/ppermute | solution.py:398
  142.0 0.6 copy-start.4
  151.6 6.8 %copy-start.5 = (s32[3,32]{1,0:T(4,128)S(1)}, s32[3,32]{1,0:T(4,128)}, u32[]{:S(2)}) copy-start(s32[3,32]{1,0:T(4,128)} %copy-done.4) | copy-start | bytes 1156
  151.6 33.3 %all-to-all-start.4 = ((bf16[32,128,128]{2,1,0:T(8,128)(2,1)}), bf16[32,128,128]{2,1,0:T(8,128)(2,1)S(1)}, u32[]{:S(2)}, u32[]{:S(2)}) async-start(bf16[32,128,128]{2,1,0:T(8,128)(2,1)} %get-tuple-element.84), calls=%async_computation.4 | async-start | bytes 2097152 | tf_op jit(solution)/shard_map/all_to_all | solution.py:396
  158.1 18.6 %collective-permute-start.12 = (bf16[16,3,128,128]{3,2,1,0:T(8,128)(2,1)}, bf16[16,3,128,128]{3,2,1,0:T(8,128)(2,1)}, u32[]{:S(2)}, u32[]{:S(2)}) collective-permute-start(bf16[16,3,128,128]{3,2,1,0:T(8,128)(2,1)} %collective-permute-done.11.blocks_ref), channel_id=1, source_target_pairs={{0,224},{32,0},{64,32},{96,64},{128,96},{160,128},{192,160},{224,1... | collective-permute-start | bytes 4718600 | tf_op jit(solution)/shard_map/ppermute | solution.py:404
  158.4 18.3 %collective-permute-start.4 = (s32[3,32]{1,0:T(4,128)S(1)}, s32[3,32]{1,0:T(4,128)S(1)}, u32[]{:S(2)}, u32[]{:S(2)}) collective-permute-start(s32[3,32]{1,0:T(4,128)S(1)} %copy-done.5), channel_id=1, source_target_pairs={{0,224},{32,0},{64,32},{96,64},{128,96},{160,128},{192,160},{224,1... | collective-permute-start | bytes 1160 | tf_op jit(solution)/shard_map/ppermute | solution.py:398
  176.6 0.6 copy-start.6
  186.8 6.5 %copy-start.7 = (s32[3,32]{1,0:T(4,128)S(1)}, s32[3,32]{1,0:T(4,128)}, u32[]{:S(2)}) copy-start(s32[3,32]{1,0:T(4,128)} %copy-done.6) | copy-start | bytes 1156
  186.8 32.4 %all-to-all-start.5 = ((bf16[32,128,128]{2,1,0:T(8,128)(2,1)}), bf16[32,128,128]{2,1,0:T(8,128)(2,1)S(1)}, u32[]{:S(2)}, u32[]{:S(2)}) async-start(bf16[32,128,128]{2,1,0:T(8,128)(2,1)} %get-tuple-element.90), calls=%async_computation.5 | async-start | bytes 2097152 | tf_op jit(solution)/shard_map/all_to_all | solution.py:396
  193.3 18.3 %collective-permute-start.13 = (bf16[16,3,128,128]{3,2,1,0:T(8,128)(2,1)}, bf16[16,3,128,128]{3,2,1,0:T(8,128)(2,1)}, u32[]{:S(2)}, u32[]{:S(2)}) collective-permute-start(bf16[16,3,128,128]{3,2,1,0:T(8,128)(2,1)} %collective-permute-done.12.blocks_ref), channel_id=1, source_target_pairs={{0,224},{32,0},{64,32},{96,64},{128,96},{160,128},{192,160},{224,1... | collective-permute-start | bytes 4718600 | tf_op jit(solution)/shard_map/ppermute | solution.py:404
  193.3 18.2 %collective-permute-start.5 = (s32[3,32]{1,0:T(4,128)S(1)}, s32[3,32]{1,0:T(4,128)S(1)}, u32[]{:S(2)}, u32[]{:S(2)}) collective-permute-start(s32[3,32]{1,0:T(4,128)S(1)} %copy-done.7), channel_id=1, source_target_pairs={{0,224},{32,0},{64,32},{96,64},{128,96},{160,128},{192,160},{224,1... | collective-permute-start | bytes 1160 | tf_op jit(solution)/shard_map/ppermute | solution.py:398
  211.6 0.6 copy-start.8
  221.2 6.7 %copy-start.9 = (s32[3,32]{1,0:T(4,128)S(1)}, s32[3,32]{1,0:T(4,128)}, u32[]{:S(2)}) copy-start(s32[3,32]{1,0:T(4,128)} %copy-done.8) | copy-start | bytes 1156
  221.2 33.1 %all-to-all-start.6 = ((bf16[32,128,128]{2,1,0:T(8,128)(2,1)}), bf16[32,128,128]{2,1,0:T(8,128)(2,1)S(1)}, u32[]{:S(2)}, u32[]{:S(2)}) async-start(bf16[32,128,128]{2,1,0:T(8,128)(2,1)} %get-tuple-element.96), calls=%async_computation.6 | async-start | bytes 2097152 | tf_op jit(solution)/shard_map/all_to_all | solution.py:396
  227.7 18.5 %collective-permute-start.14 = (bf16[16,3,128,128]{3,2,1,0:T(8,128)(2,1)}, bf16[16,3,128,128]{3,2,1,0:T(8,128)(2,1)S(1)}, u32[]{:S(2)}, u32[]{:S(2)}) collective-permute-start(bf16[16,3,128,128]{3,2,1,0:T(8,128)(2,1)} %collective-permute-done.13.blocks_ref), channel_id=1, source_target_pairs={{0,224},{32,0},{64,32},{96,64},{128,96},{160,128},{192,160},{224,1... | collective-permute-start | bytes 4718600 | tf_op jit(solution)/shard_map/ppermute | solution.py:404
  227.9 18.3 %collective-permute-start.6 = (s32[3,32]{1,0:T(4,128)S(1)}, s32[3,32]{1,0:T(4,128)S(1)}, u32[]{:S(2)}, u32[]{:S(2)}) collective-permute-start(s32[3,32]{1,0:T(4,128)S(1)} %copy-done.9), channel_id=1, source_target_pairs={{0,224},{32,0},{64,32},{96,64},{128,96},{160,128},{192,160},{224,1... | collective-permute-start | bytes 1160 | tf_op jit(solution)/shard_map/ppermute | solution.py:398
  246.2 1.2 copy-start.12
  247.4 0.6 copy-start.10
  256.2 6.5 %copy-start.11 = (s32[3,32]{1,0:T(4,128)S(1)}, s32[3,32]{1,0:T(4,128)}, u32[]{:S(2)}) copy-start(s32[3,32]{1,0:T(4,128)} %copy-done.10) | copy-start | bytes 1156
  256.3 33.5 %all-to-all-start.7 = ((bf16[32,128,128]{2,1,0:T(8,128)(2,1)}), bf16[32,128,128]{2,1,0:T(8,128)(2,1)S(1)}, u32[]{:S(2)}, u32[]{:S(2)}) async-start(bf16[32,128,128]{2,1,0:T(8,128)(2,1)} %get-tuple-element.99), calls=%async_computation.7 | async-start | bytes 2097152 | tf_op jit(solution)/shard_map/all_to_all | solution.py:396
  262.7 2.3 collective-permute-start.7
  265.0 0.6 copy-start.15
  290.2 8.3 %collective-permute-start.15 = (bf16[1,128,128]{2,1,0:T(8,128)(2,1)S(1)}, bf16[1,128,128]{2,1,0:T(8,128)(2,1)S(1)}, u32[]{:S(2)}, u32[]{:S(2)}) collective-permute-start(bf16[1,128,128]{2,1,0:T(8,128)(2,1)S(1)} %get-tuple-element.102), channel_id=1, source_target_pairs={{0,1},{1,2},{2,3},{3,4},{4,5},{5,6},{6,7},{7,8},{8,9},{9,10},{10,1... | collective-permute-start | bytes 98312 | tf_op jit(solution)/shard_map/ppermute | solution.py:408
  294.5 7.9 %collective-permute-start.16 = (bf16[1,128,128]{2,1,0:T(8,128)(2,1)S(1)}, bf16[1,128,128]{2,1,0:T(8,128)(2,1)S(1)}, u32[]{:S(2)}, u32[]{:S(2)}) collective-permute-start(bf16[1,128,128]{2,1,0:T(8,128)(2,1)S(1)} %get-tuple-element.103), channel_id=1, source_target_pairs={{1,0},{2,1},{3,2},{4,3},{5,4},{6,5},{7,6},{8,7},{9,8},{10,9},{11,1... | collective-permute-start | bytes 98312 | tf_op jit(solution)/shard_map/ppermute | solution.py:409

commit v10 on v9

--- a/solution.py
+++ b/solution.py
@@ -41,8 +41,9 @@
         copy.wait()
 
 
-def add_arrived(landed, arrived_ref, gathered):
-    gathered[...] = jnp.zeros_like(gathered)
+def add_arrived(landed, arrived_ref, local_ref, gathered):
+    gathered[: local_ref.shape[0]] = local_ref[...]
+    gathered[local_ref.shape[0]] = jnp.zeros(gathered.shape[1:], gathered.dtype)
     rows = gathered.shape[1]
     for p in range(arrived_ref.shape[0]):
         home = landed(p)
@@ -173,9 +174,9 @@
         copy.wait()
         me = lax.axis_index("tile")
         landed = lambda p: jnp.where(me == p, state_scr.shape[0], read[p, 0])
-    add_arrived(landed, arrived_ref, gathered)
+    add_arrived(landed, arrived_ref, local_ref, gathered)
     for t in range(state_scr.shape[0]):
-        state_scr[t] = (gathered[t] + local_ref[t]).astype(jnp.bfloat16)
+        state_scr[t] = gathered[t].astype(jnp.bfloat16)
     store = pltpu.make_async_copy(state_scr, state_ref, store_sem)
     store.start()
     each, points = off_ref.shape[1:3]
@@ -259,10 +260,10 @@
 
 
 def last_body(before, arrived_ref, local_ref, final_ref, low_ref, high_ref, gathered):
-    add_arrived(lambda p: before[LANDED, p], arrived_ref, gathered)
+    add_arrived(lambda p: before[LANDED, p], arrived_ref, local_ref, gathered)
     tiles = final_ref.shape[0]
     for t in range(tiles):
-        final_ref[t] = (gathered[t] + local_ref[t]).astype(jnp.bfloat16)
+        final_ref[t] = gathered[t].astype(jnp.bfloat16)
     low_ref[0] = final_ref[0]
     high_ref[0] = final_ref[tiles - 1]
 

time: 305 us -> 305 us (level)
  no operation moved by 1% of the time
where the time goes in v10:
time: 305 us; the launch traced here: 303 us
  waiting for transfers between devices  154 us (50%)
  starting transfers between devices  81.2 us (27%)
  Pallas kernels  60.1 us (20%)
  local copies, waits for them, and re-layouts  6.12 us (2%)
    ppermute x7, waiting for transfers between devices, body(): wblk = onward(wblk)  85.8 us
    all_to_all x8, waiting for transfers between devices, body(): lax.all_to_all(out, 'tile', split_axis=0, concat_axis=0, tiled=True)  62.6 us
    all_to_all x8, starting transfers between devices, body(): lax.all_to_all(out, 'tile', split_axis=0, concat_axis=0, tiled=True)  56.2 us
    pallas_call x8, Pallas kernels, keep(): pl.pallas_call(keep_body, out_shape=pltpu.VMEM((tiles, rows, points), jnp...  30 us
    ppermute x8, starting transfers between devices, body(): given = table = onward(table)  15.3 us
    pallas_call x7, Pallas kernels, send(): pl.pallas_call(send_body, out_shape=(pltpu.HBM((peers, rows, points), jnp...  14.3 us
    pallas_call x7, Pallas kernels, fetch(): pl.pallas_call(fetch_body, out_shape=(pltpu.VMEM((tiles, nnz - 1, points,...  8.75 us
  transfers between devices with their start and end apart: 25, of which 17 were waited for; matrix products, arithmetic and copies ran while one was open for 0% of the time, Pallas kernels for 14%

profile of v10, /device:TPU:56, one launch (start us, length us, event | category | flops | bytes accessed | tf_op | source)
XLA Modules:
  0.0 303.5 jit_solution(14212840740082289560)
XLA Ops:
  0.6 3.1 %shard_map.50 = (bf16[32,144,128]{2,1,0:T(8,128)(2,1)}, bf16[16,128,128]{2,1,0:T(8,128)(2,1)}) custom-call(s32[3,1,16]{2,1,0:T(1,128)} %bitcast.15, bf16[16,128,128]{2,1,0:T(8,128)(2,1)} %bitcast.14, bf16[16,3,128,128]{3,2,1,0:T(8,128)(2,1)} %bitcast.2.blocks_ref), custom_call_target="tpu_custom_call" | custom-call | flops 134217728 | bytes 4194304 | tf_op jit(solution)/shard_map/pallas_call | solution.py:96
  3.8 11.0 %all-to-all-start = ((bf16[32,144,128]{2,1,0:T(8,128)(2,1)}), bf16[32,144,128]{2,1,0:T(8,128)(2,1)S(1)}, u32[]{:S(2)}, u32[]{:S(2)}) async-start(bf16[32,144,128]{2,1,0:T(8,128)(2,1)} %get-tuple-element.57), calls=%async_computation | async-start | bytes 2359296 | tf_op jit(solution)/shard_map/all_to_all | solution.py:397
  14.8 1.6 collective-permute-start.8
  17.3 1.2 collective-permute-start
  18.5 3.7 %shard_map.52.local_ref = f32[16,128,128]{2,1,0:T(8,128)S(1)} custom-call(s32[3,32]{1,0:T(4,128)S(1)} %pad_add_fusion.table, bf16[16,128,128]{2,1,0:T(8,128)(2,1)} %get-tuple-element.58.state_ref, bf16[16,3,128,128]{3,2,1,0:T(8,128)(2,1)} %bitcast.2.blocks_ref), custom_call_target="tpu_custom_call" | custom-call | flops 201326592 | bytes 4194304 | tf_op jit(solution)/shard_map/pallas_call | solution.py:245
  22.3 12.4 %collective-permute-done.8.blocks_ref = bf16[16,3,128,128]{3,2,1,0:T(8,128)(2,1)} collective-permute-done((bf16[16,3,128,128]{3,2,1,0:T(8,128)(2,1)}, bf16[16,3,128,128]{3,2,1,0:T(8,128)(2,1)}, u32[]{:S(2)}, u32[]{:S(2)}) %collective-permute-start.8) | collective-permute-done | bytes 1572896 | tf_op jit(solution)/shard_map/ppermute | solution.py:405
  35.3 1.2 shard_map.53
  36.6 8.3 %all-to-all-done.arrived_ref = bf16[32,144,128]{2,1,0:T(8,128)(2,1)S(1)} async-done(((bf16[32,144,128]{2,1,0:T(8,128)(2,1)}), bf16[32,144,128]{2,1,0:T(8,128)(2,1)S(1)}, u32[]{:S(2)}, u32[]{:S(2)}) %all-to-all-start) | async-done | bytes 1179680 | tf_op jit(solution)/shard_map/all_to_all | solution.py:397
  44.8 2.8 shard_map.54
  47.6 6.4 %all-to-all-start.1 = ((bf16[32,128,128]{2,1,0:T(8,128)(2,1)}), bf16[32,128,128]{2,1,0:T(8,128)(2,1)S(1)}, u32[]{:S(2)}, u32[]{:S(2)}) async-start(bf16[32,128,128]{2,1,0:T(8,128)(2,1)} %get-tuple-element.66), calls=%async_computation.1 | async-start | bytes 2097152 | tf_op jit(solution)/shard_map/all_to_all | solution.py:397
  55.2 2.4 collective-permute-start.1
  57.6 3.7 %shard_map.55.local_ref = f32[16,128,128]{2,1,0:T(8,128)S(1)} custom-call(s32[3,32]{1,0:T(4,128)S(1)} %pad_add_fusion.1.table, bf16[16,128,128]{2,1,0:T(8,128)(2,1)} %get-tuple-element.63.state_ref, bf16[16,3,128,128]{3,2,1,0:T(8,128)(2,1)} %collective-permute-done.8.blocks_ref), custom_call_target="tpu_custom_call" | custom-call | flops 201326592 | bytes 4194304 | tf_op jit(solution)/shard_map/pallas_call | solution.py:245
  61.4 11.4 %collective-permute-done.9.blocks_ref = bf16[16,3,128,128]{3,2,1,0:T(8,128)(2,1)} collective-permute-done((bf16[16,3,128,128]{3,2,1,0:T(8,128)(2,1)}, bf16[16,3,128,128]{3,2,1,0:T(8,128)(2,1)}, u32[]{:S(2)}, u32[]{:S(2)}) %collective-permute-start.9) | collective-permute-done | bytes 1572896 | tf_op jit(solution)/shard_map/ppermute | solution.py:405
  73.3 1.2 shard_map.56
  74.6 5.4 %all-to-all-done.1.arrived_ref = bf16[32,128,128]{2,1,0:T(8,128)(2,1)S(1)} async-done(((bf16[32,128,128]{2,1,0:T(8,128)(2,1)}), bf16[32,128,128]{2,1,0:T(8,128)(2,1)S(1)}, u32[]{:S(2)}, u32[]{:S(2)}) %all-to-all-start.1) | async-done | bytes 1048608 | tf_op jit(solution)/shard_map/all_to_all | solution.py:397
  80.0 1.9 shard_map.57
  82.0 6.5 %all-to-all-start.2 = ((bf16[32,128,128]{2,1,0:T(8,128)(2,1)}), bf16[32,128,128]{2,1,0:T(8,128)(2,1)S(1)}, u32[]{:S(2)}, u32[]{:S(2)}) async-start(bf16[32,128,128]{2,1,0:T(8,128)(2,1)} %get-tuple-element.72), calls=%async_computation.2 | async-start | bytes 2097152 | tf_op jit(solution)/shard_map/all_to_all | solution.py:397
  88.4 0.7 collective-permute-start.10
  89.1 2.2 collective-permute-start.2
  91.3 3.8 %shard_map.58.local_ref = f32[16,128,128]{2,1,0:T(8,128)S(1)} custom-call(s32[3,32]{1,0:T(4,128)S(1)} %copy-done.1, bf16[16,128,128]{2,1,0:T(8,128)(2,1)} %get-tuple-element.69.state_ref, bf16[16,3,128,128]{3,2,1,0:T(8,128)(2,1)} %collective-permute-done.9.blocks_ref), custom_call_target="tpu_custom_call" | custom-call | flops 201326592 | bytes 4194304 | tf_op jit(solution)/shard_map/pallas_call | solution.py:245
  95.1 12.3 %collective-permute-done.10.blocks_ref = bf16[16,3,128,128]{3,2,1,0:T(8,128)(2,1)} collective-permute-done((bf16[16,3,128,128]{3,2,1,0:T(8,128)(2,1)}, bf16[16,3,128,128]{3,2,1,0:T(8,128)(2,1)}, u32[]{:S(2)}, u32[]{:S(2)}) %collective-permute-start.10) | collective-permute-done | bytes 1572896 | tf_op jit(solution)/shard_map/ppermute | solution.py:405
  107.9 1.2 shard_map.59
  109.2 6.0 %all-to-all-done.2.arrived_ref = bf16[32,128,128]{2,1,0:T(8,128)(2,1)S(1)} async-done(((bf16[32,128,128]{2,1,0:T(8,128)(2,1)}), bf16[32,128,128]{2,1,0:T(8,128)(2,1)S(1)}, u32[]{:S(2)}, u32[]{:S(2)}) %all-to-all-start.2) | async-done | bytes 1048608 | tf_op jit(solution)/shard_map/all_to_all | solution.py:397
  115.2 1.9 shard_map.60
  117.2 6.5 %all-to-all-start.3 = ((bf16[32,128,128]{2,1,0:T(8,128)(2,1)}), bf16[32,128,128]{2,1,0:T(8,128)(2,1)S(1)}, u32[]{:S(2)}, u32[]{:S(2)}) async-start(bf16[32,128,128]{2,1,0:T(8,128)(2,1)} %get-tuple-element.78), calls=%async_computation.3 | async-start | bytes 2097152 | tf_op jit(solution)/shard_map/all_to_all | solution.py:397
  123.7 2.2 collective-permute-start.3
  126.0 3.7 %shard_map.61.local_ref = f32[16,128,128]{2,1,0:T(8,128)S(1)} custom-call(s32[3,32]{1,0:T(4,128)S(1)} %copy-done.3, bf16[16,128,128]{2,1,0:T(8,128)(2,1)} %get-tuple-element.75.state_ref, bf16[16,3,128,128]{3,2,1,0:T(8,128)(2,1)} %collective-permute-done.10.blocks_ref), custom_call_target="tpu_custom_call" | custom-call | flops 201326592 | bytes 4194304 | tf_op jit(solution)/shard_map/pallas_call | solution.py:245
  129.7 12.3 %collective-permute-done.11.blocks_ref = bf16[16,3,128,128]{3,2,1,0:T(8,128)(2,1)} collective-permute-done((bf16[16,3,128,128]{3,2,1,0:T(8,128)(2,1)}, bf16[16,3,128,128]{3,2,1,0:T(8,128)(2,1)}, u32[]{:S(2)}, u32[]{:S(2)}) %collective-permute-start.11) | collective-permute-done | bytes 1572896 | tf_op jit(solution)/shard_map/ppermute | solution.py:405
  142.6 1.2 shard_map.62
  143.8 5.8 %all-to-all-done.3.arrived_ref = bf16[32,128,128]{2,1,0:T(8,128)(2,1)S(1)} async-done(((bf16[32,128,128]{2,1,0:T(8,128)(2,1)}), bf16[32,128,128]{2,1,0:T(8,128)(2,1)S(1)}, u32[]{:S(2)}, u32[]{:S(2)}) %all-to-all-start.3) | async-done | bytes 1048608 | tf_op jit(solution)/shard_map/all_to_all | solution.py:397
  149.6 1.9 shard_map.63
  151.6 6.5 %all-to-all-start.4 = ((bf16[32,128,128]{2,1,0:T(8,128)(2,1)}), bf16[32,128,128]{2,1,0:T(8,128)(2,1)S(1)}, u32[]{:S(2)}, u32[]{:S(2)}) async-start(bf16[32,128,128]{2,1,0:T(8,128)(2,1)} %get-tuple-element.84), calls=%async_computation.4 | async-start | bytes 2097152 | tf_op jit(solution)/shard_map/all_to_all | solution.py:397
  158.4 2.2 collective-permute-start.4
  160.6 3.7 %shard_map.64.local_ref = f32[16,128,128]{2,1,0:T(8,128)S(1)} custom-call(s32[3,32]{1,0:T(4,128)S(1)} %copy-done.5, bf16[16,128,128]{2,1,0:T(8,128)(2,1)} %get-tuple-element.81.state_ref, bf16[16,3,128,128]{3,2,1,0:T(8,128)(2,1)} %collective-permute-done.11.blocks_ref), custom_call_target="tpu_custom_call" | custom-call | flops 201326592 | bytes 4194304 | tf_op jit(solution)/shard_map/pallas_call | solution.py:245
  164.3 12.3 %collective-permute-done.12.blocks_ref = bf16[16,3,128,128]{3,2,1,0:T(8,128)(2,1)} collective-permute-done((bf16[16,3,128,128]{3,2,1,0:T(8,128)(2,1)}, bf16[16,3,128,128]{3,2,1,0:T(8,128)(2,1)}, u32[]{:S(2)}, u32[]{:S(2)}) %collective-permute-start.12) | collective-permute-done | bytes 1572896 | tf_op jit(solution)/shard_map/ppermute | solution.py:405
  177.2 1.2 shard_map.65
  178.5 6.4 %all-to-all-done.4.arrived_ref = bf16[32,128,128]{2,1,0:T(8,128)(2,1)S(1)} async-done(((bf16[32,128,128]{2,1,0:T(8,128)(2,1)}), bf16[32,128,128]{2,1,0:T(8,128)(2,1)S(1)}, u32[]{:S(2)}, u32[]{:S(2)}) %all-to-all-start.4) | async-done | bytes 1048608 | tf_op jit(solution)/shard_map/all_to_all | solution.py:397
  184.8 1.9 shard_map.66
  186.8 6.4 %all-to-all-start.5 = ((bf16[32,128,128]{2,1,0:T(8,128)(2,1)}), bf16[32,128,128]{2,1,0:T(8,128)(2,1)S(1)}, u32[]{:S(2)}, u32[]{:S(2)}) async-start(bf16[32,128,128]{2,1,0:T(8,128)(2,1)} %get-tuple-element.90), calls=%async_computation.5 | async-start | bytes 2097152 | tf_op jit(solution)/shard_map/all_to_all | solution.py:397
  193.3 1.9 collective-permute-start.5
  195.2 3.7 %shard_map.67.local_ref = f32[16,128,128]{2,1,0:T(8,128)S(1)} custom-call(s32[3,32]{1,0:T(4,128)S(1)} %copy-done.7, bf16[16,128,128]{2,1,0:T(8,128)(2,1)} %get-tuple-element.87.state_ref, bf16[16,3,128,128]{3,2,1,0:T(8,128)(2,1)} %collective-permute-done.12.blocks_ref), custom_call_target="tpu_custom_call" | custom-call | flops 201326592 | bytes 4194304 | tf_op jit(solution)/shard_map/pallas_call | solution.py:245
  198.9 12.6 %collective-permute-done.13.blocks_ref = bf16[16,3,128,128]{3,2,1,0:T(8,128)(2,1)} collective-permute-done((bf16[16,3,128,128]{3,2,1,0:T(8,128)(2,1)}, bf16[16,3,128,128]{3,2,1,0:T(8,128)(2,1)}, u32[]{:S(2)}, u32[]{:S(2)}) %collective-permute-start.13) | collective-permute-done | bytes 1572896 | tf_op jit(solution)/shard_map/ppermute | solution.py:405
  212.1 1.2 shard_map.68
  213.3 5.9 %all-to-all-done.5.arrived_ref = bf16[32,128,128]{2,1,0:T(8,128)(2,1)S(1)} async-done(((bf16[32,128,128]{2,1,0:T(8,128)(2,1)}), bf16[32,128,128]{2,1,0:T(8,128)(2,1)S(1)}, u32[]{:S(2)}, u32[]{:S(2)}) %all-to-all-start.5) | async-done | bytes 1048608 | tf_op jit(solution)/shard_map/all_to_all | solution.py:397
  219.3 1.9 shard_map.69
  221.2 6.4 %all-to-all-start.6 = ((bf16[32,128,128]{2,1,0:T(8,128)(2,1)}), bf16[32,128,128]{2,1,0:T(8,128)(2,1)S(1)}, u32[]{:S(2)}, u32[]{:S(2)}) async-start(bf16[32,128,128]{2,1,0:T(8,128)(2,1)} %get-tuple-element.96), calls=%async_computation.6 | async-start | bytes 2097152 | tf_op jit(solution)/shard_map/all_to_all | solution.py:397
  227.9 1.9 collective-permute-start.6
  229.8 3.7 %shard_map.70.local_ref = f32[16,128,128]{2,1,0:T(8,128)S(1)} custom-call(s32[3,32]{1,0:T(4,128)S(1)} %copy-done.9, bf16[16,128,128]{2,1,0:T(8,128)(2,1)} %get-tuple-element.93.state_ref, bf16[16,3,128,128]{3,2,1,0:T(8,128)(2,1)} %collective-permute-done.13.blocks_ref), custom_call_target="tpu_custom_call" | custom-call | flops 201326592 | bytes 4194304 | tf_op jit(solution)/shard_map/pallas_call | solution.py:245
  233.6 12.6 %collective-permute-done.14.blocks_ref = bf16[16,3,128,128]{3,2,1,0:T(8,128)(2,1)S(1)} collective-permute-done((bf16[16,3,128,128]{3,2,1,0:T(8,128)(2,1)}, bf16[16,3,128,128]{3,2,1,0:T(8,128)(2,1)S(1)}, u32[]{:S(2)}, u32[]{:S(2)}) %collective-permute-start.14) | collective-permute-done | bytes 1572896 | tf_op jit(solution)/shard_map/ppermute | solution.py:405
  246.1 1.2 copy-done.12
  247.9 1.2 shard_map.71
  249.1 5.0 %all-to-all-done.6.arrived_ref = bf16[32,128,128]{2,1,0:T(8,128)(2,1)S(1)} async-done(((bf16[32,128,128]{2,1,0:T(8,128)(2,1)}), bf16[32,128,128]{2,1,0:T(8,128)(2,1)S(1)}, u32[]{:S(2)}, u32[]{:S(2)}) %all-to-all-start.6) | async-done | bytes 1048608 | tf_op jit(solution)/shard_map/all_to_all | solution.py:397
  254.2 1.9 shard_map.72
  256.1 6.4 %all-to-all-start.7 = ((bf16[32,128,128]{2,1,0:T(8,128)(2,1)}), bf16[32,128,128]{2,1,0:T(8,128)(2,1)S(1)}, u32[]{:S(2)}, u32[]{:S(2)}) async-start(bf16[32,128,128]{2,1,0:T(8,128)(2,1)} %get-tuple-element.99), calls=%async_computation.7 | async-start | bytes 2097152 | tf_op jit(solution)/shard_map/all_to_all | solution.py:397
  262.6 1.1 collective-permute-start.7
  263.7 1.3 collective-permute-done.7.table_ref
  265.6 0.7 shard_map.51.before
  266.3 3.8 %shard_map.73.local_ref = f32[16,128,128]{2,1,0:T(8,128)S(1)} custom-call(s32[3,32]{1,0:T(4,128)S(1)} %copy-done.11, bf16[16,128,128]{2,1,0:T(8,128)(2,1)} %get-tuple-element.100.state_ref, bf16[16,3,128,128]{3,2,1,0:T(8,128)(2,1)} %copy-done.12), custom_call_target="tpu_custom_call" | custom-call | flops 201326592 | bytes 4194304 | tf_op jit(solution)/shard_map/pallas_call | solution.py:245
  270.0 19.7 %all-to-all-done.7.arrived_ref = bf16[32,128,128]{2,1,0:T(8,128)(2,1)S(1)} async-done(((bf16[32,128,128]{2,1,0:T(8,128)(2,1)}), bf16[32,128,128]{2,1,0:T(8,128)(2,1)S(1)}, u32[]{:S(2)}, u32[]{:S(2)}) %all-to-all-start.7) | async-done | bytes 1048608 | tf_op jit(solution)/shard_map/all_to_all | solution.py:397
  290.2 4.3 %collective-permute-start.15 = (bf16[1,128,128]{2,1,0:T(8,128)(2,1)S(1)}, bf16[1,128,128]{2,1,0:T(8,128)(2,1)S(1)}, u32[]{:S(2)}, u32[]{:S(2)}) collective-permute-start(bf16[1,128,128]{2,1,0:T(8,128)(2,1)S(1)} %get-tuple-element.102), channel_id=1, source_target_pairs={{0,1},{1,2},{2,3},{3,4},{4,5},{5,6},{6,7},{7,8},{8,9},{9,10},{10,1... | collective-permute-start | bytes 98312 | tf_op jit(solution)/shard_map/ppermute | solution.py:409
  294.5 1.9 collective-permute-start.16
  296.5 2.0 shard_map.75
  298.5 4.0 %collective-permute-done.16.high_ref = bf16[1,128,128]{2,1,0:T(8,128)(2,1)S(1)} collective-permute-done((bf16[1,128,128]{2,1,0:T(8,128)(2,1)S(1)}, bf16[1,128,128]{2,1,0:T(8,128)(2,1)S(1)}, u32[]{:S(2)}, u32[]{:S(2)}) %collective-permute-start.16) | collective-permute-done | bytes 32800 | tf_op jit(solution)/shard_map/ppermute | solution.py:410
  302.4 0.9 shard_map.76
  (64 shorter events, 7.6 us)
Async XLA Ops:
  3.8 12.7 %copy-start.13 = (s32[1,16,3]{1,0,2:T(1,128)S(1)}, s32[1,16,3]{1,0,2:T(1,128)}, u32[]{:S(2)}) copy-start(s32[1,16,3]{1,0,2:T(1,128)} %param.5) | copy-start | bytes 580
  3.8 41.0 %all-to-all-start = ((bf16[32,144,128]{2,1,0:T(8,128)(2,1)}), bf16[32,144,128]{2,1,0:T(8,128)(2,1)S(1)}, u32[]{:S(2)}, u32[]{:S(2)}) async-start(bf16[32,144,128]{2,1,0:T(8,128)(2,1)} %get-tuple-element.57), calls=%async_computation | async-start | bytes 2359296 | tf_op jit(solution)/shard_map/all_to_all | solution.py:397
  14.8 19.9 %collective-permute-start.8 = (bf16[16,3,128,128]{3,2,1,0:T(8,128)(2,1)}, bf16[16,3,128,128]{3,2,1,0:T(8,128)(2,1)}, u32[]{:S(2)}, u32[]{:S(2)}) collective-permute-start(bf16[16,3,128,128]{3,2,1,0:T(8,128)(2,1)} %bitcast.2.blocks_ref), channel_id=1, source_target_pairs={{0,224},{32,0},{64,32},{96,64},{128,96},{160,128},{192,160},{224,1... | collective-permute-start | bytes 4718600 | tf_op jit(solution)/shard_map/ppermute | solution.py:405
  17.3 17.5 %collective-permute-start = (s32[3,32]{1,0:T(4,128)S(1)}, s32[3,32]{1,0:T(4,128)S(1)}, u32[]{:S(2)}, u32[]{:S(2)}) collective-permute-start(s32[3,32]{1,0:T(4,128)S(1)} %pad_add_fusion.table), channel_id=1, source_target_pairs={{0,224},{32,0},{64,32},{96,64},{128,96},{160,128},{192,160},{224,1... | collective-permute-start | bytes 1160 | tf_op jit(solution)/shard_map/ppermute | solution.py:399
  34.7 0.6 copy-start.14
  47.6 7.6 %slice-start = ((s32[3,32]{1,0:T(4,128)}), s32[2,32]{1,0:T(2,128)S(1)}, s32[]{:S(2)}) async-start(s32[3,32]{1,0:T(4,128)} %copy-done.14), calls=%async_computation.8 | async-start | bytes 2048 | tf_op jit(solution)/shard_map/slice | solution.py:403
  47.6 32.4 %all-to-all-start.1 = ((bf16[32,128,128]{2,1,0:T(8,128)(2,1)}), bf16[32,128,128]{2,1,0:T(8,128)(2,1)S(1)}, u32[]{:S(2)}, u32[]{:S(2)}) async-start(bf16[32,128,128]{2,1,0:T(8,128)(2,1)} %get-tuple-element.66), calls=%async_computation.1 | async-start | bytes 2097152 | tf_op jit(solution)/shard_map/all_to_all | solution.py:397
  54.1 18.7 %collective-permute-start.9 = (bf16[16,3,128,128]{3,2,1,0:T(8,128)(2,1)}, bf16[16,3,128,128]{3,2,1,0:T(8,128)(2,1)}, u32[]{:S(2)}, u32[]{:S(2)}) collective-permute-start(bf16[16,3,128,128]{3,2,1,0:T(8,128)(2,1)} %collective-permute-done.8.blocks_ref), channel_id=1, source_target_pairs={{0,224},{32,0},{64,32},{96,64},{128,96},{160,128},{192,160},{224,1... | collective-permute-start | bytes 4718600 | tf_op jit(solution)/shard_map/ppermute | solution.py:405
  55.2 17.6 %collective-permute-start.1 = (s32[3,32]{1,0:T(4,128)S(1)}, s32[3,32]{1,0:T(4,128)S(1)}, u32[]{:S(2)}, u32[]{:S(2)}) collective-permute-start(s32[3,32]{1,0:T(4,128)S(1)} %pad_add_fusion.1.table), channel_id=1, source_target_pairs={{0,224},{32,0},{64,32},{96,64},{128,96},{160,128},{192,160},{224,1... | collective-permute-start | bytes 1160 | tf_op jit(solution)/shard_map/ppermute | solution.py:399
  72.8 0.6 copy-start
  81.9 7.2 %copy-start.1 = (s32[3,32]{1,0:T(4,128)S(1)}, s32[3,32]{1,0:T(4,128)}, u32[]{:S(2)}) copy-start(s32[3,32]{1,0:T(4,128)} %copy-done) | copy-start | bytes 1156
  82.0 33.3 %all-to-all-start.2 = ((bf16[32,128,128]{2,1,0:T(8,128)(2,1)}), bf16[32,128,128]{2,1,0:T(8,128)(2,1)S(1)}, u32[]{:S(2)}, u32[]{:S(2)}) async-start(bf16[32,128,128]{2,1,0:T(8,128)(2,1)} %get-tuple-element.72), calls=%async_computation.2 | async-start | bytes 2097152 | tf_op jit(solution)/shard_map/all_to_all | solution.py:397
  88.4 18.9 %collective-permute-start.10 = (bf16[16,3,128,128]{3,2,1,0:T(8,128)(2,1)}, bf16[16,3,128,128]{3,2,1,0:T(8,128)(2,1)}, u32[]{:S(2)}, u32[]{:S(2)}) collective-permute-start(bf16[16,3,128,128]{3,2,1,0:T(8,128)(2,1)} %collective-permute-done.9.blocks_ref), channel_id=1, source_target_pairs={{0,224},{32,0},{64,32},{96,64},{128,96},{160,128},{192,160},{224,1... | collective-permute-start | bytes 4718600 | tf_op jit(solution)/shard_map/ppermute | solution.py:405
  89.1 18.3 %collective-permute-start.2 = (s32[3,32]{1,0:T(4,128)S(1)}, s32[3,32]{1,0:T(4,128)S(1)}, u32[]{:S(2)}, u32[]{:S(2)}) collective-permute-start(s32[3,32]{1,0:T(4,128)S(1)} %copy-done.1), channel_id=1, source_target_pairs={{0,224},{32,0},{64,32},{96,64},{128,96},{160,128},{192,160},{224,1... | collective-permute-start | bytes 1160 | tf_op jit(solution)/shard_map/ppermute | solution.py:399
  107.4 0.6 copy-start.2
  117.2 6.6 %copy-start.3 = (s32[3,32]{1,0:T(4,128)S(1)}, s32[3,32]{1,0:T(4,128)}, u32[]{:S(2)}) copy-start(s32[3,32]{1,0:T(4,128)} %copy-done.2) | copy-start | bytes 1156
  117.2 32.4 %all-to-all-start.3 = ((bf16[32,128,128]{2,1,0:T(8,128)(2,1)}), bf16[32,128,128]{2,1,0:T(8,128)(2,1)S(1)}, u32[]{:S(2)}, u32[]{:S(2)}) async-start(bf16[32,128,128]{2,1,0:T(8,128)(2,1)} %get-tuple-element.78), calls=%async_computation.3 | async-start | bytes 2097152 | tf_op jit(solution)/shard_map/all_to_all | solution.py:397
  123.6 18.3 %collective-permute-start.11 = (bf16[16,3,128,128]{3,2,1,0:T(8,128)(2,1)}, bf16[16,3,128,128]{3,2,1,0:T(8,128)(2,1)}, u32[]{:S(2)}, u32[]{:S(2)}) collective-permute-start(bf16[16,3,128,128]{3,2,1,0:T(8,128)(2,1)} %collective-permute-done.10.blocks_ref), channel_id=1, source_target_pairs={{0,224},{32,0},{64,32},{96,64},{128,96},{160,128},{192,160},{224,1... | collective-permute-start | bytes 4718600 | tf_op jit(solution)/shard_map/ppermute | solution.py:405
  123.7 18.3 %collective-permute-start.3 = (s32[3,32]{1,0:T(4,128)S(1)}, s32[3,32]{1,0:T(4,128)S(1)}, u32[]{:S(2)}, u32[]{:S(2)}) collective-permute-start(s32[3,32]{1,0:T(4,128)S(1)} %copy-done.3), channel_id=1, source_target_pairs={{0,224},{32,0},{64,32},{96,64},{128,96},{160,128},{192,160},{224,1... | collective-permute-start | bytes 1160 | tf_op jit(solution)/shard_map/ppermute | solution.py:399
  142.0 0.6 copy-start.4
  151.6 6.8 %copy-start.5 = (s32[3,32]{1,0:T(4,128)S(1)}, s32[3,32]{1,0:T(4,128)}, u32[]{:S(2)}) copy-start(s32[3,32]{1,0:T(4,128)} %copy-done.4) | copy-start | bytes 1156
  151.6 33.3 %all-to-all-start.4 = ((bf16[32,128,128]{2,1,0:T(8,128)(2,1)}), bf16[32,128,128]{2,1,0:T(8,128)(2,1)S(1)}, u32[]{:S(2)}, u32[]{:S(2)}) async-start(bf16[32,128,128]{2,1,0:T(8,128)(2,1)} %get-tuple-element.84), calls=%async_computation.4 | async-start | bytes 2097152 | tf_op jit(solution)/shard_map/all_to_all | solution.py:397
  158.0 18.6 %collective-permute-start.12 = (bf16[16,3,128,128]{3,2,1,0:T(8,128)(2,1)}, bf16[16,3,128,128]{3,2,1,0:T(8,128)(2,1)}, u32[]{:S(2)}, u32[]{:S(2)}) collective-permute-start(bf16[16,3,128,128]{3,2,1,0:T(8,128)(2,1)} %collective-permute-done.11.blocks_ref), channel_id=1, source_target_pairs={{0,224},{32,0},{64,32},{96,64},{128,96},{160,128},{192,160},{224,1... | collective-permute-start | bytes 4718600 | tf_op jit(solution)/shard_map/ppermute | solution.py:405
  158.4 18.3 %collective-permute-start.4 = (s32[3,32]{1,0:T(4,128)S(1)}, s32[3,32]{1,0:T(4,128)S(1)}, u32[]{:S(2)}, u32[]{:S(2)}) collective-permute-start(s32[3,32]{1,0:T(4,128)S(1)} %copy-done.5), channel_id=1, source_target_pairs={{0,224},{32,0},{64,32},{96,64},{128,96},{160,128},{192,160},{224,1... | collective-permute-start | bytes 1160 | tf_op jit(solution)/shard_map/ppermute | solution.py:399
  176.6 0.6 copy-start.6
  186.8 6.5 %copy-start.7 = (s32[3,32]{1,0:T(4,128)S(1)}, s32[3,32]{1,0:T(4,128)}, u32[]{:S(2)}) copy-start(s32[3,32]{1,0:T(4,128)} %copy-done.6) | copy-start | bytes 1156
  186.8 32.5 %all-to-all-start.5 = ((bf16[32,128,128]{2,1,0:T(8,128)(2,1)}), bf16[32,128,128]{2,1,0:T(8,128)(2,1)S(1)}, u32[]{:S(2)}, u32[]{:S(2)}) async-start(bf16[32,128,128]{2,1,0:T(8,128)(2,1)} %get-tuple-element.90), calls=%async_computation.5 | async-start | bytes 2097152 | tf_op jit(solution)/shard_map/all_to_all | solution.py:397
  193.2 18.3 %collective-permute-start.13 = (bf16[16,3,128,128]{3,2,1,0:T(8,128)(2,1)}, bf16[16,3,128,128]{3,2,1,0:T(8,128)(2,1)}, u32[]{:S(2)}, u32[]{:S(2)}) collective-permute-start(bf16[16,3,128,128]{3,2,1,0:T(8,128)(2,1)} %collective-permute-done.12.blocks_ref), channel_id=1, source_target_pairs={{0,224},{32,0},{64,32},{96,64},{128,96},{160,128},{192,160},{224,1... | collective-permute-start | bytes 4718600 | tf_op jit(solution)/shard_map/ppermute | solution.py:405
  193.3 18.2 %collective-permute-start.5 = (s32[3,32]{1,0:T(4,128)S(1)}, s32[3,32]{1,0:T(4,128)S(1)}, u32[]{:S(2)}, u32[]{:S(2)}) collective-permute-start(s32[3,32]{1,0:T(4,128)S(1)} %copy-done.7), channel_id=1, source_target_pairs={{0,224},{32,0},{64,32},{96,64},{128,96},{160,128},{192,160},{224,1... | collective-permute-start | bytes 1160 | tf_op jit(solution)/shard_map/ppermute | solution.py:399
  211.5 0.6 copy-start.8
  221.2 6.7 %copy-start.9 = (s32[3,32]{1,0:T(4,128)S(1)}, s32[3,32]{1,0:T(4,128)}, u32[]{:S(2)}) copy-start(s32[3,32]{1,0:T(4,128)} %copy-done.8) | copy-start | bytes 1156
  221.2 32.9 %all-to-all-start.6 = ((bf16[32,128,128]{2,1,0:T(8,128)(2,1)}), bf16[32,128,128]{2,1,0:T(8,128)(2,1)S(1)}, u32[]{:S(2)}, u32[]{:S(2)}) async-start(bf16[32,128,128]{2,1,0:T(8,128)(2,1)} %get-tuple-element.96), calls=%async_computation.6 | async-start | bytes 2097152 | tf_op jit(solution)/shard_map/all_to_all | solution.py:397
  227.7 18.5 %collective-permute-start.14 = (bf16[16,3,128,128]{3,2,1,0:T(8,128)(2,1)}, bf16[16,3,128,128]{3,2,1,0:T(8,128)(2,1)S(1)}, u32[]{:S(2)}, u32[]{:S(2)}) collective-permute-start(bf16[16,3,128,128]{3,2,1,0:T(8,128)(2,1)} %collective-permute-done.13.blocks_ref), channel_id=1, source_target_pairs={{0,224},{32,0},{64,32},{96,64},{128,96},{160,128},{192,160},{224,1... | collective-permute-start | bytes 4718600 | tf_op jit(solution)/shard_map/ppermute | solution.py:405
  227.9 18.3 %collective-permute-start.6 = (s32[3,32]{1,0:T(4,128)S(1)}, s32[3,32]{1,0:T(4,128)S(1)}, u32[]{:S(2)}, u32[]{:S(2)}) collective-permute-start(s32[3,32]{1,0:T(4,128)S(1)} %copy-done.9), channel_id=1, source_target_pairs={{0,224},{32,0},{64,32},{96,64},{128,96},{160,128},{192,160},{224,1... | collective-permute-start | bytes 1160 | tf_op jit(solution)/shard_map/ppermute | solution.py:399
  246.1 1.2 copy-start.12
  247.3 0.6 copy-start.10
  256.1 6.5 %copy-start.11 = (s32[3,32]{1,0:T(4,128)S(1)}, s32[3,32]{1,0:T(4,128)}, u32[]{:S(2)}) copy-start(s32[3,32]{1,0:T(4,128)} %copy-done.10) | copy-start | bytes 1156
  256.1 33.7 %all-to-all-start.7 = ((bf16[32,128,128]{2,1,0:T(8,128)(2,1)}), bf16[32,128,128]{2,1,0:T(8,128)(2,1)S(1)}, u32[]{:S(2)}, u32[]{:S(2)}) async-start(bf16[32,128,128]{2,1,0:T(8,128)(2,1)} %get-tuple-element.99), calls=%async_computation.7 | async-start | bytes 2097152 | tf_op jit(solution)/shard_map/all_to_all | solution.py:397
  262.6 2.4 collective-permute-start.7
  265.0 0.6 copy-start.15
  290.2 8.3 %collective-permute-start.15 = (bf16[1,128,128]{2,1,0:T(8,128)(2,1)S(1)}, bf16[1,128,128]{2,1,0:T(8,128)(2,1)S(1)}, u32[]{:S(2)}, u32[]{:S(2)}) collective-permute-start(bf16[1,128,128]{2,1,0:T(8,128)(2,1)S(1)} %get-tuple-element.102), channel_id=1, source_target_pairs={{0,1},{1,2},{2,3},{3,4},{4,5},{5,6},{6,7},{7,8},{8,9},{9,10},{10,1... | collective-permute-start | bytes 98312 | tf_op jit(solution)/shard_map/ppermute | solution.py:409
  294.5 7.9 %collective-permute-start.16 = (bf16[1,128,128]{2,1,0:T(8,128)(2,1)S(1)}, bf16[1,128,128]{2,1,0:T(8,128)(2,1)S(1)}, u32[]{:S(2)}, u32[]{:S(2)}) collective-permute-start(bf16[1,128,128]{2,1,0:T(8,128)(2,1)S(1)} %get-tuple-element.103), channel_id=1, source_target_pairs={{1,0},{2,1},{3,2},{4,3},{5,4},{6,5},{7,6},{8,7},{9,8},{10,9},{11,1... | collective-permute-start | bytes 98312 | tf_op jit(solution)/shard_map/ppermute | solution.py:410
